TPU v7x, 32 devices: a whole 2x2x4 slice. The times are simulated.
32 devices in a mesh: dp: 4 (over y, core), seq: 8 (over z, x).
Axes of the slice: x: 2, y: 2, z: 4, core: 2. Of those that a mesh axis runs over, the one named last changes fastest.
Arguments:
- tokens: bfloat16 [8, 1024, 2048], P('dp', 'seq'), may hold values from -6 to 6
- lengths: int32 [8], P('dp'), may hold values from 256 to 1024, as said below
- cotangent: bfloat16 [8, 1024, 2048], P('dp', 'seq'), may hold values from -6 to 6
- mixer_gain: bfloat16 [2048], P(('dp', 'seq')), may hold values from 0.5 to 1.5
- feed_gain: bfloat16 [2048], P(('dp', 'seq')), may hold values from 0.5 to 1.5
- head_gain: bfloat16 [512], P(('dp', 'seq')), may hold values from 0.5 to 1.5
- w_query: bfloat16 [2048, 2048], P(('dp', 'seq')), may hold values from -0.25 to 0.25
- w_key: bfloat16 [2048, 2048], P(('dp', 'seq')), may hold values from -0.25 to 0.25
- w_value: bfloat16 [2048, 2048], P(('dp', 'seq')), may hold values from -0.125 to 0.125
- w_gate: bfloat16 [2048, 2048], P(('dp', 'seq')), may hold values from -0.125 to 0.125
- w_out: bfloat16 [2048, 2048], P(('dp', 'seq')), may hold values from -0.125 to 0.125
- rank_down: bfloat16 [2048, 16], P(('dp', 'seq')), may hold values from -0.125 to 0.125
- rank_up: bfloat16 [256, 16], P(('dp', 'seq')), may hold values from -1.5 to 1.5
- rank_bias: bfloat16 [256], P(('dp', 'seq')), may hold values from -1 to 9
- w_act: bfloat16 [5632, 2048], P(('dp', 'seq')), may hold values from -0.125 to 0.125
- w_lin: bfloat16 [5632, 2048], P(('dp', 'seq')), may hold values from -0.125 to 0.125
- w_down: bfloat16 [5632, 2048], P(('dp', 'seq')), may hold values from -0.078125 to 0.078125
Outputs:
- block_out: bfloat16 [8, 1024, 2048], P('dp', 'seq')
- tokens_grad: float32 [8, 1024, 2048], P('dp', 'seq')
- mixer_gain_grad: float32 [2048], P(('dp', 'seq'))
- feed_gain_grad: float32 [2048], P(('dp', 'seq'))
- head_gain_grad: float32 [512], P(('dp', 'seq'))
- w_query_grad: float32 [2048, 2048], P(('dp', 'seq'))
- w_key_grad: float32 [2048, 2048], P(('dp', 'seq'))
- w_value_grad: float32 [2048, 2048], P(('dp', 'seq'))
- w_gate_grad: float32 [2048, 2048], P(('dp', 'seq'))
- w_out_grad: float32 [2048, 2048], P(('dp', 'seq'))
- rank_down_grad: float32 [2048, 16], P(('dp', 'seq'))
- rank_up_grad: float32 [256, 16], P(('dp', 'seq'))
- rank_bias_grad: float32 [256], P(('dp', 'seq'))
- w_act_grad: float32 [5632, 2048], P(('dp', 'seq'))
- w_lin_grad: float32 [5632, 2048], P(('dp', 'seq'))
- w_down_grad: float32 [5632, 2048], P(('dp', 'seq'))
Inputs may be any that keep to these rules, and one draw needn't show every extreme that they name: `lengths`: in each group of 2 sequences on one index of dp, one sequence, which one drawn from the seed, has all 1024 tokens live; live tokens come first in every sequence.
All inputs are finite; a program needn't handle non-finite values.
Results may differ from a plain program's by a relative error of at most 0.017.
Values may be sent and summed in bfloat16 or wider, within the bound.
A program may use at most 648 MiB of HBM per device.

v0:
```python
import jax
import jax.numpy as jnp
from jax import lax
from jax.sharding import PartitionSpec as P

HEADS = 4
SLOTS = 64
BLOCK = 64


EPS = 1e-06
GATE_NORM = 8.0
PRECISION_LEVEL = lax.Precision.HIGHEST


def entering(value, axis, join, neutral):
    count, mine = (lax.axis_size(axis), lax.axis_index(axis))
    pieces = jax.tree.map(lambda part: lax.all_gather(part, axis), value)
    running = jax.tree.map(
        lambda part, zero: jnp.full_like(part, 0) + jnp.asarray(zero, part.dtype), value, neutral
    )

    def entering_turn(position, running):
        longer = join(running, jax.tree.map(lambda part: part[position], pieces))
        return jax.tree.map(lambda new, old: jnp.where(position < mine, new, old), longer, running)

    return lax.fori_loop(0, count - 1, entering_turn, running)


def prefix(x, axis, combine, identity):
    devices, position = (lax.axis_size(axis), lax.axis_index(axis))
    everything = jax.tree.map(
        lambda part, kind: lax.all_gather(part.astype(kind), axis),
        x,
        jax.tree.map(lambda a: jnp.bfloat16 if a.dtype == jnp.float32 else a.dtype, x),
    )
    start = jax.tree.map(
        lambda part, zero: jnp.broadcast_to(jnp.asarray(zero, part.dtype), part.shape), x, identity
    )

    def prefix_turn(k, before):
        at = devices - 1 - k
        reached = at > position
        new = combine(
            before, jax.tree.map(lambda part, own: part[at].astype(own.dtype), everything, x)
        )
        return jax.tree.map(lambda a, b: jnp.where(reached, a, b), new, before)

    return lax.fori_loop(0, devices, prefix_turn, start)


def rms_scale(tensor):
    return lax.rsqrt(jnp.mean(tensor * tensor, axis=-1, keepdims=True) + EPS)


def norm_apply(tensor, gain):
    return tensor * rms_scale(tensor) * gain


def contract_last(former, latter):
    return lax.dot_general(
        former, latter, (((1,), (1,)), ((), ())), preferred_element_type=jnp.float32
    )


def contract_first(former, latter):
    return lax.dot_general(
        former, latter, (((0,), (0,)), ((), ())), preferred_element_type=jnp.float32
    )


def swish_slope(tensor):
    sigma = jax.nn.sigmoid(tensor)
    return sigma * (1.0 + tensor * (1.0 - sigma))


def slot_block(states, inputs):
    key_memory_state, value_memory_state = states
    queries, key_features, value_features, log_decay = inputs
    block_len = queries.shape[1]
    scaling = queries.shape[2] ** (-0.5)
    running = jnp.cumsum(log_decay, axis=1)
    writes = -jnp.expm1(log_decay)
    causal = (jnp.arange(block_len)[:, None] >= jnp.arange(block_len)[None, :])[None, :, :, None]
    spread = running[:, :, None, :] - running[:, None, :, :]
    weight = jnp.where(causal, jnp.exp(jnp.where(causal, spread, 0.0)), 0.0) * writes[:, None, :, :]
    pair_dots = (
        jnp.einsum("htd,hid->hti", queries, key_features, precision=PRECISION_LEVEL) * scaling
    )
    carried = (
        jnp.einsum("htd,hjd->htj", queries, key_memory_state, precision=PRECISION_LEVEL) * scaling
    )
    growth = jnp.exp(running)
    scores = growth * carried + jnp.einsum(
        "hti,htij->htj", pair_dots, weight, precision=PRECISION_LEVEL
    )
    attend = jax.nn.softmax(scores, axis=-1)
    mixing = jnp.einsum("htj,htij->hti", attend, weight, precision=PRECISION_LEVEL)
    output = jnp.einsum(
        "htj,hjd->htd", attend * growth, value_memory_state, precision=PRECISION_LEVEL
    )
    output = output + jnp.einsum("hti,hid->htd", mixing, value_features, precision=PRECISION_LEVEL)
    last_total = running[:, -1, :]
    decay_factor = jnp.exp(last_total[:, None, :] - running) * writes
    retain_fraction = jnp.exp(last_total)[:, :, None]
    next_key_state = retain_fraction * key_memory_state + jnp.einsum(
        "gov,goy->gvy", decay_factor, key_features, precision=PRECISION_LEVEL
    )
    next_value_state = retain_fraction * value_memory_state + jnp.einsum(
        "gov,goy->gvy", decay_factor, value_features, precision=PRECISION_LEVEL
    )
    return ((next_key_state, next_value_state), output)


def run_member(member):
    queries, key_features, value_features, log_decay, key_in, value_in = member
    states, output = lax.scan(
        slot_block, (key_in, value_in), (queries, key_features, value_features, log_decay)
    )
    return (output, states[0], states[1])


def slot_pieces(queries, key_features, value_features, log_decay, key_in, value_in):
    return lax.map(
        jax.checkpoint(run_member),
        (queries, key_features, value_features, log_decay, key_in, value_in),
    )


def to_blocks(tensor, seq_count):
    tensor = tensor.reshape(seq_count, -1, BLOCK, tensor.shape[1], tensor.shape[2])
    return tensor.transpose(0, 1, 3, 2, 4)


def from_blocks(tensor):
    tensor = tensor.transpose(0, 1, 3, 2, 4)
    return tensor.reshape(-1, tensor.shape[3], tensor.shape[4])


def piece_summary(key_features, value_features, log_decay, seq_count):
    key_seq = key_features.reshape(seq_count, -1, key_features.shape[1], key_features.shape[2])
    value_seq = value_features.reshape(
        seq_count, -1, value_features.shape[1], value_features.shape[2]
    )
    decay_seq = log_decay.reshape(seq_count, -1, log_decay.shape[1], log_decay.shape[2])
    running = jnp.cumsum(decay_seq, axis=1)
    last_total = running[:, -1]
    decay_factor = jnp.exp(last_total[:, None] - running) * -jnp.expm1(decay_seq)
    key_sum = jnp.einsum("schm,schd->shmd", decay_factor, key_seq, precision=PRECISION_LEVEL)
    value_sum = jnp.einsum("schm,schd->shmd", decay_factor, value_seq, precision=PRECISION_LEVEL)
    return (jnp.exp(last_total), key_sum, value_sum)


def join_forward(former, latter):
    return (
        former[0] * latter[0],
        latter[0][..., None] * former[1] + latter[1],
        latter[0][..., None] * former[2] + latter[2],
    )


def join_backward(former, latter):
    return (
        latter[0] * former[0],
        latter[1] + latter[0][..., None] * former[1],
        latter[2] + latter[0][..., None] * former[2],
    )


def per_device(
    tokens,
    lengths,
    cotangent,
    mixer_gain,
    feed_gain,
    head_gain,
    w_query,
    w_key,
    w_value,
    w_gate,
    w_out,
    rank_down,
    rank_up,
    rank_bias,
    w_act,
    w_lin,
    w_down,
):
    seq_count, piece_len, model_width = tokens.shape
    row_count = seq_count * piece_len
    head_count = HEADS
    head_width = model_width // head_count
    slot_count = SLOTS
    sources = tokens.astype(jnp.float32).reshape(row_count, model_width)
    position = lax.axis_index("seq") * piece_len + jnp.arange(piece_len)
    alive = (position[None, :] < lengths[:, None]).astype(jnp.float32).reshape(row_count, 1)
    gathered = (
        lax.all_gather(mixer_gain, ("dp", "seq"), axis=0, tiled=True),
        lax.all_gather(feed_gain, ("dp", "seq"), axis=0, tiled=True),
        lax.all_gather(head_gain, ("dp", "seq"), axis=0, tiled=True),
        lax.all_gather(rank_down, ("dp", "seq"), axis=0, tiled=True),
        lax.all_gather(rank_up, ("dp", "seq"), axis=0, tiled=True),
        lax.all_gather(rank_bias, ("dp", "seq"), axis=0, tiled=True),
    )
    mixer_full = gathered[0].astype(jnp.float32)
    feed_full = gathered[1].astype(jnp.float32)
    head_full = gathered[2].astype(jnp.float32)
    down_full = gathered[3]
    up_full = gathered[4]
    bias_full = gathered[5].astype(jnp.float32)

    def mixer_rows(fold_fn, initial):
        return fold_fn(
            initial,
            (
                lax.all_gather(w_query, ("dp", "seq"), axis=0, tiled=True),
                lax.all_gather(w_key, ("dp", "seq"), axis=0, tiled=True),
                lax.all_gather(w_value, ("dp", "seq"), axis=0, tiled=True),
                lax.all_gather(w_gate, ("dp", "seq"), axis=0, tiled=True),
            ),
            jnp.int32(0),
        )

    def out_rows(fold_fn, initial):
        return fold_fn(
            initial, lax.all_gather(w_out, ("dp", "seq"), axis=0, tiled=True), jnp.int32(0)
        )

    first_normed, first_pullback = jax.vjp(norm_apply, sources, mixer_full)
    normed_in = first_normed.astype(jnp.bfloat16)
    blank = jnp.zeros((row_count, model_width), jnp.float32)

    def fill_mixer(partial_value, pieces, offset):
        return tuple((contract_last(normed_in, piece) for piece in pieces))

    query_pre, key_pre, value_pre, gate_pre = mixer_rows(fill_mixer, (blank, blank, blank, blank))
    low_rank = jnp.dot(normed_in, down_full, preferred_element_type=jnp.float32).astype(
        jnp.bfloat16
    )
    gate_logit = contract_last(low_rank, up_full) + bias_full
    log_decay = jax.nn.log_sigmoid(gate_logit) / GATE_NORM * alive
    queries = jax.nn.silu(query_pre).astype(jnp.bfloat16)
    key_features = jax.nn.silu(key_pre).astype(jnp.bfloat16)
    value_features = value_pre.astype(jnp.bfloat16)
    query_heads = queries.astype(jnp.float32).reshape(row_count, head_count, head_width)
    key_heads = key_features.astype(jnp.float32).reshape(row_count, head_count, head_width)
    value_heads = value_features.astype(jnp.float32).reshape(row_count, head_count, head_width)
    decay_heads = log_decay.reshape(row_count, head_count, slot_count)
    keep_all, key_sum, value_sum = piece_summary(key_heads, value_heads, decay_heads, seq_count)
    identity = (jnp.ones_like(keep_all), jnp.zeros_like(key_sum), jnp.zeros_like(value_sum))
    carried_in = entering((keep_all, key_sum, value_sum), "seq", join_forward, identity)
    slot_inputs = (
        to_blocks(query_heads, seq_count),
        to_blocks(key_heads, seq_count),
        to_blocks(value_heads, seq_count),
        to_blocks(decay_heads, seq_count),
        carried_in[1],
        carried_in[2],
    )
    slot_result, slot_pullback = jax.vjp(slot_pieces, *slot_inputs)
    slot_out = from_blocks(slot_result[0])

    def head_norm(tensor, gain):
        return tensor * rms_scale(tensor) * gain

    normed_out, head_pullback = jax.vjp(head_norm, slot_out, head_full)
    normed_out = normed_out.reshape(row_count, model_width)
    gate_swish = jax.nn.silu(gate_pre)
    mixed = (normed_out * gate_swish).astype(jnp.bfloat16)

    def fill_out(partial_value, piece, offset):
        return contract_last(mixed, piece)

    hidden = sources + out_rows(fill_out, blank)
    second_normed, second_pullback = jax.vjp(norm_apply, hidden, feed_full)
    normed_mid = second_normed.astype(jnp.bfloat16)

    def feed_fold(fold_fn, initial):
        return fold_fn(
            initial,
            (
                lax.all_gather(w_act, ("dp", "seq"), axis=0, tiled=True),
                lax.all_gather(w_lin, ("dp", "seq"), axis=0, tiled=True),
                lax.all_gather(w_down, ("dp", "seq"), axis=0, tiled=True),
            ),
            jnp.int32(0),
        )

    hidden_cols = w_act.shape[0] * lax.axis_size(("dp", "seq"))
    source_rows = normed_mid.shape[0]

    def add_feed(partial_value, pieces, offset):
        gate_part = contract_last(normed_mid, pieces[0])
        lin_part = contract_last(normed_mid, pieces[1])
        product = (jax.nn.silu(gate_part) * lin_part).astype(jnp.bfloat16)
        return jnp.dot(product, pieces[2], preferred_element_type=jnp.float32)

    feed_total = feed_fold(add_feed, jnp.zeros((source_rows, model_width), jnp.float32))
    result = alive * (hidden + feed_total)
    block_out = result.astype(jnp.bfloat16).reshape(seq_count, piece_len, model_width)
    grad_out = cotangent.astype(jnp.float32).reshape(row_count, model_width) * alive
    grad_source = grad_out.astype(jnp.bfloat16)

    def back_feed(partial_value, pieces, offset):
        gate_part = contract_last(normed_mid, pieces[0])
        lin_part = contract_last(normed_mid, pieces[1])
        swish = jax.nn.silu(gate_part)
        product = (swish * lin_part).astype(jnp.bfloat16)
        grad_product = contract_last(grad_source, pieces[2])
        grad_gate = (grad_product * lin_part * swish_slope(gate_part)).astype(jnp.bfloat16)
        grad_lin = (grad_product * swish).astype(jnp.bfloat16)
        grad_mid = jnp.dot(grad_gate, pieces[0], preferred_element_type=jnp.float32)
        grad_mid = grad_mid + jnp.dot(grad_lin, pieces[1], preferred_element_type=jnp.float32)
        return (grad_mid, grad_gate, grad_lin, product)

    cols_blank = jnp.zeros((source_rows, hidden_cols), jnp.bfloat16)
    grad_mid_part, gate_grads, lin_grads, products = feed_fold(
        back_feed,
        (jnp.zeros((source_rows, model_width), jnp.float32), cols_blank, cols_blank, cols_blank),
    )
    grad_mid = grad_mid_part
    feed_grad_rows = lax.psum_scatter(
        jnp.concatenate(
            [
                contract_first(gate_grads, normed_mid),
                contract_first(lin_grads, normed_mid),
                contract_first(products, grad_source),
            ],
            axis=1,
        ),
        ("dp", "seq"),
        scatter_dimension=0,
        tiled=True,
    )
    w_act_grad = feed_grad_rows[:, :model_width]
    w_lin_grad = feed_grad_rows[:, model_width : 2 * model_width]
    w_down_grad = feed_grad_rows[:, 2 * model_width :]
    grad_hidden_norm, feed_gain_grad = second_pullback(grad_mid)
    grad_hidden = grad_out + grad_hidden_norm
    grad_attn = grad_hidden.astype(jnp.bfloat16)

    def back_out(partial_value, piece, offset):
        return jnp.dot(grad_attn, piece, preferred_element_type=jnp.float32)

    grad_mixed = out_rows(back_out, blank)
    grad_gate_pre = (grad_mixed * normed_out * swish_slope(gate_pre)).astype(jnp.bfloat16)
    grad_normed = (grad_mixed * gate_swish).reshape(row_count, head_count, head_width)
    grad_slot_out, head_gain_grad = head_pullback(grad_normed)
    grad_blocks = to_blocks(grad_slot_out, seq_count)
    end_blank = (jnp.zeros_like(slot_result[1]), jnp.zeros_like(slot_result[2]))
    local_grads = slot_pullback((grad_blocks, end_blank[0], end_blank[1]))
    carried_back = prefix(
        (keep_all, local_grads[4], local_grads[5]), "seq", join_backward, identity
    )
    full_grads = slot_pullback((grad_blocks, carried_back[1], carried_back[2]))
    grad_queries = from_blocks(full_grads[0]).reshape(row_count, model_width)
    grad_key_feats = from_blocks(full_grads[1]).reshape(row_count, model_width)
    grad_value_feats = from_blocks(full_grads[2]).reshape(row_count, model_width)
    grad_log_decay = from_blocks(full_grads[3]).reshape(row_count, head_count * slot_count)
    grad_query_pre = (grad_queries * swish_slope(query_pre)).astype(jnp.bfloat16)
    grad_key_pre = (grad_key_feats * swish_slope(key_pre)).astype(jnp.bfloat16)
    grad_value_pre = grad_value_feats.astype(jnp.bfloat16)
    grad_logit = (alive * grad_log_decay * jax.nn.sigmoid(-gate_logit) / GATE_NORM).astype(
        jnp.bfloat16
    )
    bias_grad_local = jnp.sum(grad_logit.astype(jnp.float32), axis=0)
    rank_up_local = contract_first(grad_logit, low_rank)
    grad_rank = jnp.dot(grad_logit, up_full, preferred_element_type=jnp.float32).astype(
        jnp.bfloat16
    )
    rank_down_local = contract_first(normed_in, grad_rank)
    grad_pres = (grad_query_pre, grad_key_pre, grad_value_pre, grad_gate_pre)

    def back_mixer(partial_value, pieces, offset):
        for grad_pre, piece in zip(grad_pres, pieces):
            partial_value = partial_value + jnp.dot(
                grad_pre, piece, preferred_element_type=jnp.float32
            )
        return partial_value

    grad_in = mixer_rows(back_mixer, blank) + contract_last(grad_rank, down_full)
    grad_tokens_norm, mixer_gain_grad = first_pullback(grad_in)
    tokens_grad = (grad_hidden + grad_tokens_norm).reshape(seq_count, piece_len, model_width)
    mixer_grad_rows = lax.psum_scatter(
        jnp.concatenate(
            [
                contract_first(grad_query_pre, normed_in),
                contract_first(grad_key_pre, normed_in),
                contract_first(grad_value_pre, normed_in),
                contract_first(grad_gate_pre, normed_in),
                contract_first(grad_attn, mixed),
            ],
            axis=1,
        ),
        ("dp", "seq"),
        scatter_dimension=0,
        tiled=True,
    )
    small_grads = (
        lax.psum_scatter(mixer_gain_grad, ("dp", "seq"), scatter_dimension=0, tiled=True),
        lax.psum_scatter(feed_gain_grad, ("dp", "seq"), scatter_dimension=0, tiled=True),
        lax.psum_scatter(head_gain_grad, ("dp", "seq"), scatter_dimension=0, tiled=True),
        lax.psum_scatter(rank_down_local, ("dp", "seq"), scatter_dimension=0, tiled=True),
        lax.psum_scatter(rank_up_local, ("dp", "seq"), scatter_dimension=0, tiled=True),
        lax.psum_scatter(bias_grad_local, ("dp", "seq"), scatter_dimension=0, tiled=True),
    )
    return (
        block_out,
        tokens_grad,
        small_grads[0],
        small_grads[1],
        small_grads[2],
        mixer_grad_rows[:, :model_width],
        mixer_grad_rows[:, model_width : 2 * model_width],
        mixer_grad_rows[:, 2 * model_width : 3 * model_width],
        mixer_grad_rows[:, 3 * model_width : 4 * model_width],
        mixer_grad_rows[:, 4 * model_width :],
        small_grads[3],
        small_grads[4],
        small_grads[5],
        w_act_grad,
        w_lin_grad,
        w_down_grad,
    )


def solution(mesh):
    return jax.shard_map(
        per_device,
        mesh=mesh,
        in_specs=(
            P("dp", "seq", None),
            P("dp"),
            P("dp", "seq", None),
            P(("dp", "seq")),
            P(("dp", "seq")),
            P(("dp", "seq")),
            P(("dp", "seq"), None),
            P(("dp", "seq"), None),
            P(("dp", "seq"), None),
            P(("dp", "seq"), None),
            P(("dp", "seq"), None),
            P(("dp", "seq"), None),
            P(("dp", "seq"), None),
            P(("dp", "seq")),
            P(("dp", "seq"), None),
            P(("dp", "seq"), None),
            P(("dp", "seq"), None),
        ),
        out_specs=(
            P("dp", "seq", None),
            P("dp", "seq", None),
            P(("dp", "seq")),
            P(("dp", "seq")),
            P(("dp", "seq")),
            P(("dp", "seq"), None),
            P(("dp", "seq"), None),
            P(("dp", "seq"), None),
            P(("dp", "seq"), None),
            P(("dp", "seq"), None),
            P(("dp", "seq"), None),
            P(("dp", "seq"), None),
            P(("dp", "seq")),
            P(("dp", "seq"), None),
            P(("dp", "seq"), None),
            P(("dp", "seq"), None),
        ),
        check_vma=False,
    )
```

profile of v0, /device:TPU:21, one launch (start us, length us, event | category | flops | bytes accessed | tf_op | source)
XLA Modules:
  0.0 5942.1 jit_solution(16767773419745459982)
XLA Ops:
  12.9 39.9 all-reduce.12
  52.8 59.8 %all-gather.6 = bf16[32,64,16]{1,2,0:T(8,128)(2,1)S(1)} all-gather(bf16[1,64,16]{1,2,0:T(8,128)(2,1)} %bitcast.918), channel_id=1, replica_groups=mesh['dp'=4,'seq'=8] {'dp','seq'}, dimensions={0}, use_global_device_ids=true | all-gather | bytes 67584 | tf_op jit(solution)/shard_map/all_gather | solution.py:201
  112.8 66.5 %all_gather.84 = bf16[256,16]{1,0:T(8,128)(2,1)S(1)} all-gather(bf16[8,16]{1,0:T(8,128)(2,1)} %param.49), channel_id=1, replica_groups=mesh['dp'=4,'seq'=8] {'dp','seq'}, dimensions={0}, use_global_device_ids=true | all-gather | bytes 8448 | tf_op jit(solution)/shard_map/all_gather | solution.py:202
  212.0 25.2 all-gather
  269.4 105.7 %all-gather.36.cloned.1.call-done = f32[16,4,64,512]{3,2,1,0:T(8,128)} async-done(((f32[2,4,64,512]{3,2,1,0:T(8,128)}), f32[16,4,64,512]{3,2,1,0:T(8,128)}) %all-gather.36.cloned.1.call-update) | async-done | bytes 8388624 | tf_op jit(solution)/shard_map/all_gather | solution.py:18
  375.0 125.7 %all-gather.38.cloned.1.call-done = f32[16,4,64,512]{3,2,1,0:T(8,128)} async-done(((f32[2,4,64,512]{3,2,1,0:T(8,128)}), f32[16,4,64,512]{3,2,1,0:T(8,128)}) %all-gather.38.cloned.1.call-update) | async-done | bytes 8388624 | tf_op jit(solution)/shard_map/all_gather | solution.py:18
  500.7 26.3 while.351
  528.6 162.7 %while.350 = (s32[]{:T(128)}, f32[2,2,4,64,512]{4,3,2,1,0:T(8,128)}, f32[2,4,64,512]{3,2,1,0:T(8,128)}, f32[2,4,64,512]{3,2,1,0:T(8,128)}, f32[2,2,4,64,512]{4,3...) while((s32[]{:T(128)}, f32[2,2,4,64,512]{4,3,2,1,0:T(8,128)}, ...), condition=%wide.region_10.11_spmd.clone.clone, body=%wide.region_4.10_spmd.clone.clone.sunk | while | flops 628981824 | bytes 43535912 | solution.py:124
  538.0 69.5 %while.357 = (s32[]{:T(128)}, f32[4,64,512]{2,1,0:T(8,128)S(1)}, f32[4,64,512]{2,1,0:T(8,128)S(1)}, f32[2,4,64,512]{3,2,1,0:T(8,128)}, f32[2,4,64,64]{3,2,1,0:T(...) while((s32[]{:T(128)}, f32[4,64,512]{2,1,0:T(8,128)S(1)}, ...), condition=%wide.region_9.9_spmd.clone, body=%wide.region_5.8_spmd.clone.sunk | while | flops 628981824 | bytes 31735088 | solution.py:117
  555.4 15.8 fusion.474
  590.1 15.8 fusion.474
  618.9 69.6 %while.357 = (s32[]{:T(128)}, f32[4,64,512]{2,1,0:T(8,128)S(1)}, f32[4,64,512]{2,1,0:T(8,128)S(1)}, f32[2,4,64,512]{3,2,1,0:T(8,128)}, f32[2,4,64,64]{3,2,1,0:T(...) while((s32[]{:T(128)}, f32[4,64,512]{2,1,0:T(8,128)S(1)}, ...), condition=%wide.region_9.9_spmd.clone, body=%wide.region_5.8_spmd.clone.sunk | while | flops 628981824 | bytes 31735088 | solution.py:117
  636.4 15.8 fusion.474
  671.1 15.9 fusion.474
  717.4 87.8 %all-gather.30.cloned.1.call-done = bf16[5632,2048]{1,0:T(8,128)(2,1)} async-done(((bf16[176,2048]{1,0:T(8,128)(2,1)}), bf16[5632,2048]{1,0:T(8,128)(2,1)}) %all-gather.30.cloned.1.call-update) | async-done | bytes 23068688 | tf_op jit(solution)/shard_map/all_gather | solution.py:282
  805.2 13.3 fusion.271
  818.5 132.4 %all-gather.32.cloned.1.call-done = bf16[5632,2048]{1,0:T(8,128)(2,1)} async-done(((bf16[176,2048]{1,0:T(8,128)(2,1)}), bf16[5632,2048]{1,0:T(8,128)(2,1)}) %all-gather.32.cloned.1.call-update) | async-done | bytes 23068688 | tf_op jit(solution)/shard_map/all_gather | solution.py:283
  951.0 13.2 fusion.272
  964.2 132.4 %all-gather.34.cloned.1.call-done = bf16[5632,2048]{1,0:T(8,128)(2,1)} async-done(((bf16[176,2048]{1,0:T(8,128)(2,1)}), bf16[5632,2048]{1,0:T(8,128)(2,1)}) %all-gather.34.cloned.1.call-update) | async-done | bytes 23068688 | tf_op jit(solution)/shard_map/all_gather | solution.py:284
  1096.6 17.4 multiply_convert_fusion
  1114.0 13.3 fusion.273
  1127.4 12.5 multiply_reduce_fusion.4
  1158.5 178.5 %while.345 = (s32[]{:T(128)}, bf16[2,4,64,512]{3,2,1,0:T(8,128)(2,1)}, bf16[2,4,64,512]{3,2,1,0:T(8,128)(2,1)}, f32[2,2,4,64,512]{4,3,2,1,0:T(8,128)}, f32[2,2,4...) while((s32[]{:T(128)}, ...), condition=%wide.region_24.25_spmd, body=%wide.region_15.24_spmd.sunk | while | flops 830853696 | bytes 82659208 | solution.py:124
  1168.9 41.5 while.353
  1210.4 34.0 while.354
  1258.0 41.5 while.353
  1299.5 34.0 while.354
  1337.7 20.6 all-gather.5
  1359.4 20.6 fusion.277
  1380.0 20.0 fusion.276
  1400.0 20.1 fusion.278
  1420.1 62.4 %all-gather.42.cloned.1.call-done = bf16[16,4,64,512]{3,2,1,0:T(8,128)(2,1)} async-done(((bf16[2,4,64,512]{3,2,1,0:T(8,128)(2,1)}), bf16[16,4,64,512]{3,2,1,0:T(8,128)(2,1)}) %all-gather.42.cloned.1.call-update) | async-done | bytes 4194320 | tf_op jit(solution)/shard_map/all_gather | solution.py:33
  1482.5 14.1 while.352
  1500.7 596.7 %while.348 = (s32[]{:T(128)}, f32[2,2,4,64,512]{4,3,2,1,0:T(8,128)}, f32[2,2,4,64,512]{4,3,2,1,0:T(8,128)}, bf16[2,2,4,64,512]{4,3,2,1,0:T(8,128)(2,1)}, f32[2,2...) while((s32[]{:T(128)}, f32[2,2,4,64,512]{4,3,2,1,0:T(8,128)}, ...), condition=%wide.region_43.44_spmd, body=%wide.region_27.43_spmd.sunk | while | flops 1679675904 | bytes 205910512 | solution.py:124
  1518.3 94.9 %while.355 = (s32[]{:T(128)}, f32[4,64,512]{2,1,0:T(8,128)S(1)}, f32[4,64,512]{2,1,0:T(8,128)S(1)}, f32[2,4,64]{2,1,0:T(4,128)}, f32[2,4,64,512]{3,2,1,0:T(8,128...) while((s32[]{:T(128)}, f32[4,64,512]{2,1,0:T(8,128)S(1)}, ...), condition=%wide.region_32.32_spmd.clone.clone, body=%wide.region_28.31_spmd.clone.clone.sunk | while | flops 431784512 | bytes 54905424 | solution.py:117
  1538.2 15.7 fusion.482
  1554.2 10.4 fusion.483
  1585.6 15.7 fusion.482
  1601.7 10.5 fusion.483
  1616.2 167.6 %while.356 = (s32[]{:T(128)}, f32[4,64,512]{2,1,0:T(8,128)S(1)}, f32[4,64,512]{2,1,0:T(8,128)S(1)}, f32[2,4,64,512]{3,2,1,0:T(8,128)}, f32[2,4,64,512]{3,2,1,0:T...) while((s32[]{:T(128)}, f32[4,64,512]{2,1,0:T(8,128)S(1)}, ...), condition=%wide.region_42.42_spmd.clone.clone, body=%wide.region_33.41_spmd.clone.clone.sunk | while | flops 1247625216 | bytes 89264944 | solution.py:117
  1641.1 10.2 fusion.514
  1663.6 15.5 fusion.518
  1692.3 10.1 fusion.524
  1717.9 10.2 fusion.514
  1740.4 15.5 fusion.518
  1769.1 10.1 fusion.524
  1818.0 94.9 %while.355 = (s32[]{:T(128)}, f32[4,64,512]{2,1,0:T(8,128)S(1)}, f32[4,64,512]{2,1,0:T(8,128)S(1)}, f32[2,4,64]{2,1,0:T(4,128)}, f32[2,4,64,512]{3,2,1,0:T(8,128...) while((s32[]{:T(128)}, f32[4,64,512]{2,1,0:T(8,128)S(1)}, ...), condition=%wide.region_32.32_spmd.clone.clone, body=%wide.region_28.31_spmd.clone.clone.sunk | while | flops 431784512 | bytes 54905424 | solution.py:117
  1837.9 15.7 fusion.482
  1853.9 10.4 fusion.483
  1885.3 15.7 fusion.482
  1901.4 10.5 fusion.483
  1915.9 167.6 %while.356 = (s32[]{:T(128)}, f32[4,64,512]{2,1,0:T(8,128)S(1)}, f32[4,64,512]{2,1,0:T(8,128)S(1)}, f32[2,4,64,512]{3,2,1,0:T(8,128)}, f32[2,4,64,512]{3,2,1,0:T...) while((s32[]{:T(128)}, f32[4,64,512]{2,1,0:T(8,128)S(1)}, ...), condition=%wide.region_42.42_spmd.clone.clone, body=%wide.region_33.41_spmd.clone.clone.sunk | while | flops 1247625216 | bytes 89264944 | solution.py:117
  1940.8 10.2 fusion.514
  1963.3 15.5 fusion.518
  1992.0 10.1 fusion.524
  2017.6 10.2 fusion.514
  2040.1 15.5 fusion.518
  2068.8 10.1 fusion.524
  2105.6 93.8 %pad_maximum_fusion = f32[5632,6144]{0,1:T(8,128)} fusion(f32[5632,2048]{0,1:T(8,128)} %fusion.278, f32[5632,2048]{0,1:T(8,128)} %fusion.277, f32[5632,2048]{0,1:T(8,128)} %fusion.276), kind=kLoop, calls=%fused_computation.367 | loop fusion | flops 69206016 | bytes 276824064 | tf_op jit(solution)/shard_map/concatenate | solution.py:323
  2253.4 81.5 %copy.395 = f32[2048,10240]{1,0:T(8,128)} copy(f32[2048,10240]{0,1:T(8,128)} %convolution_dynamic-update-slice_fusion) | data formatting | bytes 167772160
  2335.7 14.5 fusion.231
  2369.9 41.9 all-reduce.11
  2419.6 1758.6 %all-reduce.15.cloned.1.call-done = f32[5632,6144]{0,1:T(8,128)} async-done(((f32[5632,6144]{0,1:T(8,128)}), f32[5632,6144]{0,1:T(8,128)}) %all-reduce.15.cloned.1.call-update) | async-done | bytes 138412048
  4193.2 1738.9 %reduce-scatter.8.cloned.1.call-done = f32[64,10240]{1,0:T(8,128)} async-done(((f32[2048,10240]{1,0:T(8,128)}), f32[64,10240]{1,0:T(8,128)}) %reduce-scatter.8.cloned.1.call-update) | async-done | bytes 2621456
  (1601 shorter events, 840.3 us)
Async XLA Ops:
  7.2 175.0 %copy-start.90 = (bf16[2,128,2048]{2,1,0:T(8,128)(2,1)S(1)}, bf16[2,128,2048]{2,1,0:T(8,128)(2,1)}, u32[]{:S(2)}) copy-start(bf16[2,128,2048]{2,1,0:T(8,128)(2,1)} %param.37) | copy-start | bytes 3145732
  7.2 178.4 %all-gather.20.cloned.1.call-start = ((), (), s32[]{:S(2)}) async-start(), calls=%async_computation.2 | async-start | bytes 8650752 | tf_op jit(solution)/shard_map/all_gather | solution.py:217
  7.9 187.4 %all-gather.22.cloned.1.call-start = ((), (), s32[]{:S(2)}) async-start(), calls=%async_computation.3 | async-start | bytes 8650752 | tf_op jit(solution)/shard_map/all_gather | solution.py:218
  8.7 241.4 %all-gather.24.cloned.1.call-start = ((), (), s32[]{:S(2)}) async-start(), calls=%async_computation.4 | async-start | bytes 8650752 | tf_op jit(solution)/shard_map/all_gather | solution.py:216
  9.4 365.6 %all-gather.36.cloned.1.call-start = ((), (), s32[]{:S(2)}) async-start(), calls=%async_computation.10 | async-start | bytes 9437184 | tf_op jit(solution)/shard_map/all_gather | solution.py:18
  52.8 131.2 %copy-start.140 = (f32[2048]{0:T(1024)}, f32[2048]{0:T(1024)S(1)}, u32[]{:S(2)}) copy-start(f32[2048]{0:T(1024)S(1)} %convert_element_type.165) | copy-start | bytes 24580
  112.8 71.5 %copy-start.137 = (bf16[2048,16]{0,1:T(8,128)(2,1)}, bf16[2048,16]{0,1:T(8,128)(2,1)S(1)}, u32[]{:S(2)}) copy-start(bf16[2048,16]{0,1:T(8,128)(2,1)S(1)} %reshape.633) | copy-start | bytes 196612
  182.5 67.6 %copy-start.85 = (bf16[256,2048]{1,0:T(8,128)(2,1)}, bf16[256,2048]{1,0:T(8,128)(2,1)S(1)}, u32[]{:S(2)}) copy-start(bf16[256,2048]{1,0:T(8,128)(2,1)S(1)} %fusion.238) | copy-start | bytes 3145732
  195.3 305.4 %all-gather.38.cloned.1.call-start = ((), (), s32[]{:S(2)}) async-start(), calls=%async_computation.11 | async-start | bytes 9437184 | tf_op jit(solution)/shard_map/all_gather | solution.py:18
  205.6 31.6 copy-start.161
  205.6 31.7 copy-start.114
  205.6 494.0 %all-gather.26.cloned.1.call-start = ((), (), s32[]{:S(2)}) async-start(), calls=%async_computation.5 | async-start | bytes 8650752 | tf_op jit(solution)/shard_map/all_gather | solution.py:219
  206.2 503.2 %all-gather.28.cloned.1.call-start = ((), (), s32[]{:S(2)}) async-start(), calls=%async_computation.6 | async-start | bytes 8650752 | tf_op jit(solution)/shard_map/all_gather | solution.py:226
  206.9 598.3 %all-gather.30.cloned.1.call-start = ((), (), s32[]{:S(2)}) async-start(), calls=%async_computation.7 | async-start | bytes 23789568 | tf_op jit(solution)/shard_map/all_gather | solution.py:282
  207.7 743.3 %all-gather.32.cloned.1.call-start = ((), (), s32[]{:S(2)}) async-start(), calls=%async_computation.8 | async-start | bytes 23789568 | tf_op jit(solution)/shard_map/all_gather | solution.py:283
  208.4 888.2 %all-gather.34.cloned.1.call-start = ((), (), s32[]{:S(2)}) async-start(), calls=%async_computation.9 | async-start | bytes 23789568 | tf_op jit(solution)/shard_map/all_gather | solution.py:284
  209.0 1211.1 %all-gather.40.cloned.1.call-start = ((), (), s32[]{:S(2)}) async-start(), calls=%async_computation.12 | async-start | bytes 4718592 | tf_op jit(solution)/shard_map/all_gather | solution.py:33
  555.4 15.9 copy-start.5
  555.4 15.9 copy-start.11
  555.4 15.9 copy-start.88
  590.0 15.9 copy-start.5
  590.1 15.9 copy-start.11
  590.1 15.9 copy-start.88
  636.4 15.9 copy-start.5
  636.4 15.9 copy-start.11
  636.4 15.9 copy-start.88
  671.1 15.9 copy-start.5
  671.1 15.9 copy-start.11
  671.1 15.9 copy-start.88
  717.4 233.6 %copy-start.97 = (bf16[256,2048]{1,0:T(8,128)(2,1)}, bf16[256,2048]{1,0:T(8,128)(2,1)S(1)}, u32[]{:S(2)}) copy-start(bf16[256,2048]{1,0:T(8,128)(2,1)S(1)} %multiply_convert_fusion.6) | copy-start | bytes 3145732
  1114.0 26.6 slice-start.4
  1337.1 145.5 %all-gather.42.cloned.1.call-start = ((), (), s32[]{:S(2)}) async-start(), calls=%async_computation.13 | async-start | bytes 4718592 | tf_op jit(solution)/shard_map/all_gather | solution.py:33
  1337.7 1080.5 %reduce-scatter.10.cloned.1.call-start = ((), (), s32[]{:S(2)}) async-start(), calls=%async_computation.15 | async-start | bytes 1081344
  1359.4 20.6 copy-start.98
  1380.0 20.0 copy-start.111
  1538.2 15.8 copy-start.52
  1538.2 15.8 copy-start.55
  1538.2 15.8 copy-start.58
  1538.2 15.8 copy-start.61
  1538.2 15.8 copy-start.82
  1538.2 16.0 copy-start.25
  1585.6 15.8 copy-start.55
  1585.6 15.8 copy-start.58
  1585.6 15.8 copy-start.61
  1585.6 15.8 copy-start.82
  1585.6 16.0 copy-start.25
  1663.6 17.9 copy-start.1
  1740.4 17.9 copy-start.1
  1837.8 15.8 copy-start.55
  1837.8 15.8 copy-start.58
  1837.9 15.8 copy-start.61
  1837.9 15.8 copy-start.82
  1837.9 16.0 copy-start.25
  1885.3 15.8 copy-start.55
  1885.3 15.8 copy-start.58
  1885.3 15.8 copy-start.61
  1885.3 15.8 copy-start.82
  1885.3 16.0 copy-start.25
  1963.3 17.9 copy-start.1
  2040.1 17.9 copy-start.1
  2105.6 2072.7 %all-reduce.15.cloned.1.call-start = ((), (), s32[]{:S(2)}) async-start(), calls=%async_computation.16 | async-start | bytes 276824064
  2199.5 3732.6 %reduce-scatter.8.cloned.1.call-start = ((), (), s32[]{:S(2)}) async-start(), calls=%async_computation.14 | async-start | bytes 86507520
  2208.0 19.5 copy-start.109
  2367.8 46.9 copy-start.156
  (389 other events, 2374.6 us)
Sparse Core Ops, SparseCore 0:
  11.0 79.6 all-gather.19
  93.7 76.6 all-gather.21
  173.4 76.6 all-gather.23
  252.6 122.3 all-gather.35
  377.6 123.1 all-gather.37
  503.6 76.8 all-gather.25
  583.4 75.9 all-gather.27
  662.4 142.8 all-gather.29
  808.1 142.8 all-gather.31
  953.7 142.8 all-gather.33
  1337.2 71.0 all-gather.39
  1410.8 71.6 all-gather.41
  2105.7 127.7 reduce-scatter.9
  2240.9 1937.2 all-reduce.14
  4180.6 1751.4 reduce-scatter.7
where the time goes:
time: 5960 us; the launch traced here: 5940 us
  waiting for transfers between devices  4150 us (70%)
  matrix products  698 us (12%)
  other arithmetic  391 us (7%)
  local copies, waits for them, and re-layouts  371 us (6%)
  blocking collectives  254 us (4%)
    unnamed x18, waiting for transfers between devices  3500 us
    all_gather x2, waiting for transfers between devices, entering(): pieces = jax.tree.map(lambda part: lax.all_gather(part, axis), value)  231 us
    dot_general x16, matrix products, slot_block(): jnp.einsum('htj,htij->hti', attend, weight, precision=PRECISION_LEVEL)  205 us
    all_gather x1, waiting for transfers between devices, feed_fold(): lax.all_gather(w_lin, ('dp', 'seq'), axis=0, tiled=True)  132 us
    all_gather x1, waiting for transfers between devices, feed_fold(): lax.all_gather(w_down, ('dp', 'seq'), axis=0, tiled=True)  132 us
  transfers between devices with their start and end apart: 15, of which 9 were waited for; matrix products, arithmetic and copies ran while one was open for 11% of the time, Pallas kernels for 0%

commit v1 on v0

v1 whole, which is shorter than its diff:
```python
import functools

import jax
import jax.numpy as jnp
from jax import lax
from jax.experimental import pallas as pl
from jax.experimental.pallas import tpu as pltpu
from jax.sharding import PartitionSpec as P

HEADS = 4
SLOTS = 64
EPS = 1e-06
GATE_NORM = 8.0
F32 = jnp.float32
BF16 = jnp.bfloat16
LEAF = 8
VMEM_LIMIT = 40 * 1024 * 1024


def mm(a, b, ca, cb):
    return lax.dot_general(
        a.astype(BF16), b.astype(BF16), (((ca,), (cb,)), ((), ())), preferred_element_type=F32
    )


def mm_exact(a, b, ca, cb):
    return lax.dot_general(
        a,
        b,
        (((ca,), (cb,)), ((), ())),
        precision=lax.Precision.HIGHEST,
        preferred_element_type=F32,
    )


def two_parts(x):
    high = x.astype(BF16)
    return high, (x - high.astype(F32)).astype(BF16)


def mm_left(exact, b, ca, cb):
    high, low = two_parts(b)
    return mm(exact, high, ca, cb) + mm(exact, low, ca, cb)


def mm_right(a, exact, ca, cb):
    high, low = two_parts(a)
    return mm(high, exact, ca, cb) + mm(low, exact, ca, cb)


def mm_fine(a, b, ca, cb):
    a_high, a_low = two_parts(a)
    b_high, b_low = two_parts(b)
    return mm(a_high, b_high, ca, cb) + (mm(a_high, b_low, ca, cb) + mm(a_low, b_high, ca, cb))


def contract_last(a, b):
    return mm(a, b, 1, 1)


def contract_first(a, b):
    return mm(a, b, 0, 0)


def swish_slope(v):
    sigma = jax.nn.sigmoid(v)
    return sigma * (1.0 + v * (1.0 - sigma))


def rms_scale(v):
    return lax.rsqrt(jnp.mean(v * v, axis=-1, keepdims=True) + EPS)


def grid_index(rows, cols):
    return (
        lax.broadcasted_iota(jnp.int32, (rows, cols), 0),
        lax.broadcasted_iota(jnp.int32, (rows, cols), 1),
    )


def running_sum(decay):
    length = decay.shape[0]
    row, col = grid_index(length, length)
    return mm_exact((row >= col).astype(F32), decay, 1, 0)


def levels(length):
    found = []
    half = length // 2
    while half >= LEAF:
        found.append(half)
        half //= 2
    return found


def level_factors(running, writes, half):
    length, slots = running.shape
    pairs = running.reshape(length // (2 * half), 2 * half, slots)
    anchor = jnp.broadcast_to(pairs[:, half - 1 : half, :], pairs.shape).reshape(length, slots)
    near = jnp.exp(-jnp.abs(running - anchor))
    row, _ = grid_index(length, slots)
    right = (row % (2 * half)) >= half
    return jnp.where(right, near, 0.0), jnp.where(right, 0.0, near), right


def same_block(length, size):
    row, col = grid_index(length, length)
    return (row // size) == (col // size)


def leaf_selector(length):
    row, col = grid_index(length, LEAF)
    return ((row % LEAF) == col).astype(F32)


def leaf_take(square):
    length = square.shape[0]
    kept = jnp.where(same_block(length, LEAF), square, 0.0)
    return mm_exact(kept, leaf_selector(length), 1, 0)


def leaf_spread(columns):
    length = columns.shape[0]
    wide = mm_exact(columns, leaf_selector(length), 1, 1)
    return jnp.where(same_block(length, LEAF), wide, 0.0)


def leaf_row(tensor, at):
    length, width = tensor.shape
    blocks = tensor.reshape(length // LEAF, LEAF, width)
    return jnp.broadcast_to(blocks[:, at : at + 1, :], blocks.shape).reshape(length, width)


def leaf_decay(running, at):
    length, slots = running.shape
    row, _ = grid_index(length, slots)
    reached = (row % LEAF) >= at
    spread = running - leaf_row(running, at)
    return jnp.where(reached, jnp.exp(jnp.where(reached, spread, 0.0)), 0.0)


def masked(square, half):
    length = square.shape[0]
    if 2 * half == length:
        return square
    return jnp.where(same_block(length, 2 * half), square, 0.0)


def read_in_chunk(square, running, writes):
    total = None
    for half in levels(running.shape[0]):
        right, left, _ = level_factors(running, writes, half)
        part = right * mm_fine(masked(square, half), left * writes, 1, 0)
        total = part if total is None else total + part
    columns = leaf_take(square)
    for at in range(LEAF):
        part = columns[:, at : at + 1] * (leaf_decay(running, at) * leaf_row(writes, at))
        total = part if total is None else total + part
    return total


def mix_in_chunk(attend, running, writes):
    total = None
    for half in levels(running.shape[0]):
        right, left, _ = level_factors(running, writes, half)
        part = masked(mm(attend * right, left * writes, 1, 1), half)
        total = part if total is None else total + part
    columns = [
        jnp.sum(
            attend * (leaf_decay(running, at) * leaf_row(writes, at)), axis=1, keepdims=True
        )
        for at in range(LEAF)
    ]
    part = leaf_spread(jnp.concatenate(columns, axis=1))
    return part if total is None else total + part


def summary_kernel(k_ref, v_ref, decay_ref, writes_ref, state_ref, keep_ref):
    running = running_sum(decay_ref[0])
    length = running.shape[0]
    last = running[length - 1 : length, :]
    fade = jnp.exp(last - running) * writes_ref[0]
    width = k_ref.shape[2]
    state_ref[0, :, :width] = mm(fade, k_ref[0], 0, 0)
    state_ref[0, :, width:] = mm(fade, v_ref[0], 0, 0)
    keep_ref[0] = jnp.exp(last)


def forward_kernel(
    q_ref, k_ref, v_ref, gate_ref, decay_ref, writes_ref, state_ref, gain_ref,
    mixed_ref, out_ref, attend_ref,
):
    q, k, v = q_ref[0], k_ref[0], v_ref[0]
    writes = writes_ref[0]
    width = q.shape[1]
    scale = width ** (-0.5)
    running = running_sum(decay_ref[0])
    growth = jnp.exp(running)
    state = state_ref[0]
    dots = mm(q, k, 1, 1) * scale
    scores = growth * (mm(q, state[:, :width], 1, 1) * scale)
    scores = scores + read_in_chunk(dots, running, writes)
    top = jnp.max(scores, axis=1, keepdims=True)
    raw = jnp.exp(scores - top)
    attend = raw / jnp.sum(raw, axis=1, keepdims=True)
    mixing = mix_in_chunk(attend, running, writes)
    out = mm(attend * growth, state[:, width:], 1, 0) + mm(mixing, v, 1, 0)
    out_ref[0] = out
    attend_ref[0] = attend
    gate = gate_ref[0]
    normed = out * rms_scale(out) * gain_ref[...]
    mixed_ref[0] = (normed * (gate * jax.nn.sigmoid(gate))).astype(BF16)


def back_first_kernel(
    grad_mixed_ref, gate_ref, out_ref, attend_ref, q_ref, v_ref, decay_ref, writes_ref,
    state_ref, gain_ref,
    grad_gate_ref, grad_out_ref, grad_scores_ref, adjoint_ref, gain_grad_ref,
):
    q, v = q_ref[0], v_ref[0]
    writes = writes_ref[0]
    width = q.shape[1]
    scale = width ** (-0.5)
    grad_mixed, gate, out = grad_mixed_ref[0], gate_ref[0], out_ref[0]
    gain = gain_ref[...]
    inverse = rms_scale(out)
    normed = out * inverse
    grad_gate_ref[0] = (grad_mixed * (normed * gain) * swish_slope(gate)).astype(BF16)
    e = grad_mixed * (gate * jax.nn.sigmoid(gate))
    gain_grad_ref[0] = jnp.sum(e * normed, axis=0, keepdims=True)
    eg = e * gain
    grad_out = inverse * (eg - normed * jnp.mean(eg * normed, axis=1, keepdims=True))
    grad_out_ref[0] = grad_out.astype(BF16)
    running = running_sum(decay_ref[0])
    growth = jnp.exp(running)
    attend = attend_ref[0]
    u = growth * mm_right(grad_out, state_ref[0, :, width:], 1, 1)
    u = u + read_in_chunk(mm_right(grad_out, v, 1, 1), running, writes)
    grad_scores = attend * (u - jnp.sum(attend * u, axis=1, keepdims=True))
    grad_scores_ref[0] = grad_scores
    adjoint_ref[0, :, :width] = mm(growth * grad_scores * scale, q, 0, 0)
    adjoint_ref[0, :, width:] = mm(growth * attend, grad_out.astype(BF16), 0, 0)


def back_second_kernel(
    grad_out_ref, grad_scores_ref, attend_ref, q_ref, k_ref, v_ref, decay_ref, writes_ref,
    state_ref, adjoint_ref, q_pre_ref, k_pre_ref, logit_ref, alive_ref,
    dq_ref, dk_ref, dv_ref, dlogit_ref,
):
    q, k, v, grad_out = q_ref[0], k_ref[0], v_ref[0], grad_out_ref[0]
    attend, grad_scores = attend_ref[0], grad_scores_ref[0]
    decay, writes = decay_ref[0], writes_ref[0]
    length, slots = decay.shape
    width = q.shape[1]
    scale = width ** (-0.5)
    running = running_sum(decay)
    growth = jnp.exp(running)
    keep = jnp.exp(decay)
    last = running[length - 1 : length, :]
    fade = jnp.exp(last - running)
    state, adjoint = state_ref[0], adjoint_ref[0]
    key_state, value_state = state[:, :width], state[:, width:]
    key_adjoint, value_adjoint = adjoint[:, :width], adjoint[:, width:]
    key_dots = mm(q, k, 1, 1) * scale
    value_dots = mm(grad_out, v, 1, 1)
    row, col = grid_index(length, length)

    columns_sum = jnp.zeros((length, slots), F32)
    crossing = jnp.zeros((length, slots), F32)
    mix_key = jnp.zeros((length, length), F32)
    mix_value = jnp.zeros((length, length), F32)
    for half in levels(length):
        right, left, is_right = level_factors(running, writes, half)
        key_part, value_part = masked(key_dots, half), masked(value_dots, half)
        left_w = left * writes
        gs_right, at_right = grad_scores * right, attend * right
        mix_key = mix_key + masked(mm(gs_right, left_w, 1, 1), half)
        mix_value = mix_value + masked(mm(at_right, left_w, 1, 1), half)
        rows_sum = gs_right * mm_fine(key_part, left_w, 1, 0) + at_right * mm_fine(value_part, left_w, 1, 0)
        open_sum = left * (mm_fine(key_part, gs_right, 0, 0) + mm_fine(value_part, at_right, 0, 0))
        columns_sum = columns_sum + open_sum
        sums = jnp.where(is_right, rows_sum, open_sum * writes)
        forward = jnp.where((row % (2 * half)) >= half, col - row, row - col - 1) >= 0
        wanted = ((row // half) == (col // half)) & forward
        crossing = crossing + mm_left(wanted.astype(F32), sums, 1, 0)
    key_leaf, value_leaf = leaf_take(key_dots), leaf_take(value_dots)
    leaf_at = lax.broadcasted_iota(jnp.int32, (length, slots), 0) % LEAF
    difference = jnp.zeros((length, slots), F32)
    mix_key_columns, mix_value_columns = [], []
    for at in range(LEAF):
        fall = leaf_decay(running, at)
        mass = leaf_row(writes, at)
        mix_key_columns.append(jnp.sum(grad_scores * fall * mass, axis=1, keepdims=True))
        mix_value_columns.append(jnp.sum(attend * fall * mass, axis=1, keepdims=True))
        terms = fall * (
            grad_scores * key_leaf[:, at : at + 1] + attend * value_leaf[:, at : at + 1]
        )
        blocks = terms.reshape(length // LEAF, LEAF, slots)
        whole = jnp.broadcast_to(
            jnp.sum(blocks, axis=1, keepdims=True), blocks.shape
        ).reshape(length, slots)
        columns_sum = columns_sum + jnp.where(leaf_at == at, whole, 0.0)
        later = jnp.where(leaf_at > at, terms, 0.0)
        later_blocks = later.reshape(length // LEAF, LEAF, slots)
        later_whole = jnp.broadcast_to(
            jnp.sum(later_blocks, axis=1, keepdims=True), later_blocks.shape
        ).reshape(length, slots)
        difference = difference + mass * (later - jnp.where(leaf_at == at, later_whole, 0.0))
    mix_key = mix_key + leaf_spread(jnp.concatenate(mix_key_columns, axis=1))
    mix_value = mix_value + leaf_spread(jnp.concatenate(mix_value_columns, axis=1))
    suffix_leaf = (((row // LEAF) == (col // LEAF)) & (col >= row)).astype(F32)
    crossing = crossing + mm_exact(suffix_leaf, difference, 1, 0)

    start_terms = growth * (
        grad_scores * (mm(q, key_state, 1, 1) * scale)
        + attend * mm(grad_out, value_state, 1, 1)
    )
    crossing = crossing + mm_left((col >= row).astype(F32), start_terms, 1, 0)
    end_open = fade * (mm(k, key_adjoint, 1, 1) + mm(v, value_adjoint, 1, 1))
    columns_sum = columns_sum + end_open
    crossing = crossing + mm_left((col < row).astype(F32), end_open * writes, 1, 0)
    through = mm_exact(
        jnp.ones((8, 2 * width), F32), state.astype(F32) * adjoint.astype(F32), 1, 1
    )[0:1, :]
    crossing = crossing + jnp.exp(last) * through
    grad_decay = crossing - keep * columns_sum

    grad_q = (mm(grad_scores * growth, key_state, 1, 0) + mm(mix_key, k, 1, 0)) * scale
    fade_w = fade * writes
    grad_k = mm(mix_key, q, 0, 0) * scale + mm(fade_w, key_adjoint, 1, 0)
    grad_v = mm(mix_value, grad_out, 0, 0) + mm(fade_w, value_adjoint, 1, 0)
    dq_ref[0] = (grad_q * swish_slope(q_pre_ref[0])).astype(BF16)
    dk_ref[0] = (grad_k * swish_slope(k_pre_ref[0])).astype(BF16)
    dv_ref[0] = grad_v.astype(BF16)
    dlogit_ref[0] = (
        alive_ref[0] * grad_decay * jax.nn.sigmoid(-logit_ref[0]) * (1.0 / GATE_NORM)
    ).astype(BF16)


def per_sequence(kernel, inputs, outputs, shared=()):
    count = inputs[0].shape[0]

    def spec(shape):
        return pl.BlockSpec((1,) + tuple(shape[1:]), lambda s: (s, 0, 0))

    return pl.pallas_call(
        kernel,
        grid=(count,),
        in_specs=[spec(x.shape) for x in inputs]
        + [pl.BlockSpec(x.shape, lambda s: (0, 0)) for x in shared],
        out_specs=[spec(x.shape) for x in outputs],
        out_shape=outputs,
        compiler_params=pltpu.CompilerParams(vmem_limit_bytes=VMEM_LIMIT),
    )(*inputs, *shared)


class Lanes:
    def __init__(self):
        self.seq = lax.axis_size("seq")
        self.dp = lax.axis_size("dp")
        self.outer = self.seq // 2
        self.at = lax.axis_index("seq")
        self.d = lax.axis_index("dp")
        self.inner_at = lax.rem(self.at, 2)
        self.outer_at = self.at // 2
        self.groups = [[2 * k + i for k in range(self.outer)] for i in range(2)]

    def swap_inner(self, x):
        return lax.ppermute(x, "seq", [(i, i ^ 1) for i in range(self.seq)])

    def gather_outer(self, x):
        return lax.all_gather(x, "seq", axis=0, tiled=True, axis_index_groups=self.groups)

    def scatter_outer(self, x):
        return lax.psum_scatter(
            x, "seq", scatter_dimension=0, tiled=True, axis_index_groups=self.groups
        )

    def swap_dp(self, x, bit):
        return lax.ppermute(x, "dp", [(i, i ^ bit) for i in range(self.dp)])

    def gather_dp(self, x):
        far = self.swap_dp(x, 2)
        both = jnp.concatenate([x, far], axis=0)
        return jnp.concatenate([both, self.swap_dp(both, 1)], axis=0)

    def scatter_dp(self, x):
        rows = x.shape[0] // 4
        got = self.swap_dp(x[2 * rows :].astype(BF16), 1)
        mine = x[: 2 * rows] + got.astype(F32)
        got = self.swap_dp(mine[rows:].astype(BF16), 2)
        return mine[:rows] + got.astype(F32)

    def gather_plane(self, x):
        half = x.shape[0] // 2
        a, b = x[:half], x[half:]
        a = jnp.concatenate([a, self.swap_inner(a)], axis=0)
        b = jnp.concatenate([b, self.swap_dp(b, 2)], axis=0)
        a = jnp.concatenate([a, self.swap_dp(a, 2)], axis=0)
        b = jnp.concatenate([b, self.swap_inner(b)], axis=0)
        both = jnp.concatenate([a, b], axis=0)
        return jnp.concatenate([both, self.swap_dp(both, 1)], axis=0)

    def fold(self, x, swap):
        half = x.shape[0] // 2
        return x[:half] + swap(x[half:].astype(BF16)).astype(F32)

    def scatter_plane(self, x):
        x = self.fold(x, lambda p: self.swap_dp(p, 1))
        half = x.shape[0] // 2
        a = self.fold(x[:half], lambda p: self.swap_dp(p, 2))
        b = self.fold(x[half:], self.swap_inner)
        a = self.fold(a, self.swap_inner)
        b = self.fold(b, lambda p: self.swap_dp(p, 2))
        return jnp.concatenate([a, b], axis=0)

    def scatter_grad(self, own, other):
        got = self.swap_inner(other.astype(BF16))
        return self.scatter_outer((own + got.astype(F32)).astype(BF16))

    def swap_seq(self, x, bit):
        return lax.ppermute(x, "seq", [(i, i ^ bit) for i in range(self.seq)])

    def steps(self):
        found, bit = [], 1
        while bit < self.seq:
            found.append((functools.partial(self.swap_seq, bit=bit), (self.at // bit) % 2 == 1))
            bit *= 2
        bit = 1
        while bit < self.dp:
            found.append((functools.partial(self.swap_dp, bit=bit), (self.d // bit) % 2 == 1))
            bit *= 2
        return found

    def gather_small(self, x):
        x = x[None]
        for swap, is_set in self.steps():
            got = swap(x)
            x = jnp.concatenate([jnp.where(is_set, got, x), jnp.where(is_set, x, got)], axis=0)
        return x

    def scatter_small(self, x):
        for swap, is_set in reversed(self.steps()):
            half = x.shape[0] // 2
            low, high = x[:half], x[half:]
            x = jnp.where(is_set, high, low) + swap(jnp.where(is_set, low, high))
        return x[0]

    def exchange_heads(self, blocks):
        got = [lax.dynamic_index_in_dim(blocks, self.d, 0, keepdims=False)]
        for r in range(1, self.dp):
            part = lax.dynamic_index_in_dim(
                blocks, jnp.bitwise_xor(self.d, r), 0, keepdims=False
            )
            got.append(self.swap_dp(part, r))
        bit = 1
        while bit < self.dp:
            is_set = (self.d // bit) % 2 == 1
            got = [jnp.where(is_set, got[i ^ bit], got[i]) for i in range(self.dp)]
            bit *= 2
        return jnp.stack(got)

    def pick(self, natural, axis):
        first = lax.index_in_dim(natural, 0, axis, keepdims=False)
        second = lax.index_in_dim(natural, 1, axis, keepdims=False)
        even = self.inner_at == 0
        return jnp.where(even, first, second), jnp.where(even, second, first)


def swap_halves(x, parts):
    size = x.shape[-1] // (2 * parts)
    pieces = [x[..., i * size : (i + 1) * size] for i in range(2 * parts)]
    order = [i ^ 1 for i in range(2 * parts)]
    return jnp.concatenate([pieces[i] for i in order], axis=-1)


def chain(lanes, keeps, total, backward):
    half = total.shape[0] // 2
    even = lanes.inner_at == 0
    own_t = jnp.where(even, total[:half], total[half:])
    other_t = jnp.where(even, total[half:], total[:half])
    got_t = swap_halves(lanes.swap_inner(other_t.astype(BF16)), 2).astype(F32)
    keeps = jnp.where(even, keeps[:, :half], keeps[:, half:])
    keeps = keeps.reshape(lanes.outer, 2, half, -1)
    pair = lax.dynamic_index_in_dim(keeps, lanes.outer_at, 0, keepdims=False)
    is_first = jnp.logical_not(even) if backward else even
    first_t, second_t = jnp.where(is_first, own_t, got_t), jnp.where(is_first, got_t, own_t)
    first_k, second_k = (pair[1], pair[0]) if backward else (pair[0], pair[1])
    entering = jnp.zeros(own_t.shape, F32)
    reach = jnp.ones(first_k.shape, F32)
    block_t = second_k[..., None] * first_t + second_t
    block_keeps = keeps[:, 0] * keeps[:, 1]
    bit = 1
    while bit < lanes.outer:
        at = lanes.outer_at // bit
        is_set = at % 2 == 1
        later = jnp.logical_not(is_set) if backward else is_set
        last_step = 2 * bit == lanes.outer
        moves = [
            (i, i ^ (2 * bit))
            for i in range(lanes.seq)
            if not last_step or (((i // (2 * bit)) % 2 == 1) == backward)
        ]
        got_t = lax.ppermute(block_t.astype(BF16), "seq", moves).astype(F32)
        mine_k = lax.dynamic_index_in_dim(block_keeps, at, 0, keepdims=False)
        got_k = lax.dynamic_index_in_dim(
            block_keeps, jnp.bitwise_xor(at, 1), 0, keepdims=False
        )
        entering = entering + jnp.where(later, reach, 0.0)[..., None] * got_t
        reach = jnp.where(later, reach * got_k, reach)
        ahead_t, behind_t = jnp.where(later, got_t, block_t), jnp.where(later, block_t, got_t)
        block_t = jnp.where(later, mine_k, got_k)[..., None] * ahead_t + behind_t
        block_keeps = block_keeps.reshape(-1, 2, *block_keeps.shape[1:])
        block_keeps = block_keeps[:, 0] * block_keeps[:, 1]
        bit *= 2
    after = first_k[..., None] * entering + first_t
    mine = jnp.where(is_first, entering, after)
    theirs = jnp.where(is_first, after, entering)
    got = swap_halves(lanes.swap_inner(theirs.astype(BF16)), 2)
    mine = mine.astype(BF16)
    return jnp.concatenate(
        [jnp.where(even, mine, got), jnp.where(even, got, mine)], axis=0
    )


def per_device(
    tokens, lengths, cotangent, mixer_gain, feed_gain, head_gain, w_query, w_key, w_value,
    w_gate, w_out, rank_down, rank_up, rank_bias, w_act, w_lin, w_down,
):
    lanes = Lanes()
    seq_count, piece, width = tokens.shape
    rows = seq_count * piece
    sequences = lanes.dp * seq_count
    all_rows = lanes.dp * rows
    head_width = width // HEADS
    half_width = head_width // 2
    rank = rank_down.shape[1]
    devices = lanes.dp * lanes.seq

    counts = lengths.astype(F32)
    high = jnp.floor(counts / 256.0)
    small_parts = [
        mixer_gain, feed_gain, head_gain, rank_down.reshape(-1), rank_up.reshape(-1),
        rank_bias, high.astype(BF16), (counts - 256.0 * high).astype(BF16),
    ]
    sizes = [p.shape[0] for p in small_parts]
    used = sum(sizes)
    padded = -(-used // 128) * 128
    small = jnp.concatenate(small_parts + [jnp.zeros((padded - used,), BF16)])
    smalls = lanes.gather_small(small)
    cuts, offset = [], 0
    for size in sizes:
        cuts.append(smalls[:, offset : offset + size])
        offset += size
    mixer_full = cuts[0].reshape(1, width).astype(F32)
    feed_full = cuts[1].reshape(1, width).astype(F32)
    head_natural = cuts[2].reshape(lanes.outer, 2, half_width // lanes.outer)
    head_own, head_other = lanes.pick(head_natural, 1)
    head_full = jnp.concatenate(
        [head_own.reshape(1, half_width), head_other.reshape(1, half_width)], axis=1
    ).astype(F32)
    down_full = cuts[3].reshape(width, rank)
    up_mine = lax.dynamic_index_in_dim(
        cuts[4].reshape(lanes.dp, SLOTS, rank), lanes.d, 0, keepdims=False
    )
    bias_mine = lax.dynamic_index_in_dim(
        cuts[5].reshape(lanes.dp, 1, SLOTS), lanes.d, 0, keepdims=False
    ).astype(F32)
    all_lengths = cuts[6].astype(F32) * 256.0 + cuts[7].astype(F32)
    all_lengths = all_lengths.reshape(lanes.dp, lanes.seq, seq_count)[:, 0]

    position = (lanes.at * piece + jnp.arange(piece)).astype(F32)
    alive_own = (position[None, :] < counts[:, None]).astype(F32).reshape(rows, 1)
    group_lengths = jnp.concatenate(
        [
            lax.dynamic_index_in_dim(
                all_lengths, jnp.bitwise_xor(lanes.d, r), 0, keepdims=False
            )
            for r in (0, 2, 1, 3)
        ]
    )
    alive = (position[None, :] < group_lengths[:, None]).astype(F32).reshape(all_rows, 1)

    head_rows = w_query.shape[0]

    def gather_two(first, second):
        own = lanes.gather_outer(jnp.concatenate([first, second], axis=0))
        both = [
            x.reshape(lanes.outer, 2, head_rows, width) for x in (own, lanes.swap_inner(own))
        ]
        return [[x[:, m].reshape(half_width, width) for x in both] for m in range(2)]

    (k_own, k_other), (v_own, v_other) = gather_two(w_key, w_value)
    (q_own, q_other), (g_own, g_other) = gather_two(w_query, w_gate)

    out_rows = w_out.shape[0]
    out_split = w_out.reshape(out_rows, lanes.dp, lanes.outer, 2, -1)
    out_own, out_other = lanes.pick(out_split, 3)
    out_local = jnp.concatenate(
        [
            out_own.reshape(out_rows, lanes.dp, half_width),
            out_other.reshape(out_rows, lanes.dp, half_width),
        ],
        axis=2,
    )
    out_mine = lanes.exchange_heads(out_local.transpose(1, 0, 2))
    out_own = lanes.gather_outer(out_mine[None])
    out_other = swap_halves(lanes.swap_inner(out_own), 1)
    even = lanes.inner_at == 0
    out_natural = jnp.stack(
        [jnp.where(even, out_own, out_other), jnp.where(even, out_other, out_own)], axis=2
    )
    out_full = out_natural.transpose(1, 0, 2, 3, 4).reshape(width, head_width)

    down = lanes.gather_outer(w_down)
    act = lanes.gather_outer(w_act)
    lin = lanes.gather_outer(w_lin)

    own_tokens = tokens.reshape(rows, width)
    sources = lanes.gather_dp(own_tokens).astype(F32)
    normed_in = (sources * rms_scale(sources) * mixer_full).astype(BF16)
    grad_out = cotangent.reshape(rows, width).astype(F32) * alive_own
    grad_feed = lanes.gather_plane(grad_out.astype(BF16))

    def project(own, other):
        return jnp.concatenate(
            [contract_last(normed_in, own), contract_last(normed_in, other)], axis=1
        )

    query_pre, key_pre = project(q_own, q_other), project(k_own, k_other)
    value_pre, gate_pre = project(v_own, v_other), project(g_own, g_other)
    low_rank = mm(normed_in, down_full, 1, 0).astype(BF16)
    gate_logit = contract_last(low_rank, up_mine) + bias_mine
    log_decay = jax.nn.log_sigmoid(gate_logit) / GATE_NORM * alive
    writes = -jnp.expm1(log_decay)

    def seqs(x):
        return x.reshape(sequences, piece, x.shape[1])

    def flat(x):
        return x.reshape(all_rows, x.shape[2])

    queries = seqs(jax.nn.silu(query_pre).astype(BF16))
    key_feats = seqs(jax.nn.silu(key_pre).astype(BF16))
    value_feats = seqs(value_pre.astype(BF16))
    decays, writes = seqs(log_decay), seqs(writes)
    gates = seqs(gate_pre)

    def shaped(like_rows, columns, kind):
        return jax.ShapeDtypeStruct((sequences, like_rows, columns), kind)

    summary, keep_all = per_sequence(
        summary_kernel,
        [key_feats, value_feats, decays, writes],
        [shaped(SLOTS, 2 * head_width, F32), shaped(1, SLOTS, F32)],
    )
    keep_all = keep_all.reshape(sequences, SLOTS)
    keeps = keep_all[None]
    bit = 1
    while bit < lanes.seq:
        got = lanes.swap_seq(keeps, bit)
        is_set = (lanes.at // bit) % 2 == 1
        keeps = jnp.concatenate(
            [jnp.where(is_set, got, keeps), jnp.where(is_set, keeps, got)], axis=0
        )
        bit *= 2
    state_in = chain(lanes, keeps, summary, False)
    mixed, slot_out, attend = per_sequence(
        forward_kernel,
        [queries, key_feats, value_feats, gates, decays, writes, state_in],
        [
            shaped(piece, head_width, BF16),
            shaped(piece, head_width, F32),
            shaped(piece, SLOTS, F32),
        ],
        shared=[head_full],
    )
    mixed_flat = flat(mixed)
    hidden = own_tokens.astype(F32) + lanes.scatter_dp(contract_last(mixed_flat, out_full))
    mid_scale = rms_scale(hidden)
    normed_mid = lanes.gather_plane((hidden * mid_scale * feed_full).astype(BF16))

    grad_product = contract_last(grad_feed, down)
    gate_part = contract_last(normed_mid, act)
    lin_part = contract_last(normed_mid, lin)
    sigma = jax.nn.sigmoid(gate_part)
    swish = gate_part * sigma
    product = (swish * lin_part).astype(BF16)
    grad_gate = (
        grad_product * lin_part * (sigma * (1.0 + gate_part * (1.0 - sigma)))
    ).astype(BF16)
    grad_lin = (grad_product * swish).astype(BF16)
    grad_mid = lanes.scatter_plane(mm(grad_gate, act, 1, 0) + mm(grad_lin, lin, 1, 0))
    w_down_grad = lanes.scatter_outer(contract_first(product, grad_feed).astype(BF16))
    w_act_grad = lanes.scatter_outer(contract_first(grad_gate, normed_mid).astype(BF16))
    w_lin_grad = lanes.scatter_outer(contract_first(grad_lin, normed_mid).astype(BF16))
    w_down_grad, w_act_grad, w_lin_grad = [
        x.astype(F32) for x in (w_down_grad, w_act_grad, w_lin_grad)
    ]

    mid_unit = hidden * mid_scale
    feed_gain_part = jnp.sum(grad_mid * mid_unit, axis=0)
    scaled = grad_mid * feed_full
    grad_hidden = grad_out + mid_scale * (
        scaled - mid_unit * jnp.mean(scaled * mid_unit, axis=-1, keepdims=True)
    )
    grad_attn = lanes.gather_dp(grad_hidden.astype(BF16))

    product, grad_attn = lax.optimization_barrier((product, grad_attn))
    feed_sum = lanes.scatter_plane(mm(product, down, 1, 0))
    block_out = (alive_own * (hidden + feed_sum)).astype(BF16)

    grad_mixed = mm(grad_attn, out_full, 1, 0)
    out_grad = contract_first(grad_attn, mixed_flat).astype(BF16)
    out_grad = out_grad.reshape(lanes.dp, lanes.outer, 2, out_rows, head_width)
    own_part, other_part = lanes.pick(out_grad, 2)
    got = swap_halves(lanes.swap_inner(other_part), 1)
    out_sum = (own_part.astype(F32) + got.astype(F32)).astype(BF16).transpose(1, 0, 2, 3)
    out_mine = lanes.scatter_outer(out_sum.reshape(-1, head_width))
    out_mine = out_mine.reshape(lanes.dp, out_rows, head_width)
    out_mine = lanes.exchange_heads(out_mine).transpose(1, 0, 2)
    out_mine = out_mine.reshape(out_rows, lanes.dp, 2, lanes.outer, -1)
    low_half, high_half = lanes.pick(out_mine, 2)
    w_out_grad = jnp.stack([low_half, high_half], axis=3).reshape(out_rows, width).astype(F32)

    grad_gate_pre, grad_slot, grad_scores, adjoint, head_parts = per_sequence(
        back_first_kernel,
        [seqs(grad_mixed), gates, slot_out, attend, queries, value_feats, decays, writes, state_in],
        [
            shaped(piece, head_width, BF16),
            shaped(piece, head_width, BF16),
            shaped(piece, SLOTS, F32),
            shaped(SLOTS, 2 * head_width, F32),
            shaped(1, head_width, F32),
        ],
        shared=[head_full],
    )
    adjoint_in = chain(lanes, keeps, adjoint, True)
    grad_query_pre, grad_key_pre, grad_value_pre, grad_logit = per_sequence(
        back_second_kernel,
        [
            grad_slot, grad_scores, attend, queries, key_feats, value_feats, decays, writes,
            state_in, adjoint_in, seqs(query_pre), seqs(key_pre), seqs(gate_logit), seqs(alive),
        ],
        [
            shaped(piece, head_width, BF16),
            shaped(piece, head_width, BF16),
            shaped(piece, head_width, BF16),
            shaped(piece, SLOTS, BF16),
        ],
    )
    grad_logit = flat(grad_logit)
    bias_part = jnp.sum(grad_logit.astype(F32), axis=0)
    up_part = contract_first(grad_logit, low_rank)
    grad_rank = mm(grad_logit, up_mine, 1, 0).astype(BF16)
    down_part = contract_first(normed_in, grad_rank)

    grad_in = contract_last(grad_rank, down_full)
    mixer_grads = []
    for grad_pre, (own, other) in zip(
        (grad_gate_pre, grad_query_pre, grad_key_pre, grad_value_pre),
        ((g_own, g_other), (q_own, q_other), (k_own, k_other), (v_own, v_other)),
    ):
        grad_pre = flat(grad_pre)
        low, high = grad_pre[:, :half_width], grad_pre[:, half_width:]
        grad_in = grad_in + mm(low, own, 1, 0) + mm(high, other, 1, 0)
        mixer_grads.append(
            lanes.scatter_grad(
                contract_first(low, normed_in), contract_first(high, normed_in)
            ).astype(F32)
        )
    w_gate_grad, w_query_grad, w_key_grad, w_value_grad = mixer_grads
    grad_in = lanes.scatter_dp(grad_in)
    own_sources = own_tokens.astype(F32)
    in_scale = rms_scale(own_sources)
    in_unit = own_sources * in_scale
    mixer_gain_part = jnp.sum(grad_in * in_unit, axis=0)
    scaled = grad_in * mixer_full
    tokens_grad = grad_hidden + in_scale * (
        scaled - in_unit * jnp.mean(scaled * in_unit, axis=-1, keepdims=True)
    )
    tokens_grad = tokens_grad.reshape(seq_count, piece, width)

    head_part = jnp.sum(head_parts, axis=(0, 1)).reshape(2, lanes.outer, -1)
    low_half, high_half = lanes.pick(head_part, 0)
    head_part = jnp.stack([low_half, high_half], axis=1)
    mine = (jnp.arange(lanes.dp) == lanes.d).astype(F32)
    up_all = mine[:, None] * up_part.reshape(1, -1)
    bias_all = mine[:, None] * bias_part.reshape(1, -1)
    parts = [
        mixer_gain_part.reshape(devices, -1),
        feed_gain_part.reshape(devices, -1),
        head_part.reshape(devices, -1),
        down_part.reshape(devices, -1),
        up_all.reshape(devices, -1),
        bias_all.reshape(devices, -1),
    ]
    sizes = [p.shape[1] for p in parts]
    padded = -(-sum(sizes) // 128) * 128
    parts.append(jnp.zeros((devices, padded - sum(sizes)), F32))
    reduced = lanes.scatter_small(jnp.concatenate(parts, axis=1))
    smalls, offset = [], 0
    for size in sizes:
        smalls.append(reduced[offset : offset + size])
        offset += size
    return (
        block_out.reshape(seq_count, piece, width),
        tokens_grad,
        smalls[0],
        smalls[1],
        smalls[2],
        w_query_grad,
        w_key_grad,
        w_value_grad,
        w_gate_grad,
        w_out_grad,
        smalls[3].reshape(-1, rank),
        smalls[4].reshape(-1, rank),
        smalls[5],
        w_act_grad,
        w_lin_grad,
        w_down_grad,
    )


def solution(mesh):
    vector = P(("dp", "seq"))
    matrix = P(("dp", "seq"), None)
    stream = P("dp", "seq", None)
    return jax.shard_map(
        per_device,
        mesh=mesh,
        in_specs=(
            stream, P("dp"), stream, vector, vector, vector, matrix, matrix, matrix, matrix,
            matrix, matrix, matrix, vector, matrix, matrix, matrix,
        ),
        out_specs=(
            stream, stream, vector, vector, vector, matrix, matrix, matrix, matrix, matrix,
            matrix, matrix, vector, matrix, matrix, matrix,
        ),
        check_vma=False,
    )
```

time: 5960 us -> 1060 us (0.18)
  waiting for transfers between devices: 4150 us -> 437 us
  matrix products: 698 us -> 221 us
  local copies, waits for them, and re-layouts: 371 us -> 101 us
  other arithmetic: 391 us -> 128 us
  blocking collectives: 254 us -> 0 us
  starting transfers between devices: 0.59 us -> 83.2 us
    unnamed x18 -> x14, waiting for transfers between devices: 3500 us -> 0.23 us
    all_gather x12 -> x6, waiting for transfers between devices: 652 us -> 96.2 us  [gather_outer(): lax.all_gather(x, 'seq', axis=0, tiled=True, axis_index_groups=self.groups)]
    dot_general x171 -> x42, matrix products: 696 us -> 221 us  [mm(): lax.dot_general(a.astype(BF16), b.astype(BF16), (((ca,), (cb,)), ((), ())...]
    ppermute x0 -> x63, waiting for transfers between devices: none -> 329 us  [the longest x30 157 us: swap_dp(): return lax.ppermute(x, 'dp', [(i, i ^ bit) for i in range(self.dp)])]
    all_gather x4 -> x0, blocking collectives: 172 us -> none  [the longest x1 66.5 us: per_device(): lax.all_gather(rank_up, ('dp', 'seq'), axis=0, tiled=True)]
    unnamed x170 -> x325, local copies, waits for them, and re-layouts: 115 us -> 31 us
    unnamed x2 -> x0, blocking collectives: 81.8 us -> none
    ppermute x0 -> x63, starting transfers between devices: none -> 81.3 us  [the longest x30 45.8 us: swap_dp(): return lax.ppermute(x, 'dp', [(i, i ^ bit) for i in range(self.dp)])]
  transfers between devices with their start and end apart: 15 -> 77, of which waited for: 9 -> 40; matrix products, arithmetic and copies ran while one was open for 11% -> 38% of each run, Pallas kernels for 0% -> 4%
where the time goes in v1:
time: 1060 us; the launch traced here: 1040 us
  waiting for transfers between devices  437 us (41%)
  matrix products  221 us (21%)
  other arithmetic  128 us (12%)
  local copies, waits for them, and re-layouts  101 us (10%)
  starting transfers between devices  83.2 us (8%)
  Pallas kernels  57.8 us (5%)
  between operations  16.5 us (2%)
    dot_general x42, matrix products, mm(): lax.dot_general(a.astype(BF16), b.astype(BF16), (((ca,), (cb,)), ((), ())...  221 us
    ppermute x30, waiting for transfers between devices, swap_dp(): return lax.ppermute(x, 'dp', [(i, i ^ bit) for i in range(self.dp)])  157 us
    ppermute x20, waiting for transfers between devices, swap_inner(): return lax.ppermute(x, 'seq', [(i, i ^ 1) for i in range(self.seq)])  117 us
    all_gather x6, waiting for transfers between devices, gather_outer(): lax.all_gather(x, 'seq', axis=0, tiled=True, axis_index_groups=self.groups)  96.2 us
    pallas_call x4, Pallas kernels, per_sequence(): pl.pallas_call(kernel, grid=(count,), in_specs=[spec(x.shape) for x in in...  57.8 us
    ppermute x30, starting transfers between devices, swap_dp(): return lax.ppermute(x, 'dp', [(i, i ^ bit) for i in range(self.dp)])  45.8 us
    ppermute x4, waiting for transfers between devices, chain(): got_t = lax.ppermute(block_t.astype(BF16), 'seq', moves).astype(F32)  44.7 us
    unnamed x325, local copies, waits for them, and re-layouts  31 us
  transfers between devices with their start and end apart: 77, of which 40 were waited for; matrix products, arithmetic and copies ran while one was open for 38% of the time, Pallas kernels for 4%

profile of v1, /device:TPU:21, one launch (start us, length us, event | category | flops | bytes accessed | tf_op | source)
XLA Modules:
  0.0 1044.1 jit_solution(4501343614503096901)
XLA Ops:
  28.6 3.7 collective-permute-start.5
  33.1 13.6 %collective-permute-done = bf16[256,2048]{1,0:T(8,128)(2,1)S(1)} collective-permute-done((bf16[256,2048]{1,0:T(8,128)(2,1)S(1)}, bf16[256,2048]{1,0:T(8,128)(2,1)S(1)}, u32[]{:S(2)}, u32[]{:S(2)}) %collective-permute-start) | collective-permute-done | bytes 1048608 | tf_op jit(solution)/shard_map/ppermute | solution.py:380
  49.2 3.7 collective-permute-start.1
  62.9 6.2 multiply_convert_fusion.1
  71.9 5.6 maximum_convert_fusion
  77.5 15.0 %all-gather.10.cloned.1.call-done = bf16[512,2048]{1,0:T(8,128)(2,1)} async-done(((bf16[128,2048]{1,0:T(8,128)(2,1)}), bf16[512,2048]{1,0:T(8,128)(2,1)}) %all-gather.10.cloned.1.call-update) | async-done | bytes 2097168 | tf_op jit(solution)/shard_map/all_gather | solution.py:372
  95.4 44.0 %all-gather.8.cloned.1.call-done = bf16[512,2048]{1,0:T(8,128)(2,1)} async-done(((bf16[128,2048]{1,0:T(8,128)(2,1)}), bf16[512,2048]{1,0:T(8,128)(2,1)}) %all-gather.8.cloned.1.call-update) | async-done | bytes 2097168 | tf_op jit(solution)/shard_map/all_gather | solution.py:372
  151.4 34.7 %collective-permute-done.7 = bf16[512,2048]{1,0:T(8,128)(2,1)S(1)} collective-permute-done((bf16[512,2048]{1,0:T(8,128)(2,1)}, bf16[512,2048]{1,0:T(8,128)(2,1)S(1)}, u32[]{:S(2)}, u32[]{:S(2)}) %collective-permute-start.7) | collective-permute-done | bytes 2097184 | tf_op jit(solution)/shard_map/ppermute | solution.py:369
  192.6 3.9 shard_map.288
  205.2 5.7 collective-permute-done.12
  212.8 8.4 collective-permute-done.13
  226.4 7.4 collective-permute-done.14
  247.2 14.6 %shard_map.289 = (bf16[8,128,512]{2,1,0:T(8,128)(2,1)S(1)}, f32[8,128,512]{2,1,0:T(8,128)S(1)}, f32[8,128,64]{2,1,0:T(8,128)S(1)}) custom-call(bf16[8,128,512]{2,1,0:T(8,128)(2,1)S(1)} %copy-done.6, bf16[8,128,512]{2,1,0:T(8,128)(2,1)S(1)} %copy-done.4, bf16[8,128,512]{2,1,0:T(8,128)(2,1)S(1)} %pad_maximum_fusion.9.v_ref, f32[8,128,512]{2,1,0:T(8,128)S(1)} %bitcast.255, ...), custom_call_target="tpu_custom_call" | custom-call | tf_op jit(solution)/shard_map/pallas_call | solution.py:346
  264.5 6.6 collective-permute-start.20
  273.9 12.4 %collective-permute-done.27 = bf16[128,2048]{1,0:T(8,128)(2,1)S(1)} collective-permute-done((bf16[128,2048]{1,0:T(8,128)(2,1)S(1)}, bf16[128,2048]{1,0:T(8,128)(2,1)S(1)}, u32[]{:S(2)}, u32[]{:S(2)}) %collective-permute-start.27) | collective-permute-done | bytes 524320 | tf_op jit(solution)/shard_map/ppermute | solution.py:369
  295.0 16.4 %collective-permute-done.28 = bf16[256,2048]{1,0:T(8,128)(2,1)} collective-permute-done((bf16[256,2048]{1,0:T(8,128)(2,1)}, bf16[256,2048]{1,0:T(8,128)(2,1)}, u32[]{:S(2)}, u32[]{:S(2)}) %collective-permute-start.28) | collective-permute-done | bytes 1048608 | tf_op jit(solution)/shard_map/ppermute | solution.py:380
  313.7 20.2 %collective-permute-done.21 = bf16[256,2048]{1,0:T(8,128)(2,1)} collective-permute-done((bf16[256,2048]{1,0:T(8,128)(2,1)}, bf16[256,2048]{1,0:T(8,128)(2,1)}, u32[]{:S(2)}, u32[]{:S(2)}) %collective-permute-start.21) | collective-permute-done | bytes 1048608 | tf_op jit(solution)/shard_map/ppermute | solution.py:380
  339.8 9.4 collective-permute-done.22
  352.7 21.2 %collective-permute-done.23 = bf16[256,2048]{1,0:T(8,128)(2,1)S(1)} collective-permute-done((bf16[256,2048]{1,0:T(8,128)(2,1)S(1)}, bf16[256,2048]{1,0:T(8,128)(2,1)S(1)}, u32[]{:S(2)}, u32[]{:S(2)}) %collective-permute-start.23) | collective-permute-done | bytes 1048608 | tf_op jit(solution)/shard_map/ppermute | solution.py:380
  381.2 6.0 collective-permute-done.24
  391.2 17.4 %collective-permute-done.25 = bf16[256,2048]{1,0:T(8,128)(2,1)S(1)} collective-permute-done((bf16[256,2048]{1,0:T(8,128)(2,1)S(1)}, bf16[256,2048]{1,0:T(8,128)(2,1)S(1)}, u32[]{:S(2)}, u32[]{:S(2)}) %collective-permute-start.25) | collective-permute-done | bytes 1048608 | tf_op jit(solution)/shard_map/ppermute | solution.py:369
  410.2 4.2 collective-permute-start.26
  414.7 4.8 constant_dynamic-update-slice_fusion.21
  421.5 4.8 constant_dynamic-update-slice_fusion.8
  426.3 11.0 %fusion.122 = f32[2048,704]{0,1:T(8,128)} fusion(bf16[2048,2048]{1,0:T(8,128)(2,1)} %constant_dynamic-update-slice_fusion.8, bf16[704,2048]{1,0:T(8,128)(2,1)} %all-gather.14.cloned.1.call-done), kind=kOutput, calls=%fused_computation.374 | convolution fusion | flops 5905580032 | bytes 17039360 | tf_op jit(solution)/shard_map/dot_general | solution.py:21
  437.4 11.1 %fusion.121 = f32[2048,704]{0,1:T(8,128)} fusion(bf16[2048,2048]{1,0:T(8,128)(2,1)} %constant_dynamic-update-slice_fusion.8, bf16[704,2048]{1,0:T(8,128)(2,1)} %all-gather.12.cloned.1.call-done), kind=kOutput, calls=%fused_computation.373 | convolution fusion | flops 5905580032 | bytes 17039360 | tf_op jit(solution)/shard_map/dot_general | solution.py:21
  448.5 37.3 %all-gather.16.cloned.1.call-done = bf16[704,2048]{1,0:T(8,128)(2,1)} async-done(((bf16[176,2048]{1,0:T(8,128)(2,1)}), bf16[704,2048]{1,0:T(8,128)(2,1)}) %all-gather.16.cloned.1.call-update) | async-done | bytes 2883600 | tf_op jit(solution)/shard_map/all_gather | solution.py:372
  485.7 15.4 %multiply_convert_fusion.2 = (bf16[2048,704]{0,1:T(8,128)(2,1)}, bf16[2048,704]{0,1:T(8,128)(2,1)}, bf16[2048,704]{0,1:T(8,128)(2,1)S(1)}) fusion(f32[2048,704]{0,1:T(8,128)} %fusion.121, f32[2048,704]{0,1:T(8,128)} %fusion.122, bf16[2048,2048]{1,0:T(8,128)(2,1)} %constant_dynamic-update-slice_fusion.21, bf16[704,2048]{1,0:T(8,128)(2,1)} %all-gather.16.cloned.1.call-done), kind=kOutput, calls=%fused_computation.9 | convolution fusion | flops 5927206912 | bytes 31457280 | tf_op jit(solution)/shard_map/dot_general | solution.py:21
  502.7 10.9 %convolution_convert_fusion = bf16[704,2048]{1,0:T(8,128)(2,1)} fusion(bf16[2048,704]{0,1:T(8,128)(2,1)S(1)} %get-tuple-element.35, bf16[2048,2048]{1,0:T(8,128)(2,1)} %constant_dynamic-update-slice_fusion.21), kind=kOutput, calls=%fused_computation.21 | convolution fusion | flops 5907021824 | bytes 14155776 | tf_op jit(solution)/shard_map/dot_general | solution.py:21
  513.8 12.6 %fusion.123 = f32[2048,2048]{1,0:T(8,128)} fusion(bf16[2048,704]{0,1:T(8,128)(2,1)} %get-tuple-element.173, bf16[704,2048]{1,0:T(8,128)(2,1)} %all-gather.12.cloned.1.call-done), kind=kOutput, calls=%fused_computation.375 | convolution fusion | flops 5905580032 | bytes 22544384 | tf_op jit(solution)/shard_map/dot_general | solution.py:21
  526.5 13.8 %convolution_add_fusion = f32[2048,2048]{1,0:T(8,128)} fusion(f32[2048,2048]{1,0:T(8,128)} %fusion.123, bf16[2048,704]{0,1:T(8,128)(2,1)S(1)} %copy-done.146, bf16[704,2048]{1,0:T(8,128)(2,1)S(1)} %copy-done.142), kind=kOutput, calls=%fused_computation.8 | convolution fusion | flops 5909774336 | bytes 39321600 | tf_op jit(solution)/shard_map/dot_general | solution.py:21
  540.3 6.0 slice.810
  547.0 10.9 %convolution_convert_fusion.1 = bf16[704,2048]{1,0:T(8,128)(2,1)} fusion(bf16[2048,704]{0,1:T(8,128)(2,1)S(1)} %copy-done.146, bf16[2048,2048]{1,0:T(8,128)(2,1)} %constant_dynamic-update-slice_fusion.8), kind=kOutput, calls=%fused_computation.22 | convolution fusion | flops 5907021824 | bytes 14155776 | tf_op jit(solution)/shard_map/dot_general | solution.py:21
  558.4 11.6 %fusion.97 = (bf16[1024,2048]{1,0:T(8,128)(2,1)}, f32[1024,2048]{1,0:T(8,128)}) fusion(bf16[1024,2048]{1,0:T(8,128)(2,1)} %collective-permute-done.32, f32[2048,2048]{1,0:T(8,128)} %convolution_add_fusion), kind=kLoop, calls=%fused_computation.350 | loop fusion | flops 6291456 | bytes 25165824 | tf_op jit(solution)/shard_map/convert.18
  573.2 23.4 %collective-permute-done.33 = bf16[256,2048]{1,0:T(8,128)(2,1)S(1)} collective-permute-done((bf16[256,2048]{1,0:T(8,128)(2,1)S(1)}, bf16[256,2048]{1,0:T(8,128)(2,1)S(1)}, u32[]{:S(2)}, u32[]{:S(2)}) %collective-permute-start.33) | collective-permute-done | bytes 1048608 | tf_op jit(solution)/shard_map/ppermute | solution.py:380
  596.7 4.5 slice_add_fusion.8
  604.5 11.0 %convolution_convert_fusion.2 = bf16[704,2048]{1,0:T(8,128)(2,1)} fusion(bf16[2048,704]{0,1:T(8,128)(2,1)S(1)} %copy-done.149, bf16[2048,2048]{1,0:T(8,128)(2,1)} %constant_dynamic-update-slice_fusion.8), kind=kOutput, calls=%fused_computation.23 | convolution fusion | flops 5907021824 | bytes 14155776 | tf_op jit(solution)/shard_map/dot_general | solution.py:21
  619.8 9.5 collective-permute-done.34
  633.9 22.2 %collective-permute-done.37 = bf16[256,2048]{1,0:T(8,128)(2,1)S(1)} collective-permute-done((bf16[256,2048]{1,0:T(8,128)(2,1)S(1)}, bf16[256,2048]{1,0:T(8,128)(2,1)S(1)}, u32[]{:S(2)}, u32[]{:S(2)}) %collective-permute-start.37) | collective-permute-done | bytes 1048608 | tf_op jit(solution)/shard_map/ppermute | solution.py:380
  675.2 11.4 %reduce-scatter.19.cloned.1.call-done = bf16[176,2048]{1,0:T(8,128)(2,1)} async-done(((bf16[704,2048]{1,0:T(8,128)(2,1)}), bf16[176,2048]{1,0:T(8,128)(2,1)}) %reduce-scatter.19.cloned.1.call-update) | async-done | bytes 720912 | tf_op jit(solution)/shard_map/reduce_scatter | solution.py:375
  692.3 3.7 convolution_convert_fusion.3
  698.4 13.4 %shard_map.290 = (bf16[8,128,512]{2,1,0:T(8,128)(2,1)S(1)}, bf16[8,128,512]{2,1,0:T(8,128)(2,1)S(1)}, f32[8,128,64]{2,1,0:T(8,128)S(1)}, f32[8,64,1024]{2,1,0:T(8,128)S(1)}, f32[8,1,512]{2,1,0:T(1,128)S(1)}) custom-call(f32[8,128,512]{2,1,0:T(8,128)S(1)} %fusion.125.grad_mixed_ref, f32[8,128,512]{2,1,0:T(8,128)S(1)} %bitcast.256, f32[8,128,512]{2,1,0:T(8,128)} %copy-done.19, ...), custom_call_target="tpu_custom_call" | custom-call | tf_op jit(solution)/shard_map/pallas_call | solution.py:346
  720.3 10.3 fusion.124
  733.6 14.8 %collective-permute-done.59 = bf16[4,4,64,512]{3,2,0,1:T(8,128)(2,1)} collective-permute-done((bf16[4,4,64,512]{3,2,0,1:T(8,128)(2,1)}, bf16[4,4,64,512]{3,2,0,1:T(8,128)(2,1)}, u32[]{:S(2)}, u32[]{:S(2)}) %collective-permute-start.59) | collective-permute-done | bytes 1048608 | tf_op jit(solution)/shard_map/ppermute | solution.py:369
  751.7 5.8 fusion.56
  763.8 5.8 fusion.60
  769.6 28.9 %collective-permute-done.46 = bf16[4,64,1024]{2,1,0:T(8,128)(2,1)} collective-permute-done((bf16[4,64,1024]{2,1,0:T(8,128)(2,1)}, bf16[4,64,1024]{2,1,0:T(8,128)(2,1)}, u32[]{:S(2)}, u32[]{:S(2)}) %collective-permute-start.46) | collective-permute-done | bytes 524320 | tf_op jit(solution)/shard_map/ppermute | solution.py:504
  802.8 6.2 slice.809
  818.4 26.0 %shard_map.291 = (bf16[8,128,512]{2,1,0:T(8,128)(2,1)S(1)}, bf16[8,128,512]{2,1,0:T(8,128)(2,1)S(1)}, bf16[8,128,512]{2,1,0:T(8,128)(2,1)S(1)}, bf16[8,128,64]{2,1,0:T(8,128)(2,1)S(1)}) custom-call(bf16[8,128,512]{2,1,0:T(8,128)(2,1)S(1)} %copy-done.30, f32[8,128,64]{2,1,0:T(8,128)S(1)} %copy-done.32, f32[8,128,64]{2,1,0:T(8,128)S(1)} %copy-done.22, ...), custom_call_target="tpu_custom_call" | custom-call | tf_op jit(solution)/shard_map/pallas_call | solution.py:346
  847.0 4.5 fusion.38
  856.0 4.5 fusion.42
  860.5 4.5 fusion.47
  865.0 3.7 collective-permute-done.57
  873.6 4.5 fusion.126
  878.5 5.8 fusion.51
  884.3 4.5 fusion.33
  888.8 5.6 collective-permute-done.55
  898.0 25.8 %add_add_fusion = f32[1024,2048]{1,0:T(8,128)} fusion(f32[1024,2048]{1,0:T(8,128)} %fusion.33, f32[1024,2048]{1,0:T(8,128)} %fusion.38, f32[1024,2048]{1,0:T(8,128)} %fusion.42, f32[1024,2048]{1,0:T(8,128)} %fusion.47, f32[1024,2048]{1,0:T(8,128)} %fusion.51, f32[1024,2048]{1,0:T(8,128)} %fusion.56, f32[1024,2048]{1,0:T(8,128)} %fusion.126, ...), kind=kOutput, calls=%fused_computation.4 | convolution fusion | flops 1090519040 | bytes 77070336 | tf_op jit(solution)/shard_map/dot_general | solution.py:21
  924.0 4.0 slice.811
  928.1 6.8 collective-permute-start.48
  941.3 4.8 add_convert_fusion.2
  956.0 11.6 %fusion.94 = (bf16[1024,2048]{1,0:T(8,128)(2,1)}, f32[1024,2048]{1,0:T(8,128)}) fusion(bf16[1024,2048]{1,0:T(8,128)(2,1)} %collective-permute-done.39, f32[2048,2048]{1,0:T(8,128)} %fusion.124), kind=kLoop, calls=%fused_computation.348 | loop fusion | flops 6291456 | bytes 25165824 | tf_op jit(solution)/shard_map/convert.13
  967.7 13.0 %collective-permute-done.49 = bf16[256,2048]{1,0:T(8,128)(2,1)S(1)} collective-permute-done((bf16[256,2048]{1,0:T(8,128)(2,1)S(1)}, bf16[256,2048]{1,0:T(8,128)(2,1)S(1)}, u32[]{:S(2)}, u32[]{:S(2)}) %collective-permute-start.49) | collective-permute-done | bytes 1048608 | tf_op jit(solution)/shard_map/ppermute | solution.py:380
  998.9 12.5 %collective-permute-done.40 = bf16[256,2048]{1,0:T(8,128)(2,1)} collective-permute-done((bf16[256,2048]{1,0:T(8,128)(2,1)}, bf16[256,2048]{1,0:T(8,128)(2,1)}, u32[]{:S(2)}, u32[]{:S(2)}) %collective-permute-start.40) | collective-permute-done | bytes 1048608 | tf_op jit(solution)/shard_map/ppermute | solution.py:380
  (678 shorter events, 284.1 us)
Async XLA Ops:
  7.2 52.0 %all-gather.18.cloned.1.call-start = ((), (), s32[]{:S(2)}) async-start(), calls=%async_computation.21 | async-start | bytes 1310720 | tf_op jit(solution)/shard_map/all_gather | solution.py:372
  17.2 75.3 %all-gather.10.cloned.1.call-start = ((), (), s32[]{:S(2)}) async-start(), calls=%async_computation.9 | async-start | bytes 2621440 | tf_op jit(solution)/shard_map/all_gather | solution.py:372
  18.1 121.2 %all-gather.8.cloned.1.call-start = ((), (), s32[]{:S(2)}) async-start(), calls=%async_computation.8 | async-start | bytes 2621440 | tf_op jit(solution)/shard_map/all_gather | solution.py:372
  19.1 407.2 %all-gather.14.cloned.1.call-start = ((), (), s32[]{:S(2)}) async-start(), calls=%async_computation.11 | async-start | bytes 3604480 | tf_op jit(solution)/shard_map/all_gather | solution.py:372
  24.9 21.9 %collective-permute-start = (bf16[256,2048]{1,0:T(8,128)(2,1)S(1)}, bf16[256,2048]{1,0:T(8,128)(2,1)S(1)}, u32[]{:S(2)}, u32[]{:S(2)}) collective-permute-start(bf16[256,2048]{1,0:T(8,128)(2,1)S(1)} %bitcast.292), channel_id=1, source_target_pairs={{0,16},{8,24},{16,0},{24,8},{1,17},{9,25},{17,1},{25,9},{2,18},{10... | collective-permute-start | bytes 3145736 | tf_op jit(solution)/shard_map/ppermute | solution.py:380
  32.3 405.1 %all-gather.12.cloned.1.call-start = ((), (), s32[]{:S(2)}) async-start(), calls=%async_computation.10 | async-start | bytes 3604480 | tf_op jit(solution)/shard_map/all_gather | solution.py:372
  49.2 11.2 %collective-permute-start.1 = (bf16[512,2048]{1,0:T(8,128)(2,1)}, bf16[512,2048]{1,0:T(8,128)(2,1)S(1)}, u32[]{:S(2)}, u32[]{:S(2)}) collective-permute-start(bf16[512,2048]{1,0:T(8,128)(2,1)} %pad_maximum_fusion.1), channel_id=1, source_target_pairs={{0,8},{8,0},{16,24},{24,16},{1,9},{9,1},{17,25},{25,17},{2,10},{10... | collective-permute-start | bytes 6291464 | tf_op jit(solution)/shard_map/ppermute | solution.py:380
  59.2 144.1 %collective-permute-start.19 = (bf16[4,4,64,512]{3,2,1,0:T(8,128)(2,1)}, bf16[4,4,64,512]{3,2,1,0:T(8,128)(2,1)}, u32[]{:S(2)}, u32[]{:S(2)}) collective-permute-start(bf16[4,4,64,512]{3,2,1,0:T(8,128)(2,1)} %bitcast.328), channel_id=1, source_target_pairs={{0,1},{1,0},{2,3},{3,2},{4,5},{5,4},{6,7},{7,6},{8,9},{9,8},{10,11... | collective-permute-start | bytes 3145736 | tf_op jit(solution)/shard_map/ppermute | solution.py:369
  92.5 57.0 %collective-permute-start.8 = (bf16[512,2048]{1,0:T(8,128)(2,1)}, bf16[512,2048]{1,0:T(8,128)(2,1)}, u32[]{:S(2)}, u32[]{:S(2)}) collective-permute-start(bf16[512,2048]{1,0:T(8,128)(2,1)} %all-gather.10.cloned.1.call-done), channel_id=1, source_target_pairs={{0,1},{1,0},{2,3},{3,2},{4,5},{5,4},{6,7},{7,6},{8,9},{9,8},{10,11... | collective-permute-start | bytes 6291464 | tf_op jit(solution)/shard_map/ppermute | solution.py:369
  139.4 46.8 %collective-permute-start.7 = (bf16[512,2048]{1,0:T(8,128)(2,1)}, bf16[512,2048]{1,0:T(8,128)(2,1)S(1)}, u32[]{:S(2)}, u32[]{:S(2)}) collective-permute-start(bf16[512,2048]{1,0:T(8,128)(2,1)} %all-gather.8.cloned.1.call-done), channel_id=1, source_target_pairs={{0,1},{1,0},{2,3},{3,2},{4,5},{5,4},{6,7},{7,6},{8,9},{9,8},{10,11... | collective-permute-start | bytes 6291464 | tf_op jit(solution)/shard_map/ppermute | solution.py:369
  200.0 10.9 %collective-permute-start.12 = (bf16[4,64,1024]{2,1,0:T(8,128)(2,1)S(1)}, bf16[4,64,1024]{2,1,0:T(8,128)(2,1)S(1)}, u32[]{:S(2)}, u32[]{:S(2)}) collective-permute-start(bf16[4,64,1024]{2,1,0:T(8,128)(2,1)S(1)} %select_convert_fusion.5), channel_id=1, source_target_pairs={{0,1},{1,0},{2,3},{3,2},{4,5},{5,4},{6,7},{7,6},{8,9},{9,8},{10,11... | collective-permute-start | bytes 1572872 | tf_op jit(solution)/shard_map/ppermute | solution.py:369
  211.3 9.9 collective-permute-start.13
  221.6 12.2 %collective-permute-start.14 = (bf16[4,64,1024]{2,1,0:T(8,128)(2,1)S(1)}, bf16[4,64,1024]{2,1,0:T(8,128)(2,1)S(1)}, u32[]{:S(2)}, u32[]{:S(2)}) collective-permute-start(bf16[4,64,1024]{2,1,0:T(8,128)(2,1)S(1)} %fusion.22), channel_id=1, source_target_pairs={{0,4},{1,5},{2,6},{3,7},{8,12},{9,13},{10,14},{11,15},{16,20},{17,... | collective-permute-start | bytes 1572872 | tf_op jit(solution)/shard_map/ppermute | solution.py:504
  235.1 8.3 collective-permute-start.15
  264.5 23.3 %collective-permute-start.20 = (bf16[512,2048]{1,0:T(8,128)(2,1)S(1)}, bf16[512,2048]{1,0:T(8,128)(2,1)S(1)}, u32[]{:S(2)}, u32[]{:S(2)}) collective-permute-start(bf16[512,2048]{1,0:T(8,128)(2,1)S(1)} %slice.812), channel_id=1, source_target_pairs={{0,8},{8,0},{16,24},{24,16},{1,9},{9,1},{17,25},{25,17},{2,10},{10... | collective-permute-start | bytes 6291464 | tf_op jit(solution)/shard_map/ppermute | solution.py:380
  273.1 13.3 %collective-permute-start.27 = (bf16[128,2048]{1,0:T(8,128)(2,1)S(1)}, bf16[128,2048]{1,0:T(8,128)(2,1)S(1)}, u32[]{:S(2)}, u32[]{:S(2)}) collective-permute-start(bf16[128,2048]{1,0:T(8,128)(2,1)S(1)} %get-tuple-element.203), channel_id=1, source_target_pairs={{0,1},{1,0},{2,3},{3,2},{4,5},{5,4},{6,7},{7,6},{8,9},{9,8},{10,11... | collective-permute-start | bytes 1572872 | tf_op jit(solution)/shard_map/ppermute | solution.py:369
  287.5 23.9 %collective-permute-start.28 = (bf16[256,2048]{1,0:T(8,128)(2,1)}, bf16[256,2048]{1,0:T(8,128)(2,1)}, u32[]{:S(2)}, u32[]{:S(2)}) collective-permute-start(bf16[256,2048]{1,0:T(8,128)(2,1)} %pad_maximum_fusion.14), channel_id=1, source_target_pairs={{0,16},{8,24},{16,0},{24,8},{1,17},{9,25},{17,1},{25,9},{2,18},{10... | collective-permute-start | bytes 3145736 | tf_op jit(solution)/shard_map/ppermute | solution.py:380
  291.8 42.1 %collective-permute-start.21 = (bf16[256,2048]{1,0:T(8,128)(2,1)}, bf16[256,2048]{1,0:T(8,128)(2,1)}, u32[]{:S(2)}, u32[]{:S(2)}) collective-permute-start(bf16[256,2048]{1,0:T(8,128)(2,1)} %slice.814), channel_id=1, source_target_pairs={{0,16},{8,24},{16,0},{24,8},{1,17},{9,25},{17,1},{25,9},{2,18},{10... | collective-permute-start | bytes 3145736 | tf_op jit(solution)/shard_map/ppermute | solution.py:380
  292.9 192.8 %all-gather.16.cloned.1.call-start = ((), (), s32[]{:S(2)}) async-start(), calls=%async_computation.12 | async-start | bytes 3604480 | tf_op jit(solution)/shard_map/all_gather | solution.py:372
  337.7 11.5 %collective-permute-start.22 = (bf16[128,2048]{1,0:T(8,128)(2,1)S(1)}, bf16[128,2048]{1,0:T(8,128)(2,1)S(1)}, u32[]{:S(2)}, u32[]{:S(2)}) collective-permute-start(bf16[128,2048]{1,0:T(8,128)(2,1)S(1)} %get-tuple-element.210), channel_id=1, source_target_pairs={{0,1},{1,0},{2,3},{3,2},{4,5},{5,4},{6,7},{7,6},{8,9},{9,8},{10,11... | collective-permute-start | bytes 1572872 | tf_op jit(solution)/shard_map/ppermute | solution.py:369
  339.5 11.5 %collective-permute-start.29 = (bf16[128,2048]{1,0:T(8,128)(2,1)S(1)}, bf16[128,2048]{1,0:T(8,128)(2,1)S(1)}, u32[]{:S(2)}, u32[]{:S(2)}) collective-permute-start(bf16[128,2048]{1,0:T(8,128)(2,1)S(1)} %get-tuple-element.201), channel_id=1, source_target_pairs={{0,16},{8,24},{16,0},{24,8},{1,17},{9,25},{17,1},{25,9},{2,18},{10... | collective-permute-start | bytes 1572872 | tf_op jit(solution)/shard_map/ppermute | solution.py:380
  349.3 24.6 %collective-permute-start.23 = (bf16[256,2048]{1,0:T(8,128)(2,1)S(1)}, bf16[256,2048]{1,0:T(8,128)(2,1)S(1)}, u32[]{:S(2)}, u32[]{:S(2)}) collective-permute-start(bf16[256,2048]{1,0:T(8,128)(2,1)S(1)} %pad_maximum_fusion.12), channel_id=1, source_target_pairs={{0,16},{8,24},{16,0},{24,8},{1,17},{9,25},{17,1},{25,9},{2,18},{10... | collective-permute-start | bytes 3145736 | tf_op jit(solution)/shard_map/ppermute | solution.py:380
  351.1 26.2 %collective-permute-start.30 = (bf16[256,2048]{1,0:T(8,128)(2,1)S(1)}, bf16[256,2048]{1,0:T(8,128)(2,1)S(1)}, u32[]{:S(2)}, u32[]{:S(2)}) collective-permute-start(bf16[256,2048]{1,0:T(8,128)(2,1)S(1)} %pad_maximum_fusion.15), channel_id=1, source_target_pairs={{0,1},{1,0},{2,3},{3,2},{4,5},{5,4},{6,7},{7,6},{8,9},{9,8},{10,11... | collective-permute-start | bytes 3145736 | tf_op jit(solution)/shard_map/ppermute | solution.py:369
  376.1 11.0 %collective-permute-start.24 = (bf16[128,2048]{1,0:T(8,128)(2,1)S(1)}, bf16[128,2048]{1,0:T(8,128)(2,1)S(1)}, u32[]{:S(2)}, u32[]{:S(2)}) collective-permute-start(bf16[128,2048]{1,0:T(8,128)(2,1)S(1)} %get-tuple-element.208), channel_id=1, source_target_pairs={{0,16},{8,24},{16,0},{24,8},{1,17},{9,25},{17,1},{25,9},{2,18},{10... | collective-permute-start | bytes 1572872 | tf_op jit(solution)/shard_map/ppermute | solution.py:380
  378.5 36.2 %collective-permute-start.31 = (bf16[1024,2048]{1,0:T(8,128)(2,1)}, bf16[1024,2048]{1,0:T(8,128)(2,1)}, u32[]{:S(2)}, u32[]{:S(2)}) collective-permute-start(bf16[1024,2048]{1,0:T(8,128)(2,1)} %get-tuple-element.197), channel_id=1, source_target_pairs={{0,8},{8,0},{16,24},{24,16},{1,9},{9,1},{17,25},{25,17},{2,10},{10... | collective-permute-start | bytes 12582920 | tf_op jit(solution)/shard_map/ppermute | solution.py:380
  387.2 21.4 %collective-permute-start.25 = (bf16[256,2048]{1,0:T(8,128)(2,1)S(1)}, bf16[256,2048]{1,0:T(8,128)(2,1)S(1)}, u32[]{:S(2)}, u32[]{:S(2)}) collective-permute-start(bf16[256,2048]{1,0:T(8,128)(2,1)S(1)} %pad_maximum_fusion.13), channel_id=1, source_target_pairs={{0,1},{1,0},{2,3},{3,2},{4,5},{5,4},{6,7},{7,6},{8,9},{9,8},{10,11... | collective-permute-start | bytes 3145736 | tf_op jit(solution)/shard_map/ppermute | solution.py:369
  410.2 11.4 %collective-permute-start.26 = (bf16[1024,2048]{1,0:T(8,128)(2,1)}, bf16[1024,2048]{1,0:T(8,128)(2,1)}, u32[]{:S(2)}, u32[]{:S(2)}) collective-permute-start(bf16[1024,2048]{1,0:T(8,128)(2,1)} %get-tuple-element.204), channel_id=1, source_target_pairs={{0,8},{8,0},{16,24},{24,16},{1,9},{9,1},{17,25},{25,17},{2,10},{10... | collective-permute-start | bytes 12582920 | tf_op jit(solution)/shard_map/ppermute | solution.py:380
  414.4 256.0 %reduce-scatter.23.cloned.1.call-start = ((), (), s32[]{:S(2)}) async-start(), calls=%async_computation.20 | async-start | bytes 3604480 | tf_op jit(solution)/shard_map/reduce_scatter | solution.py:375
  513.6 159.2 %reduce-scatter.21.cloned.1.call-start = ((), (), s32[]{:S(2)}) async-start(), calls=%async_computation.19 | async-start | bytes 3604480 | tf_op jit(solution)/shard_map/reduce_scatter | solution.py:375
  546.3 12.1 %collective-permute-start.32 = (bf16[1024,2048]{1,0:T(8,128)(2,1)}, bf16[1024,2048]{1,0:T(8,128)(2,1)}, u32[]{:S(2)}, u32[]{:S(2)}) collective-permute-start(bf16[1024,2048]{1,0:T(8,128)(2,1)} %slice.810), channel_id=1, source_target_pairs={{0,8},{8,0},{16,24},{24,16},{1,9},{9,1},{17,25},{25,17},{2,10},{10... | collective-permute-start | bytes 12582920 | tf_op jit(solution)/shard_map/ppermute | solution.py:380
  557.9 128.6 %reduce-scatter.19.cloned.1.call-start = ((), (), s32[]{:S(2)}) async-start(), calls=%async_computation.18 | async-start | bytes 3604480 | tf_op jit(solution)/shard_map/reduce_scatter | solution.py:375
  571.7 24.9 %collective-permute-start.33 = (bf16[256,2048]{1,0:T(8,128)(2,1)S(1)}, bf16[256,2048]{1,0:T(8,128)(2,1)S(1)}, u32[]{:S(2)}, u32[]{:S(2)}) collective-permute-start(bf16[256,2048]{1,0:T(8,128)(2,1)S(1)} %get-tuple-element.181), channel_id=1, source_target_pairs={{0,16},{8,24},{16,0},{24,8},{1,17},{9,25},{17,1},{25,9},{2,18},{10... | collective-permute-start | bytes 3145736 | tf_op jit(solution)/shard_map/ppermute | solution.py:380
  572.0 24.6 %collective-permute-start.35 = (bf16[256,2048]{1,0:T(8,128)(2,1)S(1)}, bf16[256,2048]{1,0:T(8,128)(2,1)S(1)}, u32[]{:S(2)}, u32[]{:S(2)}) collective-permute-start(bf16[256,2048]{1,0:T(8,128)(2,1)S(1)} %get-tuple-element.182), channel_id=1, source_target_pairs={{0,1},{1,0},{2,3},{3,2},{4,5},{5,4},{6,7},{7,6},{8,9},{9,8},{10,11... | collective-permute-start | bytes 3145736 | tf_op jit(solution)/shard_map/ppermute | solution.py:369
  603.4 14.9 %collective-permute-start.36 = (bf16[128,2048]{1,0:T(8,128)(2,1)}, bf16[128,2048]{1,0:T(8,128)(2,1)}, u32[]{:S(2)}, u32[]{:S(2)}) collective-permute-start(bf16[128,2048]{1,0:T(8,128)(2,1)} %slice.817), channel_id=1, source_target_pairs={{0,16},{8,24},{16,0},{24,8},{1,17},{9,25},{17,1},{25,9},{2,18},{10... | collective-permute-start | bytes 1572872 | tf_op jit(solution)/shard_map/ppermute | solution.py:380
  615.5 322.7 %reduce-scatter.17.cloned.1.call-start = ((), (), s32[]{:S(2)}) async-start(), calls=%async_computation.17 | async-start | bytes 1310720 | tf_op jit(solution)/shard_map/reduce_scatter | solution.py:375
  617.1 12.2 %collective-permute-start.34 = (bf16[128,2048]{1,0:T(8,128)(2,1)S(1)}, bf16[128,2048]{1,0:T(8,128)(2,1)S(1)}, u32[]{:S(2)}, u32[]{:S(2)}) collective-permute-start(bf16[128,2048]{1,0:T(8,128)(2,1)S(1)} %slice.818), channel_id=1, source_target_pairs={{0,1},{1,0},{2,3},{3,2},{4,5},{5,4},{6,7},{7,6},{8,9},{9,8},{10,11... | collective-permute-start | bytes 1572872 | tf_op jit(solution)/shard_map/ppermute | solution.py:369
  633.5 22.7 %collective-permute-start.37 = (bf16[256,2048]{1,0:T(8,128)(2,1)S(1)}, bf16[256,2048]{1,0:T(8,128)(2,1)S(1)}, u32[]{:S(2)}, u32[]{:S(2)}) collective-permute-start(bf16[256,2048]{1,0:T(8,128)(2,1)S(1)} %get-tuple-element.160), channel_id=1, source_target_pairs={{0,16},{8,24},{16,0},{24,8},{1,17},{9,25},{17,1},{25,9},{2,18},{10... | collective-permute-start | bytes 3145736 | tf_op jit(solution)/shard_map/ppermute | solution.py:380
  657.8 31.8 %collective-permute-start.38 = (bf16[512,2048]{1,0:T(8,128)(2,1)}, bf16[512,2048]{1,0:T(8,128)(2,1)}, u32[]{:S(2)}, u32[]{:S(2)}) collective-permute-start(bf16[512,2048]{1,0:T(8,128)(2,1)} %pad_maximum_fusion.6), channel_id=1, source_target_pairs={{0,8},{8,0},{16,24},{24,16},{1,9},{9,1},{17,25},{25,17},{2,10},{10... | collective-permute-start | bytes 6291464 | tf_op jit(solution)/shard_map/ppermute | solution.py:380
  712.8 17.9 %collective-permute-start.44 = (bf16[4,64,1024]{2,1,0:T(8,128)(2,1)}, bf16[4,64,1024]{2,1,0:T(8,128)(2,1)}, u32[]{:S(2)}, u32[]{:S(2)}) collective-permute-start(bf16[4,64,1024]{2,1,0:T(8,128)(2,1)} %select_convert_fusion.2), channel_id=1, source_target_pairs={{0,1},{1,0},{2,3},{3,2},{4,5},{5,4},{6,7},{7,6},{8,9},{9,8},{10,11... | collective-permute-start | bytes 1572872 | tf_op jit(solution)/shard_map/ppermute | solution.py:369
  718.8 29.6 %collective-permute-start.59 = (bf16[4,4,64,512]{3,2,0,1:T(8,128)(2,1)}, bf16[4,4,64,512]{3,2,0,1:T(8,128)(2,1)}, u32[]{:S(2)}, u32[]{:S(2)}) collective-permute-start(bf16[4,4,64,512]{3,2,0,1:T(8,128)(2,1)} %select_bitcast_fusion), channel_id=1, source_target_pairs={{0,1},{1,0},{2,3},{3,2},{4,5},{5,4},{6,7},{7,6},{8,9},{9,8},{10,11... | collective-permute-start | bytes 3145736 | tf_op jit(solution)/shard_map/ppermute | solution.py:369
  719.1 91.0 %collective-permute-start.58 = (bf16[256,2048]{1,0:T(8,128)(2,1)}, bf16[256,2048]{1,0:T(8,128)(2,1)}, u32[]{:S(2)}, u32[]{:S(2)}) collective-permute-start(bf16[256,2048]{1,0:T(8,128)(2,1)} %convolution_convert_fusion.4), channel_id=1, source_target_pairs={{0,1},{1,0},{2,3},{3,2},{4,5},{5,4},{6,7},{7,6},{8,9},{9,8},{10,11... | collective-permute-start | bytes 3145736 | tf_op jit(solution)/shard_map/ppermute | solution.py:369
  733.4 24.1 %collective-permute-start.45 = (bf16[4,64,1024]{2,1,0:T(8,128)(2,1)}, bf16[4,64,1024]{2,1,0:T(8,128)(2,1)}, u32[]{:S(2)}, u32[]{:S(2)}) collective-permute-start(bf16[4,64,1024]{2,1,0:T(8,128)(2,1)} %get-tuple-element.156), channel_id=1, source_target_pairs={{0,2},{1,3},{2,0},{3,1},{4,6},{5,7},{6,4},{7,5},{8,10},{9,11},{10,... | collective-permute-start | bytes 1572872 | tf_op jit(solution)/shard_map/ppermute | solution.py:504
  751.2 194.9 %reduce-scatter.15.cloned.1.call-start = ((), (), s32[]{:S(2)}) async-start(), calls=%async_computation.16 | async-start | bytes 1310720 | tf_op jit(solution)/shard_map/reduce_scatter | solution.py:375
  759.7 38.8 %collective-permute-start.46 = (bf16[4,64,1024]{2,1,0:T(8,128)(2,1)}, bf16[4,64,1024]{2,1,0:T(8,128)(2,1)}, u32[]{:S(2)}, u32[]{:S(2)}) collective-permute-start(bf16[4,64,1024]{2,1,0:T(8,128)(2,1)} %fusion.26), channel_id=1, source_target_pairs={{4,0},{5,1},{6,2},{7,3},{12,8},{13,9},{14,10},{15,11},{20,16},{21,... | collective-permute-start | bytes 1572872 | tf_op jit(solution)/shard_map/ppermute | solution.py:504
  800.9 12.9 %collective-permute-start.47 = (bf16[4,64,1024]{2,1,0:T(8,128)(2,1)}, bf16[4,64,1024]{2,1,0:T(8,128)(2,1)}, u32[]{:S(2)}, u32[]{:S(2)}) collective-permute-start(bf16[4,64,1024]{2,1,0:T(8,128)(2,1)} %select_convert_fusion), channel_id=1, source_target_pairs={{0,1},{1,0},{2,3},{3,2},{4,5},{5,4},{6,7},{7,6},{8,9},{9,8},{10,11... | collective-permute-start | bytes 1572872 | tf_op jit(solution)/shard_map/ppermute | solution.py:369
  809.0 147.1 %collective-permute-start.39 = (bf16[1024,2048]{1,0:T(8,128)(2,1)}, bf16[1024,2048]{1,0:T(8,128)(2,1)}, u32[]{:S(2)}, u32[]{:S(2)}) collective-permute-start(bf16[1024,2048]{1,0:T(8,128)(2,1)} %slice.809), channel_id=1, source_target_pairs={{0,8},{8,0},{16,24},{24,16},{1,9},{9,1},{17,25},{25,17},{2,10},{10... | collective-permute-start | bytes 12582920 | tf_op jit(solution)/shard_map/ppermute | solution.py:380
  813.7 210.7 %reduce-scatter.13.cloned.1.call-start = ((), (), s32[]{:S(2)}) async-start(), calls=%async_computation.15 | async-start | bytes 1310720 | tf_op jit(solution)/shard_map/reduce_scatter | solution.py:375
  845.7 23.0 %collective-permute-start.57 = (bf16[256,2048]{1,0:T(8,128)(2,1)S(1)}, bf16[256,2048]{1,0:T(8,128)(2,1)S(1)}, u32[]{:S(2)}, u32[]{:S(2)}) collective-permute-start(bf16[256,2048]{1,0:T(8,128)(2,1)S(1)} %convolution_convert_fusion.5), channel_id=1, source_target_pairs={{0,1},{1,0},{2,3},{3,2},{4,5},{5,4},{6,7},{7,6},{8,9},{9,8},{10,11... | collective-permute-start | bytes 3145736 | tf_op jit(solution)/shard_map/ppermute | solution.py:369
  871.0 155.3 %reduce-scatter.9.cloned.1.call-start = ((), (), s32[]{:S(2)}) async-start(), calls=%async_computation.13 | async-start | bytes 1310720 | tf_op jit(solution)/shard_map/reduce_scatter | solution.py:375
  872.1 22.4 %collective-permute-start.55 = (bf16[256,2048]{1,0:T(8,128)(2,1)}, bf16[256,2048]{1,0:T(8,128)(2,1)}, u32[]{:S(2)}, u32[]{:S(2)}) collective-permute-start(bf16[256,2048]{1,0:T(8,128)(2,1)} %convolution_convert_fusion.7), channel_id=1, source_target_pairs={{0,1},{1,0},{2,3},{3,2},{4,5},{5,4},{6,7},{7,6},{8,9},{9,8},{10,11... | collective-permute-start | bytes 3145736 | tf_op jit(solution)/shard_map/ppermute | solution.py:369
  873.3 66.2 %collective-permute-start.56 = (bf16[256,2048]{1,0:T(8,128)(2,1)}, bf16[256,2048]{1,0:T(8,128)(2,1)}, u32[]{:S(2)}, u32[]{:S(2)}) collective-permute-start(bf16[256,2048]{1,0:T(8,128)(2,1)} %convolution_convert_fusion.6), channel_id=1, source_target_pairs={{0,1},{1,0},{2,3},{3,2},{4,5},{5,4},{6,7},{7,6},{8,9},{9,8},{10,11... | collective-permute-start | bytes 3145736 | tf_op jit(solution)/shard_map/ppermute | solution.py:369
  898.0 130.1 %reduce-scatter.11.cloned.1.call-start = ((), (), s32[]{:S(2)}) async-start(), calls=%async_computation.14 | async-start | bytes 1310720 | tf_op jit(solution)/shard_map/reduce_scatter | solution.py:375
  928.1 22.0 %collective-permute-start.48 = (bf16[512,2048]{1,0:T(8,128)(2,1)}, bf16[512,2048]{1,0:T(8,128)(2,1)}, u32[]{:S(2)}, u32[]{:S(2)}) collective-permute-start(bf16[512,2048]{1,0:T(8,128)(2,1)} %slice.811), channel_id=1, source_target_pairs={{0,8},{8,0},{16,24},{24,16},{1,9},{9,1},{17,25},{25,17},{2,10},{10... | collective-permute-start | bytes 6291464 | tf_op jit(solution)/shard_map/ppermute | solution.py:380
  939.1 8.8 collective-permute-start.62
  939.2 8.7 collective-permute-start.61
  939.5 8.4 collective-permute-start.60
  955.7 25.0 %collective-permute-start.49 = (bf16[256,2048]{1,0:T(8,128)(2,1)S(1)}, bf16[256,2048]{1,0:T(8,128)(2,1)S(1)}, u32[]{:S(2)}, u32[]{:S(2)}) collective-permute-start(bf16[256,2048]{1,0:T(8,128)(2,1)S(1)} %slice.813), channel_id=1, source_target_pairs={{0,16},{8,24},{16,0},{24,8},{1,17},{9,25},{17,1},{25,9},{2,18},{10... | collective-permute-start | bytes 3145736 | tf_op jit(solution)/shard_map/ppermute | solution.py:380
  984.0 5.8 collective-permute-start.50
  987.4 24.0 %collective-permute-start.40 = (bf16[256,2048]{1,0:T(8,128)(2,1)}, bf16[256,2048]{1,0:T(8,128)(2,1)}, u32[]{:S(2)}, u32[]{:S(2)}) collective-permute-start(bf16[256,2048]{1,0:T(8,128)(2,1)} %get-tuple-element.179), channel_id=1, source_target_pairs={{0,16},{8,24},{16,0},{24,8},{1,17},{9,25},{17,1},{25,9},{2,18},{10... | collective-permute-start | bytes 3145736 | tf_op jit(solution)/shard_map/ppermute | solution.py:380
  988.7 23.8 %collective-permute-start.42 = (bf16[256,2048]{1,0:T(8,128)(2,1)}, bf16[256,2048]{1,0:T(8,128)(2,1)}, u32[]{:S(2)}, u32[]{:S(2)}) collective-permute-start(bf16[256,2048]{1,0:T(8,128)(2,1)} %get-tuple-element.180), channel_id=1, source_target_pairs={{0,1},{1,0},{2,3},{3,2},{4,5},{5,4},{6,7},{7,6},{8,9},{9,8},{10,11... | collective-permute-start | bytes 3145736 | tf_op jit(solution)/shard_map/ppermute | solution.py:369
  995.5 23.7 %collective-permute-start.52 = (f32[4,1408]{1,0:T(4,128)S(1)}, f32[4,1408]{1,0:T(4,128)S(1)}, u32[]{:S(2)}, u32[]{:S(2)}) collective-permute-start(f32[4,1408]{1,0:T(4,128)S(1)} %slice_select_fusion.4), channel_id=1, source_target_pairs={{0,4},{1,5},{2,6},{3,7},{4,0},{5,1},{6,2},{7,3},{8,12},{9,13},{10,... | collective-permute-start | bytes 67592 | tf_op jit(solution)/shard_map/ppermute | solution.py:422
  1017.7 15.4 %collective-permute-start.43 = (bf16[128,2048]{1,0:T(8,128)(2,1)}, bf16[128,2048]{1,0:T(8,128)(2,1)}, u32[]{:S(2)}, u32[]{:S(2)}) collective-permute-start(bf16[128,2048]{1,0:T(8,128)(2,1)} %slice.815), channel_id=1, source_target_pairs={{0,16},{8,24},{16,0},{24,8},{1,17},{9,25},{17,1},{25,9},{2,18},{10... | collective-permute-start | bytes 1572872 | tf_op jit(solution)/shard_map/ppermute | solution.py:380
  1018.0 16.6 %collective-permute-start.41 = (bf16[128,2048]{1,0:T(8,128)(2,1)}, bf16[128,2048]{1,0:T(8,128)(2,1)}, u32[]{:S(2)}, u32[]{:S(2)}) collective-permute-start(bf16[128,2048]{1,0:T(8,128)(2,1)} %slice.816), channel_id=1, source_target_pairs={{0,1},{1,0},{2,3},{3,2},{4,5},{5,4},{6,7},{7,6},{8,9},{9,8},{10,11... | collective-permute-start | bytes 1572872 | tf_op jit(solution)/shard_map/ppermute | solution.py:369
  1021.9 7.9 collective-permute-start.54
  (165 other events, 2386.3 us)
Sparse Core Ops, SparseCore 0:
  17.3 28.1 all-gather.17
  47.6 44.8 all-gather.9
  94.7 44.6 all-gather.7
  140.8 57.9 all-gather.13
  293.1 73.0 all-gather.11
  414.6 71.1 all-gather.15
  513.7 56.0 reduce-scatter.22
  572.1 56.0 reduce-scatter.20
  630.5 56.0 reduce-scatter.18
  751.3 43.2 reduce-scatter.16
  813.8 25.3 reduce-scatter.14
  871.1 29.0 reduce-scatter.12
  902.5 28.6 reduce-scatter.8
  946.2 26.4 reduce-scatter.10

commit v2 on v1

--- a/solution.py
+++ b/solution.py
@@ -175,15 +175,12 @@
     return part if total is None else total + part
 
 
-def summary_kernel(k_ref, v_ref, decay_ref, writes_ref, state_ref, keep_ref):
-    running = running_sum(decay_ref[0])
+def summary(k, v, decay, writes):
+    running = running_sum(decay)
     length = running.shape[0]
     last = running[length - 1 : length, :]
-    fade = jnp.exp(last - running) * writes_ref[0]
-    width = k_ref.shape[2]
-    state_ref[0, :, :width] = mm(fade, k_ref[0], 0, 0)
-    state_ref[0, :, width:] = mm(fade, v_ref[0], 0, 0)
-    keep_ref[0] = jnp.exp(last)
+    fade = jnp.exp(last - running) * writes
+    return jnp.concatenate([mm(fade, k, 0, 0), mm(fade, v, 0, 0)], axis=1), jnp.exp(last)
 
 
 def forward_kernel(
@@ -245,7 +242,7 @@
 def back_second_kernel(
     grad_out_ref, grad_scores_ref, attend_ref, q_ref, k_ref, v_ref, decay_ref, writes_ref,
     state_ref, adjoint_ref, q_pre_ref, k_pre_ref, logit_ref, alive_ref,
-    dq_ref, dk_ref, dv_ref, dlogit_ref,
+    grad_pre_ref, dlogit_ref,
 ):
     q, k, v, grad_out = q_ref[0], k_ref[0], v_ref[0], grad_out_ref[0]
     attend, grad_scores = attend_ref[0], grad_scores_ref[0]
@@ -329,29 +326,829 @@
     fade_w = fade * writes
     grad_k = mm(mix_key, q, 0, 0) * scale + mm(fade_w, key_adjoint, 1, 0)
     grad_v = mm(mix_value, grad_out, 0, 0) + mm(fade_w, value_adjoint, 1, 0)
-    dq_ref[0] = (grad_q * swish_slope(q_pre_ref[0])).astype(BF16)
-    dk_ref[0] = (grad_k * swish_slope(k_pre_ref[0])).astype(BF16)
-    dv_ref[0] = grad_v.astype(BF16)
+    grad_pre_ref[0, :, :width] = (grad_k * swish_slope(k_pre_ref[0])).astype(BF16)
+    grad_pre_ref[0, :, width : 2 * width] = (grad_q * swish_slope(q_pre_ref[0])).astype(BF16)
+    grad_pre_ref[0, :, 2 * width :] = grad_v.astype(BF16)
     dlogit_ref[0] = (
         alive_ref[0] * grad_decay * jax.nn.sigmoid(-logit_ref[0]) * (1.0 / GATE_NORM)
     ).astype(BF16)
 
 
 def per_sequence(kernel, inputs, outputs, shared=()):
-    count = inputs[0].shape[0]
-
-    def spec(shape):
-        return pl.BlockSpec((1,) + tuple(shape[1:]), lambda s: (s, 0, 0))
+    inputs = [x if isinstance(x, tuple) else (x, None) for x in inputs]
+    count = inputs[0][0].shape[0]
+
+    def spec(shape, at=None):
+        if at is None:
+            return pl.BlockSpec((1,) + tuple(shape[1:]), lambda s: (s, 0, 0))
+        return pl.BlockSpec((1, shape[1], shape[2] // 3), lambda s: (s, 0, at))
 
     return pl.pallas_call(
         kernel,
         grid=(count,),
-        in_specs=[spec(x.shape) for x in inputs]
+        in_specs=[spec(x.shape, at) for x, at in inputs]
         + [pl.BlockSpec(x.shape, lambda s: (0, 0)) for x in shared],
         out_specs=[spec(x.shape) for x in outputs],
         out_shape=outputs,
         compiler_params=pltpu.CompilerParams(vmem_limit_bytes=VMEM_LIMIT),
-    )(*inputs, *shared)
+    )(*[x for x, _ in inputs], *shared)
+
+
+CHUNKS = 8
+STRIP = 16
+
+
+def send(src, dst, send_sem, recv_sem, where):
+    copy = pltpu.make_async_remote_copy(
+        src_ref=src,
+        dst_ref=dst,
+        send_sem=send_sem,
+        recv_sem=recv_sem,
+        device_id=where,
+        device_id_type=pl.DeviceIdType.MESH,
+    )
+    copy.start()
+    return copy
+
+
+def greet(partners):
+    barrier = pltpu.get_barrier_semaphore()
+    for where in partners:
+        pl.semaphore_signal(
+            barrier, inc=1, device_id=where, device_id_type=pl.DeviceIdType.MESH
+        )
+    return barrier
+
+
+def near_partners():
+    d, at = lax.axis_index("dp"), lax.axis_index("seq")
+    x = {"seq": jnp.bitwise_xor(at, 1)}
+    y = {"dp": jnp.bitwise_xor(d, 2)}
+    core = {"dp": jnp.bitwise_xor(d, 1)}
+    return x, y, core
+
+
+def everyone(seq, dp, act):
+    me = lax.axis_index("dp") * seq + lax.axis_index("seq")
+
+    def turn(r, carry):
+        other = jnp.bitwise_xor(me, r)
+        act(r, {"dp": other // seq, "seq": other % seq})
+        return carry
+
+    lax.fori_loop(1, seq * dp, turn, 0)
+
+
+def greet_everyone(seq, dp):
+    barrier = pltpu.get_barrier_semaphore()
+    everyone(
+        seq,
+        dp,
+        lambda r, where: pl.semaphore_signal(
+            barrier, inc=1, device_id=where, device_id_type=pl.DeviceIdType.MESH
+        ),
+    )
+    pl.semaphore_wait(barrier, seq * dp - 1)
+
+
+def gather_kernel(outer, dp, *refs):
+    mats, refs = refs[:4], refs[4:]
+    tok, small, refs = refs[0], refs[1], refs[2:]
+    three, gate, out_tok, out_small, refs = refs[0], refs[1], refs[2], refs[3], refs[4:]
+    (
+        local_sem, up_send, up_recv, down_send, down_recv, x_send, x_recv,
+        tok_send, tok_recv, small_send, small_recv,
+    ) = refs
+    outs = [three.at[0], three.at[1], three.at[2], gate]
+    seq = 2 * outer
+    at = lax.axis_index("seq")
+    me = lax.axis_index("dp") * seq + at
+    z = at // 2
+    x, y, core = near_partners()
+    above, below = {"seq": at + 2}, {"seq": at - 2}
+    has_above, has_below = z < outer - 1, z > 0
+    greet_everyone(seq, dp)
+
+    def push(r, where):
+        return pltpu.make_async_remote_copy(
+            src_ref=small, dst_ref=out_small.at[me], send_sem=small_send.at[r],
+            recv_sem=small_recv.at[r], device_id=where, device_id_type=pl.DeviceIdType.MESH,
+        )
+
+    everyone(seq, dp, lambda r, where: push(r, where).start())
+
+    def up(m, k, src, origin):
+        return pltpu.make_async_remote_copy(
+            src_ref=src, dst_ref=outs[m].at[0, origin], send_sem=up_send.at[m, k],
+            recv_sem=up_recv.at[m, k], device_id=above, device_id_type=pl.DeviceIdType.MESH,
+        )
+
+    def down(m, k, src, origin):
+        return pltpu.make_async_remote_copy(
+            src_ref=src, dst_ref=outs[m].at[0, origin], send_sem=down_send.at[m, k],
+            recv_sem=down_recv.at[m, k], device_id=below, device_id_type=pl.DeviceIdType.MESH,
+        )
+
+    def across(m, src, origin):
+        return pltpu.make_async_remote_copy(
+            src_ref=src, dst_ref=outs[m].at[1, origin], send_sem=x_send.at[m, origin],
+            recv_sem=x_recv.at[m, origin], device_id=x, device_id_type=pl.DeviceIdType.MESH,
+        )
+
+    for m in range(4):
+        @pl.when(has_above)
+        def _():
+            up(m, 0, mats[m], z).start()
+
+        @pl.when(has_below)
+        def _():
+            down(m, 0, mats[m], z).start()
+
+        across(m, mats[m], z).start()
+    tok_y = send(tok, out_tok.at[1], tok_send.at[0], tok_recv.at[0], y)
+    tok_core = send(tok, out_tok.at[2], tok_send.at[1], tok_recv.at[1], core)
+    own_small = pltpu.make_async_copy(small, out_small.at[me], local_sem.at[0])
+    own_small.start()
+    own_tok = pltpu.make_async_copy(tok, out_tok.at[0], local_sem.at[1])
+    own_tok.start()
+    own_mats = []
+    for m in range(4):
+        copy = pltpu.make_async_copy(mats[m], outs[m].at[0, z], local_sem.at[2 + m])
+        copy.start()
+        own_mats.append(copy)
+
+    def pass_on(k, carry):
+        for m in range(4):
+            @pl.when(z - k >= 0)
+            def _():
+                slot = outs[m].at[0, z - k]
+                up(m, k - 1, slot, z - k).wait_recv()
+
+                @pl.when(has_above)
+                def _():
+                    up(m, k, slot, z - k).start()
+
+                across(m, slot, z - k).start()
+
+            @pl.when(z + k < outer)
+            def _():
+                slot = outs[m].at[0, z + k]
+                down(m, k - 1, slot, z + k).wait_recv()
+
+                @pl.when(has_below)
+                def _():
+                    down(m, k, slot, z + k).start()
+
+                across(m, slot, z + k).start()
+
+        return carry
+
+    lax.fori_loop(1, outer, pass_on, 0)
+    tok_y.wait()
+    tok_last = send(out_tok.at[1], out_tok.at[3], tok_send.at[2], tok_recv.at[2], core)
+
+    def arrived(r, where):
+        push(r, where).wait_send()
+        theirs = out_small.at[jnp.bitwise_xor(me, r)]
+        pltpu.make_async_remote_copy(
+            src_ref=theirs, dst_ref=theirs, send_sem=small_send.at[r],
+            recv_sem=small_recv.at[r], device_id=where, device_id_type=pl.DeviceIdType.MESH,
+        ).wait_recv()
+
+    everyone(seq, dp, arrived)
+
+    def complete(o, carry):
+        for m in range(4):
+            across(m, outs[m].at[0, o], o).wait()
+
+            @pl.when(has_above & (o <= z))
+            def _():
+                up(m, o, outs[m].at[0, z], z).wait_send()
+
+            @pl.when(has_below & (o <= outer - 1 - z))
+            def _():
+                down(m, o, outs[m].at[0, z], z).wait_send()
+
+        return carry
+
+    lax.fori_loop(0, outer, complete, 0)
+    for copy in own_mats:
+        copy.wait()
+    own_small.wait()
+    own_tok.wait()
+    tok_core.wait()
+    tok_last.wait()
+
+
+def in_hbm():
+    return pl.BlockSpec(memory_space=pl.ANY)
+
+
+def in_vmem():
+    return pl.BlockSpec(memory_space=pltpu.VMEM)
+
+
+def gather_all(outer, dp, mats, tok, small):
+    seq = 2 * outer
+    rows, width = mats[0].shape
+    dma = pltpu.SemaphoreType.DMA
+    return pl.pallas_call(
+        functools.partial(gather_kernel, outer, dp),
+        in_specs=[in_hbm()] * 6,
+        out_specs=[in_hbm()] * 4,
+        out_shape=[
+            jax.ShapeDtypeStruct((3, 2, outer, rows, width), BF16),
+            jax.ShapeDtypeStruct((2, outer, rows, width), BF16),
+            jax.ShapeDtypeStruct((dp,) + tok.shape, BF16),
+            jax.ShapeDtypeStruct((seq * dp,) + small.shape, BF16),
+        ],
+        scratch_shapes=[
+            dma((6,)), dma((4, outer)), dma((4, outer)), dma((4, outer)), dma((4, outer)),
+            dma((4, outer)), dma((4, outer)), dma((3,)), dma((3,)), dma((seq * dp,)),
+            dma((seq * dp,)),
+        ],
+        compiler_params=pltpu.CompilerParams(
+            collective_id=1, has_side_effects=True, vmem_limit_bytes=VMEM_LIMIT
+        ),
+    )(*mats, tok, small)
+
+
+def turned(x):
+    row, col = grid_index(x.shape[1], x.shape[1])
+    return mm_exact((row == col).astype(F32), x, 1, 1)
+
+
+def flipped(x):
+    size = x.shape[-1] // 4
+    return jnp.concatenate([x[:, size * i : size * (i + 1)] for i in (1, 0, 3, 2)], axis=1)
+
+
+def relay_kernel(outer, backward, *refs):
+    if backward:
+        totals, keeps, refs = refs[0], refs[1], refs[2:]
+        states, refs = refs[0], refs[1:]
+    else:
+        feats, decays, writes, refs = refs[0], refs[1], refs[2], refs[3:]
+        states, keeps, refs = refs[0], refs[1], refs[2:]
+    (
+        own, to_x, from_x, to_z, from_z, to_back, from_back, keep_mine, keep_theirs,
+        x_s, x_r, z_s, z_r, b_s, b_r, k_s, k_r,
+    ) = refs
+    half = own.shape[0]
+    at = lax.axis_index("seq")
+    inner, z = at % 2, at // 2
+    x, _, _ = near_partners()
+    above, below = {"seq": at + 2}, {"seq": at - 2}
+    has_above, has_below = z < outer - 1, z > 0
+    ahead, has_ahead, has_source = (
+        (below, has_below, has_above) if backward else (above, has_above, has_below)
+    )
+    barrier = greet([x])
+
+    @pl.when(has_above)
+    def _():
+        greet([above])
+
+    @pl.when(has_below)
+    def _():
+        greet([below])
+
+    pl.semaphore_wait(
+        barrier, 1 + has_above.astype(jnp.int32) + has_below.astype(jnp.int32)
+    )
+
+    def compute(s):
+        if backward:
+            return totals[s]
+        width = feats.shape[2] // 3
+        total, keep = summary(
+            feats[s, :, :width], feats[s, :, 2 * width :], decays[s], writes[s]
+        )
+        keep_mine[s] = keep
+        return total
+
+    crossing = []
+    for i in range(half):
+        to_x[i] = compute((1 - inner) * half + i).astype(BF16)
+        crossing.append(send(to_x.at[i], from_x.at[i], x_s.at[i], x_r.at[i], x))
+    for i in range(half):
+        own[i] = compute(inner * half + i)
+    if backward:
+        keep_a, keep_b = keeps[0], keeps[1]
+    else:
+        send(keep_mine, keep_theirs, k_s.at[0], k_r.at[0], x).wait()
+        mine = jnp.concatenate([keep_mine[s] for s in range(2 * half)], axis=0)
+        theirs = jnp.concatenate([keep_theirs[s] for s in range(2 * half)], axis=0)
+        keep_a = jnp.where(inner == 0, mine, theirs)
+        keep_b = jnp.where(inner == 0, theirs, mine)
+        keeps[0] = keep_a
+        keeps[1] = keep_b
+    if backward:
+        keep_a, keep_b = keep_b, keep_a
+    first_k = turned(jnp.where(inner == 0, keep_a[:half], keep_a[half:]))
+    second_k = turned(jnp.where(inner == 0, keep_b[:half], keep_b[half:]))
+    is_first = (inner == 1) if backward else (inner == 0)
+
+    def along(i):
+        return pltpu.make_async_remote_copy(
+            src_ref=to_z.at[i], dst_ref=from_z.at[i], send_sem=z_s.at[i], recv_sem=z_r.at[i],
+            device_id=ahead, device_id_type=pl.DeviceIdType.MESH,
+        )
+
+    returning = []
+    for i in range(half):
+        crossing[i].wait()
+
+        @pl.when(jnp.logical_not(has_source))
+        def _():
+            from_z[i] = jnp.zeros_like(from_z[i])
+
+        @pl.when(has_source)
+        def _():
+            along(i).wait_recv()
+
+        got = flipped(from_x[i]).astype(F32)
+        mine = own[i]
+        first = jnp.where(is_first, mine, got)
+        second = jnp.where(is_first, got, mine)
+        entering = from_z[i].astype(F32)
+        after = first_k[:, i : i + 1] * entering + first
+        to_z[i] = (second_k[:, i : i + 1] * after + second).astype(BF16)
+
+        @pl.when(has_ahead)
+        def _():
+            along(i).start()
+
+        states[inner * half + i] = jnp.where(is_first, entering, after).astype(BF16)
+        to_back[i] = jnp.where(is_first, after, entering).astype(BF16)
+        returning.append(send(to_back.at[i], from_back.at[i], b_s.at[i], b_r.at[i], x))
+    for i in range(half):
+        returning[i].wait()
+        states[(1 - inner) * half + i] = flipped(from_back[i])
+
+        @pl.when(has_ahead)
+        def _():
+            along(i).wait_send()
+
+
+def relay(outer, backward, inputs, sequences, slots, width):
+    half = sequences // 2
+    dma = pltpu.SemaphoreType.DMA
+    held = pltpu.VMEM((half, slots, width), BF16)
+    states = jax.ShapeDtypeStruct((sequences, slots, width), BF16)
+    keeps = jax.ShapeDtypeStruct((2, sequences, slots), F32)
+    keep = pltpu.VMEM((sequences, 1, slots), F32)
+    return pl.pallas_call(
+        functools.partial(relay_kernel, outer, backward),
+        in_specs=[in_vmem()] * len(inputs),
+        out_specs=in_vmem() if backward else [in_vmem()] * 2,
+        out_shape=states if backward else [states, keeps],
+        scratch_shapes=[pltpu.VMEM((half, slots, width), F32)] + [held] * 6 + [keep] * 2
+        + [dma((half,))] * 6 + [dma((1,))] * 2,
+        compiler_params=pltpu.CompilerParams(
+            collective_id=7 if backward else 6, has_side_effects=True,
+            vmem_limit_bytes=VMEM_LIMIT,
+        ),
+    )(*inputs)
+
+
+def middle_kernel(
+    parts, tok, gain, extra, hidden, mid, extra_all, from_core, to_y, from_y, normed,
+    core_s, core_r, y_s, y_r, local_sem, gx_s, gx_r, gy_s, gy_r, gd_s, gd_r,
+    ex_s, ex_r, ey_s, ey_r, ed_s, ed_r, extra_sem, gc_s, gc_r, ec_s, ec_r,
+):
+    rows = tok.shape[0]
+    size = rows // CHUNKS
+    x, y, core = near_partners()
+    pl.semaphore_wait(greet([x, y, core]), 3)
+    cuts = [pl.ds(c * size, size) for c in range(CHUNKS)]
+    first = [
+        send(parts.at[pl.ds(2, 2), cut], from_core.at[:, cut], core_s.at[c], core_r.at[c], core)
+        for c, cut in enumerate(cuts)
+    ]
+    second = []
+    for c, cut in enumerate(cuts):
+        first[c].wait()
+
+        def add(r, carry, c=c):
+            at = pl.ds(c * size + r * STRIP, STRIP)
+            to_y[at] = (parts[1, at].astype(F32) + from_core[1, at].astype(F32)).astype(BF16)
+            return carry
+
+        lax.fori_loop(0, size // STRIP, add, 0)
+        second.append(send(to_y.at[cut], from_y.at[cut], y_s.at[c], y_r.at[c], y))
+    rest = []
+    own_extra = pltpu.make_async_copy(extra, extra_all.at[0], extra_sem.at[0])
+    own_extra.start()
+    rest.append(own_extra)
+    extra_x = [
+        send(extra.at[cut], extra_all.at[1, cut], ex_s.at[c], ex_r.at[c], x)
+        for c, cut in enumerate(cuts)
+    ]
+    rest.append(send(extra, extra_all.at[4], ec_s.at[0], ec_r.at[0], core))
+    over_x, over_y, diagonal = [], [], []
+    for c in range(CHUNKS + 2):
+        if c < CHUNKS:
+            cut = cuts[c]
+            second[c].wait()
+
+            def norm(r, carry, c=c):
+                at = pl.ds(c * size + r * STRIP, STRIP)
+                total = tok[at].astype(F32) + (
+                    (parts[0, at].astype(F32) + from_core[0, at].astype(F32))
+                    + from_y[at].astype(F32)
+                )
+                hidden[at] = total
+                normed[at] = (total * rms_scale(total) * gain[...]).astype(BF16)
+                return carry
+
+            lax.fori_loop(0, size // STRIP, norm, 0)
+            over_y.append(send(normed.at[cut], mid.at[2, cut], gy_s.at[c], gy_r.at[c], y))
+            over_x.append(send(normed.at[cut], mid.at[1, cut], gx_s.at[c], gx_r.at[c], x))
+            rest.append(send(normed.at[cut], mid.at[4, cut], gc_s.at[0, c], gc_r.at[0, c], core))
+            own = pltpu.make_async_copy(normed.at[cut], mid.at[0, cut], local_sem.at[c])
+            own.start()
+            rest.append(own)
+        if c >= 2:
+            at, cut = c - 2, cuts[c - 2]
+            over_y[at].wait()
+            diagonal.append(send(mid.at[2, cut], mid.at[3, cut], gd_s.at[at], gd_r.at[at], x))
+            rest.append(send(mid.at[2, cut], mid.at[6, cut], gc_s.at[2, at], gc_r.at[2, at], core))
+    extra_y = [
+        send(extra.at[cut], extra_all.at[2, cut], ey_s.at[c], ey_r.at[c], y)
+        for c, cut in enumerate(cuts)
+    ]
+    extra_d = []
+    for c, cut in enumerate(cuts):
+        extra_x[c].wait()
+        extra_d.append(
+            send(extra_all.at[1, cut], extra_all.at[3, cut], ed_s.at[c], ed_r.at[c], y)
+        )
+        over_x[c].wait()
+        rest.append(send(mid.at[1, cut], mid.at[5, cut], gc_s.at[1, c], gc_r.at[1, c], core))
+    rest.append(send(extra_all.at[1], extra_all.at[5], ec_s.at[1], ec_r.at[1], core))
+    for c, cut in enumerate(cuts):
+        diagonal[c].wait()
+        rest.append(send(mid.at[3, cut], mid.at[7, cut], gc_s.at[3, c], gc_r.at[3, c], core))
+    for copy in extra_y + extra_d:
+        copy.wait()
+    rest.append(
+        send(extra_all.at[pl.ds(2, 2)], extra_all.at[pl.ds(6, 2)], ec_s.at[2], ec_r.at[2], core)
+    )
+    for copy in rest:
+        copy.wait()
+
+
+def middle(parts, tok, gain, extra):
+    rows, width = tok.shape
+    dma = pltpu.SemaphoreType.DMA
+    buffer = pltpu.VMEM((rows, width), BF16)
+    return pl.pallas_call(
+        middle_kernel,
+        in_specs=[in_vmem()] * 3 + [in_hbm()],
+        out_specs=[in_vmem(), in_hbm(), in_hbm()],
+        out_shape=[
+            jax.ShapeDtypeStruct((rows, width), F32),
+            jax.ShapeDtypeStruct((8, rows, width), BF16),
+            jax.ShapeDtypeStruct((8, rows, width), BF16),
+        ],
+        scratch_shapes=[pltpu.VMEM((2, rows, width), BF16), buffer, buffer, buffer]
+        + [dma((CHUNKS,))] * 17
+        + [dma((1,))]
+        + [dma((4, CHUNKS))] * 2
+        + [dma((3,))] * 2,
+        compiler_params=pltpu.CompilerParams(
+            collective_id=2, has_side_effects=True, vmem_limit_bytes=VMEM_LIMIT
+        ),
+    )(parts, tok, gain, extra)
+
+
+def middle_back_kernel(
+    parts, hidden, grad_out, gain, grad_hidden, gain_grad, attn,
+    from_core, to_x, from_x, to_y, from_y, rounded,
+    core_s, core_r, x_s, x_r, y_s, y_r, local_sem, gy_s, gy_r, gc_s, gc_r,
+):
+    rows, width = hidden.shape
+    size = rows // CHUNKS
+    x, y, core = near_partners()
+    pl.semaphore_wait(greet([x, y, core]), 3)
+    cuts = [pl.ds(c * size, size) for c in range(CHUNKS)]
+    first = [
+        send(parts.at[pl.ds(4, 4), cut], from_core.at[:, cut], core_s.at[c], core_r.at[c], core)
+        for c, cut in enumerate(cuts)
+    ]
+    second, third = [], []
+    for c, cut in enumerate(cuts):
+        first[c].wait()
+
+        def add_core(r, carry, c=c):
+            at = pl.ds(c * size + r * STRIP, STRIP)
+            for j in range(2):
+                g = 2 * j + 1
+                to_x[j, at] = (
+                    parts[g, at].astype(F32) + from_core[g, at].astype(F32)
+                ).astype(BF16)
+            return carry
+
+        lax.fori_loop(0, size // STRIP, add_core, 0)
+        second.append(send(to_x.at[:, cut], from_x.at[:, cut], x_s.at[c], x_r.at[c], x))
+    gain_grad[...] = jnp.zeros_like(gain_grad)
+    pending, over_y = [], []
+    for step in range(CHUNKS + 2):
+        if step < CHUNKS:
+            c, cut = step, cuts[step]
+            second[c].wait()
+
+            def add_x(r, carry, c=c):
+                at = pl.ds(c * size + r * STRIP, STRIP)
+                to_y[at] = (
+                    parts[2, at].astype(F32) + from_core[2, at].astype(F32)
+                    + from_x[1, at].astype(F32)
+                ).astype(BF16)
+                return carry
+
+            lax.fori_loop(0, size // STRIP, add_x, 0)
+            third.append(send(to_y.at[cut], from_y.at[cut], y_s.at[c], y_r.at[c], y))
+        if 1 <= step <= CHUNKS:
+            c, cut = step - 1, cuts[step - 1]
+            third[c].wait()
+
+            def back(r, carry, c=c):
+                at = pl.ds(c * size + r * STRIP, STRIP)
+                grad_mid = (
+                    (parts[0, at].astype(F32) + from_core[0, at].astype(F32))
+                    + from_x[0, at].astype(F32)
+                ) + from_y[at].astype(F32)
+                value = hidden[at]
+                scale = rms_scale(value)
+                unit = value * scale
+                gain_grad[...] += jnp.sum(grad_mid * unit, axis=0, keepdims=True)
+                scaled = grad_mid * gain[...]
+                total = grad_out[at] + scale * (
+                    scaled - unit * jnp.mean(scaled * unit, axis=1, keepdims=True)
+                )
+                grad_hidden[at] = total
+                rounded[at] = total.astype(BF16)
+                return carry
+
+            lax.fori_loop(0, size // STRIP, back, 0)
+            over_y.append(send(rounded.at[cut], attn.at[1, cut], gy_s.at[c], gy_r.at[c], y))
+            pending.append(
+                send(rounded.at[cut], attn.at[2, cut], gc_s.at[0, c], gc_r.at[0, c], core)
+            )
+            own = pltpu.make_async_copy(rounded.at[cut], attn.at[0, cut], local_sem.at[c])
+            own.start()
+            pending.append(own)
+        if step >= 2:
+            c, cut = step - 2, cuts[step - 2]
+            over_y[c].wait()
+            pending.append(
+                send(attn.at[1, cut], attn.at[3, cut], gc_s.at[1, c], gc_r.at[1, c], core)
+            )
+    for copy in pending:
+        copy.wait()
+
+
+def middle_back(parts, hidden, grad_out, gain):
+    rows, width = hidden.shape
+    dma = pltpu.SemaphoreType.DMA
+
+    def buffer(*lead):
+        return pltpu.VMEM(lead + (rows, width), BF16)
+
+    return pl.pallas_call(
+        middle_back_kernel,
+        in_specs=[in_vmem()] * 4,
+        out_specs=[in_vmem(), in_vmem(), in_hbm()],
+        out_shape=[
+            jax.ShapeDtypeStruct((rows, width), F32),
+            jax.ShapeDtypeStruct((1, width), F32),
+            jax.ShapeDtypeStruct((4, rows, width), BF16),
+        ],
+        scratch_shapes=[buffer(4), buffer(2), buffer(2), buffer(), buffer(), buffer()]
+        + [dma((CHUNKS,))] * 9
+        + [dma((2, CHUNKS))] * 2,
+        compiler_params=pltpu.CompilerParams(
+            collective_id=3, has_side_effects=True, vmem_limit_bytes=VMEM_LIMIT
+        ),
+    )(parts, hidden, grad_out, gain)
+
+
+def final_kernel(outer, dp, mats, parts, tok, base, gain, small, *refs):
+    out, tokens_grad, out_small, refs = refs[0], refs[1], refs[2], refs[3:]
+    (
+        from_x, from_below, from_above, total, from_core, to_y, from_y, gain_grad,
+        to_all, from_all,
+        x_s, x_r, up_s, up_r, down_s, down_r, core_s, core_r, y_s, y_r, all_s, all_r,
+    ) = refs
+    rows, width = tok.shape
+    size = rows // CHUNKS
+    high = total.shape[2]
+    seq = 2 * outer
+    at = lax.axis_index("seq")
+    me = lax.axis_index("dp") * seq + at
+    z = at // 2
+    x, y, core = near_partners()
+    above, below = {"seq": at + 2}, {"seq": at - 2}
+    has_above, has_below = z < outer - 1, z > 0
+    greet_everyone(seq, dp)
+    cuts = [pl.ds(c * size, size) for c in range(CHUNKS)]
+    first = [
+        send(parts.at[pl.ds(2, 2), cut], from_core.at[:, cut], core_s.at[c], core_r.at[c], core)
+        for c, cut in enumerate(cuts)
+    ]
+
+    def block_of(i):
+        return jnp.where(i % 2 == 0, outer - 1 - i // 2, i // 2)
+
+    def across(m, b):
+        return pltpu.make_async_remote_copy(
+            src_ref=mats.at[m, 1, b], dst_ref=from_x.at[m, b], send_sem=x_s.at[m, b],
+            recv_sem=x_r.at[m, b], device_id=x, device_id_type=pl.DeviceIdType.MESH,
+        )
+
+    def up(m, b):
+        return pltpu.make_async_remote_copy(
+            src_ref=total.at[m, b], dst_ref=from_below.at[m, b], send_sem=up_s.at[m, b],
+            recv_sem=up_r.at[m, b], device_id=above, device_id_type=pl.DeviceIdType.MESH,
+        )
+
+    def down(m, b):
+        return pltpu.make_async_remote_copy(
+            src_ref=total.at[m, b], dst_ref=from_above.at[m, b], send_sem=down_s.at[m, b],
+            recv_sem=down_r.at[m, b], device_id=below, device_id_type=pl.DeviceIdType.MESH,
+        )
+
+    def start_x(i, carry):
+        for m in range(3):
+            across(m, block_of(i)).start()
+        return carry
+
+    lax.fori_loop(0, outer, start_x, 0)
+    second = []
+    for c, cut in enumerate(cuts):
+        first[c].wait()
+
+        def add(r, carry, c=c):
+            strip = pl.ds(c * size + r * STRIP, STRIP)
+            to_y[strip] = (
+                parts[1, strip].astype(F32) + from_core[1, strip].astype(F32)
+            ).astype(BF16)
+            return carry
+
+        lax.fori_loop(0, size // STRIP, add, 0)
+        second.append(send(to_y.at[cut], from_y.at[cut], y_s.at[c], y_r.at[c], y))
+
+    def add_into(m, b, other):
+        def strip_sum(r, carry):
+            strip = pl.ds(r * STRIP, STRIP)
+            total[m, b, strip] = (
+                total[m, b, strip].astype(F32) + other[m, b, strip].astype(F32)
+            ).astype(BF16)
+            return carry
+
+        lax.fori_loop(0, high // STRIP, strip_sum, 0)
+
+    def reduce_block(i, carry):
+        b = block_of(i)
+        for m in range(3):
+            across(m, b).wait()
+
+            def strip_sum(r, carry, m=m):
+                strip = pl.ds(r * STRIP, STRIP)
+                total[m, b, strip] = (
+                    mats[m, 0, b, strip].astype(F32) + from_x[m, b, strip].astype(F32)
+                ).astype(BF16)
+                return carry
+
+            lax.fori_loop(0, high // STRIP, strip_sum, 0)
+
+            @pl.when(b > z)
+            def _():
+                @pl.when(has_below)
+                def _():
+                    up(m, b).wait_recv()
+                    add_into(m, b, from_below)
+
+                up(m, b).start()
+
+            @pl.when(b < z)
+            def _():
+                @pl.when(has_above)
+                def _():
+                    down(m, b).wait_recv()
+                    add_into(m, b, from_above)
+
+                down(m, b).start()
+
+        return carry
+
+    lax.fori_loop(0, outer // 2, reduce_block, 0)
+    gain_grad[...] = jnp.zeros_like(gain_grad)
+    for c in range(CHUNKS):
+        second[c].wait()
+
+        def back(r, carry, c=c):
+            strip = pl.ds(c * size + r * STRIP, STRIP)
+            grad = (
+                parts[0, strip].astype(F32) + from_core[0, strip].astype(F32)
+            ) + from_y[strip].astype(F32)
+            value = tok[strip].astype(F32)
+            scale = rms_scale(value)
+            unit = value * scale
+            gain_grad[...] += jnp.sum(grad * unit, axis=0, keepdims=True)
+            scaled = grad * gain[...]
+            tokens_grad[strip] = base[strip] + scale * (
+                scaled - unit * jnp.mean(scaled * unit, axis=1, keepdims=True)
+            )
+            return carry
+
+        lax.fori_loop(0, size // STRIP, back, 0)
+    devices = seq * dp
+    each = width // devices
+    row, col = grid_index(devices, width)
+    spread = jnp.where(col // each == row, gain_grad[...], 0.0)
+    picked_row, picked_col = grid_index(width, 128)
+    gathered = mm_exact(spread, ((picked_row % each) == picked_col).astype(F32), 1, 0)
+    height = small.shape[1]
+    to_all[:, :height] = small[...]
+    to_all[:, height:] = jnp.broadcast_to(
+        gathered.reshape(devices, 1, 128), (devices, to_all.shape[1] - height, 128)
+    )
+
+    def push(r, where):
+        return pltpu.make_async_remote_copy(
+            src_ref=to_all.at[jnp.bitwise_xor(me, r)], dst_ref=from_all.at[r],
+            send_sem=all_s.at[r], recv_sem=all_r.at[r], device_id=where,
+            device_id_type=pl.DeviceIdType.MESH,
+        )
+
+    everyone(seq, dp, lambda r, where: push(r, where).start())
+    lax.fori_loop(outer // 2, outer, reduce_block, 0)
+    out_small[...] = to_all[me]
+
+    def add_small(r, where):
+        push(r, where).wait()
+        out_small[...] += from_all[r]
+
+    everyone(seq, dp, add_small)
+    for m in range(3):
+        out[m] = total[m, z].astype(F32)
+
+        @pl.when(has_below)
+        def _():
+            up(m, z).wait_recv()
+            out[m] += from_below[m, z].astype(F32)
+
+        @pl.when(has_above)
+        def _():
+            down(m, z).wait_recv()
+            out[m] += from_above[m, z].astype(F32)
+
+    def sent(b, carry):
+        for m in range(3):
+            @pl.when(b > z)
+            def _():
+                up(m, b).wait_send()
+
+            @pl.when(b < z)
+            def _():
+                down(m, b).wait_send()
+
+        return carry
+
+    lax.fori_loop(0, outer, sent, 0)
+
+
+def finish(outer, dp, mats, parts, tok, base, gain, small):
+    rows, width = tok.shape
+    high = mats.shape[3]
+    devices = 2 * outer * dp
+    dma = pltpu.SemaphoreType.DMA
+    blocks = pltpu.VMEM((3, outer, high, width), BF16)
+    buffer = pltpu.VMEM((rows, width), BF16)
+    payload = (small.shape[1] + 8, 128)
+    return pl.pallas_call(
+        functools.partial(final_kernel, outer, dp),
+        in_specs=[in_vmem()] * 6,
+        out_specs=[in_vmem()] * 3,
+        out_shape=[
+            jax.ShapeDtypeStruct((3, high, width), F32),
+            jax.ShapeDtypeStruct((rows, width), F32),
+            jax.ShapeDtypeStruct(payload, F32),
+        ],
+        scratch_shapes=[blocks] * 4
+        + [
+            pltpu.VMEM((2, rows, width), BF16), buffer, buffer, pltpu.VMEM((1, width), F32),
+            pltpu.VMEM((devices,) + payload, F32), pltpu.VMEM((devices,) + payload, F32),
+        ]
+        + [dma((3, outer))] * 6
+        + [dma((CHUNKS,))] * 4
+        + [dma((devices,))] * 2,
+        compiler_params=pltpu.CompilerParams(
+            collective_id=4, has_side_effects=True, vmem_limit_bytes=VMEM_LIMIT
+        ),
+    )(mats, parts, tok, base, gain, small)
 
 
 class Lanes:
@@ -379,72 +1176,12 @@
     def swap_dp(self, x, bit):
         return lax.ppermute(x, "dp", [(i, i ^ bit) for i in range(self.dp)])
 
-    def gather_dp(self, x):
-        far = self.swap_dp(x, 2)
-        both = jnp.concatenate([x, far], axis=0)
-        return jnp.concatenate([both, self.swap_dp(both, 1)], axis=0)
-
-    def scatter_dp(self, x):
-        rows = x.shape[0] // 4
-        got = self.swap_dp(x[2 * rows :].astype(BF16), 1)
-        mine = x[: 2 * rows] + got.astype(F32)
-        got = self.swap_dp(mine[rows:].astype(BF16), 2)
-        return mine[:rows] + got.astype(F32)
-
-    def gather_plane(self, x):
-        half = x.shape[0] // 2
-        a, b = x[:half], x[half:]
-        a = jnp.concatenate([a, self.swap_inner(a)], axis=0)
-        b = jnp.concatenate([b, self.swap_dp(b, 2)], axis=0)
-        a = jnp.concatenate([a, self.swap_dp(a, 2)], axis=0)
-        b = jnp.concatenate([b, self.swap_inner(b)], axis=0)
-        both = jnp.concatenate([a, b], axis=0)
-        return jnp.concatenate([both, self.swap_dp(both, 1)], axis=0)
-
     def fold(self, x, swap):
         half = x.shape[0] // 2
         return x[:half] + swap(x[half:].astype(BF16)).astype(F32)
 
-    def scatter_plane(self, x):
-        x = self.fold(x, lambda p: self.swap_dp(p, 1))
-        half = x.shape[0] // 2
-        a = self.fold(x[:half], lambda p: self.swap_dp(p, 2))
-        b = self.fold(x[half:], self.swap_inner)
-        a = self.fold(a, self.swap_inner)
-        b = self.fold(b, lambda p: self.swap_dp(p, 2))
-        return jnp.concatenate([a, b], axis=0)
-
-    def scatter_grad(self, own, other):
-        got = self.swap_inner(other.astype(BF16))
-        return self.scatter_outer((own + got.astype(F32)).astype(BF16))
-
     def swap_seq(self, x, bit):
         return lax.ppermute(x, "seq", [(i, i ^ bit) for i in range(self.seq)])
-
-    def steps(self):
-        found, bit = [], 1
-        while bit < self.seq:
-            found.append((functools.partial(self.swap_seq, bit=bit), (self.at // bit) % 2 == 1))
-            bit *= 2
-        bit = 1
-        while bit < self.dp:
-            found.append((functools.partial(self.swap_dp, bit=bit), (self.d // bit) % 2 == 1))
-            bit *= 2
-        return found
-
-    def gather_small(self, x):
-        x = x[None]
-        for swap, is_set in self.steps():
-            got = swap(x)
-            x = jnp.concatenate([jnp.where(is_set, got, x), jnp.where(is_set, x, got)], axis=0)
-        return x
-
-    def scatter_small(self, x):
-        for swap, is_set in reversed(self.steps()):
-            half = x.shape[0] // 2
-            low, high = x[:half], x[half:]
-            x = jnp.where(is_set, high, low) + swap(jnp.where(is_set, low, high))
-        return x[0]
 
     def exchange_heads(self, blocks):
         got = [lax.dynamic_index_in_dim(blocks, self.d, 0, keepdims=False)]
@@ -474,55 +1211,6 @@
     return jnp.concatenate([pieces[i] for i in order], axis=-1)
 
 
-def chain(lanes, keeps, total, backward):
-    half = total.shape[0] // 2
-    even = lanes.inner_at == 0
-    own_t = jnp.where(even, total[:half], total[half:])
-    other_t = jnp.where(even, total[half:], total[:half])
-    got_t = swap_halves(lanes.swap_inner(other_t.astype(BF16)), 2).astype(F32)
-    keeps = jnp.where(even, keeps[:, :half], keeps[:, half:])
-    keeps = keeps.reshape(lanes.outer, 2, half, -1)
-    pair = lax.dynamic_index_in_dim(keeps, lanes.outer_at, 0, keepdims=False)
-    is_first = jnp.logical_not(even) if backward else even
-    first_t, second_t = jnp.where(is_first, own_t, got_t), jnp.where(is_first, got_t, own_t)
-    first_k, second_k = (pair[1], pair[0]) if backward else (pair[0], pair[1])
-    entering = jnp.zeros(own_t.shape, F32)
-    reach = jnp.ones(first_k.shape, F32)
-    block_t = second_k[..., None] * first_t + second_t
-    block_keeps = keeps[:, 0] * keeps[:, 1]
-    bit = 1
-    while bit < lanes.outer:
-        at = lanes.outer_at // bit
-        is_set = at % 2 == 1
-        later = jnp.logical_not(is_set) if backward else is_set
-        last_step = 2 * bit == lanes.outer
-        moves = [
-            (i, i ^ (2 * bit))
-            for i in range(lanes.seq)
-            if not last_step or (((i // (2 * bit)) % 2 == 1) == backward)
-        ]
-        got_t = lax.ppermute(block_t.astype(BF16), "seq", moves).astype(F32)
-        mine_k = lax.dynamic_index_in_dim(block_keeps, at, 0, keepdims=False)
-        got_k = lax.dynamic_index_in_dim(
-            block_keeps, jnp.bitwise_xor(at, 1), 0, keepdims=False
-        )
-        entering = entering + jnp.where(later, reach, 0.0)[..., None] * got_t
-        reach = jnp.where(later, reach * got_k, reach)
-        ahead_t, behind_t = jnp.where(later, got_t, block_t), jnp.where(later, block_t, got_t)
-        block_t = jnp.where(later, mine_k, got_k)[..., None] * ahead_t + behind_t
-        block_keeps = block_keeps.reshape(-1, 2, *block_keeps.shape[1:])
-        block_keeps = block_keeps[:, 0] * block_keeps[:, 1]
-        bit *= 2
-    after = first_k[..., None] * entering + first_t
-    mine = jnp.where(is_first, entering, after)
-    theirs = jnp.where(is_first, after, entering)
-    got = swap_halves(lanes.swap_inner(theirs.astype(BF16)), 2)
-    mine = mine.astype(BF16)
-    return jnp.concatenate(
-        [jnp.where(even, mine, got), jnp.where(even, got, mine)], axis=0
-    )
-
-
 def per_device(
     tokens, lengths, cotangent, mixer_gain, feed_gain, head_gain, w_query, w_key, w_value,
     w_gate, w_out, rank_down, rank_up, rank_bias, w_act, w_lin, w_down,
@@ -545,9 +1233,16 @@
     ]
     sizes = [p.shape[0] for p in small_parts]
     used = sum(sizes)
-    padded = -(-used // 128) * 128
+    padded = -(-used // 2048) * 2048
     small = jnp.concatenate(small_parts + [jnp.zeros((padded - used,), BF16)])
-    smalls = lanes.gather_small(small)
+    own_tokens = tokens.reshape(rows, width)
+    w_kqv, w_g, plane_tokens, smalls = gather_all(
+        lanes.outer, lanes.dp, [w_key, w_query, w_value, w_gate], own_tokens,
+        small.reshape(-1, 128),
+    )
+    w_kqv = w_kqv.reshape(3 * head_width, width)
+    w_g = w_g.reshape(head_width, width)
+    smalls = smalls.reshape(devices, padded)
     cuts, offset = [], 0
     for size in sizes:
         cuts.append(smalls[:, offset : offset + size])
@@ -581,18 +1276,7 @@
     )
     alive = (position[None, :] < group_lengths[:, None]).astype(F32).reshape(all_rows, 1)
 
-    head_rows = w_query.shape[0]
-
-    def gather_two(first, second):
-        own = lanes.gather_outer(jnp.concatenate([first, second], axis=0))
-        both = [
-            x.reshape(lanes.outer, 2, head_rows, width) for x in (own, lanes.swap_inner(own))
-        ]
-        return [[x[:, m].reshape(half_width, width) for x in both] for m in range(2)]
-
-    (k_own, k_other), (v_own, v_other) = gather_two(w_key, w_value)
-    (q_own, q_other), (g_own, g_other) = gather_two(w_query, w_gate)
-
+    w_out, smalls = lax.optimization_barrier((w_out, smalls))
     out_rows = w_out.shape[0]
     out_split = w_out.reshape(out_rows, lanes.dp, lanes.outer, 2, -1)
     out_own, out_other = lanes.pick(out_split, 3)
@@ -604,31 +1288,11 @@
         axis=2,
     )
     out_mine = lanes.exchange_heads(out_local.transpose(1, 0, 2))
-    out_own = lanes.gather_outer(out_mine[None])
-    out_other = swap_halves(lanes.swap_inner(out_own), 1)
-    even = lanes.inner_at == 0
-    out_natural = jnp.stack(
-        [jnp.where(even, out_own, out_other), jnp.where(even, out_other, out_own)], axis=2
-    )
-    out_full = out_natural.transpose(1, 0, 2, 3, 4).reshape(width, head_width)
-
-    down = lanes.gather_outer(w_down)
-    act = lanes.gather_outer(w_act)
-    lin = lanes.gather_outer(w_lin)
-
-    own_tokens = tokens.reshape(rows, width)
-    sources = lanes.gather_dp(own_tokens).astype(F32)
+    sources = plane_tokens.reshape(all_rows, width).astype(F32)
     normed_in = (sources * rms_scale(sources) * mixer_full).astype(BF16)
     grad_out = cotangent.reshape(rows, width).astype(F32) * alive_own
-    grad_feed = lanes.gather_plane(grad_out.astype(BF16))
-
-    def project(own, other):
-        return jnp.concatenate(
-            [contract_last(normed_in, own), contract_last(normed_in, other)], axis=1
-        )
-
-    query_pre, key_pre = project(q_own, q_other), project(k_own, k_other)
-    value_pre, gate_pre = project(v_own, v_other), project(g_own, g_other)
+
+    pre = contract_last(normed_in, w_kqv)
     low_rank = mm(normed_in, down_full, 1, 0).astype(BF16)
     gate_logit = contract_last(low_rank, up_mine) + bias_mine
     log_decay = jax.nn.log_sigmoid(gate_logit) / GATE_NORM * alive
@@ -640,34 +1304,36 @@
     def flat(x):
         return x.reshape(all_rows, x.shape[2])
 
-    queries = seqs(jax.nn.silu(query_pre).astype(BF16))
-    key_feats = seqs(jax.nn.silu(key_pre).astype(BF16))
-    value_feats = seqs(value_pre.astype(BF16))
+    is_value = jnp.arange(3 * head_width) >= 2 * head_width
+    feats = seqs(jnp.where(is_value, pre, pre * jax.nn.sigmoid(pre)).astype(BF16))
+    pre = seqs(pre)
     decays, writes = seqs(log_decay), seqs(writes)
-    gates = seqs(gate_pre)
 
     def shaped(like_rows, columns, kind):
         return jax.ShapeDtypeStruct((sequences, like_rows, columns), kind)
 
-    summary, keep_all = per_sequence(
-        summary_kernel,
-        [key_feats, value_feats, decays, writes],
-        [shaped(SLOTS, 2 * head_width, F32), shaped(1, SLOTS, F32)],
-    )
-    keep_all = keep_all.reshape(sequences, SLOTS)
-    keeps = keep_all[None]
-    bit = 1
-    while bit < lanes.seq:
-        got = lanes.swap_seq(keeps, bit)
-        is_set = (lanes.at // bit) % 2 == 1
-        keeps = jnp.concatenate(
-            [jnp.where(is_set, got, keeps), jnp.where(is_set, keeps, got)], axis=0
-        )
-        bit *= 2
-    state_in = chain(lanes, keeps, summary, False)
+    out_own = lanes.gather_outer(out_mine[None])
+    out_own, feats = lax.optimization_barrier((out_own, feats))
+    keys, queries, values = (feats, 0), (feats, 1), (feats, 2)
+    state_in, keeps = relay(
+        lanes.outer, False, [feats, decays, writes], sequences, SLOTS, 2 * head_width
+    )
+    gates = seqs(contract_last(normed_in, w_g))
+    out_other = swap_halves(lanes.swap_inner(out_own), 1)
+    even = lanes.inner_at == 0
+    natural = jnp.stack(
+        [jnp.where(even, out_own, out_other), jnp.where(even, out_other, out_own)], axis=2
+    )
+    out_full = natural.transpose(1, 0, 2, 3, 4).reshape(width, head_width)
+    w_down, w_act, w_lin, state_in = lax.optimization_barrier((w_down, w_act, w_lin, state_in))
+    feed = lax.all_gather(
+        jnp.stack([w_down, w_act, w_lin]), "seq", axis=1, tiled=True,
+        axis_index_groups=lanes.groups,
+    )
+    down, act, lin = feed[0], feed[1], feed[2]
     mixed, slot_out, attend = per_sequence(
         forward_kernel,
-        [queries, key_feats, value_feats, gates, decays, writes, state_in],
+        [queries, keys, values, gates, decays, writes, state_in],
         [
             shaped(piece, head_width, BF16),
             shaped(piece, head_width, F32),
@@ -676,9 +1342,12 @@
         shared=[head_full],
     )
     mixed_flat = flat(mixed)
-    hidden = own_tokens.astype(F32) + lanes.scatter_dp(contract_last(mixed_flat, out_full))
-    mid_scale = rms_scale(hidden)
-    normed_mid = lanes.gather_plane((hidden * mid_scale * feed_full).astype(BF16))
+    parts = contract_last(mixed_flat, out_full).astype(BF16)
+    hidden, normed_mid, grad_feed = middle(
+        parts.reshape(4, rows, width), own_tokens, feed_full, grad_out.astype(BF16)
+    )
+    normed_mid = normed_mid.reshape(8 * rows, width)
+    grad_feed = grad_feed.reshape(8 * rows, width)
 
     grad_product = contract_last(grad_feed, down)
     gate_part = contract_last(normed_mid, act)
@@ -690,42 +1359,27 @@
         grad_product * lin_part * (sigma * (1.0 + gate_part * (1.0 - sigma)))
     ).astype(BF16)
     grad_lin = (grad_product * swish).astype(BF16)
-    grad_mid = lanes.scatter_plane(mm(grad_gate, act, 1, 0) + mm(grad_lin, lin, 1, 0))
-    w_down_grad = lanes.scatter_outer(contract_first(product, grad_feed).astype(BF16))
-    w_act_grad = lanes.scatter_outer(contract_first(grad_gate, normed_mid).astype(BF16))
-    w_lin_grad = lanes.scatter_outer(contract_first(grad_lin, normed_mid).astype(BF16))
-    w_down_grad, w_act_grad, w_lin_grad = [
-        x.astype(F32) for x in (w_down_grad, w_act_grad, w_lin_grad)
-    ]
-
-    mid_unit = hidden * mid_scale
-    feed_gain_part = jnp.sum(grad_mid * mid_unit, axis=0)
-    scaled = grad_mid * feed_full
-    grad_hidden = grad_out + mid_scale * (
-        scaled - mid_unit * jnp.mean(scaled * mid_unit, axis=-1, keepdims=True)
-    )
-    grad_attn = lanes.gather_dp(grad_hidden.astype(BF16))
-
-    product, grad_attn = lax.optimization_barrier((product, grad_attn))
-    feed_sum = lanes.scatter_plane(mm(product, down, 1, 0))
-    block_out = (alive_own * (hidden + feed_sum)).astype(BF16)
+    feed_grads = jnp.stack(
+        [
+            contract_first(product, grad_feed).astype(BF16),
+            contract_first(grad_gate, normed_mid).astype(BF16),
+            contract_first(grad_lin, normed_mid).astype(BF16),
+        ]
+    )
+    grad_gate, grad_lin, feed_grads = lax.optimization_barrier((grad_gate, grad_lin, feed_grads))
+    feed_grads = lax.psum_scatter(
+        feed_grads, "seq", scatter_dimension=1, tiled=True, axis_index_groups=lanes.groups
+    )
+    mid_parts = (mm(grad_gate, act, 1, 0) + mm(grad_lin, lin, 1, 0)).astype(BF16)
+    grad_hidden, feed_gain_part, grad_attn = middle_back(
+        mid_parts.reshape(8, rows, width), hidden, grad_out, feed_full
+    )
+    grad_attn = grad_attn.reshape(all_rows, width)
 
     grad_mixed = mm(grad_attn, out_full, 1, 0)
-    out_grad = contract_first(grad_attn, mixed_flat).astype(BF16)
-    out_grad = out_grad.reshape(lanes.dp, lanes.outer, 2, out_rows, head_width)
-    own_part, other_part = lanes.pick(out_grad, 2)
-    got = swap_halves(lanes.swap_inner(other_part), 1)
-    out_sum = (own_part.astype(F32) + got.astype(F32)).astype(BF16).transpose(1, 0, 2, 3)
-    out_mine = lanes.scatter_outer(out_sum.reshape(-1, head_width))
-    out_mine = out_mine.reshape(lanes.dp, out_rows, head_width)
-    out_mine = lanes.exchange_heads(out_mine).transpose(1, 0, 2)
-    out_mine = out_mine.reshape(out_rows, lanes.dp, 2, lanes.outer, -1)
-    low_half, high_half = lanes.pick(out_mine, 2)
-    w_out_grad = jnp.stack([low_half, high_half], axis=3).reshape(out_rows, width).astype(F32)
-
     grad_gate_pre, grad_slot, grad_scores, adjoint, head_parts = per_sequence(
         back_first_kernel,
-        [seqs(grad_mixed), gates, slot_out, attend, queries, value_feats, decays, writes, state_in],
+        [seqs(grad_mixed), gates, slot_out, attend, queries, values, decays, writes, state_in],
         [
             shaped(piece, head_width, BF16),
             shaped(piece, head_width, BF16),
@@ -735,19 +1389,33 @@
         ],
         shared=[head_full],
     )
-    adjoint_in = chain(lanes, keeps, adjoint, True)
-    grad_query_pre, grad_key_pre, grad_value_pre, grad_logit = per_sequence(
+    grad_gate_flat = flat(grad_gate_pre)
+    out_grad = contract_first(grad_attn, mixed_flat).astype(BF16)
+    out_grad = out_grad.reshape(lanes.dp, lanes.outer, 2, out_rows, head_width)
+    own_part, other_part = lanes.pick(out_grad, 2)
+    got = swap_halves(lanes.swap_inner(other_part), 1)
+    out_sum = (own_part.astype(F32) + got.astype(F32)).astype(BF16).transpose(1, 0, 2, 3)
+    gate_grad = contract_first(grad_gate_flat, normed_in).astype(BF16)
+    gate_in = mm(grad_gate_flat, w_g, 1, 0)
+    feed_parts = mm(product, down, 1, 0).astype(BF16)
+    feed_parts = lanes.fold(feed_parts, lambda p: lanes.swap_dp(p, 1))
+    adjoint, out_sum, gate_grad, gate_in, feed_parts = lax.optimization_barrier(
+        (adjoint, out_sum, gate_grad, gate_in, feed_parts)
+    )
+    feed_got = lanes.swap_dp(feed_parts[2 * rows :].astype(BF16), 2)
+    adjoint_in = relay(
+        lanes.outer, True, [adjoint, keeps], sequences, SLOTS, 2 * head_width
+    )
+    gate_grad, out_sum, adjoint_in = lax.optimization_barrier((gate_grad, out_sum, adjoint_in))
+    out_mine = lanes.scatter_outer(out_sum.reshape(-1, head_width))
+    gate_got = lanes.swap_inner(gate_grad[half_width:])
+    grad_pre, grad_logit = per_sequence(
         back_second_kernel,
         [
-            grad_slot, grad_scores, attend, queries, key_feats, value_feats, decays, writes,
-            state_in, adjoint_in, seqs(query_pre), seqs(key_pre), seqs(gate_logit), seqs(alive),
+            grad_slot, grad_scores, attend, queries, keys, values, decays, writes,
+            state_in, adjoint_in, (pre, 1), (pre, 0), seqs(gate_logit), seqs(alive),
         ],
-        [
-            shaped(piece, head_width, BF16),
-            shaped(piece, head_width, BF16),
-            shaped(piece, head_width, BF16),
-            shaped(piece, SLOTS, BF16),
-        ],
+        [shaped(piece, 3 * head_width, BF16), shaped(piece, SLOTS, BF16)],
     )
     grad_logit = flat(grad_logit)
     bias_part = jnp.sum(grad_logit.astype(F32), axis=0)
@@ -755,31 +1423,17 @@
     grad_rank = mm(grad_logit, up_mine, 1, 0).astype(BF16)
     down_part = contract_first(normed_in, grad_rank)
 
-    grad_in = contract_last(grad_rank, down_full)
-    mixer_grads = []
-    for grad_pre, (own, other) in zip(
-        (grad_gate_pre, grad_query_pre, grad_key_pre, grad_value_pre),
-        ((g_own, g_other), (q_own, q_other), (k_own, k_other), (v_own, v_other)),
-    ):
-        grad_pre = flat(grad_pre)
-        low, high = grad_pre[:, :half_width], grad_pre[:, half_width:]
-        grad_in = grad_in + mm(low, own, 1, 0) + mm(high, other, 1, 0)
-        mixer_grads.append(
-            lanes.scatter_grad(
-                contract_first(low, normed_in), contract_first(high, normed_in)
-            ).astype(F32)
-        )
-    w_gate_grad, w_query_grad, w_key_grad, w_value_grad = mixer_grads
-    grad_in = lanes.scatter_dp(grad_in)
-    own_sources = own_tokens.astype(F32)
-    in_scale = rms_scale(own_sources)
-    in_unit = own_sources * in_scale
-    mixer_gain_part = jnp.sum(grad_in * in_unit, axis=0)
-    scaled = grad_in * mixer_full
-    tokens_grad = grad_hidden + in_scale * (
-        scaled - in_unit * jnp.mean(scaled * in_unit, axis=-1, keepdims=True)
-    )
-    tokens_grad = tokens_grad.reshape(seq_count, piece, width)
+    grad_pre, feed_got, gate_got, out_mine = lax.optimization_barrier(
+        (flat(grad_pre), feed_got, gate_got, out_mine)
+    )
+    gate_sum = (gate_grad[:half_width].astype(F32) + gate_got.astype(F32)).astype(BF16)
+    gate_sum, grad_pre = lax.optimization_barrier((gate_sum, grad_pre))
+    gate_sum = lanes.scatter_outer(gate_sum)
+    feed_parts = feed_parts[: 2 * rows] + feed_got.astype(F32)
+    feed_got = lanes.swap_inner(feed_parts[rows:].astype(BF16))
+    grad_in = mm(grad_pre, w_kqv, 1, 0) + gate_in + contract_last(grad_rank, down_full)
+    mixer_grads = contract_first(grad_pre, normed_in).astype(BF16)
+    mixer_grads = mixer_grads.reshape(3, 2, lanes.outer, -1, width)
 
     head_part = jnp.sum(head_parts, axis=(0, 1)).reshape(2, lanes.outer, -1)
     low_half, high_half = lanes.pick(head_part, 0)
@@ -788,7 +1442,6 @@
     up_all = mine[:, None] * up_part.reshape(1, -1)
     bias_all = mine[:, None] * bias_part.reshape(1, -1)
     parts = [
-        mixer_gain_part.reshape(devices, -1),
         feed_gain_part.reshape(devices, -1),
         head_part.reshape(devices, -1),
         down_part.reshape(devices, -1),
@@ -796,9 +1449,28 @@
         bias_all.reshape(devices, -1),
     ]
     sizes = [p.shape[1] for p in parts]
-    padded = -(-sum(sizes) // 128) * 128
+    padded = -(-sum(sizes) // 1024) * 1024
     parts.append(jnp.zeros((devices, padded - sum(sizes)), F32))
-    reduced = lanes.scatter_small(jnp.concatenate(parts, axis=1))
+    small_parts = jnp.concatenate(parts, axis=1).reshape(devices, -1, 128)
+    grad_in, mixer_grads, feed_got, gate_sum = lax.optimization_barrier(
+        (grad_in.astype(BF16), mixer_grads, feed_got, gate_sum)
+    )
+    w_gate_grad = gate_sum.astype(F32)
+    out_mine = out_mine.reshape(lanes.dp, out_rows, head_width)
+    out_mine = lanes.exchange_heads(out_mine).transpose(1, 0, 2)
+    out_mine = out_mine.reshape(out_rows, lanes.dp, 2, lanes.outer, -1)
+    low_half, high_half = lanes.pick(out_mine, 2)
+    w_out_grad = jnp.stack([low_half, high_half], axis=3).reshape(out_rows, width).astype(F32)
+    feed_sum = feed_parts[:rows] + feed_got.astype(F32)
+    block_out = (alive_own * (hidden + feed_sum)).astype(BF16)
+    weight_grads, tokens_grad, reduced = finish(
+        lanes.outer, lanes.dp, mixer_grads, grad_in.reshape(4, rows, width), own_tokens,
+        grad_hidden, mixer_full, small_parts,
+    )
+    w_key_grad, w_query_grad, w_value_grad = weight_grads[0], weight_grads[1], weight_grads[2]
+    tokens_grad = tokens_grad.reshape(seq_count, piece, width)
+    mixer_gain_grad = reduced[padded // 128, : width // devices]
+    reduced = reduced.reshape(-1)
     smalls, offset = [], 0
     for size in sizes:
         smalls.append(reduced[offset : offset + size])
@@ -806,20 +1478,20 @@
     return (
         block_out.reshape(seq_count, piece, width),
         tokens_grad,
+        mixer_gain_grad,
         smalls[0],
         smalls[1],
-        smalls[2],
         w_query_grad,
         w_key_grad,
         w_value_grad,
         w_gate_grad,
         w_out_grad,
+        smalls[2].reshape(-1, rank),
         smalls[3].reshape(-1, rank),
-        smalls[4].reshape(-1, rank),
-        smalls[5],
-        w_act_grad,
-        w_lin_grad,
-        w_down_grad,
+        smalls[4],
+        feed_grads[1].astype(F32),
+        feed_grads[2].astype(F32),
+        feed_grads[0].astype(F32),
     )
 
 

time: 1060 us -> 935 us (0.88); the launches traced: 1040 us -> 931 us
  Pallas kernels: 57.8 us -> 575 us
  waiting for transfers between devices: 437 us -> 46 us
  starting transfers between devices: 83.2 us -> 11.2 us
  other arithmetic: 128 us -> 56.7 us
  matrix products: 221 us -> 157 us
  local copies, waits for them, and re-layouts: 101 us -> 70.2 us
    pallas_call x4 -> x9, Pallas kernels: 57.8 us -> 575 us  [the longest x1 184 us: finish(): pl.pallas_call(functools.partial(final_kernel, outer, dp), in_specs=[in_v...]
    ppermute x30 -> x8, waiting for transfers between devices: 157 us -> 4.81 us  [swap_dp(): return lax.ppermute(x, 'dp', [(i, i ^ bit) for i in range(self.dp)])]
    ppermute x20 -> x4, waiting for transfers between devices: 117 us -> 0.01 us  [swap_inner(): return lax.ppermute(x, 'seq', [(i, i ^ 1) for i in range(self.seq)])]
    all_gather x6 -> x1, waiting for transfers between devices: 96.2 us -> 14.8 us  [gather_outer(): lax.all_gather(x, 'seq', axis=0, tiled=True, axis_index_groups=self.groups)]
    dot_general x42 -> x24, matrix products: 221 us -> 157 us  [mm(): lax.dot_general(a.astype(BF16), b.astype(BF16), (((ca,), (cb,)), ((), ())...]
    ppermute x13 -> x0, waiting for transfers between devices: 55.2 us -> none  [the longest x4 44.7 us: chain(): got_t = lax.ppermute(block_t.astype(BF16), 'seq', moves).astype(F32)]
    ppermute x30 -> x8, starting transfers between devices: 45.8 us -> 7.25 us  [swap_dp(): return lax.ppermute(x, 'dp', [(i, i ^ bit) for i in range(self.dp)])]
    all_gather x0 -> x1, waiting for transfers between devices: none -> 25.7 us  [per_device(): lax.all_gather(jnp.stack([w_down, w_act, w_lin]), 'seq', axis=1, tiled=Tr...]
  transfers between devices with their start and end apart: 77 -> 17, of which waited for: 40 -> 3; matrix products, arithmetic and copies ran while one was open for 38% -> 16% of each run, Pallas kernels for 4% -> 44%
where the time goes in v2:
time: 935 us; the launch traced here: 931 us
  Pallas kernels  575 us (61%)
  matrix products  157 us (17%)
  local copies, waits for them, and re-layouts  70.2 us (8%)
  other arithmetic  56.7 us (6%)
  waiting for transfers between devices  46 us (5%)
  between operations  15.2 us (2%)
  starting transfers between devices  11.2 us (1%)
    pallas_call x1, Pallas kernels, finish(): pl.pallas_call(functools.partial(final_kernel, outer, dp), in_specs=[in_v...  184 us
    dot_general x24, matrix products, mm(): lax.dot_general(a.astype(BF16), b.astype(BF16), (((ca,), (cb,)), ((), ())...  157 us
    pallas_call x1, Pallas kernels, middle(): pl.pallas_call(middle_kernel, in_specs=[in_vmem()] * 3 + [in_hbm()], out_...  105 us
    pallas_call x1, Pallas kernels, gather_all(): pl.pallas_call(functools.partial(gather_kernel, outer, dp), in_specs=[in_...  97.1 us
    pallas_call x2, Pallas kernels, relay(): pl.pallas_call(functools.partial(relay_kernel, outer, backward), in_specs...  68.3 us
    pallas_call x1, Pallas kernels, middle_back(): pl.pallas_call(middle_back_kernel, in_specs=[in_vmem()] * 4, out_specs=[i...  65.6 us
    pallas_call x3, Pallas kernels, per_sequence(): pl.pallas_call(kernel, grid=(count,), in_specs=[spec(x.shape, at) for x,...  54.5 us
    unnamed x197, local copies, waits for them, and re-layouts  35.6 us
  transfers between devices with their start and end apart: 17, of which 3 were waited for; matrix products, arithmetic and copies ran while one was open for 16% of the time, Pallas kernels for 44%

profile of v2, /device:TPU:21, one launch (start us, length us, event | category | flops | bytes accessed | tf_op | source)
XLA Modules:
  0.0 930.7 jit_solution(3600227279804157557)
XLA Ops:
  9.6 2.7 concatenate.33
  17.3 97.1 %shard_map.288 = (bf16[3,2,4,64,2048]{4,3,2,1,0:T(8,128)(2,1)}, bf16[2,4,64,2048]{3,2,1,0:T(8,128)(2,1)S(1)}, bf16[4,256,2048]{2,1,0:T(8,128)(2,1)S(1)}, bf16[32,16,128]{2,1,0:T(8,128)(2,1)S(1)}) custom-call(bf16[64,2048]{1,0:T(8,128)(2,1)S(1)} %copy-done.41, bf16[64,2048]{1,0:T(8,128)(2,1)S(1)} %copy-done.42, bf16[64,2048]{1,0:T(8,128)(2,1)S(1)} %copy-done.43, ...), custom_call_target="tpu_custom_call" | custom-call | tf_op jit(solution)/shard_map/pallas_call | solution.py:555
  114.4 2.0 copy-done.2
  116.4 1.3 copy-done.49
  117.8 1.5 reshape.613
  120.8 1.9 collective-permute-start
  123.6 3.1 multiply_reduce_fusion
  128.4 3.3 multiply_convert_fusion
  137.0 12.4 %fusion.2 = (bf16[1024,1536]{1,0:T(8,128)(2,1)S(1)}, f32[1024,1536]{1,0:T(8,128)}) fusion(pred[1536]{0:T(1024)(128)(4,1)S(1)} %iota_compare_fusion, bf16[1024,2048]{1,0:T(8,128)(2,1)} %bitcast.282, bf16[1536,2048]{1,0:T(8,128)(2,1)} %bitcast.318), kind=kOutput, calls=%fused_computation.12 | convolution fusion | flops 6451888128 | bytes 19924480 | tf_op jit(solution)/shard_map/dot_general | solution.py:21
  149.4 14.8 %all-gather.6.cloned.1.call-done = bf16[16,64,512]{2,1,0:T(8,128)(2,1)} async-done(((bf16[4,64,512]{2,1,0:T(8,128)(2,1)}), bf16[16,64,512]{2,1,0:T(8,128)(2,1)}) %all-gather.6.cloned.1.call-update) | async-done | bytes 1048592 | tf_op jit(solution)/shard_map/all_gather | solution.py:1169
  166.3 43.4 %shard_map.289 = (bf16[8,64,1024]{2,1,0:T(8,128)(2,1)S(1)}, f32[2,8,64]{2,1,0:T(8,128)S(1)}) custom-call(bf16[8,128,1536]{2,1,0:T(8,128)(2,1)S(1)} %bitcast.239, f32[8,128,64]{2,1,0:T(8,128)S(1)} %bitcast.249, f32[8,128,64]{2,1,0:T(8,128)S(1)} %bitcast.253), custom_call_target="tpu_custom_call" | custom-call | tf_op jit(solution)/shard_map/pallas_call | solution.py:701
  210.7 1.6 pad_maximum_fusion.1
  212.9 1.5 collective-permute-start.3
  214.4 2.9 convert_multiply_fusion
  217.3 4.7 fusion.46.gate_ref
  222.1 14.9 %shard_map.290 = (bf16[8,128,512]{2,1,0:T(8,128)(2,1)S(1)}, f32[8,128,512]{2,1,0:T(8,128)S(1)}, f32[8,128,64]{2,1,0:T(8,128)S(1)}) custom-call(bf16[8,128,1536]{2,1,0:T(8,128)(2,1)S(1)} %bitcast.240, bf16[8,128,1536]{2,1,0:T(8,128)(2,1)S(1)} %bitcast.241, bf16[8,128,1536]{2,1,0:T(8,128)(2,1)S(1)} %bitcast.242, f32[8,128,512]{2,1,0:T(8,128)S(1)} %fusion.46.gate_ref, ...), custom_call_target="tpu_custom_call" | custom-call | tf_op jit(solution)/shard_map/pallas_call | solution.py:346
  238.8 2.4 convolution_convert_fusion.2
  241.2 105.1 %shard_map.291 = (f32[256,2048]{1,0:T(8,128)S(1)}, bf16[8,256,2048]{2,1,0:T(8,128)(2,1)}, bf16[8,256,2048]{2,1,0:T(8,128)(2,1)}) custom-call(bf16[4,256,2048]{2,1,0:T(8,128)(2,1)S(1)} %bitcast.260, bf16[256,2048]{1,0:T(8,128)(2,1)S(1)} %bitcast.258, f32[1,2048]{1,0:T(1,128)S(1)} %reshape.652.gain, bf16[256,2048]{1,0:T(8,128)(2,1)S(1)} %get-tuple-element.224.extra), custom_call_target="tpu_custom_call" | custom-call | tf_op jit(solution)/shard_map/pallas_call | solution.py:806
  346.3 25.7 %all-gather.4.cloned.1.call-done = bf16[3,704,2048]{2,1,0:T(8,128)(2,1)} async-done(((bf16[3,176,2048]{2,1,0:T(8,128)(2,1)}), bf16[3,704,2048]{2,1,0:T(8,128)(2,1)}) %all-gather.4.cloned.1.call-update) | async-done | bytes 8650768 | tf_op jit(solution)/shard_map/all_gather | solution.py:1329
  372.1 11.9 %fusion.10 = f32[2048,704]{0,1:T(8,128)} fusion(bf16[2048,2048]{1,0:T(8,128)(2,1)} %bitcast.314, bf16[3,704,2048]{2,1,0:T(8,128)(2,1)} %all-gather.4.cloned.1.call-done), kind=kOutput, calls=%fused_computation.35 | convolution fusion | flops 5905580032 | bytes 17039360 | tf_op jit(solution)/shard_map/dot_general | solution.py:21
  384.0 7.9 fusion.7
  391.9 15.8 %multiply_convert_fusion.1 = (bf16[2048,704]{0,1:T(8,128)(2,1)}, bf16[2048,704]{0,1:T(8,128)(2,1)}, bf16[2048,704]{0,1:T(8,128)(2,1)S(1)}) fusion(f32[2048,704]{0,1:T(8,128)} %fusion.10, f32[2048,704]{0,1:T(8,128)} %fusion.7, bf16[2048,2048]{1,0:T(8,128)(2,1)} %bitcast.315, bf16[3,704,2048]{2,1,0:T(8,128)(2,1)S(1)} %copy-done.84), kind=kOutput, calls=%fused_computation.13 | convolution fusion | flops 5927206912 | bytes 31457280 | tf_op jit(solution)/shard_map/dot_general | solution.py:21
  407.8 9.6 %fusion.6 = bf16[1,704,2048]{2,1,0:T(8,128)(2,1)S(1)} fusion(bf16[2048,704]{0,1:T(8,128)(2,1)S(1)} %get-tuple-element.86, bf16[2048,2048]{1,0:T(8,128)(2,1)} %bitcast.316), kind=kOutput, calls=%fused_computation.28 | convolution fusion | flops 5907021824 | bytes 14155776 | tf_op jit(solution)/shard_map/dot_general | solution.py:21
  417.4 8.7 fusion.5
  426.1 6.3 fusion.4
  432.5 4.0 pad_maximum_fusion
  436.5 9.4 %convolution_convert_fusion.1 = bf16[2048,2048]{1,0:T(8,128)(2,1)S(1)} fusion(bf16[2048,704]{0,1:T(8,128)(2,1)} %get-tuple-element.210, bf16[3,704,2048]{2,1,0:T(8,128)(2,1)} %all-gather.4.cloned.1.call-done), kind=kOutput, calls=%fused_computation.11 | convolution fusion | flops 5909774336 | bytes 14155776 | tf_op jit(solution)/shard_map/dot_general | solution.py:21
  445.9 2.5 slice.246
  448.4 2.6 copy-done.59
  451.7 12.3 %fusion.9 = f32[2048,2048]{1,0:T(8,128)} fusion(bf16[2048,704]{0,1:T(8,128)(2,1)S(1)} %copy-done.90, bf16[3,704,2048]{2,1,0:T(8,128)(2,1)} %all-gather.4.cloned.1.call-done), kind=kOutput, calls=%fused_computation.34 | convolution fusion | flops 5905580032 | bytes 22544384 | tf_op jit(solution)/shard_map/dot_general | solution.py:21
  464.0 13.3 %add_convert_fusion = bf16[2048,2048]{1,0:T(8,128)(2,1)} fusion(f32[2048,2048]{1,0:T(8,128)} %fusion.9, bf16[2048,704]{0,1:T(8,128)(2,1)S(1)} %copy-done.88, bf16[3,704,2048]{2,1,0:T(8,128)(2,1)} %all-gather.4.cloned.1.call-done), kind=kOutput, calls=%fused_computation | convolution fusion | flops 5913968640 | bytes 30932992 | tf_op jit(solution)/shard_map/dot_general | solution.py:21
  477.2 65.6 %shard_map.292 = (f32[256,2048]{1,0:T(8,128)S(1)}, f32[1,2048]{1,0:T(1,128)S(1)}, bf16[4,256,2048]{2,1,0:T(8,128)(2,1)S(1)}) custom-call(bf16[8,256,2048]{2,1,0:T(8,128)(2,1)} %bitcast.287, f32[256,2048]{1,0:T(8,128)S(1)} %get-tuple-element.79.hidden, f32[256,2048]{1,0:T(8,128)S(1)} %copy-done.19, f32[1,2048]{1,0:T(1,128)S(1)} %reshape.652.gain), custom_call_target="tpu_custom_call" | custom-call | tf_op jit(solution)/shard_map/pallas_call | solution.py:919
  542.9 2.4 convolution_convert_fusion.7
  546.9 2.3 fusion.47.grad_mixed_ref
  549.9 13.5 %shard_map.293 = (bf16[8,128,512]{2,1,0:T(8,128)(2,1)S(1)}, bf16[8,128,512]{2,1,0:T(8,128)(2,1)S(1)}, f32[8,128,64]{2,1,0:T(8,128)S(1)}, f32[8,64,1024]{2,1,0:T(8,128)S(1)}, f32[8,1,512]{2,1,0:T(1,128)S(1)}) custom-call(f32[8,128,512]{2,1,0:T(8,128)S(1)} %fusion.47.grad_mixed_ref, f32[8,128,512]{2,1,0:T(8,128)S(1)} %copy-done.23, ...), custom_call_target="tpu_custom_call" | custom-call | tf_op jit(solution)/shard_map/pallas_call | solution.py:346
  563.5 5.7 fusion.48
  569.2 3.8 convolution_convert_fusion.6
  573.1 1.5 fusion.15
  574.6 5.4 convert_add_fusion
  580.0 24.9 %shard_map.294.adjoint_ref = bf16[8,64,1024]{2,1,0:T(8,128)(2,1)S(1)} custom-call(f32[8,64,1024]{2,1,0:T(8,128)S(1)} %get-tuple-element.97.refs_0_, f32[2,8,64]{2,1,0:T(8,128)S(1)} %get-tuple-element.98.refs_1_), custom_call_target="tpu_custom_call" | custom-call | tf_op jit(solution)/shard_map/pallas_call | solution.py:701
  605.9 1.6 slice.304
  608.2 2.3 slice.202
  621.4 26.2 %shard_map.295 = (bf16[8,128,1536]{2,1,0:T(8,128)(2,1)S(1)}, bf16[8,128,64]{2,1,0:T(8,128)(2,1)S(1)}) custom-call(bf16[8,128,512]{2,1,0:T(8,128)(2,1)S(1)} %copy-done.38, f32[8,128,64]{2,1,0:T(8,128)S(1)} %copy-done.40, f32[8,128,64]{2,1,0:T(8,128)S(1)} %copy-done.28, bf16[8,128,1536]{2,1,0:T(8,128)(2,1)S(1)} %bitcast.245, ...), custom_call_target="tpu_custom_call" | custom-call | tf_op jit(solution)/shard_map/pallas_call | solution.py:346
  647.6 1.6 copy-done.47
  649.2 4.8 collective-permute-done.6
  654.0 2.9 add_convert_fusion.2
  657.9 5.3 fusion.1
  665.7 3.6 fusion.51
  672.1 3.6 convert_add_fusion.1
  677.6 3.0 collective-permute-start.9
  681.2 11.1 %fusion.49 = f32[1024,2048]{1,0:T(8,128)} fusion(bf16[1024,1536]{1,0:T(8,128)(2,1)S(1)} %bitcast.273, bf16[1536,2048]{1,0:T(8,128)(2,1)} %bitcast.319), kind=kOutput, calls=%fused_computation.155 | convolution fusion | flops 6442450944 | bytes 17825792 | tf_op jit(solution)/shard_map/dot_general | solution.py:21
  692.3 8.8 convolution_convert_fusion
  701.1 8.8 add_convert_fusion.1
  710.7 2.2 reshape.648
  714.3 1.8 copy.110
  716.1 3.0 reshape.657
  719.1 2.2 copy-done.3
  721.3 184.0 %shard_map.296 = (f32[3,64,2048]{2,1,0:T(8,128)S(1)}, f32[256,2048]{1,0:T(8,128)S(1)}, f32[24,128]{1,0:T(8,128)S(1)}) custom-call(bf16[3,2,4,64,2048]{4,3,2,1,0:T(8,128)(2,1)} %bitcast.288, bf16[4,256,2048]{2,1,0:T(8,128)(2,1)S(1)} %bitcast.248, bf16[256,2048]{1,0:T(8,128)(2,1)S(1)} %bitcast.259, f32[256,2048]{1,0:T(8,128)S(1)} %copy-done.33, ...), custom_call_target="tpu_custom_call" | custom-call | tf_op jit(solution)/shard_map/pallas_call | solution.py:1131
  905.3 1.3 copy-done.30
  910.2 1.8 convert_element_type.301
  913.1 2.5 slice_bitcast_fusion.12
  915.7 3.1 fusion.13
  918.8 3.9 fusion.16
  922.7 1.3 copy.141
  (314 shorter events, 53.3 us)
Async XLA Ops:
  7.2 157.0 %all-gather.6.cloned.1.call-start = ((), (), s32[]{:S(2)}) async-start(), calls=%async_computation.7 | async-start | bytes 1310720 | tf_op jit(solution)/shard_map/all_gather | solution.py:1169
  120.8 15.3 %collective-permute-start = (bf16[64,512]{1,0:T(8,128)(2,1)S(1)}, bf16[64,512]{1,0:T(8,128)(2,1)S(1)}, u32[]{:S(2)}, u32[]{:S(2)}) collective-permute-start(bf16[64,512]{1,0:T(8,128)(2,1)S(1)} %get-tuple-element.250), channel_id=1, source_target_pairs={{0,24},{8,16},{16,8},{24,0},{1,25},{9,17},{17,9},{25,1},{2,26},{10... | collective-permute-start | bytes 196616 | tf_op jit(solution)/shard_map/ppermute | solution.py:1177
  122.7 13.4 %collective-permute-start.1 = (bf16[64,512]{1,0:T(8,128)(2,1)S(1)}, bf16[64,512]{1,0:T(8,128)(2,1)S(1)}, u32[]{:S(2)}, u32[]{:S(2)}) collective-permute-start(bf16[64,512]{1,0:T(8,128)(2,1)S(1)} %get-tuple-element.249), channel_id=1, source_target_pairs={{0,16},{8,24},{16,0},{24,8},{1,17},{9,25},{17,1},{25,9},{2,18},{10... | collective-permute-start | bytes 196616 | tf_op jit(solution)/shard_map/ppermute | solution.py:1177
  122.9 13.2 %collective-permute-start.2 = (bf16[64,512]{1,0:T(8,128)(2,1)S(1)}, bf16[64,512]{1,0:T(8,128)(2,1)S(1)}, u32[]{:S(2)}, u32[]{:S(2)}) collective-permute-start(bf16[64,512]{1,0:T(8,128)(2,1)S(1)} %get-tuple-element.248), channel_id=1, source_target_pairs={{0,8},{8,0},{16,24},{24,16},{1,9},{9,1},{17,25},{25,17},{2,10},{10... | collective-permute-start | bytes 196616 | tf_op jit(solution)/shard_map/ppermute | solution.py:1177
  123.2 4.6 copy-start.72
  123.6 8.0 copy-start.75
  127.3 85.5 %copy-start.82 = (f32[128]{0:T(128)}, f32[128]{0:T(128)S(1)}, u32[]{:S(2)}) copy-start(f32[128]{0:T(128)S(1)} %add_convert_fusion.3) | copy-start | bytes 1540
  128.3 4.7 copy-start.74
  136.9 235.1 %all-gather.4.cloned.1.call-start = ((), (), s32[]{:S(2)}) async-start(), calls=%async_computation.3 | async-start | bytes 10813440 | tf_op jit(solution)/shard_map/all_gather | solution.py:1329
  149.4 72.6 %copy-start = (bf16[1024,1536]{1,0:T(8,128)(2,1)}, bf16[1024,1536]{1,0:T(8,128)(2,1)S(1)}, u32[]{:S(2)}) copy-start(bf16[1024,1536]{1,0:T(8,128)(2,1)S(1)} %get-tuple-element.261) | copy-start | bytes 9437188
  166.3 44.4 %copy-start.65 = (bf16[176,2048]{1,0:T(8,128)(2,1)S(1)}, bf16[176,2048]{1,0:T(8,128)(2,1)}, u32[]{:S(2)}) copy-start(bf16[176,2048]{1,0:T(8,128)(2,1)} %param.32) | copy-start | bytes 2162692
  166.3 44.4 %copy-start.66 = (bf16[176,2048]{1,0:T(8,128)(2,1)S(1)}, bf16[176,2048]{1,0:T(8,128)(2,1)}, u32[]{:S(2)}) copy-start(bf16[176,2048]{1,0:T(8,128)(2,1)} %param.31) | copy-start | bytes 2162692
  166.3 44.4 %copy-start.67 = (bf16[176,2048]{1,0:T(8,128)(2,1)S(1)}, bf16[176,2048]{1,0:T(8,128)(2,1)}, u32[]{:S(2)}) copy-start(bf16[176,2048]{1,0:T(8,128)(2,1)} %param.33) | copy-start | bytes 2162692
  212.3 441.7 %reduce-scatter.4.cloned.1.call-start = ((), (), s32[]{:S(2)}) async-start(), calls=%async_computation.4 | async-start | bytes 1310720 | tf_op jit(solution)/shard_map/reduce_scatter | solution.py:1172
  212.8 9.2 copy-start.45
  212.9 9.2 copy-start.78
  212.9 24.1 %collective-permute-start.3 = (bf16[4,4,64,512]{3,2,1,0:T(8,128)(2,1)}, bf16[4,4,64,512]{3,2,1,0:T(8,128)(2,1)S(1)}, u32[]{:S(2)}, u32[]{:S(2)}) collective-permute-start(bf16[4,4,64,512]{3,2,1,0:T(8,128)(2,1)} %bitcast.293), channel_id=1, source_target_pairs={{0,1},{1,0},{2,3},{3,2},{4,5},{5,4},{6,7},{7,6},{8,9},{9,8},{10,11... | collective-permute-start | bytes 3145736 | tf_op jit(solution)/shard_map/ppermute | solution.py:1166
  217.3 4.7 copy-start.5
  217.3 4.8 copy-start.9
  217.3 4.8 copy-start.13
  222.1 14.9 %copy-start.22 = (f32[8,128,512]{2,1,0:T(8,128)}, f32[8,128,512]{2,1,0:T(8,128)S(1)}, u32[]{:S(2)}) copy-start(f32[8,128,512]{2,1,0:T(8,128)S(1)} %fusion.46.gate_ref) | copy-start | bytes 6291460
  222.1 15.1 %copy-start.64 = (bf16[16,64,512]{2,1,0:T(8,128)(2,1)S(1)}, bf16[16,64,512]{2,1,0:T(8,128)(2,1)}, u32[]{:S(2)}) copy-start(bf16[16,64,512]{2,1,0:T(8,128)(2,1)} %all-gather.6.cloned.1.call-done) | copy-start | bytes 3145732
  346.3 130.9 %copy-start.20 = (f32[256,2048]{1,0:T(8,128)}, f32[256,2048]{1,0:T(8,128)S(1)}, u32[]{:S(2)}) copy-start(f32[256,2048]{1,0:T(8,128)S(1)} %get-tuple-element.79.hidden) | copy-start | bytes 6291460
  372.1 11.9 %copy-start.84 = (bf16[3,704,2048]{2,1,0:T(8,128)(2,1)S(1)}, bf16[3,704,2048]{2,1,0:T(8,128)(2,1)}, u32[]{:S(2)}) copy-start(bf16[3,704,2048]{2,1,0:T(8,128)(2,1)} %all-gather.4.cloned.1.call-done) | copy-start | bytes 25952260
  372.1 11.9 %copy-start.85 = (bf16[8,256,2048]{2,1,0:T(8,128)(2,1)S(1)}, bf16[8,256,2048]{2,1,0:T(8,128)(2,1)}, u32[]{:S(2)}) copy-start(bf16[8,256,2048]{2,1,0:T(8,128)(2,1)} %get-tuple-element.80) | copy-start | bytes 25165828
  407.7 9.7 %copy-start.87 = (bf16[2048,704]{0,1:T(8,128)(2,1)}, bf16[2048,704]{0,1:T(8,128)(2,1)S(1)}, u32[]{:S(2)}) copy-start(bf16[2048,704]{0,1:T(8,128)(2,1)S(1)} %get-tuple-element.86) | copy-start | bytes 8650756
  407.7 9.7 %copy-start.89 = (bf16[2048,704]{0,1:T(8,128)(2,1)S(1)}, bf16[2048,704]{0,1:T(8,128)(2,1)}, u32[]{:S(2)}) copy-start(bf16[2048,704]{0,1:T(8,128)(2,1)} %get-tuple-element.85) | copy-start | bytes 8650756
  407.7 18.4 %slice-start = ((s8[8388608]{0:T(1024)(128)(4,1)}), s8[4194304]{0:T(1024)(128)(4,1)S(1)}, s32[]{:S(2)}) async-start(s8[8388608]{0:T(1024)(128)(4,1)} %bitcast.311), calls=%async_computation.8 | async-start | bytes 8388608
  417.4 8.7 slice-start.1
  417.4 8.7 copy-start.91
  445.9 5.1 copy-start.59
  445.9 5.8 copy-start.90
  451.0 13.0 %copy-start.88 = (bf16[2048,704]{0,1:T(8,128)(2,1)S(1)}, bf16[2048,704]{0,1:T(8,128)(2,1)}, u32[]{:S(2)}) copy-start(bf16[2048,704]{0,1:T(8,128)(2,1)} %copy-done.87) | copy-start | bytes 8650756
  451.0 123.6 %collective-permute-start.5 = (bf16[1024,2048]{1,0:T(8,128)(2,1)}, bf16[1024,2048]{1,0:T(8,128)(2,1)}, u32[]{:S(2)}, u32[]{:S(2)}) collective-permute-start(bf16[1024,2048]{1,0:T(8,128)(2,1)} %slice.246), channel_id=1, source_target_pairs={{0,8},{8,0},{16,24},{24,16},{1,9},{9,1},{17,25},{25,17},{2,10},{10... | collective-permute-start | bytes 12582920 | tf_op jit(solution)/shard_map/ppermute | solution.py:1177
  464.0 13.3 %copy-start.19 = (f32[256,2048]{1,0:T(8,128)S(1)}, f32[256,2048]{1,0:T(8,128)}, u32[]{:S(2)}) copy-start(f32[256,2048]{1,0:T(8,128)} %get-tuple-element.223.grad_out) | copy-start | bytes 6291460
  477.2 65.6 %copy-start.53 = (bf16[8,128,512]{2,1,0:T(8,128)(2,1)S(1)}, bf16[8,128,512]{2,1,0:T(8,128)(2,1)}, u32[]{:S(2)}) copy-start(bf16[8,128,512]{2,1,0:T(8,128)(2,1)} %copy-done.52) | copy-start | bytes 3145732
  545.6 27.4 %collective-permute-start.4 = (bf16[4,4,64,512]{3,2,0,1:T(8,128)(2,1)S(1)}, bf16[4,4,64,512]{3,2,0,1:T(8,128)(2,1)S(1)}, u32[]{:S(2)}, u32[]{:S(2)}) collective-permute-start(bf16[4,4,64,512]{3,2,0,1:T(8,128)(2,1)S(1)} %select_bitcast_fusion), channel_id=1, source_target_pairs={{0,1},{1,0},{2,3},{3,2},{4,5},{5,4},{6,7},{7,6},{8,9},{9,8},{10,11... | collective-permute-start | bytes 3145736 | tf_op jit(solution)/shard_map/ppermute | solution.py:1166
  549.9 13.6 %copy-start.51 = (bf16[2,4,64,2048]{3,2,1,0:T(8,128)(2,1)S(1)}, bf16[2,4,64,2048]{3,2,1,0:T(8,128)(2,1)}, u32[]{:S(2)}) copy-start(bf16[2,4,64,2048]{3,2,1,0:T(8,128)(2,1)} %copy-done.49) | copy-start | bytes 6291460
  563.4 5.8 copy-start.37
  563.5 5.7 copy-start.39
  563.5 5.7 copy-start.55
  580.0 24.9 %copy-start.56 = (f32[1024,2048]{1,0:T(8,128)}, f32[1024,2048]{1,0:T(8,128)S(1)}, u32[]{:S(2)}) copy-start(f32[1024,2048]{1,0:T(8,128)S(1)} %convert_add_fusion) | copy-start | bytes 25165828
  605.9 5.5 copy-start.68
  605.9 6.5 copy-start.81
  605.9 6.5 copy-start.83
  605.9 6.6 copy-start.1
  607.5 46.5 %collective-permute-start.6 = (bf16[512,2048]{1,0:T(8,128)(2,1)}, bf16[512,2048]{1,0:T(8,128)(2,1)}, u32[]{:S(2)}, u32[]{:S(2)}) collective-permute-start(bf16[512,2048]{1,0:T(8,128)(2,1)} %slice.304), channel_id=1, source_target_pairs={{0,16},{8,24},{16,0},{24,8},{1,17},{9,25},{17,1},{25,9},{2,18},{10... | collective-permute-start | bytes 6291464 | tf_op jit(solution)/shard_map/ppermute | solution.py:1177
  608.2 110.9 %reduce-scatter.6.cloned.1.call-start = ((), (), s32[]{:S(2)}) async-start(), calls=%async_computation.5 | async-start | bytes 1310720 | tf_op jit(solution)/shard_map/reduce_scatter | solution.py:1172
  610.5 38.7 %collective-permute-start.7 = (bf16[256,2048]{1,0:T(8,128)(2,1)}, bf16[256,2048]{1,0:T(8,128)(2,1)}, u32[]{:S(2)}, u32[]{:S(2)}) collective-permute-start(bf16[256,2048]{1,0:T(8,128)(2,1)} %slice.202), channel_id=1, source_target_pairs={{0,1},{1,0},{2,3},{3,2},{4,5},{5,4},{6,7},{7,6},{8,9},{9,8},{10,11... | collective-permute-start | bytes 3145736 | tf_op jit(solution)/shard_map/ppermute | solution.py:1166
  657.0 261.8 %reduce-scatter.8.cloned.1.call-start = ((), (), s32[]{:S(2)}) async-start(), calls=%async_computation.6 | async-start | bytes 10813440 | tf_op jit(solution)/shard_map/reduce_scatter | solution.py:1370
  663.2 6.7 copy-start.71
  665.7 5.2 copy-start.61
  672.1 5.5 copy-start.69
  672.1 9.1 copy-start.48
  675.7 5.5 copy-start.58
  677.0 42.1 %collective-permute-start.8 = (bf16[256,2048]{1,0:T(8,128)(2,1)}, bf16[256,2048]{1,0:T(8,128)(2,1)}, u32[]{:S(2)}, u32[]{:S(2)}) collective-permute-start(bf16[256,2048]{1,0:T(8,128)(2,1)} %slice.305), channel_id=1, source_target_pairs={{0,1},{1,0},{2,3},{3,2},{4,5},{5,4},{6,7},{7,6},{8,9},{9,8},{10,11... | collective-permute-start | bytes 3145736 | tf_op jit(solution)/shard_map/ppermute | solution.py:1166
  677.6 32.2 %collective-permute-start.9 = (bf16[64,512]{1,0:T(8,128)(2,1)S(1)}, bf16[64,512]{1,0:T(8,128)(2,1)S(1)}, u32[]{:S(2)}, u32[]{:S(2)}) collective-permute-start(bf16[64,512]{1,0:T(8,128)(2,1)S(1)} %get-tuple-element.247), channel_id=1, source_target_pairs={{0,24},{8,16},{16,8},{24,0},{1,25},{9,17},{17,9},{25,1},{2,26},{10... | collective-permute-start | bytes 196616 | tf_op jit(solution)/shard_map/ppermute | solution.py:1177
  680.6 29.3 %collective-permute-start.10 = (bf16[64,512]{1,0:T(8,128)(2,1)S(1)}, bf16[64,512]{1,0:T(8,128)(2,1)S(1)}, u32[]{:S(2)}, u32[]{:S(2)}) collective-permute-start(bf16[64,512]{1,0:T(8,128)(2,1)S(1)} %get-tuple-element.246), channel_id=1, source_target_pairs={{0,16},{8,24},{16,0},{24,8},{1,17},{9,25},{17,1},{25,9},{2,18},{10... | collective-permute-start | bytes 196616 | tf_op jit(solution)/shard_map/ppermute | solution.py:1177
  681.2 11.1 %copy-start.57 = (bf16[1024,2048]{1,0:T(8,128)(2,1)S(1)}, bf16[1024,2048]{1,0:T(8,128)(2,1)}, u32[]{:S(2)}) copy-start(bf16[1024,2048]{1,0:T(8,128)(2,1)} %fusion.1) | copy-start | bytes 12582916
  681.2 28.7 %collective-permute-start.11 = (bf16[64,512]{1,0:T(8,128)(2,1)S(1)}, bf16[64,512]{1,0:T(8,128)(2,1)S(1)}, u32[]{:S(2)}, u32[]{:S(2)}) collective-permute-start(bf16[64,512]{1,0:T(8,128)(2,1)S(1)} %get-tuple-element.245), channel_id=1, source_target_pairs={{0,8},{8,0},{16,24},{24,16},{1,9},{9,1},{17,25},{25,17},{2,10},{10... | collective-permute-start | bytes 196616 | tf_op jit(solution)/shard_map/ppermute | solution.py:1177
  710.7 8.4 copy-start.18
  710.7 8.4 copy-start.33
  721.3 194.3 %copy-start.79 = (f32[256]{0:T(256)S(1)}, f32[256]{0:T(256)}, u32[]{:S(2)}) copy-start(f32[256]{0:T(256)} %copy-done.78) | copy-start | bytes 3076
  907.8 7.9 copy-start.21
  (47 other events, 82.8 us)
Sparse Core Ops, SparseCore 0:
  137.1 27.0 all-gather.5
  212.4 159.5 all-gather.3
  608.3 34.1 reduce-scatter.3
  657.1 33.3 reduce-scatter.5
  692.7 205.8 reduce-scatter.7

commit v3 on v2

--- a/solution.py
+++ b/solution.py
@@ -14,7 +14,7 @@
 F32 = jnp.float32
 BF16 = jnp.bfloat16
 LEAF = 8
-VMEM_LIMIT = 40 * 1024 * 1024
+VMEM_LIMIT = 48 * 1024 * 1024
 
 
 def mm(a, b, ca, cb):
@@ -412,17 +412,19 @@
 
 
 def gather_kernel(outer, dp, *refs):
-    mats, refs = refs[:4], refs[4:]
-    tok, small, refs = refs[0], refs[1], refs[2:]
-    three, gate, out_tok, out_small, refs = refs[0], refs[1], refs[2], refs[3], refs[4:]
+    mats, refs = refs[:3], refs[3:]
+    toks, small, w_out, refs = refs[:2], refs[2], refs[3], refs[4:]
+    three, heads, refs = refs[0], refs[1], refs[2:]
+    out_toks, out_small, refs = refs[:2], refs[2], refs[3:]
     (
         local_sem, up_send, up_recv, down_send, down_recv, x_send, x_recv,
-        tok_send, tok_recv, small_send, small_recv,
+        tok_send, tok_recv, small_send, small_recv, head_send, head_recv,
     ) = refs
-    outs = [three.at[0], three.at[1], three.at[2], gate]
+    outs = [three.at[0], three.at[1], three.at[2]]
     seq = 2 * outer
     at = lax.axis_index("seq")
-    me = lax.axis_index("dp") * seq + at
+    d = lax.axis_index("dp")
+    me = d * seq + at
     z = at // 2
     x, y, core = near_partners()
     above, below = {"seq": at + 2}, {"seq": at - 2}
@@ -436,6 +438,20 @@
         )
 
     everyone(seq, dp, lambda r, where: push(r, where).start())
+    head = heads.shape[2]
+
+    def columns(owner):
+        return w_out.at[:, pl.ds(pl.multiple_of(owner * head, head), head)]
+
+    own_head = pltpu.make_async_copy(columns(d), heads.at[d], local_sem.at[5])
+    own_head.start()
+    other_heads = [
+        send(
+            columns(jnp.bitwise_xor(d, r)), heads.at[d], head_send.at[r], head_recv.at[r],
+            {"dp": jnp.bitwise_xor(d, r)},
+        )
+        for r in range(1, dp)
+    ]
 
     def up(m, k, src, origin):
         return pltpu.make_async_remote_copy(
@@ -455,7 +471,7 @@
             recv_sem=x_recv.at[m, origin], device_id=x, device_id_type=pl.DeviceIdType.MESH,
         )
 
-    for m in range(4):
+    for m in range(3):
         @pl.when(has_above)
         def _():
             up(m, 0, mats[m], z).start()
@@ -465,20 +481,25 @@
             down(m, 0, mats[m], z).start()
 
         across(m, mats[m], z).start()
-    tok_y = send(tok, out_tok.at[1], tok_send.at[0], tok_recv.at[0], y)
-    tok_core = send(tok, out_tok.at[2], tok_send.at[1], tok_recv.at[1], core)
+    tok_y, tok_rest = [], []
+    for n, (tok, out_tok) in enumerate(zip(toks, out_toks)):
+        tok_y.append(send(tok, out_tok.at[1], tok_send.at[3 * n], tok_recv.at[3 * n], y))
+        tok_rest.append(
+            send(tok, out_tok.at[2], tok_send.at[3 * n + 1], tok_recv.at[3 * n + 1], core)
+        )
+        copy = pltpu.make_async_copy(tok, out_tok.at[0], local_sem.at[1 + 5 * n])
+        copy.start()
+        tok_rest.append(copy)
     own_small = pltpu.make_async_copy(small, out_small.at[me], local_sem.at[0])
     own_small.start()
-    own_tok = pltpu.make_async_copy(tok, out_tok.at[0], local_sem.at[1])
-    own_tok.start()
     own_mats = []
-    for m in range(4):
+    for m in range(3):
         copy = pltpu.make_async_copy(mats[m], outs[m].at[0, z], local_sem.at[2 + m])
         copy.start()
         own_mats.append(copy)
 
     def pass_on(k, carry):
-        for m in range(4):
+        for m in range(3):
             @pl.when(z - k >= 0)
             def _():
                 slot = outs[m].at[0, z - k]
@@ -504,8 +525,11 @@
         return carry
 
     lax.fori_loop(1, outer, pass_on, 0)
-    tok_y.wait()
-    tok_last = send(out_tok.at[1], out_tok.at[3], tok_send.at[2], tok_recv.at[2], core)
+    for n, out_tok in enumerate(out_toks):
+        tok_y[n].wait()
+        tok_rest.append(
+            send(out_tok.at[1], out_tok.at[3], tok_send.at[3 * n + 2], tok_recv.at[3 * n + 2], core)
+        )
 
     def arrived(r, where):
         push(r, where).wait_send()
@@ -518,7 +542,7 @@
     everyone(seq, dp, arrived)
 
     def complete(o, carry):
-        for m in range(4):
+        for m in range(3):
             across(m, outs[m].at[0, o], o).wait()
 
             @pl.when(has_above & (o <= z))
@@ -534,10 +558,18 @@
     lax.fori_loop(0, outer, complete, 0)
     for copy in own_mats:
         copy.wait()
+    own_head.wait()
+    for r, copy in enumerate(other_heads, 1):
+        copy.wait_send()
+        theirs = heads.at[jnp.bitwise_xor(d, r)]
+        pltpu.make_async_remote_copy(
+            src_ref=theirs, dst_ref=theirs, send_sem=head_send.at[r],
+            recv_sem=head_recv.at[r], device_id={"dp": jnp.bitwise_xor(d, r)},
+            device_id_type=pl.DeviceIdType.MESH,
+        ).wait_recv()
     own_small.wait()
-    own_tok.wait()
-    tok_core.wait()
-    tok_last.wait()
+    for copy in tok_rest:
+        copy.wait()
 
 
 def in_hbm():
@@ -548,29 +580,101 @@
     return pl.BlockSpec(memory_space=pltpu.VMEM)
 
 
-def gather_all(outer, dp, mats, tok, small):
+def gather_all(outer, dp, mats, toks, small, w_out):
     seq = 2 * outer
     rows, width = mats[0].shape
     dma = pltpu.SemaphoreType.DMA
     return pl.pallas_call(
         functools.partial(gather_kernel, outer, dp),
-        in_specs=[in_hbm()] * 6,
-        out_specs=[in_hbm()] * 4,
+        in_specs=[in_vmem()] * 5 + [in_hbm()] * 2,
+        out_specs=[in_hbm()] * 5,
         out_shape=[
             jax.ShapeDtypeStruct((3, 2, outer, rows, width), BF16),
-            jax.ShapeDtypeStruct((2, outer, rows, width), BF16),
-            jax.ShapeDtypeStruct((dp,) + tok.shape, BF16),
+            jax.ShapeDtypeStruct((dp, w_out.shape[0], w_out.shape[1] // dp), BF16),
+            jax.ShapeDtypeStruct((dp,) + toks[0].shape, BF16),
+            jax.ShapeDtypeStruct((dp,) + toks[1].shape, BF16),
             jax.ShapeDtypeStruct((seq * dp,) + small.shape, BF16),
         ],
-        scratch_shapes=[
-            dma((6,)), dma((4, outer)), dma((4, outer)), dma((4, outer)), dma((4, outer)),
-            dma((4, outer)), dma((4, outer)), dma((3,)), dma((3,)), dma((seq * dp,)),
-            dma((seq * dp,)),
-        ],
+        scratch_shapes=[dma((7,))] + [dma((3, outer))] * 6
+        + [dma((6,))] * 2 + [dma((seq * dp,))] * 2 + [dma((dp,))] * 2,
         compiler_params=pltpu.CompilerParams(
             collective_id=1, has_side_effects=True, vmem_limit_bytes=VMEM_LIMIT
         ),
-    )(*mats, tok, small)
+    )(*mats, *toks, small, w_out)
+
+
+def feed_kernel(mid, grad_feed, w_down, w_act, w_lin, product, grad_gate, grad_lin):
+    gate = mm(mid[...], w_act[0], 1, 1)
+    lin = mm(mid[...], w_lin[0], 1, 1)
+    grad_product = mm(grad_feed[...], w_down[0], 1, 1)
+    sigma = jax.nn.sigmoid(gate)
+    swish = gate * sigma
+    product[...] = (swish * lin).astype(BF16)
+    grad_gate[...] = (grad_product * lin * (sigma * (1.0 + gate * (1.0 - sigma)))).astype(BF16)
+    grad_lin[...] = (grad_product * swish).astype(BF16)
+
+
+def feed_back_kernel(
+    product, grad_gate, grad_lin, w_down, w_act, w_lin, feed, grad_mid
+):
+    grad_mid[...] = (
+        mm(grad_gate[...], w_act[0], 1, 0) + mm(grad_lin[...], w_lin[0], 1, 0)
+    ).astype(BF16)
+    feed[...] = mm(product[...], w_down[0], 1, 0).astype(BF16)
+
+
+def grad_in_kernel(grad_pre, grad_gate, grad_logit, w_kqv, w_g, up, down, grad_in, grad_rank):
+    rank = mm(grad_logit[...], up[...], 1, 0).astype(BF16)
+    grad_rank[...] = rank
+    grad_in[...] = (
+        mm(grad_pre[...], w_kqv[...], 1, 0)
+        + (mm(grad_gate[...], w_g[...], 1, 0) + mm(rank, down[...], 1, 1))
+    ).astype(BF16)
+
+
+def grad_in_tiles(tiles, shared, widths):
+    rows = tiles[0].shape[0]
+    step = min(256, rows)
+    return pl.pallas_call(
+        grad_in_kernel,
+        grid=(rows // step,),
+        in_specs=[pl.BlockSpec((step, x.shape[1]), lambda t: (t, 0)) for x in tiles]
+        + [
+            pl.BlockSpec(x.shape, lambda t: (0, 0), pipeline_mode=pl.Buffered(1))
+            for x in shared
+        ],
+        out_specs=[pl.BlockSpec((step, columns), lambda t: (t, 0)) for columns in widths],
+        out_shape=[jax.ShapeDtypeStruct((rows, columns), BF16) for columns in widths],
+        compiler_params=pltpu.CompilerParams(vmem_limit_bytes=VMEM_LIMIT),
+    )(*tiles, *shared)
+
+
+def feed_tiles(kernel, tiles, weights, widths):
+    rows = tiles[0].shape[0]
+    step = min(256, rows)
+    _, units, width = weights.shape
+    each = 2 * step * units * width
+
+    def spec(columns):
+        return pl.BlockSpec((step, columns), lambda t: (t, 0))
+
+    def weight(at):
+        return pl.BlockSpec(
+            (1, units, width), lambda t: (at, 0, 0), pipeline_mode=pl.Buffered(1)
+        )
+
+    return pl.pallas_call(
+        kernel,
+        grid=(rows // step,),
+        in_specs=[spec(x.shape[1]) for x in tiles] + [weight(m) for m in range(3)],
+        out_specs=[spec(columns) for columns in widths],
+        out_shape=[jax.ShapeDtypeStruct((rows, columns), BF16) for columns in widths],
+        cost_estimate=pl.CostEstimate(
+            flops=3 * each * (rows // step), bytes_accessed=6 * units * width + 8 * rows * width,
+            transcendentals=rows * units,
+        ),
+        compiler_params=pltpu.CompilerParams(vmem_limit_bytes=VMEM_LIMIT),
+    )(*tiles, weights, weights, weights)
 
 
 def turned(x):
@@ -585,8 +689,9 @@
 
 def relay_kernel(outer, backward, *refs):
     if backward:
-        totals, keeps, refs = refs[0], refs[1], refs[2:]
-        states, refs = refs[0], refs[1:]
+        totals, keeps, parts, refs = refs[0], refs[1], refs[2], refs[3:]
+        states, sums, refs = refs[0], refs[1], refs[2:]
+        side, refs = refs[-7:], refs[:-7]
     else:
         feats, decays, writes, refs = refs[0], refs[1], refs[2], refs[3:]
         states, keeps, refs = refs[0], refs[1], refs[2:]
@@ -597,13 +702,13 @@
     half = own.shape[0]
     at = lax.axis_index("seq")
     inner, z = at % 2, at // 2
-    x, _, _ = near_partners()
+    x, y, core = near_partners()
     above, below = {"seq": at + 2}, {"seq": at - 2}
     has_above, has_below = z < outer - 1, z > 0
     ahead, has_ahead, has_source = (
         (below, has_below, has_above) if backward else (above, has_above, has_below)
     )
-    barrier = greet([x])
+    barrier = greet([x, y, core] if backward else [x])
 
     @pl.when(has_above)
     def _():
@@ -614,7 +719,8 @@
         greet([below])
 
     pl.semaphore_wait(
-        barrier, 1 + has_above.astype(jnp.int32) + has_below.astype(jnp.int32)
+        barrier,
+        (3 if backward else 1) + has_above.astype(jnp.int32) + has_below.astype(jnp.int32),
     )
 
     def compute(s):
@@ -631,6 +737,8 @@
     for i in range(half):
         to_x[i] = compute((1 - inner) * half + i).astype(BF16)
         crossing.append(send(to_x.at[i], from_x.at[i], x_s.at[i], x_r.at[i], x))
+    if backward:
+        side = plane_sum_start(parts, side, y, core)
     for i in range(half):
         own[i] = compute(inner * half + i)
     if backward:
@@ -690,6 +798,53 @@
         def _():
             along(i).wait_send()
 
+    if backward:
+        plane_sum_end(parts, sums, side)
+
+
+def plane_sum_start(parts, side, y, core):
+    from_core, to_y, from_y, core_s, core_r, y_s, y_r = side
+    rows = parts.shape[1]
+    size = rows // CHUNKS
+    cuts = [pl.ds(c * size, size) for c in range(CHUNKS)]
+    first = [
+        send(parts.at[pl.ds(4, 4), cut], from_core.at[:, cut], core_s.at[c], core_r.at[c], core)
+        for c, cut in enumerate(cuts)
+    ]
+    second = []
+    for c, cut in enumerate(cuts):
+        first[c].wait()
+
+        def add(r, carry, c=c):
+            at = pl.ds(c * size + r * STRIP, STRIP)
+            for j in range(2):
+                to_y[j, at] = (
+                    parts[2 + j, at].astype(F32) + from_core[2 + j, at].astype(F32)
+                ).astype(BF16)
+            return carry
+
+        lax.fori_loop(0, size // STRIP, add, 0)
+        second.append(send(to_y.at[:, cut], from_y.at[:, cut], y_s.at[c], y_r.at[c], y))
+    return from_core, from_y, second
+
+
+def plane_sum_end(parts, sums, side):
+    from_core, from_y, second = side
+    size = parts.shape[1] // CHUNKS
+    for c in range(CHUNKS):
+        second[c].wait()
+
+        def add(r, carry, c=c):
+            at = pl.ds(c * size + r * STRIP, STRIP)
+            for j in range(2):
+                sums[j, at] = (
+                    parts[j, at].astype(F32) + from_core[j, at].astype(F32)
+                    + from_y[j, at].astype(F32)
+                ).astype(BF16)
+            return carry
+
+        lax.fori_loop(0, size // STRIP, add, 0)
+
 
 def relay(outer, backward, inputs, sequences, slots, width):
     half = sequences // 2
@@ -698,13 +853,21 @@
     states = jax.ShapeDtypeStruct((sequences, slots, width), BF16)
     keeps = jax.ShapeDtypeStruct((2, sequences, slots), F32)
     keep = pltpu.VMEM((sequences, 1, slots), F32)
+    second, side = keeps, []
+    if backward:
+        rows, columns = inputs[2].shape[1:]
+        second = jax.ShapeDtypeStruct((2, rows, columns), BF16)
+        side = [
+            pltpu.VMEM((4, rows, columns), BF16), pltpu.VMEM((2, rows, columns), BF16),
+            pltpu.VMEM((2, rows, columns), BF16),
+        ] + [dma((CHUNKS,))] * 4
     return pl.pallas_call(
         functools.partial(relay_kernel, outer, backward),
         in_specs=[in_vmem()] * len(inputs),
-        out_specs=in_vmem() if backward else [in_vmem()] * 2,
-        out_shape=states if backward else [states, keeps],
+        out_specs=[in_vmem()] * 2,
+        out_shape=[states, second],
         scratch_shapes=[pltpu.VMEM((half, slots, width), F32)] + [held] * 6 + [keep] * 2
-        + [dma((half,))] * 6 + [dma((1,))] * 2,
+        + [dma((half,))] * 6 + [dma((1,))] * 2 + side,
         compiler_params=pltpu.CompilerParams(
             collective_id=7 if backward else 6, has_side_effects=True,
             vmem_limit_bytes=VMEM_LIMIT,
@@ -715,7 +878,7 @@
 def middle_kernel(
     parts, tok, gain, extra, hidden, mid, extra_all, from_core, to_y, from_y, normed,
     core_s, core_r, y_s, y_r, local_sem, gx_s, gx_r, gy_s, gy_r, gd_s, gd_r,
-    ex_s, ex_r, ey_s, ey_r, ed_s, ed_r, extra_sem, gc_s, gc_r, ec_s, ec_r,
+    ex_s, ex_r, ed_s, ed_r, extra_sem, gc_s, gc_r, ec_s, ec_r,
 ):
     rows = tok.shape[0]
     size = rows // CHUNKS
@@ -738,14 +901,14 @@
         lax.fori_loop(0, size // STRIP, add, 0)
         second.append(send(to_y.at[cut], from_y.at[cut], y_s.at[c], y_r.at[c], y))
     rest = []
-    own_extra = pltpu.make_async_copy(extra, extra_all.at[0], extra_sem.at[0])
-    own_extra.start()
-    rest.append(own_extra)
+    for j in range(4):
+        copy = pltpu.make_async_copy(extra.at[j], extra_all.at[2 * j], extra_sem.at[j])
+        copy.start()
+        rest.append(copy)
     extra_x = [
-        send(extra.at[cut], extra_all.at[1, cut], ex_s.at[c], ex_r.at[c], x)
+        send(extra.at[0, cut], extra_all.at[1, cut], ex_s.at[c], ex_r.at[c], x)
         for c, cut in enumerate(cuts)
     ]
-    rest.append(send(extra, extra_all.at[4], ec_s.at[0], ec_r.at[0], core))
     over_x, over_y, diagonal = [], [], []
     for c in range(CHUNKS + 2):
         if c < CHUNKS:
@@ -774,10 +937,6 @@
             over_y[at].wait()
             diagonal.append(send(mid.at[2, cut], mid.at[3, cut], gd_s.at[at], gd_r.at[at], x))
             rest.append(send(mid.at[2, cut], mid.at[6, cut], gc_s.at[2, at], gc_r.at[2, at], core))
-    extra_y = [
-        send(extra.at[cut], extra_all.at[2, cut], ey_s.at[c], ey_r.at[c], y)
-        for c, cut in enumerate(cuts)
-    ]
     extra_d = []
     for c, cut in enumerate(cuts):
         extra_x[c].wait()
@@ -786,15 +945,13 @@
         )
         over_x[c].wait()
         rest.append(send(mid.at[1, cut], mid.at[5, cut], gc_s.at[1, c], gc_r.at[1, c], core))
-    rest.append(send(extra_all.at[1], extra_all.at[5], ec_s.at[1], ec_r.at[1], core))
+    rest.append(send(extra_all.at[1], extra_all.at[5], ec_s.at[0], ec_r.at[0], core))
     for c, cut in enumerate(cuts):
         diagonal[c].wait()
         rest.append(send(mid.at[3, cut], mid.at[7, cut], gc_s.at[3, c], gc_r.at[3, c], core))
-    for copy in extra_y + extra_d:
+    for copy in extra_d:
         copy.wait()
-    rest.append(
-        send(extra_all.at[pl.ds(2, 2)], extra_all.at[pl.ds(6, 2)], ec_s.at[2], ec_r.at[2], core)
-    )
+    rest.append(send(extra_all.at[3], extra_all.at[7], ec_s.at[1], ec_r.at[1], core))
     for copy in rest:
         copy.wait()
 
@@ -805,7 +962,7 @@
     buffer = pltpu.VMEM((rows, width), BF16)
     return pl.pallas_call(
         middle_kernel,
-        in_specs=[in_vmem()] * 3 + [in_hbm()],
+        in_specs=[in_vmem()] * 4,
         out_specs=[in_vmem(), in_hbm(), in_hbm()],
         out_shape=[
             jax.ShapeDtypeStruct((rows, width), F32),
@@ -813,10 +970,10 @@
             jax.ShapeDtypeStruct((8, rows, width), BF16),
         ],
         scratch_shapes=[pltpu.VMEM((2, rows, width), BF16), buffer, buffer, buffer]
-        + [dma((CHUNKS,))] * 17
-        + [dma((1,))]
+        + [dma((CHUNKS,))] * 15
+        + [dma((4,))]
         + [dma((4, CHUNKS))] * 2
-        + [dma((3,))] * 2,
+        + [dma((2,))] * 2,
         compiler_params=pltpu.CompilerParams(
             collective_id=2, has_side_effects=True, vmem_limit_bytes=VMEM_LIMIT
         ),
@@ -934,7 +1091,7 @@
     )(parts, hidden, grad_out, gain)
 
 
-def final_kernel(outer, dp, mats, parts, tok, base, gain, small, *refs):
+def final_kernel(outer, dp, mats, gates, parts, tok, base, gain, small, *refs):
     out, tokens_grad, out_small, refs = refs[0], refs[1], refs[2], refs[3:]
     (
         from_x, from_below, from_above, total, from_core, to_y, from_y, gain_grad,
@@ -1011,17 +1168,20 @@
 
     def reduce_block(i, carry):
         b = block_of(i)
-        for m in range(3):
-            across(m, b).wait()
-
-            def strip_sum(r, carry, m=m):
-                strip = pl.ds(r * STRIP, STRIP)
-                total[m, b, strip] = (
-                    mats[m, 0, b, strip].astype(F32) + from_x[m, b, strip].astype(F32)
-                ).astype(BF16)
-                return carry
-
-            lax.fori_loop(0, high // STRIP, strip_sum, 0)
+        for m in (3, 0, 1, 2):
+            if m == 3:
+                total[m, b] = gates[b]
+            else:
+                across(m, b).wait()
+
+                def strip_sum(r, carry, m=m):
+                    strip = pl.ds(r * STRIP, STRIP)
+                    total[m, b, strip] = (
+                        mats[m, 0, b, strip].astype(F32) + from_x[m, b, strip].astype(F32)
+                    ).astype(BF16)
+                    return carry
+
+                lax.fori_loop(0, high // STRIP, strip_sum, 0)
 
             @pl.when(b > z)
             def _():
@@ -1092,7 +1252,7 @@
         out_small[...] += from_all[r]
 
     everyone(seq, dp, add_small)
-    for m in range(3):
+    for m in range(4):
         out[m] = total[m, z].astype(F32)
 
         @pl.when(has_below)
@@ -1106,7 +1266,7 @@
             out[m] += from_above[m, z].astype(F32)
 
     def sent(b, carry):
-        for m in range(3):
+        for m in range(4):
             @pl.when(b > z)
             def _():
                 up(m, b).wait_send()
@@ -1120,20 +1280,20 @@
     lax.fori_loop(0, outer, sent, 0)
 
 
-def finish(outer, dp, mats, parts, tok, base, gain, small):
+def finish(outer, dp, mats, gates, parts, tok, base, gain, small):
     rows, width = tok.shape
     high = mats.shape[3]
     devices = 2 * outer * dp
     dma = pltpu.SemaphoreType.DMA
-    blocks = pltpu.VMEM((3, outer, high, width), BF16)
+    blocks = pltpu.VMEM((4, outer, high, width), BF16)
     buffer = pltpu.VMEM((rows, width), BF16)
     payload = (small.shape[1] + 8, 128)
     return pl.pallas_call(
         functools.partial(final_kernel, outer, dp),
-        in_specs=[in_vmem()] * 6,
+        in_specs=[in_vmem()] * 7,
         out_specs=[in_vmem()] * 3,
         out_shape=[
-            jax.ShapeDtypeStruct((3, high, width), F32),
+            jax.ShapeDtypeStruct((4, high, width), F32),
             jax.ShapeDtypeStruct((rows, width), F32),
             jax.ShapeDtypeStruct(payload, F32),
         ],
@@ -1142,13 +1302,13 @@
             pltpu.VMEM((2, rows, width), BF16), buffer, buffer, pltpu.VMEM((1, width), F32),
             pltpu.VMEM((devices,) + payload, F32), pltpu.VMEM((devices,) + payload, F32),
         ]
-        + [dma((3, outer))] * 6
+        + [dma((4, outer))] * 6
         + [dma((CHUNKS,))] * 4
         + [dma((devices,))] * 2,
         compiler_params=pltpu.CompilerParams(
             collective_id=4, has_side_effects=True, vmem_limit_bytes=VMEM_LIMIT
         ),
-    )(mats, parts, tok, base, gain, small)
+    )(mats, gates, parts, tok, base, gain, small)
 
 
 class Lanes:
@@ -1175,10 +1335,6 @@
 
     def swap_dp(self, x, bit):
         return lax.ppermute(x, "dp", [(i, i ^ bit) for i in range(self.dp)])
-
-    def fold(self, x, swap):
-        half = x.shape[0] // 2
-        return x[:half] + swap(x[half:].astype(BF16)).astype(F32)
 
     def swap_seq(self, x, bit):
         return lax.ppermute(x, "seq", [(i, i ^ bit) for i in range(self.seq)])
@@ -1236,12 +1392,28 @@
     padded = -(-used // 2048) * 2048
     small = jnp.concatenate(small_parts + [jnp.zeros((padded - used,), BF16)])
     own_tokens = tokens.reshape(rows, width)
-    w_kqv, w_g, plane_tokens, smalls = gather_all(
-        lanes.outer, lanes.dp, [w_key, w_query, w_value, w_gate], own_tokens,
-        small.reshape(-1, 128),
+    position = (lanes.at * piece + jnp.arange(piece)).astype(F32)
+    alive_own = (position[None, :] < counts[:, None]).astype(F32).reshape(rows, 1)
+    grad_out = cotangent.reshape(rows, width).astype(F32) * alive_own
+    w_kqv, out_mine, plane_tokens, grad_feed, smalls = gather_all(
+        lanes.outer, lanes.dp, [w_key, w_query, w_value], [own_tokens, grad_out.astype(BF16)],
+        small.reshape(-1, 128), w_out,
     )
     w_kqv = w_kqv.reshape(3 * head_width, width)
-    w_g = w_g.reshape(head_width, width)
+    out_rows = w_out.shape[0]
+    out_own, out_other = lanes.pick(
+        out_mine.reshape(lanes.dp, out_rows, lanes.outer, 2, -1), 3
+    )
+    out_mine = jnp.concatenate(
+        [
+            out_own.reshape(lanes.dp, out_rows, half_width),
+            out_other.reshape(lanes.dp, out_rows, half_width),
+        ],
+        axis=2,
+    )
+    gate_and_out = lanes.gather_outer(
+        jnp.concatenate([w_gate, out_mine.reshape(out_rows, width)], axis=0)
+    )
     smalls = smalls.reshape(devices, padded)
     cuts, offset = [], 0
     for size in sizes:
@@ -1264,8 +1436,6 @@
     all_lengths = cuts[6].astype(F32) * 256.0 + cuts[7].astype(F32)
     all_lengths = all_lengths.reshape(lanes.dp, lanes.seq, seq_count)[:, 0]
 
-    position = (lanes.at * piece + jnp.arange(piece)).astype(F32)
-    alive_own = (position[None, :] < counts[:, None]).astype(F32).reshape(rows, 1)
     group_lengths = jnp.concatenate(
         [
             lax.dynamic_index_in_dim(
@@ -1276,21 +1446,8 @@
     )
     alive = (position[None, :] < group_lengths[:, None]).astype(F32).reshape(all_rows, 1)
 
-    w_out, smalls = lax.optimization_barrier((w_out, smalls))
-    out_rows = w_out.shape[0]
-    out_split = w_out.reshape(out_rows, lanes.dp, lanes.outer, 2, -1)
-    out_own, out_other = lanes.pick(out_split, 3)
-    out_local = jnp.concatenate(
-        [
-            out_own.reshape(out_rows, lanes.dp, half_width),
-            out_other.reshape(out_rows, lanes.dp, half_width),
-        ],
-        axis=2,
-    )
-    out_mine = lanes.exchange_heads(out_local.transpose(1, 0, 2))
     sources = plane_tokens.reshape(all_rows, width).astype(F32)
     normed_in = (sources * rms_scale(sources) * mixer_full).astype(BF16)
-    grad_out = cotangent.reshape(rows, width).astype(F32) * alive_own
 
     pre = contract_last(normed_in, w_kqv)
     low_rank = mm(normed_in, down_full, 1, 0).astype(BF16)
@@ -1312,25 +1469,28 @@
     def shaped(like_rows, columns, kind):
         return jax.ShapeDtypeStruct((sequences, like_rows, columns), kind)
 
-    out_own = lanes.gather_outer(out_mine[None])
-    out_own, feats = lax.optimization_barrier((out_own, feats))
+    gate_and_out, feats = lax.optimization_barrier((gate_and_out, feats))
     keys, queries, values = (feats, 0), (feats, 1), (feats, 2)
     state_in, keeps = relay(
         lanes.outer, False, [feats, decays, writes], sequences, SLOTS, 2 * head_width
     )
+    feed = jnp.stack([w_down, w_act, w_lin])
+    feed, state_in, gate_and_out = lax.optimization_barrier((feed, state_in, gate_and_out))
+    feed = lax.all_gather(
+        feed, "seq", axis=1, tiled=True, axis_index_groups=lanes.groups
+    )
+    gate_and_out = gate_and_out.reshape(lanes.outer, 2, out_rows, width)
+    gate_own, out_own = gate_and_out[:, 0], gate_and_out[:, 1]
+    gate_other = lanes.swap_inner(gate_own)
+    w_g = jnp.concatenate([gate_own, gate_other], axis=0).reshape(head_width, width)
     gates = seqs(contract_last(normed_in, w_g))
+    out_own = out_own.reshape(lanes.outer, lanes.dp, out_rows, head_width)
     out_other = swap_halves(lanes.swap_inner(out_own), 1)
     even = lanes.inner_at == 0
     natural = jnp.stack(
         [jnp.where(even, out_own, out_other), jnp.where(even, out_other, out_own)], axis=2
     )
     out_full = natural.transpose(1, 0, 2, 3, 4).reshape(width, head_width)
-    w_down, w_act, w_lin, state_in = lax.optimization_barrier((w_down, w_act, w_lin, state_in))
-    feed = lax.all_gather(
-        jnp.stack([w_down, w_act, w_lin]), "seq", axis=1, tiled=True,
-        axis_index_groups=lanes.groups,
-    )
-    down, act, lin = feed[0], feed[1], feed[2]
     mixed, slot_out, attend = per_sequence(
         forward_kernel,
         [queries, keys, values, gates, decays, writes, state_in],
@@ -1344,21 +1504,15 @@
     mixed_flat = flat(mixed)
     parts = contract_last(mixed_flat, out_full).astype(BF16)
     hidden, normed_mid, grad_feed = middle(
-        parts.reshape(4, rows, width), own_tokens, feed_full, grad_out.astype(BF16)
+        parts.reshape(4, rows, width), own_tokens, feed_full, grad_feed
     )
     normed_mid = normed_mid.reshape(8 * rows, width)
     grad_feed = grad_feed.reshape(8 * rows, width)
 
-    grad_product = contract_last(grad_feed, down)
-    gate_part = contract_last(normed_mid, act)
-    lin_part = contract_last(normed_mid, lin)
-    sigma = jax.nn.sigmoid(gate_part)
-    swish = gate_part * sigma
-    product = (swish * lin_part).astype(BF16)
-    grad_gate = (
-        grad_product * lin_part * (sigma * (1.0 + gate_part * (1.0 - sigma)))
-    ).astype(BF16)
-    grad_lin = (grad_product * swish).astype(BF16)
+    units = feed.shape[1]
+    product, grad_gate, grad_lin = feed_tiles(
+        feed_kernel, [normed_mid, grad_feed], feed, [units] * 3
+    )
     feed_grads = jnp.stack(
         [
             contract_first(product, grad_feed).astype(BF16),
@@ -1366,15 +1520,20 @@
             contract_first(grad_lin, normed_mid).astype(BF16),
         ]
     )
-    grad_gate, grad_lin, feed_grads = lax.optimization_barrier((grad_gate, grad_lin, feed_grads))
+    product, grad_gate, grad_lin, feed_grads = lax.optimization_barrier(
+        (product, grad_gate, grad_lin, feed_grads)
+    )
     feed_grads = lax.psum_scatter(
         feed_grads, "seq", scatter_dimension=1, tiled=True, axis_index_groups=lanes.groups
     )
-    mid_parts = (mm(grad_gate, act, 1, 0) + mm(grad_lin, lin, 1, 0)).astype(BF16)
+    feed_parts, mid_parts = feed_tiles(
+        feed_back_kernel, [product, grad_gate, grad_lin], feed, [width] * 2
+    )
     grad_hidden, feed_gain_part, grad_attn = middle_back(
         mid_parts.reshape(8, rows, width), hidden, grad_out, feed_full
     )
     grad_attn = grad_attn.reshape(all_rows, width)
+    feed_parts, grad_attn = lax.optimization_barrier((feed_parts, grad_attn))
 
     grad_mixed = mm(grad_attn, out_full, 1, 0)
     grad_gate_pre, grad_slot, grad_scores, adjoint, head_parts = per_sequence(
@@ -1396,17 +1555,17 @@
     got = swap_halves(lanes.swap_inner(other_part), 1)
     out_sum = (own_part.astype(F32) + got.astype(F32)).astype(BF16).transpose(1, 0, 2, 3)
     gate_grad = contract_first(grad_gate_flat, normed_in).astype(BF16)
-    gate_in = mm(grad_gate_flat, w_g, 1, 0)
-    feed_parts = mm(product, down, 1, 0).astype(BF16)
-    feed_parts = lanes.fold(feed_parts, lambda p: lanes.swap_dp(p, 1))
-    adjoint, out_sum, gate_grad, gate_in, feed_parts = lax.optimization_barrier(
-        (adjoint, out_sum, gate_grad, gate_in, feed_parts)
-    )
-    feed_got = lanes.swap_dp(feed_parts[2 * rows :].astype(BF16), 2)
-    adjoint_in = relay(
-        lanes.outer, True, [adjoint, keeps], sequences, SLOTS, 2 * head_width
-    )
-    gate_grad, out_sum, adjoint_in = lax.optimization_barrier((gate_grad, out_sum, adjoint_in))
+    adjoint, out_sum, gate_grad, feed_parts = lax.optimization_barrier(
+        (adjoint, out_sum, gate_grad, feed_parts)
+    )
+    adjoint_in, feed_sums = relay(
+        lanes.outer, True, [adjoint, keeps, feed_parts.reshape(8, rows, width)], sequences,
+        SLOTS, 2 * head_width,
+    )
+    feed_got = lanes.swap_inner(feed_sums[1])
+    gate_grad, out_sum, adjoint_in, feed_grads = lax.optimization_barrier(
+        (gate_grad, out_sum, adjoint_in, feed_grads)
+    )
     out_mine = lanes.scatter_outer(out_sum.reshape(-1, head_width))
     gate_got = lanes.swap_inner(gate_grad[half_width:])
     grad_pre, grad_logit = per_sequence(
@@ -1417,21 +1576,18 @@
         ],
         [shaped(piece, 3 * head_width, BF16), shaped(piece, SLOTS, BF16)],
     )
+    grad_pre, gate_got, out_mine = lax.optimization_barrier(
+        (flat(grad_pre), gate_got, out_mine)
+    )
+    gate_sum = (gate_grad[:half_width].astype(F32) + gate_got.astype(F32)).astype(BF16)
     grad_logit = flat(grad_logit)
     bias_part = jnp.sum(grad_logit.astype(F32), axis=0)
     up_part = contract_first(grad_logit, low_rank)
-    grad_rank = mm(grad_logit, up_mine, 1, 0).astype(BF16)
+    grad_in, grad_rank = grad_in_tiles(
+        [grad_pre, grad_gate_flat, grad_logit], [w_kqv, w_g, up_mine, down_full], [width, rank]
+    )
     down_part = contract_first(normed_in, grad_rank)
 
-    grad_pre, feed_got, gate_got, out_mine = lax.optimization_barrier(
-        (flat(grad_pre), feed_got, gate_got, out_mine)
-    )
-    gate_sum = (gate_grad[:half_width].astype(F32) + gate_got.astype(F32)).astype(BF16)
-    gate_sum, grad_pre = lax.optimization_barrier((gate_sum, grad_pre))
-    gate_sum = lanes.scatter_outer(gate_sum)
-    feed_parts = feed_parts[: 2 * rows] + feed_got.astype(F32)
-    feed_got = lanes.swap_inner(feed_parts[rows:].astype(BF16))
-    grad_in = mm(grad_pre, w_kqv, 1, 0) + gate_in + contract_last(grad_rank, down_full)
     mixer_grads = contract_first(grad_pre, normed_in).astype(BF16)
     mixer_grads = mixer_grads.reshape(3, 2, lanes.outer, -1, width)
 
@@ -1452,22 +1608,20 @@
     padded = -(-sum(sizes) // 1024) * 1024
     parts.append(jnp.zeros((devices, padded - sum(sizes)), F32))
     small_parts = jnp.concatenate(parts, axis=1).reshape(devices, -1, 128)
-    grad_in, mixer_grads, feed_got, gate_sum = lax.optimization_barrier(
-        (grad_in.astype(BF16), mixer_grads, feed_got, gate_sum)
-    )
-    w_gate_grad = gate_sum.astype(F32)
+    grad_in, mixer_grads, feed_got = lax.optimization_barrier((grad_in, mixer_grads, feed_got))
     out_mine = out_mine.reshape(lanes.dp, out_rows, head_width)
     out_mine = lanes.exchange_heads(out_mine).transpose(1, 0, 2)
     out_mine = out_mine.reshape(out_rows, lanes.dp, 2, lanes.outer, -1)
     low_half, high_half = lanes.pick(out_mine, 2)
     w_out_grad = jnp.stack([low_half, high_half], axis=3).reshape(out_rows, width).astype(F32)
-    feed_sum = feed_parts[:rows] + feed_got.astype(F32)
+    feed_sum = feed_sums[0].astype(F32) + feed_got.astype(F32)
     block_out = (alive_own * (hidden + feed_sum)).astype(BF16)
     weight_grads, tokens_grad, reduced = finish(
-        lanes.outer, lanes.dp, mixer_grads, grad_in.reshape(4, rows, width), own_tokens,
+        lanes.outer, lanes.dp, mixer_grads,
+        gate_sum.reshape(lanes.outer, -1, width), grad_in.reshape(4, rows, width), own_tokens,
         grad_hidden, mixer_full, small_parts,
     )
-    w_key_grad, w_query_grad, w_value_grad = weight_grads[0], weight_grads[1], weight_grads[2]
+    w_key_grad, w_query_grad, w_value_grad, w_gate_grad = [weight_grads[m] for m in range(4)]
     tokens_grad = tokens_grad.reshape(seq_count, piece, width)
     mixer_gain_grad = reduced[padded // 128, : width // devices]
     reduced = reduced.reshape(-1)

time: 935 us -> 819 us (0.88)
  matrix products: 157 us -> 72.9 us
  waiting for transfers between devices: 46 us -> 69.4 us
  local copies, waits for them, and re-layouts: 70.2 us -> 49 us
  Pallas kernels: 575 us -> 555 us
  other arithmetic: 56.7 us -> 38.6 us
    dot_general x24 -> x14, matrix products: 157 us -> 72.9 us  [mm(): lax.dot_general(a.astype(BF16), b.astype(BF16), (((ca,), (cb,)), ((), ())...]
    pallas_call x1, Pallas kernels: 184 us -> 109 us  [finish(): pl.pallas_call(functools.partial(final_kernel, outer, dp), in_specs=[in_v...]
    ppermute x4 -> x5, waiting for transfers between devices: 0.01 us -> 51.9 us  [swap_inner(): return lax.ppermute(x, 'seq', [(i, i ^ 1) for i in range(self.seq)])]
    pallas_call x1 -> x4, Pallas kernels: 105 us -> 156 us  [the longest x1 86.9 us: middle(): pl.pallas_call(middle_kernel, in_specs=[in_vmem()] * 4, out_specs=[in_vme...]
    all_gather x1, waiting for transfers between devices: 25.7 us -> 0.01 us  [per_device(): lax.all_gather(feed, 'seq', axis=1, tiled=True, axis_index_groups=lanes.g...]
    pallas_call x2, Pallas kernels: 68.3 us -> 91.8 us  [relay(): pl.pallas_call(functools.partial(relay_kernel, outer, backward), in_specs...]
    pallas_call x1, Pallas kernels: 97.1 us -> 75 us  [gather_all(): pl.pallas_call(functools.partial(gather_kernel, outer, dp), in_specs=[in_...]
    unnamed x197 -> x143, local copies, waits for them, and re-layouts: 35.6 us -> 20.7 us
  transfers between devices with their start and end apart: 17 -> 12, of which waited for: 3 -> 5; matrix products, arithmetic and copies ran while one was open for 16% -> 12% of each run, Pallas kernels for 44% -> 38%
where the time goes in v3:
time: 819 us; the launch traced here: 807 us
  Pallas kernels  555 us (68%)
  matrix products  72.9 us (9%)
  waiting for transfers between devices  69.4 us (8%)
  local copies, waits for them, and re-layouts  49 us (6%)
  other arithmetic  38.6 us (5%)
  between operations  15.3 us (2%)
    pallas_call x1, Pallas kernels, finish(): pl.pallas_call(functools.partial(final_kernel, outer, dp), in_specs=[in_v...  109 us
    pallas_call x2, Pallas kernels, relay(): pl.pallas_call(functools.partial(relay_kernel, outer, backward), in_specs...  91.8 us
    pallas_call x1, Pallas kernels, middle(): pl.pallas_call(middle_kernel, in_specs=[in_vmem()] * 4, out_specs=[in_vme...  86.9 us
    pallas_call x1, Pallas kernels, gather_all(): pl.pallas_call(functools.partial(gather_kernel, outer, dp), in_specs=[in_...  75 us
    dot_general x14, matrix products, mm(): lax.dot_general(a.astype(BF16), b.astype(BF16), (((ca,), (cb,)), ((), ())...  72.9 us
    pallas_call x1, Pallas kernels, middle_back(): pl.pallas_call(middle_back_kernel, in_specs=[in_vmem()] * 4, out_specs=[i...  66.3 us
    pallas_call x3, Pallas kernels, per_sequence(): pl.pallas_call(kernel, grid=(count,), in_specs=[spec(x.shape, at) for x,...  57 us
    pallas_call x2, Pallas kernels, feed_tiles(): pl.pallas_call(kernel, grid=(rows // step,), in_specs=[spec(x.shape[1]) f...  53.8 us
  transfers between devices with their start and end apart: 12, of which 5 were waited for; matrix products, arithmetic and copies ran while one was open for 12% of the time, Pallas kernels for 38%

profile of v3, /device:TPU:21, one launch (start us, length us, event | category | flops | bytes accessed | tf_op | source)
XLA Modules:
  0.0 807.2 jit_solution(3836220120752300206)
XLA Ops:
  10.5 2.8 convert_multiply_fusion
  13.5 75.0 %shard_map.288 = (bf16[3,2,4,64,2048]{4,3,2,1,0:T(8,128)(2,1)}, bf16[4,64,512]{2,1,0:T(8,128)(2,1)S(1)}, bf16[4,256,2048]{2,1,0:T(8,128)(2,1)}, bf16[4,256,2048]{2,1,0:T(8,128)(2,1)}, bf16[32,16,128]{2,1,0:T(8,128)(2,1)S(1)}) custom-call(bf16[64,2048]{1,0:T(8,128)(2,1)S(1)} %copy-done.33, bf16[64,2048]{1,0:T(8,128)(2,1)S(1)} %copy-done.34, ...), custom_call_target="tpu_custom_call" | custom-call | tf_op jit(solution)/shard_map/pallas_call | solution.py:587
  91.9 3.1 multiply_reduce_fusion
  96.2 3.4 multiply_convert_fusion
  99.7 1.2 convolution_convert_fusion.7
  101.8 1.0 exponential-minus-one_negate_fusion
  102.8 1.0 copy.90
  103.8 1.0 copy.91
  104.8 1.6 pad_maximum_fusion.1
  106.4 12.4 %fusion.2 = (bf16[1024,1536]{1,0:T(8,128)(2,1)S(1)}, f32[1024,1536]{1,0:T(8,128)}) fusion(pred[1536]{0:T(1024)(128)(4,1)S(1)} %iota_compare_fusion, bf16[1024,2048]{1,0:T(8,128)(2,1)} %bitcast.249, bf16[1536,2048]{1,0:T(8,128)(2,1)} %bitcast.258), kind=kOutput, calls=%fused_computation.8 | convolution fusion | flops 6451888128 | bytes 19924480 | tf_op jit(solution)/shard_map/dot_general | solution.py:21
  118.8 17.3 %all-gather.3.cloned.1.call-done = bf16[512,2048]{1,0:T(8,128)(2,1)} async-done(((bf16[128,2048]{1,0:T(8,128)(2,1)}), bf16[512,2048]{1,0:T(8,128)(2,1)}) %all-gather.3.cloned.1.call-update) | async-done | bytes 2097168 | tf_op jit(solution)/shard_map/all_gather | solution.py:1329
  136.1 1.0 copy-done.1
  137.2 1.0 copy-done.3
  138.2 33.7 %shard_map.289 = (bf16[8,64,1024]{2,1,0:T(8,128)(2,1)S(1)}, f32[2,8,64]{2,1,0:T(8,128)S(1)}) custom-call(bf16[8,128,1536]{2,1,0:T(8,128)(2,1)S(1)} %bitcast.212, f32[8,128,64]{2,1,0:T(8,128)S(1)} %bitcast.221, f32[8,128,64]{2,1,0:T(8,128)S(1)} %bitcast.225), custom_call_target="tpu_custom_call" | custom-call | tf_op jit(solution)/shard_map/pallas_call | solution.py:864
  173.0 2.7 slice_bitcast_fusion.2
  175.7 1.4 reshape_squeeze.6
  177.6 1.0 collective-permute-start
  179.6 18.8 %collective-permute-done.1 = bf16[4,4,64,512]{3,2,1,0:T(8,128)(2,1)S(1)} collective-permute-done((bf16[4,4,64,512]{3,2,1,0:T(8,128)(2,1)}, bf16[4,4,64,512]{3,2,1,0:T(8,128)(2,1)S(1)}, u32[]{:S(2)}, u32[]{:S(2)}) %collective-permute-start.1) | collective-permute-done | bytes 1048608 | tf_op jit(solution)/shard_map/ppermute | solution.py:1326
  199.5 21.5 %collective-permute-done = bf16[4,64,2048]{2,1,0:T(8,128)(2,1)} collective-permute-done((bf16[4,64,2048]{2,1,0:T(8,128)(2,1)}, bf16[4,64,2048]{2,1,0:T(8,128)(2,1)}, u32[]{:S(2)}, u32[]{:S(2)}) %collective-permute-start) | collective-permute-done | bytes 1048608 | tf_op jit(solution)/shard_map/ppermute | solution.py:1326
  221.1 1.7 pad_maximum_fusion.2
  222.8 3.7 fusion.30.gate_ref
  226.6 1.4 copy-done.9
  227.9 15.9 %shard_map.290 = (bf16[8,128,512]{2,1,0:T(8,128)(2,1)S(1)}, f32[8,128,512]{2,1,0:T(8,128)S(1)}, f32[8,128,64]{2,1,0:T(8,128)S(1)}) custom-call(bf16[8,128,1536]{2,1,0:T(8,128)(2,1)} %bitcast.213, bf16[8,128,1536]{2,1,0:T(8,128)(2,1)} %bitcast.214, bf16[8,128,1536]{2,1,0:T(8,128)(2,1)} %bitcast.215, f32[8,128,512]{2,1,0:T(8,128)} %fusion.30.gate_ref, ...), custom_call_target="tpu_custom_call" | custom-call | tf_op jit(solution)/shard_map/pallas_call | solution.py:346
  243.9 4.3 convolution_convert_fusion.1
  248.2 86.9 %shard_map.291 = (f32[256,2048]{1,0:T(8,128)S(1)}, bf16[8,256,2048]{2,1,0:T(8,128)(2,1)}, bf16[8,256,2048]{2,1,0:T(8,128)(2,1)}) custom-call(bf16[4,256,2048]{2,1,0:T(8,128)(2,1)} %bitcast.263, bf16[256,2048]{1,0:T(8,128)(2,1)S(1)} %bitcast.230, f32[1,2048]{1,0:T(1,128)S(1)} %reshape.734.gain, bf16[4,256,2048]{2,1,0:T(8,128)(2,1)} %get-tuple-element.86.extra), custom_call_target="tpu_custom_call" | custom-call | tf_op jit(solution)/shard_map/pallas_call | solution.py:963
  335.2 1.3 copy-done.11
  336.5 27.0 %shard_map.292 = (bf16[2048,704]{1,0:T(8,128)(2,1)S(1)}, bf16[2048,704]{1,0:T(8,128)(2,1)}, bf16[2048,704]{1,0:T(8,128)(2,1)}) custom-call(bf16[2048,2048]{1,0:T(8,128)(2,1)} %bitcast.289, bf16[2048,2048]{1,0:T(8,128)(2,1)} %bitcast.285, bf16[3,704,2048]{2,1,0:T(8,128)(2,1)} %all-gather.5.cloned.1.call-done.w_down.w_act.w_lin, ...), custom_call_target="tpu_custom_call" | custom-call | flops 17716740096 | bytes 42205184 | tf_op jit(solution)/shard_map/pallas_call | solution.py:666
  363.5 11.4 %fusion.5 = bf16[1,704,2048]{2,1,0:T(8,128)(2,1)S(1)} fusion(bf16[2048,704]{1,0:T(8,128)(2,1)} %get-tuple-element.96.grad_lin, bf16[2048,2048]{1,0:T(8,128)(2,1)} %bitcast.290), kind=kOutput, calls=%fused_computation.17 | convolution fusion | flops 5907021824 | bytes 14155776 | tf_op jit(solution)/shard_map/dot_general | solution.py:21
  374.9 6.5 fusion.4
  381.5 6.5 fusion.3
  388.0 3.9 pad_maximum_fusion
  392.1 1.9 copy.97
  395.1 5.3 fusion.1
  400.4 26.9 %shard_map.293 = (bf16[2048,2048]{1,0:T(8,128)(2,1)}, bf16[2048,2048]{1,0:T(8,128)(2,1)}) custom-call(bf16[2048,704]{1,0:T(8,128)(2,1)S(1)} %copy-done.40, bf16[2048,704]{1,0:T(8,128)(2,1)} %get-tuple-element.95.grad_gate, bf16[2048,704]{1,0:T(8,128)(2,1)} %get-tuple-element.96.grad_lin, ...), custom_call_target="tpu_custom_call" | custom-call | flops 17716740096 | bytes 42205184 | tf_op jit(solution)/shard_map/pallas_call | solution.py:666
  427.3 66.3 %shard_map.294 = (f32[256,2048]{1,0:T(8,128)S(1)}, f32[1,2048]{1,0:T(1,128)S(1)}, bf16[4,256,2048]{2,1,0:T(8,128)(2,1)}) custom-call(bf16[8,256,2048]{2,1,0:T(8,128)(2,1)} %bitcast.255, f32[256,2048]{1,0:T(8,128)S(1)} %copy-done.12, f32[256,2048]{1,0:T(8,128)} %get-tuple-element.219.grad_out, f32[1,2048]{1,0:T(1,128)S(1)} %reshape.734.gain), custom_call_target="tpu_custom_call" | custom-call | tf_op jit(solution)/shard_map/pallas_call | solution.py:1076
  493.6 5.4 convolution_convert_fusion.6
  499.0 1.1 select_bitcast_fusion
  501.7 3.7 fusion.31.grad_mixed_ref
  505.4 14.3 %shard_map.295 = (bf16[8,128,512]{2,1,0:T(8,128)(2,1)S(1)}, bf16[8,128,512]{2,1,0:T(8,128)(2,1)S(1)}, f32[8,128,64]{2,1,0:T(8,128)S(1)}, f32[8,64,1024]{2,1,0:T(8,128)}, f32[8,1,512]{2,1,0:T(1,128)S(1)}) custom-call(f32[8,128,512]{2,1,0:T(8,128)} %fusion.31.grad_mixed_ref, f32[8,128,512]{2,1,0:T(8,128)} %fusion.30.gate_ref, f32[8,128,512]{2,1,0:T(8,128)} %copy-done.24, ...), custom_call_target="tpu_custom_call" | custom-call | tf_op jit(solution)/shard_map/pallas_call | solution.py:346
  520.6 1.0 copy-done.29
  522.5 6.4 convolution_convert_fusion.5
  528.9 1.4 fusion.26
  530.3 1.4 fusion.10
  531.8 58.2 %shard_map.296 = (bf16[8,64,1024]{2,1,0:T(8,128)(2,1)S(1)}, bf16[2,256,2048]{2,1,0:T(8,128)(2,1)S(1)}) custom-call(f32[8,64,1024]{2,1,0:T(8,128)S(1)} %copy-done.25, f32[2,8,64]{2,1,0:T(8,128)S(1)} %get-tuple-element.107.refs_1_, bf16[8,256,2048]{2,1,0:T(8,128)(2,1)} %bitcast.254), custom_call_target="tpu_custom_call" | custom-call | tf_op jit(solution)/shard_map/pallas_call | solution.py:864
  590.0 1.3 copy-done.22
  592.3 2.3 copy.99
  596.2 2.5 slice_bitcast_fusion.4
  599.0 2.3 slice.184
  601.4 1.0 collective-permute-start.3
  602.4 26.9 %shard_map.297 = (bf16[8,128,1536]{2,1,0:T(8,128)(2,1)}, bf16[8,128,64]{2,1,0:T(8,128)(2,1)S(1)}) custom-call(bf16[8,128,512]{2,1,0:T(8,128)(2,1)S(1)} %copy-done.27, f32[8,128,64]{2,1,0:T(8,128)S(1)} %copy-done.32, f32[8,128,64]{2,1,0:T(8,128)S(1)} %copy-done.18, bf16[8,128,1536]{2,1,0:T(8,128)(2,1)} %bitcast.218, bf16[8,128,1536]{2,1,0:T(8,128)(2,1)} %bitcast.219, ...), custom_call_target="tpu_custom_call" | custom-call | tf_op jit(solution)/shard_map/pallas_call | solution.py:346
  630.0 3.9 bitcast_convert_fusion
  633.9 11.5 %collective-permute-done.3 = bf16[256,2048]{1,0:T(8,128)(2,1)} collective-permute-done((bf16[256,2048]{1,0:T(8,128)(2,1)}, bf16[256,2048]{1,0:T(8,128)(2,1)}, u32[]{:S(2)}, u32[]{:S(2)}) %collective-permute-start.3) | collective-permute-done | bytes 1048608 | tf_op jit(solution)/shard_map/ppermute | solution.py:1326
  645.4 1.0 copy-done.15
  646.4 1.2 copy-done.30
  647.7 15.0 %shard_map.298 = (bf16[1024,2048]{1,0:T(8,128)(2,1)}, bf16[1024,16]{1,0:T(8,128)(2,1)S(1)}) custom-call(bf16[1024,1536]{1,0:T(8,128)(2,1)} %bitcast.264, bf16[1024,512]{1,0:T(8,128)(2,1)S(1)} %bitcast.240, bf16[1024,64]{1,0:T(8,128)(2,1)S(1)} %bitcast.236, bf16[1536,2048]{1,0:T(8,128)(2,1)} %bitcast.259, bf16[512,2048]{1,0:T(8,128)(2,1)S(1)} %bitcast.233, ...), custom_call_target="tpu_custom_call" | custom-call | tf_op jit(solution)/shard_map/pallas_call | solution.py:638
  662.7 8.9 %convolution_convert_fusion = bf16[1536,2048]{1,0:T(8,128)(2,1)} fusion(bf16[1024,1536]{1,0:T(8,128)(2,1)S(1)} %bitcast.265, bf16[1024,2048]{1,0:T(8,128)(2,1)S(1)} %copy-done.43), kind=kOutput, calls=%fused_computation.7 | convolution fusion | flops 6445596672 | bytes 13631488 | tf_op jit(solution)/shard_map/dot_general | solution.py:21
  671.6 2.9 fusion.8
  674.5 1.6 add_convert_fusion
  676.1 1.3 fusion.32
  678.3 108.6 %shard_map.299 = (f32[4,64,2048]{2,1,0:T(8,128)S(1)}, f32[256,2048]{1,0:T(8,128)}, f32[24,128]{1,0:T(8,128)S(1)}) custom-call(bf16[3,2,4,64,2048]{4,3,2,1,0:T(8,128)(2,1)} %bitcast.260, bf16[4,64,2048]{2,1,0:T(8,128)(2,1)S(1)} %bitcast.234, bf16[4,256,2048]{2,1,0:T(8,128)(2,1)} %bitcast.261, bf16[256,2048]{1,0:T(8,128)(2,1)S(1)} %bitcast.231, ...), custom_call_target="tpu_custom_call" | custom-call | tf_op jit(solution)/shard_map/pallas_call | solution.py:1291
  787.0 1.4 slice_bitcast_fusion.7
  788.3 3.0 collective-permute-start.5
  797.2 1.8 reshape.739
  798.9 1.3 copy.132
  (239 shorter events, 27.3 us)
Async XLA Ops:
  7.2 6.1 copy-start.58
  7.2 6.1 copy-start.59
  7.2 6.1 copy-start.60
  7.2 6.1 copy-start.61
  7.2 6.2 copy-start.33
  7.2 6.2 copy-start.34
  7.2 6.2 copy-start.35
  7.3 6.2 copy-start.7
  7.3 6.2 copy-start.36
  7.3 128.9 %all-gather.3.cloned.1.call-start = ((), (), s32[]{:S(2)}) async-start(), calls=%async_computation.2 | async-start | bytes 2621440 | tf_op jit(solution)/shard_map/all_gather | solution.py:1329
  10.5 2.8 copy-start.56
  91.3 245.2 %all-gather.5.cloned.1.call-start = ((), (), s32[]{:S(2)}) async-start(), calls=%async_computation.3 | async-start | bytes 10813440 | tf_op jit(solution)/shard_map/all_gather | solution.py:1479
  96.2 3.4 copy-start.14
  99.6 5.2 copy-start.51
  99.6 5.2 copy-start.52
  99.7 5.2 copy-start.53
  118.8 54.1 %copy-start = (bf16[1024,1536]{1,0:T(8,128)(2,1)}, bf16[1024,1536]{1,0:T(8,128)(2,1)S(1)}, u32[]{:S(2)}) copy-start(bf16[1024,1536]{1,0:T(8,128)(2,1)S(1)} %get-tuple-element.250) | copy-start | bytes 9437188
  172.9 419.3 %reduce-scatter.3.cloned.1.call-start = ((), (), s32[]{:S(2)}) async-start(), calls=%async_computation.4 | async-start | bytes 10813440 | tf_op jit(solution)/shard_map/reduce_scatter | solution.py:1526
  177.1 21.4 %collective-permute-start.1 = (bf16[4,4,64,512]{3,2,1,0:T(8,128)(2,1)}, bf16[4,4,64,512]{3,2,1,0:T(8,128)(2,1)S(1)}, u32[]{:S(2)}, u32[]{:S(2)}) collective-permute-start(bf16[4,4,64,512]{3,2,1,0:T(8,128)(2,1)} %reshape_squeeze.6), channel_id=1, source_target_pairs={{0,1},{1,0},{2,3},{3,2},{4,5},{5,4},{6,7},{7,6},{8,9},{9,8},{10,11... | collective-permute-start | bytes 3145736 | tf_op jit(solution)/shard_map/ppermute | solution.py:1326
  177.6 43.5 %collective-permute-start = (bf16[4,64,2048]{2,1,0:T(8,128)(2,1)}, bf16[4,64,2048]{2,1,0:T(8,128)(2,1)}, u32[]{:S(2)}, u32[]{:S(2)}) collective-permute-start(bf16[4,64,2048]{2,1,0:T(8,128)(2,1)} %get-tuple-element.218), channel_id=1, source_target_pairs={{0,1},{1,0},{2,3},{3,2},{4,5},{5,4},{6,7},{7,6},{8,9},{9,8},{10,11... | collective-permute-start | bytes 3145736 | tf_op jit(solution)/shard_map/ppermute | solution.py:1326
  199.5 44.4 %copy-start.48 = (bf16[4,4,2,64,512]{4,3,2,1,0:T(8,128)(2,1)}, bf16[4,4,2,64,512]{4,3,2,1,0:T(8,128)(2,1)S(1)}, u32[]{:S(2)}) copy-start(bf16[4,4,2,64,512]{4,3,2,1,0:T(8,128)(2,1)S(1)} %copy.94) | copy-start | bytes 6291460
  199.5 23.3 %copy-start.42 = (bf16[4,256,2048]{2,1,0:T(8,128)(2,1)S(1)}, bf16[4,256,2048]{2,1,0:T(8,128)(2,1)}, u32[]{:S(2)}) copy-start(bf16[4,256,2048]{2,1,0:T(8,128)(2,1)} %copy-done.41) | copy-start | bytes 12582916
  222.8 5.1 copy-start.2
  222.8 5.1 copy-start.4
  222.8 5.1 copy-start.6
  243.8 4.4 copy-start.16
  243.8 4.4 copy-start.24
  243.8 4.4 copy-start.37
  243.9 4.3 copy-start.8
  363.5 18.0 %copy-start.39 = (bf16[2048,704]{1,0:T(8,128)(2,1)}, bf16[2048,704]{1,0:T(8,128)(2,1)S(1)}, u32[]{:S(2)}) copy-start(bf16[2048,704]{1,0:T(8,128)(2,1)S(1)} %get-tuple-element.94.product) | copy-start | bytes 8650756
  363.5 11.4 %copy-start.62 = (bf16[8,256,2048]{2,1,0:T(8,128)(2,1)S(1)}, bf16[8,256,2048]{2,1,0:T(8,128)(2,1)}, u32[]{:S(2)}) copy-start(bf16[8,256,2048]{2,1,0:T(8,128)(2,1)} %get-tuple-element.88) | copy-start | bytes 25165828
  363.5 11.4 %copy-start.64 = (bf16[2048,704]{1,0:T(8,128)(2,1)S(1)}, bf16[2048,704]{1,0:T(8,128)(2,1)}, u32[]{:S(2)}) copy-start(bf16[2048,704]{1,0:T(8,128)(2,1)} %get-tuple-element.95.grad_gate) | copy-start | bytes 8650756
  363.5 18.0 %slice-start = ((s8[8388608]{0:T(1024)(128)(4,1)}), s8[4194304]{0:T(1024)(128)(4,1)S(1)}, s32[]{:S(2)}) async-start(s8[8388608]{0:T(1024)(128)(4,1)} %bitcast.286), calls=%async_computation.6 | async-start | bytes 8388608
  374.9 6.6 slice-start.1
  391.9 253.4 %reduce-scatter.5.cloned.1.call-start = ((), (), s32[]{:S(2)}) async-start(), calls=%async_computation.5 | async-start | bytes 1310720 | tf_op jit(solution)/shard_map/reduce_scatter | solution.py:1332
  395.1 5.3 copy-start.40
  400.4 26.9 %copy-start.12 = (f32[256,2048]{1,0:T(8,128)S(1)}, f32[256,2048]{1,0:T(8,128)}, u32[]{:S(2)}) copy-start(f32[256,2048]{1,0:T(8,128)} %copy-done.11) | copy-start | bytes 6291460
  427.3 66.3 %copy-start.38 = (bf16[8,128,512]{2,1,0:T(8,128)(2,1)S(1)}, bf16[8,128,512]{2,1,0:T(8,128)(2,1)}, u32[]{:S(2)}) copy-start(bf16[8,128,512]{2,1,0:T(8,128)(2,1)} %copy-done.37) | copy-start | bytes 3145732
  493.6 5.4 copy-start.21
  493.6 7.4 copy-start.63
  499.0 6.4 copy-start.44
  499.0 2.7 copy-start.49
  500.1 28.8 %collective-permute-start.2 = (bf16[4,4,64,512]{3,2,1,0:T(8,128)(2,1)}, bf16[4,4,64,512]{3,2,1,0:T(8,128)(2,1)}, u32[]{:S(2)}, u32[]{:S(2)}) collective-permute-start(bf16[4,4,64,512]{3,2,1,0:T(8,128)(2,1)} %select_bitcast_fusion), channel_id=1, source_target_pairs={{0,1},{1,0},{2,3},{3,2},{4,5},{5,4},{6,7},{7,6},{8,9},{9,8},{10,11... | collective-permute-start | bytes 3145736 | tf_op jit(solution)/shard_map/ppermute | solution.py:1326
  501.7 3.7 copy-start.17
  522.5 7.8 copy-start.45
  528.9 2.9 copy-start.25
  596.1 6.3 copy-start.18
  596.1 6.3 copy-start.19
  596.1 6.3 copy-start.20
  596.1 6.3 copy-start.27
  596.1 6.3 copy-start.32
  598.6 73.0 %collective-permute-start.4 = (bf16[256,2048]{1,0:T(8,128)(2,1)}, bf16[256,2048]{1,0:T(8,128)(2,1)}, u32[]{:S(2)}, u32[]{:S(2)}) collective-permute-start(bf16[256,2048]{1,0:T(8,128)(2,1)} %slice_bitcast_fusion.4), channel_id=1, source_target_pairs={{0,1},{1,0},{2,3},{3,2},{4,5},{5,4},{6,7},{7,6},{8,9},{9,8},{10,11... | collective-permute-start | bytes 3145736 | tf_op jit(solution)/shard_map/ppermute | solution.py:1326
  601.4 44.0 %collective-permute-start.3 = (bf16[256,2048]{1,0:T(8,128)(2,1)}, bf16[256,2048]{1,0:T(8,128)(2,1)}, u32[]{:S(2)}, u32[]{:S(2)}) collective-permute-start(bf16[256,2048]{1,0:T(8,128)(2,1)} %slice.184), channel_id=1, source_target_pairs={{0,1},{1,0},{2,3},{3,2},{4,5},{5,4},{6,7},{7,6},{8,9},{9,8},{10,11... | collective-permute-start | bytes 3145736 | tf_op jit(solution)/shard_map/ppermute | solution.py:1326
  630.0 15.4 %copy-start.10 = (bf16[8,64,2048]{2,1,0:T(8,128)(2,1)S(1)}, bf16[8,64,2048]{2,1,0:T(8,128)(2,1)}, u32[]{:S(2)}) copy-start(bf16[8,64,2048]{2,1,0:T(8,128)(2,1)} %copy-done.9) | copy-start | bytes 6291460
  647.7 15.0 %copy-start.43 = (bf16[1024,2048]{1,0:T(8,128)(2,1)S(1)}, bf16[1024,2048]{1,0:T(8,128)(2,1)}, u32[]{:S(2)}) copy-start(bf16[1024,2048]{1,0:T(8,128)(2,1)} %fusion.1) | copy-start | bytes 12582916
  647.7 15.0 %copy-start.46 = (bf16[8,128,1536]{2,1,0:T(8,128)(2,1)S(1)}, bf16[8,128,1536]{2,1,0:T(8,128)(2,1)}, u32[]{:S(2)}) copy-start(bf16[8,128,1536]{2,1,0:T(8,128)(2,1)} %get-tuple-element.117) | copy-start | bytes 9437188
  662.7 9.0 %copy-start.13 = (f32[256,2048]{1,0:T(8,128)S(1)}, f32[256,2048]{1,0:T(8,128)}, u32[]{:S(2)}) copy-start(f32[256,2048]{1,0:T(8,128)} %copy-done.11) | copy-start | bytes 6291460
  662.7 9.0 %copy-start.23 = (bf16[2,256,2048]{2,1,0:T(8,128)(2,1)S(1)}, bf16[2,256,2048]{2,1,0:T(8,128)(2,1)}, u32[]{:S(2)}) copy-start(bf16[2,256,2048]{2,1,0:T(8,128)(2,1)} %copy-done.22) | copy-start | bytes 6291460
  662.7 9.0 %copy-start.57 = (f32[256]{0:T(256)S(1)}, f32[256]{0:T(256)}, u32[]{:S(2)}) copy-start(f32[256]{0:T(256)} %copy-done.56) | copy-start | bytes 3076
  671.6 2.9 copy-start.47
  788.3 7.1 collective-permute-start.5
  791.4 4.2 collective-permute-start.6
  791.8 3.8 collective-permute-start.7
  796.1 2.8 copy-start.50
  (15 other events, 18.6 us)
Sparse Core Ops, SparseCore 0:
  91.5 44.6 all-gather.2
  173.0 159.0 all-gather.4
  392.1 153.7 reduce-scatter.2
  594.7 25.9 reduce-scatter.4

commit v4 on v3

--- a/solution.py
+++ b/solution.py
@@ -623,32 +623,6 @@
     feed[...] = mm(product[...], w_down[0], 1, 0).astype(BF16)
 
 
-def grad_in_kernel(grad_pre, grad_gate, grad_logit, w_kqv, w_g, up, down, grad_in, grad_rank):
-    rank = mm(grad_logit[...], up[...], 1, 0).astype(BF16)
-    grad_rank[...] = rank
-    grad_in[...] = (
-        mm(grad_pre[...], w_kqv[...], 1, 0)
-        + (mm(grad_gate[...], w_g[...], 1, 0) + mm(rank, down[...], 1, 1))
-    ).astype(BF16)
-
-
-def grad_in_tiles(tiles, shared, widths):
-    rows = tiles[0].shape[0]
-    step = min(256, rows)
-    return pl.pallas_call(
-        grad_in_kernel,
-        grid=(rows // step,),
-        in_specs=[pl.BlockSpec((step, x.shape[1]), lambda t: (t, 0)) for x in tiles]
-        + [
-            pl.BlockSpec(x.shape, lambda t: (0, 0), pipeline_mode=pl.Buffered(1))
-            for x in shared
-        ],
-        out_specs=[pl.BlockSpec((step, columns), lambda t: (t, 0)) for columns in widths],
-        out_shape=[jax.ShapeDtypeStruct((rows, columns), BF16) for columns in widths],
-        compiler_params=pltpu.CompilerParams(vmem_limit_bytes=VMEM_LIMIT),
-    )(*tiles, *shared)
-
-
 def feed_tiles(kernel, tiles, weights, widths):
     rows = tiles[0].shape[0]
     step = min(256, rows)
@@ -689,9 +663,10 @@
 
 def relay_kernel(outer, backward, *refs):
     if backward:
-        totals, keeps, parts, refs = refs[0], refs[1], refs[2], refs[3:]
-        states, sums, refs = refs[0], refs[1], refs[2:]
-        side, refs = refs[-7:], refs[:-7]
+        totals, keeps, parts, gate_sent, refs = refs[0], refs[1], refs[2], refs[3], refs[4:]
+        states, sums, gate_got, refs = refs[0], refs[1], refs[2], refs[3:]
+        gate_s, gate_r = refs[-2:]
+        side, refs = refs[-9:-2], refs[:-9]
     else:
         feats, decays, writes, refs = refs[0], refs[1], refs[2], refs[3:]
         states, keeps, refs = refs[0], refs[1], refs[2:]
@@ -738,6 +713,7 @@
         to_x[i] = compute((1 - inner) * half + i).astype(BF16)
         crossing.append(send(to_x.at[i], from_x.at[i], x_s.at[i], x_r.at[i], x))
     if backward:
+        gate_copy = send(gate_sent, gate_got, gate_s.at[0], gate_r.at[0], x)
         side = plane_sum_start(parts, side, y, core)
     for i in range(half):
         own[i] = compute(inner * half + i)
@@ -800,6 +776,7 @@
 
     if backward:
         plane_sum_end(parts, sums, side)
+        gate_copy.wait()
 
 
 def plane_sum_start(parts, side, y, core):
@@ -815,15 +792,8 @@
     for c, cut in enumerate(cuts):
         first[c].wait()
 
-        def add(r, carry, c=c):
-            at = pl.ds(c * size + r * STRIP, STRIP)
-            for j in range(2):
-                to_y[j, at] = (
-                    parts[2 + j, at].astype(F32) + from_core[2 + j, at].astype(F32)
-                ).astype(BF16)
-            return carry
-
-        lax.fori_loop(0, size // STRIP, add, 0)
+        for j in range(2):
+            to_y[j, cut] = parts[2 + j, cut] + from_core[2 + j, cut]
         second.append(send(to_y.at[:, cut], from_y.at[:, cut], y_s.at[c], y_r.at[c], y))
     return from_core, from_y, second
 
@@ -853,19 +823,20 @@
     states = jax.ShapeDtypeStruct((sequences, slots, width), BF16)
     keeps = jax.ShapeDtypeStruct((2, sequences, slots), F32)
     keep = pltpu.VMEM((sequences, 1, slots), F32)
-    second, side = keeps, []
+    outs, side = [states, keeps], []
     if backward:
         rows, columns = inputs[2].shape[1:]
-        second = jax.ShapeDtypeStruct((2, rows, columns), BF16)
+        outs = [states, jax.ShapeDtypeStruct((2, rows, columns), BF16)]
+        outs.append(jax.ShapeDtypeStruct(inputs[3].shape, BF16))
         side = [
             pltpu.VMEM((4, rows, columns), BF16), pltpu.VMEM((2, rows, columns), BF16),
             pltpu.VMEM((2, rows, columns), BF16),
-        ] + [dma((CHUNKS,))] * 4
+        ] + [dma((CHUNKS,))] * 4 + [dma((1,))] * 2
     return pl.pallas_call(
         functools.partial(relay_kernel, outer, backward),
-        in_specs=[in_vmem()] * len(inputs),
-        out_specs=[in_vmem()] * 2,
-        out_shape=[states, second],
+        in_specs=[in_vmem()] * 3 + [in_hbm()] * (len(inputs) - 3),
+        out_specs=[in_vmem()] * 2 + [in_hbm()] * (len(outs) - 2),
+        out_shape=outs,
         scratch_shapes=[pltpu.VMEM((half, slots, width), F32)] + [held] * 6 + [keep] * 2
         + [dma((half,))] * 6 + [dma((1,))] * 2 + side,
         compiler_params=pltpu.CompilerParams(
@@ -893,12 +864,7 @@
     for c, cut in enumerate(cuts):
         first[c].wait()
 
-        def add(r, carry, c=c):
-            at = pl.ds(c * size + r * STRIP, STRIP)
-            to_y[at] = (parts[1, at].astype(F32) + from_core[1, at].astype(F32)).astype(BF16)
-            return carry
-
-        lax.fori_loop(0, size // STRIP, add, 0)
+        to_y[cut] = parts[1, cut] + from_core[1, cut]
         second.append(send(to_y.at[cut], from_y.at[cut], y_s.at[c], y_r.at[c], y))
     rest = []
     for j in range(4):
@@ -998,16 +964,8 @@
     for c, cut in enumerate(cuts):
         first[c].wait()
 
-        def add_core(r, carry, c=c):
-            at = pl.ds(c * size + r * STRIP, STRIP)
-            for j in range(2):
-                g = 2 * j + 1
-                to_x[j, at] = (
-                    parts[g, at].astype(F32) + from_core[g, at].astype(F32)
-                ).astype(BF16)
-            return carry
-
-        lax.fori_loop(0, size // STRIP, add_core, 0)
+        for j in range(2):
+            to_x[j, cut] = parts[2 * j + 1, cut] + from_core[2 * j + 1, cut]
         second.append(send(to_x.at[:, cut], from_x.at[:, cut], x_s.at[c], x_r.at[c], x))
     gain_grad[...] = jnp.zeros_like(gain_grad)
     pending, over_y = [], []
@@ -1091,12 +1049,17 @@
     )(parts, hidden, grad_out, gain)
 
 
-def final_kernel(outer, dp, mats, gates, parts, tok, base, gain, small, *refs):
-    out, tokens_grad, out_small, refs = refs[0], refs[1], refs[2], refs[3:]
+def final_kernel(
+    outer, dp, mats, gates, feed_sums, pre_hbm, gate_hbm, kqv_hbm, g_hbm, grad_rank, w_rank, tok,
+    base, gain, small, *refs,
+):
+    out, tokens_grad, out_small, feed_got, refs = refs[0], refs[1], refs[2], refs[3], refs[4:]
     (
-        from_x, from_below, from_above, total, from_core, to_y, from_y, gain_grad,
+        grad_pre, grad_gate, w_kqv, w_g,
+        from_x, from_below, from_above, total, parts, from_core, to_y, from_y, gain_grad,
         to_all, from_all,
-        x_s, x_r, up_s, up_r, down_s, down_r, core_s, core_r, y_s, y_r, all_s, all_r,
+        load, x_s, x_r, up_s, up_r, down_s, down_r, core_s, core_r, y_s, y_r, feed_s, feed_r,
+        all_s, all_r,
     ) = refs
     rows, width = tok.shape
     size = rows // CHUNKS
@@ -1109,14 +1072,14 @@
     above, below = {"seq": at + 2}, {"seq": at - 2}
     has_above, has_below = z < outer - 1, z > 0
     greet_everyone(seq, dp)
-    cuts = [pl.ds(c * size, size) for c in range(CHUNKS)]
-    first = [
-        send(parts.at[pl.ds(2, 2), cut], from_core.at[:, cut], core_s.at[c], core_r.at[c], core)
-        for c, cut in enumerate(cuts)
-    ]
 
     def block_of(i):
-        return jnp.where(i % 2 == 0, outer - 1 - i // 2, i // 2)
+        ups = outer - 1 - z
+        up_at = jnp.where(z < outer // 2, i, i - z)
+        down_at = jnp.where(z < outer // 2, i - ups, i)
+        is_up = (up_at >= 0) & (up_at < ups)
+        block = jnp.where(is_up, outer - 1 - up_at, down_at)
+        return jnp.where(i == outer - 1, z, block)
 
     def across(m, b):
         return pltpu.make_async_remote_copy(
@@ -1142,74 +1105,54 @@
         return carry
 
     lax.fori_loop(0, outer, start_x, 0)
-    second = []
-    for c, cut in enumerate(cuts):
-        first[c].wait()
-
-        def add(r, carry, c=c):
-            strip = pl.ds(c * size + r * STRIP, STRIP)
-            to_y[strip] = (
-                parts[1, strip].astype(F32) + from_core[1, strip].astype(F32)
-            ).astype(BF16)
-            return carry
-
-        lax.fori_loop(0, size // STRIP, add, 0)
-        second.append(send(to_y.at[cut], from_y.at[cut], y_s.at[c], y_r.at[c], y))
-
-    def add_into(m, b, other):
-        def strip_sum(r, carry):
-            strip = pl.ds(r * STRIP, STRIP)
-            total[m, b, strip] = (
-                total[m, b, strip].astype(F32) + other[m, b, strip].astype(F32)
-            ).astype(BF16)
-            return carry
-
-        lax.fori_loop(0, high // STRIP, strip_sum, 0)
-
-    def reduce_block(i, carry):
-        b = block_of(i)
-        for m in (3, 0, 1, 2):
-            if m == 3:
-                total[m, b] = gates[b]
-            else:
-                across(m, b).wait()
-
-                def strip_sum(r, carry, m=m):
-                    strip = pl.ds(r * STRIP, STRIP)
-                    total[m, b, strip] = (
-                        mats[m, 0, b, strip].astype(F32) + from_x[m, b, strip].astype(F32)
-                    ).astype(BF16)
-                    return carry
-
-                lax.fori_loop(0, high // STRIP, strip_sum, 0)
-
-            @pl.when(b > z)
-            def _():
-                @pl.when(has_below)
-                def _():
-                    up(m, b).wait_recv()
-                    add_into(m, b, from_below)
-
-                up(m, b).start()
-
-            @pl.when(b < z)
-            def _():
-                @pl.when(has_above)
-                def _():
-                    down(m, b).wait_recv()
-                    add_into(m, b, from_above)
-
-                down(m, b).start()
-
-        return carry
-
-    lax.fori_loop(0, outer // 2, reduce_block, 0)
+    last_x = send(feed_sums.at[1], feed_got, feed_s.at[0], feed_r.at[0], x)
+    operands = [
+        pltpu.make_async_copy(src, dst, load.at[4 + n])
+        for n, (src, dst) in enumerate(
+            [(pre_hbm, grad_pre), (gate_hbm, grad_gate), (kqv_hbm, w_kqv), (g_hbm, w_g)]
+        )
+    ]
+    loads = [
+        pltpu.make_async_copy(mats.at[m, 0] if m < 3 else gates, total.at[m], load.at[m])
+        for m in range(4)
+    ]
+    for copy in operands + loads:
+        copy.start()
+    for copy in operands:
+        copy.wait()
+
+    def grad_in(g):
+        some = pl.ds(g * rows, rows)
+        parts[g] = (
+            mm(grad_pre[some], w_kqv[...], 1, 0)
+            + (mm(grad_gate[some], w_g[...], 1, 0) + mm(grad_rank[some], w_rank[...], 1, 1))
+        ).astype(BF16)
+
+    grad_in(3)
+    first = send(parts.at[3], from_core.at[1], core_s.at[1], core_r.at[1], core)
+    grad_in(1)
+    first.wait()
+
+    to_y[...] = parts[1] + from_core[1]
+
+    def over_y():
+        return pltpu.make_async_remote_copy(
+            src_ref=to_y, dst_ref=from_y, send_sem=y_s.at[0], recv_sem=y_r.at[0], device_id=y,
+            device_id_type=pl.DeviceIdType.MESH,
+        )
+
+    over_y().start()
+    grad_in(2)
+    first = send(parts.at[2], from_core.at[0], core_s.at[0], core_r.at[0], core)
+    grad_in(0)
+    first.wait()
     gain_grad[...] = jnp.zeros_like(gain_grad)
-    for c in range(CHUNKS):
-        second[c].wait()
-
-        def back(r, carry, c=c):
-            strip = pl.ds(c * size + r * STRIP, STRIP)
+    for copy in loads:
+        copy.wait()
+
+    def back(c):
+        def strip_back(r, carry):
+            strip = pl.ds(pl.multiple_of(c * size + r * STRIP, STRIP), STRIP)
             grad = (
                 parts[0, strip].astype(F32) + from_core[0, strip].astype(F32)
             ) + from_y[strip].astype(F32)
@@ -1223,7 +1166,51 @@
             )
             return carry
 
-        lax.fori_loop(0, size // STRIP, back, 0)
+        lax.fori_loop(0, size // STRIP, strip_back, 0)
+
+    def add_into(m, b, other):
+        total[m, b] = total[m, b] + other[m, b]
+
+    def reduce_block(i, carry):
+        b = block_of(i)
+        for m in (3, 0, 1, 2):
+            if m < 3:
+                across(m, b).wait()
+                add_into(m, b, from_x)
+
+            @pl.when(b > z)
+            def _():
+                @pl.when(has_below)
+                def _():
+                    up(m, b).wait_recv()
+                    add_into(m, b, from_below)
+
+                up(m, b).start()
+
+            @pl.when(b < z)
+            def _():
+                @pl.when(has_above)
+                def _():
+                    down(m, b).wait_recv()
+                    add_into(m, b, from_above)
+
+                down(m, b).start()
+
+            if m < 3:
+                turn = 2 * (3 * (i - 1) + m)
+                if m == 0:
+                    @pl.when(i == 1)
+                    def _():
+                        over_y().wait()
+
+                @pl.when((turn >= 0) & (turn < CHUNKS))
+                def _():
+                    back(turn)
+                    back(turn + 1)
+
+        return carry
+
+    lax.fori_loop(0, outer - 1, reduce_block, 0)
     devices = seq * dp
     each = width // devices
     row, col = grid_index(devices, width)
@@ -1244,7 +1231,6 @@
         )
 
     everyone(seq, dp, lambda r, where: push(r, where).start())
-    lax.fori_loop(outer // 2, outer, reduce_block, 0)
     out_small[...] = to_all[me]
 
     def add_small(r, where):
@@ -1252,6 +1238,7 @@
         out_small[...] += from_all[r]
 
     everyone(seq, dp, add_small)
+    lax.fori_loop(outer - 1, outer, reduce_block, 0)
     for m in range(4):
         out[m] = total[m, z].astype(F32)
 
@@ -1278,10 +1265,11 @@
         return carry
 
     lax.fori_loop(0, outer, sent, 0)
-
-
-def finish(outer, dp, mats, gates, parts, tok, base, gain, small):
-    rows, width = tok.shape
+    last_x.wait()
+
+
+def finish(outer, dp, mats, gates, feed_sums, operands, rest, small):
+    rows, width = rest[-3].shape
     high = mats.shape[3]
     devices = 2 * outer * dp
     dma = pltpu.SemaphoreType.DMA
@@ -1290,25 +1278,31 @@
     payload = (small.shape[1] + 8, 128)
     return pl.pallas_call(
         functools.partial(final_kernel, outer, dp),
-        in_specs=[in_vmem()] * 7,
-        out_specs=[in_vmem()] * 3,
+        in_specs=[in_hbm()] * (3 + len(operands)) + [in_vmem()] * (len(rest) + 1),
+        out_specs=[in_vmem()] * 3 + [in_hbm()],
         out_shape=[
             jax.ShapeDtypeStruct((4, high, width), F32),
             jax.ShapeDtypeStruct((rows, width), F32),
             jax.ShapeDtypeStruct(payload, F32),
+            jax.ShapeDtypeStruct((rows, width), BF16),
         ],
-        scratch_shapes=[blocks] * 4
+        scratch_shapes=[pltpu.VMEM(x.shape, BF16) for x in operands]
+        + [pltpu.VMEM((3, outer, high, width), BF16)]
+        + [blocks] * 3
         + [
-            pltpu.VMEM((2, rows, width), BF16), buffer, buffer, pltpu.VMEM((1, width), F32),
+            pltpu.VMEM((4, rows, width), BF16), pltpu.VMEM((2, rows, width), BF16), buffer,
+            buffer, pltpu.VMEM((1, width), F32),
             pltpu.VMEM((devices,) + payload, F32), pltpu.VMEM((devices,) + payload, F32),
+            dma((8,)),
         ]
         + [dma((4, outer))] * 6
-        + [dma((CHUNKS,))] * 4
+        + [dma((2,))] * 2
+        + [dma((1,))] * 4
         + [dma((devices,))] * 2,
         compiler_params=pltpu.CompilerParams(
-            collective_id=4, has_side_effects=True, vmem_limit_bytes=VMEM_LIMIT
+            collective_id=4, has_side_effects=True, vmem_limit_bytes=60 * 1024 * 1024
         ),
-    )(mats, gates, parts, tok, base, gain, small)
+    )(mats, gates, feed_sums, *operands, *rest, small)
 
 
 class Lanes:
@@ -1558,16 +1552,15 @@
     adjoint, out_sum, gate_grad, feed_parts = lax.optimization_barrier(
         (adjoint, out_sum, gate_grad, feed_parts)
     )
-    adjoint_in, feed_sums = relay(
-        lanes.outer, True, [adjoint, keeps, feed_parts.reshape(8, rows, width)], sequences,
+    adjoint_in, feed_sums, gate_got = relay(
+        lanes.outer, True,
+        [adjoint, keeps, feed_parts.reshape(8, rows, width), gate_grad[half_width:]], sequences,
         SLOTS, 2 * head_width,
     )
-    feed_got = lanes.swap_inner(feed_sums[1])
     gate_grad, out_sum, adjoint_in, feed_grads = lax.optimization_barrier(
         (gate_grad, out_sum, adjoint_in, feed_grads)
     )
     out_mine = lanes.scatter_outer(out_sum.reshape(-1, head_width))
-    gate_got = lanes.swap_inner(gate_grad[half_width:])
     grad_pre, grad_logit = per_sequence(
         back_second_kernel,
         [
@@ -1576,16 +1569,11 @@
         ],
         [shaped(piece, 3 * head_width, BF16), shaped(piece, SLOTS, BF16)],
     )
-    grad_pre, gate_got, out_mine = lax.optimization_barrier(
-        (flat(grad_pre), gate_got, out_mine)
-    )
-    gate_sum = (gate_grad[:half_width].astype(F32) + gate_got.astype(F32)).astype(BF16)
+    grad_pre, out_mine = lax.optimization_barrier((flat(grad_pre), out_mine))
     grad_logit = flat(grad_logit)
     bias_part = jnp.sum(grad_logit.astype(F32), axis=0)
     up_part = contract_first(grad_logit, low_rank)
-    grad_in, grad_rank = grad_in_tiles(
-        [grad_pre, grad_gate_flat, grad_logit], [w_kqv, w_g, up_mine, down_full], [width, rank]
-    )
+    grad_rank = mm(grad_logit, up_mine, 1, 0).astype(BF16)
     down_part = contract_first(normed_in, grad_rank)
 
     mixer_grads = contract_first(grad_pre, normed_in).astype(BF16)
@@ -1608,21 +1596,23 @@
     padded = -(-sum(sizes) // 1024) * 1024
     parts.append(jnp.zeros((devices, padded - sum(sizes)), F32))
     small_parts = jnp.concatenate(parts, axis=1).reshape(devices, -1, 128)
-    grad_in, mixer_grads, feed_got = lax.optimization_barrier((grad_in, mixer_grads, feed_got))
+    gate_sum = (gate_grad[:half_width].astype(F32) + gate_got.astype(F32)).astype(BF16)
     out_mine = out_mine.reshape(lanes.dp, out_rows, head_width)
     out_mine = lanes.exchange_heads(out_mine).transpose(1, 0, 2)
     out_mine = out_mine.reshape(out_rows, lanes.dp, 2, lanes.outer, -1)
     low_half, high_half = lanes.pick(out_mine, 2)
     w_out_grad = jnp.stack([low_half, high_half], axis=3).reshape(out_rows, width).astype(F32)
+    weight_grads, tokens_grad, reduced, feed_got = finish(
+        lanes.outer, lanes.dp, mixer_grads,
+        gate_sum.reshape(lanes.outer, -1, width), feed_sums,
+        [grad_pre, grad_gate_flat, w_kqv, w_g],
+        [grad_rank, down_full, own_tokens, grad_hidden, mixer_full],
+        small_parts,
+    )
+    w_key_grad, w_query_grad, w_value_grad, w_gate_grad = [weight_grads[m] for m in range(4)]
+    tokens_grad = tokens_grad.reshape(seq_count, piece, width)
     feed_sum = feed_sums[0].astype(F32) + feed_got.astype(F32)
     block_out = (alive_own * (hidden + feed_sum)).astype(BF16)
-    weight_grads, tokens_grad, reduced = finish(
-        lanes.outer, lanes.dp, mixer_grads,
-        gate_sum.reshape(lanes.outer, -1, width), grad_in.reshape(4, rows, width), own_tokens,
-        grad_hidden, mixer_full, small_parts,
-    )
-    w_key_grad, w_query_grad, w_value_grad, w_gate_grad = [weight_grads[m] for m in range(4)]
-    tokens_grad = tokens_grad.reshape(seq_count, piece, width)
     mixer_gain_grad = reduced[padded // 128, : width // devices]
     reduced = reduced.reshape(-1)
     smalls, offset = [], 0

time: 819 us -> 790 us (0.965)
  Pallas kernels: 555 us -> 538 us
  waiting for transfers between devices: 69.4 us -> 55.9 us
    pallas_call x2 -> x1, Pallas kernels: 124 us -> 106 us  [finish(): pl.pallas_call(functools.partial(final_kernel, outer, dp), in_specs=[in_h...]
    ppermute x5 -> x3, waiting for transfers between devices: 51.9 us -> 39.2 us  [swap_inner(): return lax.ppermute(x, 'seq', [(i, i ^ 1) for i in range(self.seq)])]
    unnamed x143 -> x159, local copies, waits for them, and re-layouts: 20.7 us -> 26.7 us
    dot_general x14 -> x15, matrix products: 72.9 us -> 73.5 us  [mm(): lax.dot_general(a.astype(BF16), b.astype(BF16), (((ca,), (cb,)), ((), ())...]
  transfers between devices with their start and end apart: 12 -> 10, of which waited for: 5 -> 3; matrix products, arithmetic and copies ran while one was open for 12% -> 11% of each run, Pallas kernels for 38% -> 38%
where the time goes in v4:
time: 790 us; the launch traced here: 778 us
  Pallas kernels  538 us (68%)
  matrix products  73.5 us (9%)
  waiting for transfers between devices  55.9 us (7%)
  local copies, waits for them, and re-layouts  51 us (6%)
  other arithmetic  39.6 us (5%)
  between operations  15 us (2%)
    pallas_call x1, Pallas kernels, finish(): pl.pallas_call(functools.partial(final_kernel, outer, dp), in_specs=[in_h...  106 us
    pallas_call x2, Pallas kernels, relay(): pl.pallas_call(functools.partial(relay_kernel, outer, backward), in_specs...  92.7 us
    pallas_call x1, Pallas kernels, middle(): pl.pallas_call(middle_kernel, in_specs=[in_vmem()] * 4, out_specs=[in_vme...  86.8 us
    pallas_call x1, Pallas kernels, gather_all(): pl.pallas_call(functools.partial(gather_kernel, outer, dp), in_specs=[in_...  75 us
    dot_general x15, matrix products, mm(): lax.dot_general(a.astype(BF16), b.astype(BF16), (((ca,), (cb,)), ((), ())...  73.5 us
    pallas_call x1, Pallas kernels, middle_back(): pl.pallas_call(middle_back_kernel, in_specs=[in_vmem()] * 4, out_specs=[i...  65.9 us
    pallas_call x3, Pallas kernels, per_sequence(): pl.pallas_call(kernel, grid=(count,), in_specs=[spec(x.shape, at) for x,...  57.7 us
    pallas_call x2, Pallas kernels, feed_tiles(): pl.pallas_call(kernel, grid=(rows // step,), in_specs=[spec(x.shape[1]) f...  53.8 us
  transfers between devices with their start and end apart: 10, of which 3 were waited for; matrix products, arithmetic and copies ran while one was open for 11% of the time, Pallas kernels for 38%

profile of v4, /device:TPU:21, one launch (start us, length us, event | category | flops | bytes accessed | tf_op | source)
XLA Modules:
  0.0 777.7 jit_solution(4154525074627380853)
XLA Ops:
  10.5 2.8 convert_multiply_fusion
  13.5 75.0 %shard_map.288 = (bf16[3,2,4,64,2048]{4,3,2,1,0:T(8,128)(2,1)}, bf16[4,64,512]{2,1,0:T(8,128)(2,1)S(1)}, bf16[4,256,2048]{2,1,0:T(8,128)(2,1)}, bf16[4,256,2048]{2,1,0:T(8,128)(2,1)}, bf16[32,16,128]{2,1,0:T(8,128)(2,1)S(1)}) custom-call(bf16[64,2048]{1,0:T(8,128)(2,1)S(1)} %copy-done.24, bf16[64,2048]{1,0:T(8,128)(2,1)S(1)} %copy-done.25, ...), custom_call_target="tpu_custom_call" | custom-call | tf_op jit(solution)/shard_map/pallas_call | solution.py:587
  92.5 3.1 multiply_reduce_fusion
  97.4 3.5 multiply_convert_fusion
  101.0 1.2 convolution_convert_fusion.8
  103.5 1.0 copy.93
  104.5 1.0 copy.94
  105.5 1.6 pad_maximum_fusion.1
  107.1 12.4 %fusion.2 = (bf16[1024,1536]{1,0:T(8,128)(2,1)S(1)}, f32[1024,1536]{1,0:T(8,128)}) fusion(pred[1536]{0:T(1024)(128)(4,1)S(1)} %iota_compare_fusion, bf16[1024,2048]{1,0:T(8,128)(2,1)} %bitcast.244, bf16[1536,2048]{1,0:T(8,128)(2,1)} %bitcast.255), kind=kOutput, calls=%fused_computation.8 | convolution fusion | flops 6451888128 | bytes 19924480 | tf_op jit(solution)/shard_map/dot_general | solution.py:21
  119.5 16.7 %all-gather.3.cloned.1.call-done = bf16[512,2048]{1,0:T(8,128)(2,1)} async-done(((bf16[128,2048]{1,0:T(8,128)(2,1)}), bf16[512,2048]{1,0:T(8,128)(2,1)}) %all-gather.3.cloned.1.call-update) | async-done | bytes 2097168 | tf_op jit(solution)/shard_map/all_gather | solution.py:1323
  136.2 1.0 copy-done.1
  137.2 1.0 copy-done.3
  138.2 33.5 %shard_map.289 = (bf16[8,64,1024]{2,1,0:T(8,128)(2,1)S(1)}, f32[2,8,64]{2,1,0:T(8,128)S(1)}) custom-call(bf16[8,128,1536]{2,1,0:T(8,128)(2,1)S(1)} %bitcast.214, f32[8,128,64]{2,1,0:T(8,128)S(1)} %bitcast.223, f32[8,128,64]{2,1,0:T(8,128)S(1)} %bitcast.227), custom_call_target="tpu_custom_call" | custom-call | tf_op jit(solution)/shard_map/pallas_call | solution.py:835
  172.8 2.7 slice_bitcast_fusion.2
  175.5 1.4 reshape_squeeze.6
  177.2 1.2 collective-permute-start
  179.5 18.9 %collective-permute-done.1 = bf16[4,4,64,512]{3,2,1,0:T(8,128)(2,1)} collective-permute-done((bf16[4,4,64,512]{3,2,1,0:T(8,128)(2,1)}, bf16[4,4,64,512]{3,2,1,0:T(8,128)(2,1)}, u32[]{:S(2)}, u32[]{:S(2)}) %collective-permute-start.1) | collective-permute-done | bytes 1048608 | tf_op jit(solution)/shard_map/ppermute | solution.py:1320
  198.5 1.3 slice_bitcast_fusion.5
  200.7 20.2 %collective-permute-done = bf16[4,64,2048]{2,1,0:T(8,128)(2,1)} collective-permute-done((bf16[4,64,2048]{2,1,0:T(8,128)(2,1)}, bf16[4,64,2048]{2,1,0:T(8,128)(2,1)}, u32[]{:S(2)}, u32[]{:S(2)}) %collective-permute-start) | collective-permute-done | bytes 1048608 | tf_op jit(solution)/shard_map/ppermute | solution.py:1320
  220.9 1.7 pad_maximum_fusion.2
  222.7 1.4 copy-done.35
  224.0 3.7 fusion.36.gate_ref
  227.8 15.9 %shard_map.290 = (bf16[8,128,512]{2,1,0:T(8,128)(2,1)S(1)}, f32[8,128,512]{2,1,0:T(8,128)S(1)}, f32[8,128,64]{2,1,0:T(8,128)S(1)}) custom-call(bf16[8,128,1536]{2,1,0:T(8,128)(2,1)} %bitcast.215, bf16[8,128,1536]{2,1,0:T(8,128)(2,1)} %bitcast.216, bf16[8,128,1536]{2,1,0:T(8,128)(2,1)} %bitcast.217, f32[8,128,512]{2,1,0:T(8,128)} %fusion.36.gate_ref, ...), custom_call_target="tpu_custom_call" | custom-call | tf_op jit(solution)/shard_map/pallas_call | solution.py:346
  243.7 1.3 copy-done.15
  245.0 4.3 convolution_convert_fusion.1
  249.4 86.8 %shard_map.291 = (f32[256,2048]{1,0:T(8,128)S(1)}, bf16[8,256,2048]{2,1,0:T(8,128)(2,1)}, bf16[8,256,2048]{2,1,0:T(8,128)(2,1)}) custom-call(bf16[4,256,2048]{2,1,0:T(8,128)(2,1)} %bitcast.260, bf16[256,2048]{1,0:T(8,128)(2,1)S(1)} %bitcast.233, f32[1,2048]{1,0:T(1,128)S(1)} %reshape.730.gain, bf16[4,256,2048]{2,1,0:T(8,128)(2,1)} %get-tuple-element.82.extra), custom_call_target="tpu_custom_call" | custom-call | tf_op jit(solution)/shard_map/pallas_call | solution.py:929
  336.2 1.4 copy-done.9
  337.6 27.0 %shard_map.292 = (bf16[2048,704]{1,0:T(8,128)(2,1)S(1)}, bf16[2048,704]{1,0:T(8,128)(2,1)}, bf16[2048,704]{1,0:T(8,128)(2,1)}) custom-call(bf16[2048,2048]{1,0:T(8,128)(2,1)} %bitcast.290, bf16[2048,2048]{1,0:T(8,128)(2,1)} %bitcast.286, bf16[3,704,2048]{2,1,0:T(8,128)(2,1)} %all-gather.5.cloned.1.call-done.w_down.w_act.w_lin, ...), custom_call_target="tpu_custom_call" | custom-call | flops 17716740096 | bytes 42205184 | tf_op jit(solution)/shard_map/pallas_call | solution.py:640
  364.6 11.3 %fusion.5 = bf16[1,704,2048]{2,1,0:T(8,128)(2,1)S(1)} fusion(bf16[2048,704]{1,0:T(8,128)(2,1)} %get-tuple-element.92.grad_lin, bf16[2048,2048]{1,0:T(8,128)(2,1)} %bitcast.291), kind=kOutput, calls=%fused_computation.17 | convolution fusion | flops 5907021824 | bytes 14155776 | tf_op jit(solution)/shard_map/dot_general | solution.py:21
  375.9 6.5 fusion.4
  382.5 6.5 fusion.3
  389.0 3.9 pad_maximum_fusion
  395.6 5.3 fusion.1
  401.0 26.8 %shard_map.293 = (bf16[2048,2048]{1,0:T(8,128)(2,1)}, bf16[2048,2048]{1,0:T(8,128)(2,1)}) custom-call(bf16[2048,704]{1,0:T(8,128)(2,1)S(1)} %copy-done.31, bf16[2048,704]{1,0:T(8,128)(2,1)} %get-tuple-element.91.grad_gate, bf16[2048,704]{1,0:T(8,128)(2,1)} %get-tuple-element.92.grad_lin, ...), custom_call_target="tpu_custom_call" | custom-call | flops 17716740096 | bytes 42205184 | tf_op jit(solution)/shard_map/pallas_call | solution.py:640
  427.8 65.9 %shard_map.294 = (f32[256,2048]{1,0:T(8,128)S(1)}, f32[1,2048]{1,0:T(1,128)S(1)}, bf16[4,256,2048]{2,1,0:T(8,128)(2,1)}) custom-call(bf16[8,256,2048]{2,1,0:T(8,128)(2,1)} %bitcast.252, f32[256,2048]{1,0:T(8,128)S(1)} %copy-done.10, f32[256,2048]{1,0:T(8,128)} %get-tuple-element.211.grad_out, f32[1,2048]{1,0:T(1,128)S(1)} %reshape.730.gain), custom_call_target="tpu_custom_call" | custom-call | tf_op jit(solution)/shard_map/pallas_call | solution.py:1034
  493.7 5.4 convolution_convert_fusion.6
  499.1 1.1 select_bitcast_fusion
  500.2 1.2 collective-permute-start.2
  501.8 3.7 fusion.37.grad_mixed_ref
  506.8 14.4 %shard_map.295 = (bf16[8,128,512]{2,1,0:T(8,128)(2,1)S(1)}, bf16[8,128,512]{2,1,0:T(8,128)(2,1)S(1)}, f32[8,128,64]{2,1,0:T(8,128)S(1)}, f32[8,64,1024]{2,1,0:T(8,128)}, f32[8,1,512]{2,1,0:T(1,128)S(1)}) custom-call(f32[8,128,512]{2,1,0:T(8,128)} %fusion.37.grad_mixed_ref, f32[8,128,512]{2,1,0:T(8,128)} %fusion.36.gate_ref, f32[8,128,512]{2,1,0:T(8,128)} %copy-done.15, ...), custom_call_target="tpu_custom_call" | custom-call | tf_op jit(solution)/shard_map/pallas_call | solution.py:346
  521.1 1.0 copy-done.16
  522.1 1.0 copy-done.19
  524.2 4.9 convolution_convert_fusion.5
  529.1 2.1 fusion.32
  531.8 1.4 fusion.10
  533.3 59.2 %shard_map.296 = (bf16[8,64,1024]{2,1,0:T(8,128)(2,1)S(1)}, bf16[2,256,2048]{2,1,0:T(8,128)(2,1)S(1)}, bf16[256,2048]{1,0:T(8,128)(2,1)S(1)}) custom-call(f32[8,64,1024]{2,1,0:T(8,128)} %get-tuple-element.102.refs_0_, f32[2,8,64]{2,1,0:T(8,128)S(1)} %get-tuple-element.103.refs_1_, bf16[8,256,2048]{2,1,0:T(8,128)(2,1)} %bitcast.251, ...), custom_call_target="tpu_custom_call" | custom-call | tf_op jit(solution)/shard_map/pallas_call | solution.py:835
  592.5 1.3 copy-done.12
  593.8 1.0 copy-done.18
  595.8 2.3 copy.102
  598.1 1.0 copy-done.13
  599.2 1.2 copy-done.17
  600.4 1.0 copy-done.23
  601.4 27.4 %shard_map.297 = (bf16[8,128,1536]{2,1,0:T(8,128)(2,1)}, bf16[8,128,64]{2,1,0:T(8,128)(2,1)S(1)}) custom-call(bf16[8,128,512]{2,1,0:T(8,128)(2,1)S(1)} %copy-done.17, f32[8,128,64]{2,1,0:T(8,128)S(1)} %copy-done.23, f32[8,128,64]{2,1,0:T(8,128)S(1)} %get-tuple-element.98.attend_ref, bf16[8,128,1536]{2,1,0:T(8,128)(2,1)} %bitcast.220, ...), custom_call_target="tpu_custom_call" | custom-call | tf_op jit(solution)/shard_map/pallas_call | solution.py:346
  629.8 1.3 fusion.38
  633.4 2.6 add_convert_fusion
  636.0 2.4 bitcast_convert_fusion
  638.3 1.1 copy-done.39
  639.4 10.9 %convolution_convert_fusion = bf16[1536,2048]{1,0:T(8,128)(2,1)} fusion(bf16[1024,1536]{1,0:T(8,128)(2,1)S(1)} %bitcast.262, bf16[1024,2048]{1,0:T(8,128)(2,1)} %fusion.1), kind=kOutput, calls=%fused_computation.7 | convolution fusion | flops 6445596672 | bytes 13631488 | tf_op jit(solution)/shard_map/dot_general | solution.py:21
  650.3 105.7 %shard_map.298 = (f32[4,64,2048]{2,1,0:T(8,128)}, f32[256,2048]{1,0:T(8,128)}, f32[24,128]{1,0:T(8,128)}, bf16[256,2048]{1,0:T(8,128)(2,1)}) custom-call(bf16[3,2,4,64,2048]{4,3,2,1,0:T(8,128)(2,1)} %bitcast.257, bf16[4,64,2048]{2,1,0:T(8,128)(2,1)} %bitcast.258, bf16[2,256,2048]{2,1,0:T(8,128)(2,1)} %copy-done.12, bf16[1024,1536]{1,0:T(8,128)(2,1)} %bitcast.261, ...), custom_call_target="tpu_custom_call" | custom-call | tf_op jit(solution)/shard_map/pallas_call | solution.py:1279
  756.0 3.2 fusion.8
  759.1 1.4 slice_bitcast_fusion.6
  760.5 1.4 collective-permute-start.3
  767.9 1.8 reshape.735
  769.7 1.3 copy.137
  (249 shorter events, 29.9 us)
Async XLA Ops:
  7.2 6.2 copy-start.66
  7.2 6.1 copy-start.67
  7.2 6.1 copy-start.68
  7.2 6.1 copy-start.69
  7.2 6.2 copy-start.24
  7.2 6.2 copy-start.25
  7.2 6.2 copy-start.26
  7.3 6.2 copy-start.7
  7.3 6.2 copy-start.27
  7.3 128.9 %all-gather.3.cloned.1.call-start = ((), (), s32[]{:S(2)}) async-start(), calls=%async_computation.2 | async-start | bytes 2621440 | tf_op jit(solution)/shard_map/all_gather | solution.py:1323
  8.8 87.9 %copy-start.64 = (f32[128]{0:T(128)}, f32[128]{0:T(128)S(1)}, u32[]{:S(2)}) copy-start(f32[128]{0:T(128)S(1)} %add_convert_fusion.1) | copy-start | bytes 1540
  10.5 2.9 copy-start.60
  88.5 1.9 copy-start.51
  91.3 246.2 %all-gather.5.cloned.1.call-start = ((), (), s32[]{:S(2)}) async-start(), calls=%async_computation.3 | async-start | bytes 10813440 | tf_op jit(solution)/shard_map/all_gather | solution.py:1473
  92.1 4.7 copy-start.54
  96.7 4.2 copy-start.62
  97.3 3.7 copy-start.38
  97.4 4.8 copy-start.56
  100.9 2.1 copy-start.32
  101.0 4.5 copy-start.47
  101.0 4.5 copy-start.48
  101.0 4.5 copy-start.49
  103.1 4.0 copy-start.52
  119.5 53.3 %copy-start = (bf16[1024,1536]{1,0:T(8,128)(2,1)}, bf16[1024,1536]{1,0:T(8,128)(2,1)S(1)}, u32[]{:S(2)}) copy-start(bf16[1024,1536]{1,0:T(8,128)(2,1)S(1)} %get-tuple-element.242) | copy-start | bytes 9437188
  172.8 423.0 %reduce-scatter.3.cloned.1.call-start = ((), (), s32[]{:S(2)}) async-start(), calls=%async_computation.4 | async-start | bytes 10813440 | tf_op jit(solution)/shard_map/reduce_scatter | solution.py:1520
  172.8 5.9 copy-start.57
  177.0 21.5 %collective-permute-start.1 = (bf16[4,4,64,512]{3,2,1,0:T(8,128)(2,1)}, bf16[4,4,64,512]{3,2,1,0:T(8,128)(2,1)}, u32[]{:S(2)}, u32[]{:S(2)}) collective-permute-start(bf16[4,4,64,512]{3,2,1,0:T(8,128)(2,1)} %reshape_squeeze.6), channel_id=1, source_target_pairs={{0,1},{1,0},{2,3},{3,2},{4,5},{5,4},{6,7},{7,6},{8,9},{9,8},{10,11... | collective-permute-start | bytes 3145736 | tf_op jit(solution)/shard_map/ppermute | solution.py:1320
  177.2 43.7 %collective-permute-start = (bf16[4,64,2048]{2,1,0:T(8,128)(2,1)}, bf16[4,64,2048]{2,1,0:T(8,128)(2,1)}, u32[]{:S(2)}, u32[]{:S(2)}) collective-permute-start(bf16[4,64,2048]{2,1,0:T(8,128)(2,1)} %get-tuple-element.210), channel_id=1, source_target_pairs={{0,1},{1,0},{2,3},{3,2},{4,5},{5,4},{6,7},{7,6},{8,9},{9,8},{10,11... | collective-permute-start | bytes 3145736 | tf_op jit(solution)/shard_map/ppermute | solution.py:1320
  200.7 44.4 %copy-start.43 = (bf16[4,4,2,64,512]{4,3,2,1,0:T(8,128)(2,1)}, bf16[4,4,2,64,512]{4,3,2,1,0:T(8,128)(2,1)S(1)}, u32[]{:S(2)}) copy-start(bf16[4,4,2,64,512]{4,3,2,1,0:T(8,128)(2,1)S(1)} %copy.97) | copy-start | bytes 6291460
  200.7 23.4 %copy-start.33 = (bf16[4,256,2048]{2,1,0:T(8,128)(2,1)S(1)}, bf16[4,256,2048]{2,1,0:T(8,128)(2,1)}, u32[]{:S(2)}) copy-start(bf16[4,256,2048]{2,1,0:T(8,128)(2,1)} %copy-done.32) | copy-start | bytes 12582916
  224.0 3.7 copy-start.2
  224.0 3.7 copy-start.4
  224.0 3.7 copy-start.6
  245.0 4.3 copy-start.28
  245.0 4.3 copy-start.8
  364.6 17.9 %copy-start.30 = (bf16[2048,704]{1,0:T(8,128)(2,1)}, bf16[2048,704]{1,0:T(8,128)(2,1)S(1)}, u32[]{:S(2)}) copy-start(bf16[2048,704]{1,0:T(8,128)(2,1)S(1)} %get-tuple-element.90.product) | copy-start | bytes 8650756
  364.6 11.3 %copy-start.70 = (bf16[8,256,2048]{2,1,0:T(8,128)(2,1)S(1)}, bf16[8,256,2048]{2,1,0:T(8,128)(2,1)}, u32[]{:S(2)}) copy-start(bf16[8,256,2048]{2,1,0:T(8,128)(2,1)} %get-tuple-element.84) | copy-start | bytes 25165828
  364.6 11.3 %copy-start.72 = (bf16[2048,704]{1,0:T(8,128)(2,1)S(1)}, bf16[2048,704]{1,0:T(8,128)(2,1)}, u32[]{:S(2)}) copy-start(bf16[2048,704]{1,0:T(8,128)(2,1)} %get-tuple-element.91.grad_gate) | copy-start | bytes 8650756
  364.6 17.9 %slice-start = ((s8[8388608]{0:T(1024)(128)(4,1)}), s8[4194304]{0:T(1024)(128)(4,1)S(1)}, s32[]{:S(2)}) async-start(s8[8388608]{0:T(1024)(128)(4,1)} %bitcast.287), calls=%async_computation.6 | async-start | bytes 8388608
  375.9 6.6 slice-start.1
  393.0 245.3 %reduce-scatter.5.cloned.1.call-start = ((), (), s32[]{:S(2)}) async-start(), calls=%async_computation.5 | async-start | bytes 1310720 | tf_op jit(solution)/shard_map/reduce_scatter | solution.py:1326
  395.6 5.3 copy-start.31
  401.0 26.8 %copy-start.10 = (f32[256,2048]{1,0:T(8,128)S(1)}, f32[256,2048]{1,0:T(8,128)}, u32[]{:S(2)}) copy-start(f32[256,2048]{1,0:T(8,128)} %copy-done.9) | copy-start | bytes 6291460
  427.8 65.9 %copy-start.29 = (bf16[8,128,512]{2,1,0:T(8,128)(2,1)S(1)}, bf16[8,128,512]{2,1,0:T(8,128)(2,1)}, u32[]{:S(2)}) copy-start(bf16[8,128,512]{2,1,0:T(8,128)(2,1)} %copy-done.28) | copy-start | bytes 3145732
  493.7 5.4 copy-start.14
  493.7 7.7 copy-start.71
  499.1 6.4 copy-start.36
  499.1 2.7 copy-start.44
  500.2 28.9 %collective-permute-start.2 = (bf16[4,4,64,512]{3,2,1,0:T(8,128)(2,1)}, bf16[4,4,64,512]{3,2,1,0:T(8,128)(2,1)}, u32[]{:S(2)}, u32[]{:S(2)}) collective-permute-start(bf16[4,4,64,512]{3,2,1,0:T(8,128)(2,1)} %select_bitcast_fusion), channel_id=1, source_target_pairs={{0,1},{1,0},{2,3},{3,2},{4,5},{5,4},{6,7},{7,6},{8,9},{9,8},{10,11... | collective-permute-start | bytes 3145736 | tf_op jit(solution)/shard_map/ppermute | solution.py:1320
  529.1 4.1 copy-start.42
  529.1 2.7 copy-start.37
  601.4 28.3 %copy-start.34 = (bf16[1024,2048]{1,0:T(8,128)(2,1)S(1)}, bf16[1024,2048]{1,0:T(8,128)(2,1)}, u32[]{:S(2)}) copy-start(bf16[1024,2048]{1,0:T(8,128)(2,1)} %fusion.1) | copy-start | bytes 12582916
  629.7 1.9 copy-start.40
  629.8 3.6 copy-start.21
  632.6 3.4 copy-start.41
  636.0 3.5 copy-start.39
  650.3 105.7 %copy-start.11 = (f32[256,2048]{1,0:T(8,128)S(1)}, f32[256,2048]{1,0:T(8,128)}, u32[]{:S(2)}) copy-start(f32[256,2048]{1,0:T(8,128)} %copy-done.9) | copy-start | bytes 6291460
  650.3 105.7 %copy-start.61 = (f32[256]{0:T(256)S(1)}, f32[256]{0:T(256)}, u32[]{:S(2)}) copy-start(f32[256]{0:T(256)} %copy-done.60) | copy-start | bytes 3076
  756.0 3.2 copy-start.46
  759.1 3.6 copy-start.59
  760.5 5.8 collective-permute-start.3
  761.9 4.4 collective-permute-start.4
  762.4 3.9 collective-permute-start.5
  766.8 2.8 copy-start.45
  (21 other events, 25.6 us)
Sparse Core Ops, SparseCore 0:
  91.5 44.6 all-gather.2
  172.9 159.0 all-gather.4
  393.1 153.8 reduce-scatter.2
  598.3 25.9 reduce-scatter.4

commit v5 on v4

--- a/solution.py
+++ b/solution.py
@@ -1050,16 +1050,15 @@
 
 
 def final_kernel(
-    outer, dp, mats, gates, feed_sums, pre_hbm, gate_hbm, kqv_hbm, g_hbm, grad_rank, w_rank, tok,
+    outer, dp, mats, gates, pre_hbm, gate_hbm, kqv_hbm, g_hbm, grad_rank, w_rank, tok,
     base, gain, small, *refs,
 ):
-    out, tokens_grad, out_small, feed_got, refs = refs[0], refs[1], refs[2], refs[3], refs[4:]
+    out, tokens_grad, out_small, refs = refs[0], refs[1], refs[2], refs[3:]
     (
         grad_pre, grad_gate, w_kqv, w_g,
         from_x, from_below, from_above, total, parts, from_core, to_y, from_y, gain_grad,
         to_all, from_all,
-        load, x_s, x_r, up_s, up_r, down_s, down_r, core_s, core_r, y_s, y_r, feed_s, feed_r,
-        all_s, all_r,
+        load, x_s, x_r, up_s, up_r, down_s, down_r, core_s, core_r, y_s, y_r, all_s, all_r,
     ) = refs
     rows, width = tok.shape
     size = rows // CHUNKS
@@ -1105,7 +1104,6 @@
         return carry
 
     lax.fori_loop(0, outer, start_x, 0)
-    last_x = send(feed_sums.at[1], feed_got, feed_s.at[0], feed_r.at[0], x)
     operands = [
         pltpu.make_async_copy(src, dst, load.at[4 + n])
         for n, (src, dst) in enumerate(
@@ -1265,10 +1263,9 @@
         return carry
 
     lax.fori_loop(0, outer, sent, 0)
-    last_x.wait()
-
-
-def finish(outer, dp, mats, gates, feed_sums, operands, rest, small):
+
+
+def finish(outer, dp, mats, gates, operands, rest, small):
     rows, width = rest[-3].shape
     high = mats.shape[3]
     devices = 2 * outer * dp
@@ -1278,13 +1275,12 @@
     payload = (small.shape[1] + 8, 128)
     return pl.pallas_call(
         functools.partial(final_kernel, outer, dp),
-        in_specs=[in_hbm()] * (3 + len(operands)) + [in_vmem()] * (len(rest) + 1),
-        out_specs=[in_vmem()] * 3 + [in_hbm()],
+        in_specs=[in_hbm()] * (2 + len(operands)) + [in_vmem()] * (len(rest) + 1),
+        out_specs=[in_vmem()] * 3,
         out_shape=[
             jax.ShapeDtypeStruct((4, high, width), F32),
             jax.ShapeDtypeStruct((rows, width), F32),
             jax.ShapeDtypeStruct(payload, F32),
-            jax.ShapeDtypeStruct((rows, width), BF16),
         ],
         scratch_shapes=[pltpu.VMEM(x.shape, BF16) for x in operands]
         + [pltpu.VMEM((3, outer, high, width), BF16)]
@@ -1297,12 +1293,12 @@
         ]
         + [dma((4, outer))] * 6
         + [dma((2,))] * 2
-        + [dma((1,))] * 4
+        + [dma((1,))] * 2
         + [dma((devices,))] * 2,
         compiler_params=pltpu.CompilerParams(
             collective_id=4, has_side_effects=True, vmem_limit_bytes=60 * 1024 * 1024
         ),
-    )(mats, gates, feed_sums, *operands, *rest, small)
+    )(mats, gates, *operands, *rest, small)
 
 
 class Lanes:
@@ -1441,7 +1437,9 @@
     alive = (position[None, :] < group_lengths[:, None]).astype(F32).reshape(all_rows, 1)
 
     sources = plane_tokens.reshape(all_rows, width).astype(F32)
-    normed_in = (sources * rms_scale(sources) * mixer_full).astype(BF16)
+    normed_in = lax.optimization_barrier(
+        (sources * rms_scale(sources) * mixer_full).astype(BF16)
+    )
 
     pre = contract_last(normed_in, w_kqv)
     low_rank = mm(normed_in, down_full, 1, 0).astype(BF16)
@@ -1569,6 +1567,7 @@
         ],
         [shaped(piece, 3 * head_width, BF16), shaped(piece, SLOTS, BF16)],
     )
+    feed_got = lanes.swap_inner(feed_sums[1])
     grad_pre, out_mine = lax.optimization_barrier((flat(grad_pre), out_mine))
     grad_logit = flat(grad_logit)
     bias_part = jnp.sum(grad_logit.astype(F32), axis=0)
@@ -1602,9 +1601,12 @@
     out_mine = out_mine.reshape(out_rows, lanes.dp, 2, lanes.outer, -1)
     low_half, high_half = lanes.pick(out_mine, 2)
     w_out_grad = jnp.stack([low_half, high_half], axis=3).reshape(out_rows, width).astype(F32)
-    weight_grads, tokens_grad, reduced, feed_got = finish(
+    mixer_grads, feed_got, w_out_grad = lax.optimization_barrier(
+        (mixer_grads, feed_got, w_out_grad)
+    )
+    weight_grads, tokens_grad, reduced = finish(
         lanes.outer, lanes.dp, mixer_grads,
-        gate_sum.reshape(lanes.outer, -1, width), feed_sums,
+        gate_sum.reshape(lanes.outer, -1, width),
         [grad_pre, grad_gate_flat, w_kqv, w_g],
         [grad_rank, down_full, own_tokens, grad_hidden, mixer_full],
         small_parts,

time: 790 us -> 788 us (level)
    unnamed x159 -> x141, local copies, waits for them, and re-layouts: 26.7 us -> 23.7 us
    ppermute x3 -> x4, waiting for transfers between devices: 39.2 us -> 39.2 us  [swap_inner(): return lax.ppermute(x, 'seq', [(i, i ^ 1) for i in range(self.seq)])]
  transfers between devices with their start and end apart: 10 -> 11, of which waited for: 3 -> 3; matrix products, arithmetic and copies ran while one was open for 11% -> 12% of each run, Pallas kernels for 38% -> 38%
where the time goes in v5:
time: 788 us; the launch traced here: 774 us
  Pallas kernels  535 us (68%)
  matrix products  76.6 us (10%)
  local copies, waits for them, and re-layouts  55.1 us (7%)
  waiting for transfers between devices  54.1 us (7%)
  other arithmetic  33.1 us (4%)
  between operations  15 us (2%)
    pallas_call x1, Pallas kernels, finish(): pl.pallas_call(functools.partial(final_kernel, outer, dp), in_specs=[in_h...  102 us
    pallas_call x2, Pallas kernels, relay(): pl.pallas_call(functools.partial(relay_kernel, outer, backward), in_specs...  94 us
    pallas_call x1, Pallas kernels, middle(): pl.pallas_call(middle_kernel, in_specs=[in_vmem()] * 4, out_specs=[in_vme...  86.9 us
    dot_general x15, matrix products, mm(): lax.dot_general(a.astype(BF16), b.astype(BF16), (((ca,), (cb,)), ((), ())...  76.6 us
    pallas_call x1, Pallas kernels, gather_all(): pl.pallas_call(functools.partial(gather_kernel, outer, dp), in_specs=[in_...  75 us
    pallas_call x1, Pallas kernels, middle_back(): pl.pallas_call(middle_back_kernel, in_specs=[in_vmem()] * 4, out_specs=[i...  66.1 us
    pallas_call x3, Pallas kernels, per_sequence(): pl.pallas_call(kernel, grid=(count,), in_specs=[spec(x.shape, at) for x,...  57.7 us
    pallas_call x2, Pallas kernels, feed_tiles(): pl.pallas_call(kernel, grid=(rows // step,), in_specs=[spec(x.shape[1]) f...  53 us
  transfers between devices with their start and end apart: 11, of which 3 were waited for; matrix products, arithmetic and copies ran while one was open for 12% of the time, Pallas kernels for 38%

profile of v5, /device:TPU:21, one launch (start us, length us, event | category | flops | bytes accessed | tf_op | source)
XLA Modules:
  0.0 774.1 jit_solution(13665925198768974528)
XLA Ops:
  10.5 2.8 convert_multiply_fusion
  13.5 75.0 %shard_map.288 = (bf16[3,2,4,64,2048]{4,3,2,1,0:T(8,128)(2,1)}, bf16[4,64,512]{2,1,0:T(8,128)(2,1)S(1)}, bf16[4,256,2048]{2,1,0:T(8,128)(2,1)}, bf16[4,256,2048]{2,1,0:T(8,128)(2,1)}, bf16[32,16,128]{2,1,0:T(8,128)(2,1)S(1)}) custom-call(bf16[64,2048]{1,0:T(8,128)(2,1)S(1)} %copy-done.26, bf16[64,2048]{1,0:T(8,128)(2,1)S(1)} %copy-done.27, ...), custom_call_target="tpu_custom_call" | custom-call | tf_op jit(solution)/shard_map/pallas_call | solution.py:587
  91.9 3.2 multiply_reduce_fusion
  95.4 3.0 fusion.1
  99.5 3.7 convolution_convert_fusion.8
  103.2 1.2 exponential-minus-one_negate_fusion
  104.4 1.9 copy.93
  107.4 1.6 pad_maximum_fusion.1
  109.0 12.3 %fusion.2 = (bf16[1024,1536]{1,0:T(8,128)(2,1)S(1)}, f32[1024,1536]{1,0:T(8,128)}) fusion(pred[1536]{0:T(1024)(128)(4,1)S(1)} %iota_compare_fusion, bf16[1024,2048]{1,0:T(8,128)(2,1)} %fusion.1, bf16[1536,2048]{1,0:T(8,128)(2,1)} %bitcast.253), kind=kOutput, calls=%fused_computation.7 | convolution fusion | flops 6451888128 | bytes 19924480 | tf_op jit(solution)/shard_map/dot_general | solution.py:21
  121.3 14.8 %all-gather.3.cloned.1.call-done = bf16[512,2048]{1,0:T(8,128)(2,1)} async-done(((bf16[128,2048]{1,0:T(8,128)(2,1)}), bf16[512,2048]{1,0:T(8,128)(2,1)}) %all-gather.3.cloned.1.call-update) | async-done | bytes 2097168 | tf_op jit(solution)/shard_map/all_gather | solution.py:1319
  136.1 1.0 copy-done.1
  138.2 33.5 %shard_map.289 = (bf16[8,64,1024]{2,1,0:T(8,128)(2,1)S(1)}, f32[2,8,64]{2,1,0:T(8,128)S(1)}) custom-call(bf16[8,128,1536]{2,1,0:T(8,128)(2,1)S(1)} %bitcast.215, f32[8,128,64]{2,1,0:T(8,128)S(1)} %bitcast.224, f32[8,128,64]{2,1,0:T(8,128)S(1)} %bitcast.228), custom_call_target="tpu_custom_call" | custom-call | tf_op jit(solution)/shard_map/pallas_call | solution.py:835
  172.8 1.7 slice_bitcast_fusion.2
  174.6 1.5 reshape_squeeze.6
  176.3 1.2 collective-permute-start
  178.5 18.9 %collective-permute-done.1 = bf16[4,4,64,512]{3,2,1,0:T(8,128)(2,1)} collective-permute-done((bf16[4,4,64,512]{3,2,1,0:T(8,128)(2,1)}, bf16[4,4,64,512]{3,2,1,0:T(8,128)(2,1)}, u32[]{:S(2)}, u32[]{:S(2)}) %collective-permute-start.1) | collective-permute-done | bytes 1048608 | tf_op jit(solution)/shard_map/ppermute | solution.py:1316
  197.5 1.3 slice_bitcast_fusion.6
  199.7 20.2 %collective-permute-done = bf16[4,64,2048]{2,1,0:T(8,128)(2,1)} collective-permute-done((bf16[4,64,2048]{2,1,0:T(8,128)(2,1)S(1)}, bf16[4,64,2048]{2,1,0:T(8,128)(2,1)}, u32[]{:S(2)}, u32[]{:S(2)}) %collective-permute-start) | collective-permute-done | bytes 1048608 | tf_op jit(solution)/shard_map/ppermute | solution.py:1316
  219.9 1.4 pad_maximum_fusion.2
  221.4 1.3 copy-done.39
  222.7 3.7 fusion.35.gate_ref
  226.4 15.9 %shard_map.290 = (bf16[8,128,512]{2,1,0:T(8,128)(2,1)S(1)}, f32[8,128,512]{2,1,0:T(8,128)S(1)}, f32[8,128,64]{2,1,0:T(8,128)S(1)}) custom-call(bf16[8,128,1536]{2,1,0:T(8,128)(2,1)} %bitcast.216, bf16[8,128,1536]{2,1,0:T(8,128)(2,1)} %bitcast.217, bf16[8,128,1536]{2,1,0:T(8,128)(2,1)} %bitcast.218, f32[8,128,512]{2,1,0:T(8,128)} %fusion.35.gate_ref, ...), custom_call_target="tpu_custom_call" | custom-call | tf_op jit(solution)/shard_map/pallas_call | solution.py:346
  242.4 1.3 copy-done.16
  243.7 4.3 convolution_convert_fusion.1
  248.0 86.9 %shard_map.291 = (f32[256,2048]{1,0:T(8,128)S(1)}, bf16[8,256,2048]{2,1,0:T(8,128)(2,1)}, bf16[8,256,2048]{2,1,0:T(8,128)(2,1)}) custom-call(bf16[4,256,2048]{2,1,0:T(8,128)(2,1)} %bitcast.258, bf16[256,2048]{1,0:T(8,128)(2,1)S(1)} %bitcast.234, f32[1,2048]{1,0:T(1,128)S(1)} %reshape.674.gain, bf16[4,256,2048]{2,1,0:T(8,128)(2,1)} %get-tuple-element.84.extra), custom_call_target="tpu_custom_call" | custom-call | tf_op jit(solution)/shard_map/pallas_call | solution.py:929
  335.0 1.3 copy-done.9
  336.3 27.0 %shard_map.292 = (bf16[2048,704]{1,0:T(8,128)(2,1)S(1)}, bf16[2048,704]{1,0:T(8,128)(2,1)}, bf16[2048,704]{1,0:T(8,128)(2,1)}) custom-call(bf16[2048,2048]{1,0:T(8,128)(2,1)} %bitcast.288, bf16[2048,2048]{1,0:T(8,128)(2,1)} %bitcast.284, bf16[3,704,2048]{2,1,0:T(8,128)(2,1)} %all-gather.5.cloned.1.call-done.w_down.w_act.w_lin, ...), custom_call_target="tpu_custom_call" | custom-call | flops 17716740096 | bytes 42205184 | tf_op jit(solution)/shard_map/pallas_call | solution.py:640
  363.3 11.4 %fusion.5 = bf16[1,704,2048]{2,1,0:T(8,128)(2,1)S(1)} fusion(bf16[2048,704]{1,0:T(8,128)(2,1)} %get-tuple-element.94.grad_lin, bf16[2048,2048]{1,0:T(8,128)(2,1)} %bitcast.289), kind=kOutput, calls=%fused_computation.16 | convolution fusion | flops 5907021824 | bytes 14155776 | tf_op jit(solution)/shard_map/dot_general | solution.py:21
  374.8 6.5 fusion.4
  381.4 6.5 fusion.3
  387.9 4.0 pad_maximum_fusion
  394.2 1.9 copy-done.33
  396.0 26.0 %shard_map.293 = (bf16[2048,2048]{1,0:T(8,128)(2,1)}, bf16[2048,2048]{1,0:T(8,128)(2,1)}) custom-call(bf16[2048,704]{1,0:T(8,128)(2,1)S(1)} %copy-done.33, bf16[2048,704]{1,0:T(8,128)(2,1)} %get-tuple-element.93.grad_gate, bf16[2048,704]{1,0:T(8,128)(2,1)} %get-tuple-element.94.grad_lin, ...), custom_call_target="tpu_custom_call" | custom-call | flops 17716740096 | bytes 42205184 | tf_op jit(solution)/shard_map/pallas_call | solution.py:640
  422.1 66.1 %shard_map.294 = (f32[256,2048]{1,0:T(8,128)S(1)}, f32[1,2048]{1,0:T(1,128)S(1)}, bf16[4,256,2048]{2,1,0:T(8,128)(2,1)}) custom-call(bf16[8,256,2048]{2,1,0:T(8,128)(2,1)} %bitcast.248, f32[256,2048]{1,0:T(8,128)S(1)} %copy-done.10, f32[256,2048]{1,0:T(8,128)} %get-tuple-element.215.grad_out, f32[1,2048]{1,0:T(1,128)S(1)} %reshape.674.gain), custom_call_target="tpu_custom_call" | custom-call | tf_op jit(solution)/shard_map/pallas_call | solution.py:1034
  488.3 5.4 convolution_convert_fusion.6
  493.7 1.1 select_bitcast_fusion
  494.7 1.1 collective-permute-start.2
  496.4 3.7 fusion.36.grad_mixed_ref
  501.9 14.4 %shard_map.295 = (bf16[8,128,512]{2,1,0:T(8,128)(2,1)S(1)}, bf16[8,128,512]{2,1,0:T(8,128)(2,1)S(1)}, f32[8,128,64]{2,1,0:T(8,128)S(1)}, f32[8,64,1024]{2,1,0:T(8,128)}, f32[8,1,512]{2,1,0:T(1,128)S(1)}) custom-call(f32[8,128,512]{2,1,0:T(8,128)} %fusion.36.grad_mixed_ref, f32[8,128,512]{2,1,0:T(8,128)} %fusion.35.gate_ref, f32[8,128,512]{2,1,0:T(8,128)} %copy-done.16, ...), custom_call_target="tpu_custom_call" | custom-call | tf_op jit(solution)/shard_map/pallas_call | solution.py:346
  519.3 4.9 convolution_convert_fusion.5
  524.2 2.1 fusion.31
  526.9 1.4 fusion.10
  528.4 60.5 %shard_map.296 = (bf16[8,64,1024]{2,1,0:T(8,128)(2,1)S(1)}, bf16[2,256,2048]{2,1,0:T(8,128)(2,1)S(1)}, bf16[256,2048]{1,0:T(8,128)(2,1)S(1)}) custom-call(f32[8,64,1024]{2,1,0:T(8,128)} %get-tuple-element.104.refs_0_, f32[2,8,64]{2,1,0:T(8,128)S(1)} %get-tuple-element.105.refs_1_, bf16[8,256,2048]{2,1,0:T(8,128)(2,1)} %bitcast.247, ...), custom_call_target="tpu_custom_call" | custom-call | tf_op jit(solution)/shard_map/pallas_call | solution.py:835
  588.9 1.3 copy-done.15
  590.2 1.1 slice_bitcast_fusion.4
  591.6 2.3 copy.102
  594.9 1.2 copy-done.19
  596.2 1.0 copy-done.25
  597.2 27.4 %shard_map.297 = (bf16[8,128,1536]{2,1,0:T(8,128)(2,1)}, bf16[8,128,64]{2,1,0:T(8,128)(2,1)S(1)}) custom-call(bf16[8,128,512]{2,1,0:T(8,128)(2,1)S(1)} %copy-done.19, f32[8,128,64]{2,1,0:T(8,128)S(1)} %copy-done.25, f32[8,128,64]{2,1,0:T(8,128)S(1)} %copy-done.13, bf16[8,128,1536]{2,1,0:T(8,128)(2,1)} %bitcast.221, bf16[8,128,1536]{2,1,0:T(8,128)(2,1)} %bitcast.222, ...), custom_call_target="tpu_custom_call" | custom-call | tf_op jit(solution)/shard_map/pallas_call | solution.py:346
  624.8 1.3 fusion.37
  628.4 2.6 add_convert_fusion
  631.0 2.4 bitcast_convert_fusion
  633.4 1.1 dynamic-slice_bitcast_fusion
  634.5 2.1 collective-permute-start.4
  637.1 11.3 %convolution_convert_fusion = bf16[1536,2048]{1,0:T(8,128)(2,1)} fusion(bf16[1024,1536]{1,0:T(8,128)(2,1)S(1)} %bitcast.260, bf16[1024,2048]{1,0:T(8,128)(2,1)} %fusion.1), kind=kOutput, calls=%fused_computation.6 | convolution fusion | flops 6445596672 | bytes 13631488 | tf_op jit(solution)/shard_map/dot_general | solution.py:21
  650.8 1.8 reshape.677
  652.6 101.8 %shard_map.298 = (f32[4,64,2048]{2,1,0:T(8,128)}, f32[256,2048]{1,0:T(8,128)}, f32[24,128]{1,0:T(8,128)}) custom-call(bf16[3,2,4,64,2048]{4,3,2,1,0:T(8,128)(2,1)} %bitcast.255, bf16[4,64,2048]{2,1,0:T(8,128)(2,1)} %bitcast.256, bf16[1024,1536]{1,0:T(8,128)(2,1)} %bitcast.259, bf16[1024,512]{1,0:T(8,128)(2,1)} %bitcast.239, bf16[1536,2048]{1,0:T(8,128)(2,1)} %bitcast.254, ...), custom_call_target="tpu_custom_call" | custom-call | tf_op jit(solution)/shard_map/pallas_call | solution.py:1276
  754.3 1.2 slice_bitcast_fusion.11
  755.5 1.2 slice.228
  756.7 1.3 slice.229
  759.4 1.3 slice.232
  760.7 3.0 fusion.8
  763.7 1.4 slice_bitcast_fusion.7
  766.0 1.3 copy.137
  (233 shorter events, 30.7 us)
Async XLA Ops:
  7.2 6.1 copy-start.57
  7.2 6.1 copy-start.58
  7.2 6.1 copy-start.59
  7.2 6.1 copy-start.60
  7.2 6.2 copy-start.26
  7.2 6.2 copy-start.27
  7.2 6.2 copy-start.28
  7.3 6.2 copy-start.7
  7.3 6.2 copy-start.29
  7.3 128.9 %all-gather.3.cloned.1.call-start = ((), (), s32[]{:S(2)}) async-start(), calls=%async_computation.2 | async-start | bytes 2621440 | tf_op jit(solution)/shard_map/all_gather | solution.py:1319
  10.5 2.9 copy-start.55
  88.5 1.9 copy-start.53
  91.3 245.0 %all-gather.5.cloned.1.call-start = ((), (), s32[]{:S(2)}) async-start(), calls=%async_computation.3 | async-start | bytes 10813440 | tf_op jit(solution)/shard_map/all_gather | solution.py:1471
  91.9 3.5 copy-start.36
  99.4 3.9 copy-start.40
  99.5 7.9 %copy-start.49 = (bf16[176,2048]{1,0:T(8,128)(2,1)S(1)}, bf16[176,2048]{1,0:T(8,128)(2,1)}, u32[]{:S(2)}) copy-start(bf16[176,2048]{1,0:T(8,128)(2,1)} %param.32) | copy-start | bytes 2162692
  99.5 7.8 %copy-start.50 = (bf16[176,2048]{1,0:T(8,128)(2,1)S(1)}, bf16[176,2048]{1,0:T(8,128)(2,1)}, u32[]{:S(2)}) copy-start(bf16[176,2048]{1,0:T(8,128)(2,1)} %param.31) | copy-start | bytes 2162692
  99.5 7.8 %copy-start.51 = (bf16[176,2048]{1,0:T(8,128)(2,1)S(1)}, bf16[176,2048]{1,0:T(8,128)(2,1)}, u32[]{:S(2)}) copy-start(bf16[176,2048]{1,0:T(8,128)(2,1)} %param.33) | copy-start | bytes 2162692
  121.3 51.5 %copy-start = (bf16[1024,1536]{1,0:T(8,128)(2,1)}, bf16[1024,1536]{1,0:T(8,128)(2,1)S(1)}, u32[]{:S(2)}) copy-start(bf16[1024,1536]{1,0:T(8,128)(2,1)S(1)} %get-tuple-element.244) | copy-start | bytes 9437188
  172.8 418.8 %reduce-scatter.3.cloned.1.call-start = ((), (), s32[]{:S(2)}) async-start(), calls=%async_computation.4 | async-start | bytes 10813440 | tf_op jit(solution)/shard_map/reduce_scatter | solution.py:1518
  176.0 21.5 %collective-permute-start.1 = (bf16[4,4,64,512]{3,2,1,0:T(8,128)(2,1)}, bf16[4,4,64,512]{3,2,1,0:T(8,128)(2,1)}, u32[]{:S(2)}, u32[]{:S(2)}) collective-permute-start(bf16[4,4,64,512]{3,2,1,0:T(8,128)(2,1)} %reshape_squeeze.6), channel_id=1, source_target_pairs={{0,1},{1,0},{2,3},{3,2},{4,5},{5,4},{6,7},{7,6},{8,9},{9,8},{10,11... | collective-permute-start | bytes 3145736 | tf_op jit(solution)/shard_map/ppermute | solution.py:1316
  176.3 43.6 %collective-permute-start = (bf16[4,64,2048]{2,1,0:T(8,128)(2,1)S(1)}, bf16[4,64,2048]{2,1,0:T(8,128)(2,1)}, u32[]{:S(2)}, u32[]{:S(2)}) collective-permute-start(bf16[4,64,2048]{2,1,0:T(8,128)(2,1)S(1)} %get-tuple-element.214), channel_id=1, source_target_pairs={{0,1},{1,0},{2,3},{3,2},{4,5},{5,4},{6,7},{7,6},{8,9},{9,8},{10,11... | collective-permute-start | bytes 3145736 | tf_op jit(solution)/shard_map/ppermute | solution.py:1316
  199.7 44.0 %copy-start.45 = (bf16[4,4,2,64,512]{4,3,2,1,0:T(8,128)(2,1)}, bf16[4,4,2,64,512]{4,3,2,1,0:T(8,128)(2,1)S(1)}, u32[]{:S(2)}) copy-start(bf16[4,4,2,64,512]{4,3,2,1,0:T(8,128)(2,1)S(1)} %copy.97) | copy-start | bytes 6291460
  199.7 23.0 %copy-start.34 = (bf16[1024,2048]{1,0:T(8,128)(2,1)S(1)}, bf16[1024,2048]{1,0:T(8,128)(2,1)}, u32[]{:S(2)}) copy-start(bf16[1024,2048]{1,0:T(8,128)(2,1)} %fusion.1) | copy-start | bytes 12582916
  222.7 3.7 copy-start.2
  222.7 3.7 copy-start.4
  222.7 3.7 copy-start.6
  243.7 4.3 copy-start.12
  243.7 4.3 copy-start.30
  243.7 4.3 copy-start.8
  335.0 1.3 copy-start.9
  363.3 18.1 %copy-start.32 = (bf16[2048,704]{1,0:T(8,128)(2,1)}, bf16[2048,704]{1,0:T(8,128)(2,1)S(1)}, u32[]{:S(2)}) copy-start(bf16[2048,704]{1,0:T(8,128)(2,1)S(1)} %get-tuple-element.92.product) | copy-start | bytes 8650756
  363.3 11.5 %copy-start.61 = (bf16[8,256,2048]{2,1,0:T(8,128)(2,1)S(1)}, bf16[8,256,2048]{2,1,0:T(8,128)(2,1)}, u32[]{:S(2)}) copy-start(bf16[8,256,2048]{2,1,0:T(8,128)(2,1)} %get-tuple-element.86) | copy-start | bytes 25165828
  363.3 11.5 %copy-start.63 = (bf16[2048,704]{1,0:T(8,128)(2,1)S(1)}, bf16[2048,704]{1,0:T(8,128)(2,1)}, u32[]{:S(2)}) copy-start(bf16[2048,704]{1,0:T(8,128)(2,1)} %get-tuple-element.93.grad_gate) | copy-start | bytes 8650756
  363.3 18.1 %slice-start = ((s8[8388608]{0:T(1024)(128)(4,1)}), s8[4194304]{0:T(1024)(128)(4,1)S(1)}, s32[]{:S(2)}) async-start(s8[8388608]{0:T(1024)(128)(4,1)} %bitcast.285), calls=%async_computation.6 | async-start | bytes 8388608
  374.8 6.6 slice-start.1
  391.9 241.5 %reduce-scatter.5.cloned.1.call-start = ((), (), s32[]{:S(2)}) async-start(), calls=%async_computation.5 | async-start | bytes 1310720 | tf_op jit(solution)/shard_map/reduce_scatter | solution.py:1322
  394.1 1.9 copy-start.33
  396.0 26.0 %copy-start.10 = (f32[256,2048]{1,0:T(8,128)S(1)}, f32[256,2048]{1,0:T(8,128)}, u32[]{:S(2)}) copy-start(f32[256,2048]{1,0:T(8,128)} %copy-done.9) | copy-start | bytes 6291460
  422.1 66.2 %copy-start.31 = (bf16[8,128,512]{2,1,0:T(8,128)(2,1)S(1)}, bf16[8,128,512]{2,1,0:T(8,128)(2,1)}, u32[]{:S(2)}) copy-start(bf16[8,128,512]{2,1,0:T(8,128)(2,1)} %copy-done.30) | copy-start | bytes 3145732
  488.2 5.4 copy-start.17
  488.3 7.6 copy-start.62
  493.6 6.4 copy-start.37
  493.7 2.7 copy-start.46
  494.7 29.5 %collective-permute-start.2 = (bf16[4,4,64,512]{3,2,1,0:T(8,128)(2,1)}, bf16[4,4,64,512]{3,2,1,0:T(8,128)(2,1)}, u32[]{:S(2)}, u32[]{:S(2)}) collective-permute-start(bf16[4,4,64,512]{3,2,1,0:T(8,128)(2,1)} %select_bitcast_fusion), channel_id=1, source_target_pairs={{0,1},{1,0},{2,3},{3,2},{4,5},{5,4},{6,7},{7,6},{8,9},{9,8},{10,11... | collective-permute-start | bytes 3145736 | tf_op jit(solution)/shard_map/ppermute | solution.py:1316
  496.4 5.5 copy-start.13
  524.2 4.1 copy-start.44
  524.2 2.7 copy-start.38
  588.9 2.4 copy-start.20
  588.9 2.4 copy-start.22
  591.3 61.2 %collective-permute-start.3 = (bf16[256,2048]{1,0:T(8,128)(2,1)}, bf16[256,2048]{1,0:T(8,128)(2,1)}, u32[]{:S(2)}, u32[]{:S(2)}) collective-permute-start(bf16[256,2048]{1,0:T(8,128)(2,1)} %slice_bitcast_fusion.4), channel_id=1, source_target_pairs={{0,1},{1,0},{2,3},{3,2},{4,5},{5,4},{6,7},{7,6},{8,9},{9,8},{10,11... | collective-permute-start | bytes 3145736 | tf_op jit(solution)/shard_map/ppermute | solution.py:1316
  597.2 27.6 %copy-start.35 = (bf16[1024,2048]{1,0:T(8,128)(2,1)S(1)}, bf16[1024,2048]{1,0:T(8,128)(2,1)}, u32[]{:S(2)}) copy-start(bf16[1024,2048]{1,0:T(8,128)(2,1)} %fusion.1) | copy-start | bytes 12582916
  624.8 2.0 copy-start.42
  624.8 2.7 copy-start.54
  624.8 3.6 copy-start.23
  627.7 3.4 copy-start.43
  631.0 6.0 copy-start.41
  634.5 13.9 %collective-permute-start.4 = (bf16[64,512]{1,0:T(8,128)(2,1)S(1)}, bf16[64,512]{1,0:T(8,128)(2,1)S(1)}, u32[]{:S(2)}, u32[]{:S(2)}) collective-permute-start(bf16[64,512]{1,0:T(8,128)(2,1)S(1)} %get-tuple-element.235), channel_id=1, source_target_pairs={{0,24},{8,16},{16,8},{24,0},{1,25},{9,17},{17,9},{25,1},{2,26},{10... | collective-permute-start | bytes 196616 | tf_op jit(solution)/shard_map/ppermute | solution.py:1327
  636.6 11.8 %collective-permute-start.5 = (bf16[64,512]{1,0:T(8,128)(2,1)S(1)}, bf16[64,512]{1,0:T(8,128)(2,1)S(1)}, u32[]{:S(2)}, u32[]{:S(2)}) collective-permute-start(bf16[64,512]{1,0:T(8,128)(2,1)S(1)} %get-tuple-element.234), channel_id=1, source_target_pairs={{0,16},{8,24},{16,0},{24,8},{1,17},{9,25},{17,1},{25,9},{2,18},{10... | collective-permute-start | bytes 196616 | tf_op jit(solution)/shard_map/ppermute | solution.py:1327
  636.9 11.5 %collective-permute-start.6 = (bf16[64,512]{1,0:T(8,128)(2,1)S(1)}, bf16[64,512]{1,0:T(8,128)(2,1)S(1)}, u32[]{:S(2)}, u32[]{:S(2)}) collective-permute-start(bf16[64,512]{1,0:T(8,128)(2,1)S(1)} %get-tuple-element.233), channel_id=1, source_target_pairs={{0,8},{8,0},{16,24},{24,16},{1,9},{9,1},{17,25},{25,17},{2,10},{10... | collective-permute-start | bytes 196616 | tf_op jit(solution)/shard_map/ppermute | solution.py:1327
  652.5 108.1 %copy-start.11 = (f32[256,2048]{1,0:T(8,128)S(1)}, f32[256,2048]{1,0:T(8,128)}, u32[]{:S(2)}) copy-start(f32[256,2048]{1,0:T(8,128)} %copy-done.9) | copy-start | bytes 6291460
  652.5 108.1 %copy-start.56 = (f32[256]{0:T(256)S(1)}, f32[256]{0:T(256)}, u32[]{:S(2)}) copy-start(f32[256]{0:T(256)} %copy-done.55) | copy-start | bytes 3076
  758.8 4.9 copy-start.48
  763.7 2.3 copy-start.47
  (13 other events, 14.0 us)
Sparse Core Ops, SparseCore 0:
  91.5 44.6 all-gather.2
  172.9 159.1 all-gather.4
  392.0 153.8 reduce-scatter.2
  594.0 26.2 reduce-scatter.4

commit v6 on v5

--- a/solution.py
+++ b/solution.py
@@ -1098,12 +1098,8 @@
             recv_sem=down_r.at[m, b], device_id=below, device_id_type=pl.DeviceIdType.MESH,
         )
 
-    def start_x(i, carry):
-        for m in range(3):
-            across(m, block_of(i)).start()
-        return carry
-
-    lax.fori_loop(0, outer, start_x, 0)
+    for m in range(3):
+        across(m, block_of(0)).start()
     operands = [
         pltpu.make_async_copy(src, dst, load.at[4 + n])
         for n, (src, dst) in enumerate(
@@ -1174,6 +1170,11 @@
         for m in (3, 0, 1, 2):
             if m < 3:
                 across(m, b).wait()
+
+                @pl.when(i + 1 < outer)
+                def _():
+                    across(m, block_of(i + 1)).start()
+
                 add_into(m, b, from_x)
 
             @pl.when(b > z)
@@ -1229,6 +1230,7 @@
         )
 
     everyone(seq, dp, lambda r, where: push(r, where).start())
+    lax.fori_loop(outer - 1, outer, reduce_block, 0)
     out_small[...] = to_all[me]
 
     def add_small(r, where):
@@ -1236,7 +1238,6 @@
         out_small[...] += from_all[r]
 
     everyone(seq, dp, add_small)
-    lax.fori_loop(outer - 1, outer, reduce_block, 0)
     for m in range(4):
         out[m] = total[m, z].astype(F32)
 

time: 788 us -> 787 us (level)
  no operation moved by 1% of the time
where the time goes in v6:
time: 787 us; the launch traced here: 774 us
  Pallas kernels  534 us (68%)
  matrix products  76.6 us (10%)
  local copies, waits for them, and re-layouts  55.1 us (7%)
  waiting for transfers between devices  54.1 us (7%)
  other arithmetic  33.1 us (4%)
  between operations  15 us (2%)
    pallas_call x1, Pallas kernels, finish(): pl.pallas_call(functools.partial(final_kernel, outer, dp), in_specs=[in_h...  102 us
    pallas_call x2, Pallas kernels, relay(): pl.pallas_call(functools.partial(relay_kernel, outer, backward), in_specs...  94 us
    pallas_call x1, Pallas kernels, middle(): pl.pallas_call(middle_kernel, in_specs=[in_vmem()] * 4, out_specs=[in_vme...  86.9 us
    dot_general x15, matrix products, mm(): lax.dot_general(a.astype(BF16), b.astype(BF16), (((ca,), (cb,)), ((), ())...  76.6 us
    pallas_call x1, Pallas kernels, gather_all(): pl.pallas_call(functools.partial(gather_kernel, outer, dp), in_specs=[in_...  75 us
    pallas_call x1, Pallas kernels, middle_back(): pl.pallas_call(middle_back_kernel, in_specs=[in_vmem()] * 4, out_specs=[i...  66.1 us
    pallas_call x3, Pallas kernels, per_sequence(): pl.pallas_call(kernel, grid=(count,), in_specs=[spec(x.shape, at) for x,...  57.7 us
    pallas_call x2, Pallas kernels, feed_tiles(): pl.pallas_call(kernel, grid=(rows // step,), in_specs=[spec(x.shape[1]) f...  53 us
  transfers between devices with their start and end apart: 11, of which 3 were waited for; matrix products, arithmetic and copies ran while one was open for 12% of the time, Pallas kernels for 38%

profile of v6, /device:TPU:21, one launch (start us, length us, event | category | flops | bytes accessed | tf_op | source)
XLA Modules:
  0.0 774.0 jit_solution(10716230262917374478)
XLA Ops:
  10.5 2.8 convert_multiply_fusion
  13.5 75.0 %shard_map.288 = (bf16[3,2,4,64,2048]{4,3,2,1,0:T(8,128)(2,1)}, bf16[4,64,512]{2,1,0:T(8,128)(2,1)S(1)}, bf16[4,256,2048]{2,1,0:T(8,128)(2,1)}, bf16[4,256,2048]{2,1,0:T(8,128)(2,1)}, bf16[32,16,128]{2,1,0:T(8,128)(2,1)S(1)}) custom-call(bf16[64,2048]{1,0:T(8,128)(2,1)S(1)} %copy-done.26, bf16[64,2048]{1,0:T(8,128)(2,1)S(1)} %copy-done.27, ...), custom_call_target="tpu_custom_call" | custom-call | tf_op jit(solution)/shard_map/pallas_call | solution.py:587
  91.9 3.2 multiply_reduce_fusion
  95.4 3.0 fusion.1
  99.5 3.7 convolution_convert_fusion.8
  103.2 1.2 exponential-minus-one_negate_fusion
  104.4 1.9 copy.93
  107.4 1.6 pad_maximum_fusion.1
  109.0 12.3 %fusion.2 = (bf16[1024,1536]{1,0:T(8,128)(2,1)S(1)}, f32[1024,1536]{1,0:T(8,128)}) fusion(pred[1536]{0:T(1024)(128)(4,1)S(1)} %iota_compare_fusion, bf16[1024,2048]{1,0:T(8,128)(2,1)} %fusion.1, bf16[1536,2048]{1,0:T(8,128)(2,1)} %bitcast.253), kind=kOutput, calls=%fused_computation.7 | convolution fusion | flops 6451888128 | bytes 19924480 | tf_op jit(solution)/shard_map/dot_general | solution.py:21
  121.3 14.8 %all-gather.3.cloned.1.call-done = bf16[512,2048]{1,0:T(8,128)(2,1)} async-done(((bf16[128,2048]{1,0:T(8,128)(2,1)}), bf16[512,2048]{1,0:T(8,128)(2,1)}) %all-gather.3.cloned.1.call-update) | async-done | bytes 2097168 | tf_op jit(solution)/shard_map/all_gather | solution.py:1320
  136.1 1.0 copy-done.1
  137.2 1.0 copy-done.3
  138.2 33.5 %shard_map.289 = (bf16[8,64,1024]{2,1,0:T(8,128)(2,1)S(1)}, f32[2,8,64]{2,1,0:T(8,128)S(1)}) custom-call(bf16[8,128,1536]{2,1,0:T(8,128)(2,1)S(1)} %bitcast.215, f32[8,128,64]{2,1,0:T(8,128)S(1)} %bitcast.224, f32[8,128,64]{2,1,0:T(8,128)S(1)} %bitcast.228), custom_call_target="tpu_custom_call" | custom-call | tf_op jit(solution)/shard_map/pallas_call | solution.py:835
  172.8 1.7 slice_bitcast_fusion.2
  174.6 1.5 reshape_squeeze.6
  176.3 1.2 collective-permute-start
  178.5 18.9 %collective-permute-done.1 = bf16[4,4,64,512]{3,2,1,0:T(8,128)(2,1)} collective-permute-done((bf16[4,4,64,512]{3,2,1,0:T(8,128)(2,1)}, bf16[4,4,64,512]{3,2,1,0:T(8,128)(2,1)}, u32[]{:S(2)}, u32[]{:S(2)}) %collective-permute-start.1) | collective-permute-done | bytes 1048608 | tf_op jit(solution)/shard_map/ppermute | solution.py:1317
  197.5 1.3 slice_bitcast_fusion.6
  199.7 20.2 %collective-permute-done = bf16[4,64,2048]{2,1,0:T(8,128)(2,1)} collective-permute-done((bf16[4,64,2048]{2,1,0:T(8,128)(2,1)S(1)}, bf16[4,64,2048]{2,1,0:T(8,128)(2,1)}, u32[]{:S(2)}, u32[]{:S(2)}) %collective-permute-start) | collective-permute-done | bytes 1048608 | tf_op jit(solution)/shard_map/ppermute | solution.py:1317
  219.9 1.4 pad_maximum_fusion.2
  221.4 1.3 copy-done.39
  222.7 3.7 fusion.35.gate_ref
  226.4 15.9 %shard_map.290 = (bf16[8,128,512]{2,1,0:T(8,128)(2,1)S(1)}, f32[8,128,512]{2,1,0:T(8,128)S(1)}, f32[8,128,64]{2,1,0:T(8,128)S(1)}) custom-call(bf16[8,128,1536]{2,1,0:T(8,128)(2,1)} %bitcast.216, bf16[8,128,1536]{2,1,0:T(8,128)(2,1)} %bitcast.217, bf16[8,128,1536]{2,1,0:T(8,128)(2,1)} %bitcast.218, f32[8,128,512]{2,1,0:T(8,128)} %fusion.35.gate_ref, ...), custom_call_target="tpu_custom_call" | custom-call | tf_op jit(solution)/shard_map/pallas_call | solution.py:346
  242.4 1.3 copy-done.16
  243.7 4.3 convolution_convert_fusion.1
  248.0 86.9 %shard_map.291 = (f32[256,2048]{1,0:T(8,128)S(1)}, bf16[8,256,2048]{2,1,0:T(8,128)(2,1)}, bf16[8,256,2048]{2,1,0:T(8,128)(2,1)}) custom-call(bf16[4,256,2048]{2,1,0:T(8,128)(2,1)} %bitcast.258, bf16[256,2048]{1,0:T(8,128)(2,1)S(1)} %bitcast.234, f32[1,2048]{1,0:T(1,128)S(1)} %reshape.674.gain, bf16[4,256,2048]{2,1,0:T(8,128)(2,1)} %get-tuple-element.84.extra), custom_call_target="tpu_custom_call" | custom-call | tf_op jit(solution)/shard_map/pallas_call | solution.py:929
  335.0 1.3 copy-done.9
  336.3 27.0 %shard_map.292 = (bf16[2048,704]{1,0:T(8,128)(2,1)S(1)}, bf16[2048,704]{1,0:T(8,128)(2,1)}, bf16[2048,704]{1,0:T(8,128)(2,1)}) custom-call(bf16[2048,2048]{1,0:T(8,128)(2,1)} %bitcast.288, bf16[2048,2048]{1,0:T(8,128)(2,1)} %bitcast.284, bf16[3,704,2048]{2,1,0:T(8,128)(2,1)} %all-gather.5.cloned.1.call-done.w_down.w_act.w_lin, ...), custom_call_target="tpu_custom_call" | custom-call | flops 17716740096 | bytes 42205184 | tf_op jit(solution)/shard_map/pallas_call | solution.py:640
  363.3 11.4 %fusion.5 = bf16[1,704,2048]{2,1,0:T(8,128)(2,1)S(1)} fusion(bf16[2048,704]{1,0:T(8,128)(2,1)} %get-tuple-element.94.grad_lin, bf16[2048,2048]{1,0:T(8,128)(2,1)} %bitcast.289), kind=kOutput, calls=%fused_computation.16 | convolution fusion | flops 5907021824 | bytes 14155776 | tf_op jit(solution)/shard_map/dot_general | solution.py:21
  374.8 6.5 fusion.4
  381.4 6.5 fusion.3
  387.9 4.0 pad_maximum_fusion
  394.2 1.9 copy-done.33
  396.0 26.0 %shard_map.293 = (bf16[2048,2048]{1,0:T(8,128)(2,1)}, bf16[2048,2048]{1,0:T(8,128)(2,1)}) custom-call(bf16[2048,704]{1,0:T(8,128)(2,1)S(1)} %copy-done.33, bf16[2048,704]{1,0:T(8,128)(2,1)} %get-tuple-element.93.grad_gate, bf16[2048,704]{1,0:T(8,128)(2,1)} %get-tuple-element.94.grad_lin, ...), custom_call_target="tpu_custom_call" | custom-call | flops 17716740096 | bytes 42205184 | tf_op jit(solution)/shard_map/pallas_call | solution.py:640
  422.1 66.1 %shard_map.294 = (f32[256,2048]{1,0:T(8,128)S(1)}, f32[1,2048]{1,0:T(1,128)S(1)}, bf16[4,256,2048]{2,1,0:T(8,128)(2,1)}) custom-call(bf16[8,256,2048]{2,1,0:T(8,128)(2,1)} %bitcast.248, f32[256,2048]{1,0:T(8,128)S(1)} %copy-done.10, f32[256,2048]{1,0:T(8,128)} %get-tuple-element.215.grad_out, f32[1,2048]{1,0:T(1,128)S(1)} %reshape.674.gain), custom_call_target="tpu_custom_call" | custom-call | tf_op jit(solution)/shard_map/pallas_call | solution.py:1034
  488.3 5.4 convolution_convert_fusion.6
  493.7 1.1 select_bitcast_fusion
  494.7 1.1 collective-permute-start.2
  496.4 3.7 fusion.36.grad_mixed_ref
  501.9 14.4 %shard_map.295 = (bf16[8,128,512]{2,1,0:T(8,128)(2,1)S(1)}, bf16[8,128,512]{2,1,0:T(8,128)(2,1)S(1)}, f32[8,128,64]{2,1,0:T(8,128)S(1)}, f32[8,64,1024]{2,1,0:T(8,128)}, f32[8,1,512]{2,1,0:T(1,128)S(1)}) custom-call(f32[8,128,512]{2,1,0:T(8,128)} %fusion.36.grad_mixed_ref, f32[8,128,512]{2,1,0:T(8,128)} %fusion.35.gate_ref, f32[8,128,512]{2,1,0:T(8,128)} %copy-done.16, ...), custom_call_target="tpu_custom_call" | custom-call | tf_op jit(solution)/shard_map/pallas_call | solution.py:346
  519.3 4.9 convolution_convert_fusion.5
  524.2 2.1 fusion.31
  526.9 1.4 fusion.10
  528.4 60.5 %shard_map.296 = (bf16[8,64,1024]{2,1,0:T(8,128)(2,1)S(1)}, bf16[2,256,2048]{2,1,0:T(8,128)(2,1)S(1)}, bf16[256,2048]{1,0:T(8,128)(2,1)S(1)}) custom-call(f32[8,64,1024]{2,1,0:T(8,128)} %get-tuple-element.104.refs_0_, f32[2,8,64]{2,1,0:T(8,128)S(1)} %get-tuple-element.105.refs_1_, bf16[8,256,2048]{2,1,0:T(8,128)(2,1)} %bitcast.247, ...), custom_call_target="tpu_custom_call" | custom-call | tf_op jit(solution)/shard_map/pallas_call | solution.py:835
  588.9 1.3 copy-done.15
  590.2 1.1 slice_bitcast_fusion.4
  591.6 2.3 copy.102
  594.9 1.2 copy-done.19
  597.2 27.4 %shard_map.297 = (bf16[8,128,1536]{2,1,0:T(8,128)(2,1)}, bf16[8,128,64]{2,1,0:T(8,128)(2,1)S(1)}) custom-call(bf16[8,128,512]{2,1,0:T(8,128)(2,1)S(1)} %copy-done.19, f32[8,128,64]{2,1,0:T(8,128)S(1)} %copy-done.25, f32[8,128,64]{2,1,0:T(8,128)S(1)} %copy-done.13, bf16[8,128,1536]{2,1,0:T(8,128)(2,1)} %bitcast.221, bf16[8,128,1536]{2,1,0:T(8,128)(2,1)} %bitcast.222, ...), custom_call_target="tpu_custom_call" | custom-call | tf_op jit(solution)/shard_map/pallas_call | solution.py:346
  624.8 1.3 fusion.37
  628.4 2.6 add_convert_fusion
  631.0 2.4 bitcast_convert_fusion
  633.4 1.1 dynamic-slice_bitcast_fusion
  634.5 2.1 collective-permute-start.4
  637.1 11.3 %convolution_convert_fusion = bf16[1536,2048]{1,0:T(8,128)(2,1)} fusion(bf16[1024,1536]{1,0:T(8,128)(2,1)S(1)} %bitcast.260, bf16[1024,2048]{1,0:T(8,128)(2,1)} %fusion.1), kind=kOutput, calls=%fused_computation.6 | convolution fusion | flops 6445596672 | bytes 13631488 | tf_op jit(solution)/shard_map/dot_general | solution.py:21
  650.8 1.8 reshape.677
  652.6 101.7 %shard_map.298 = (f32[4,64,2048]{2,1,0:T(8,128)}, f32[256,2048]{1,0:T(8,128)}, f32[24,128]{1,0:T(8,128)}) custom-call(bf16[3,2,4,64,2048]{4,3,2,1,0:T(8,128)(2,1)} %bitcast.255, bf16[4,64,2048]{2,1,0:T(8,128)(2,1)} %bitcast.256, bf16[1024,1536]{1,0:T(8,128)(2,1)} %bitcast.259, bf16[1024,512]{1,0:T(8,128)(2,1)} %bitcast.239, bf16[1536,2048]{1,0:T(8,128)(2,1)} %bitcast.254, ...), custom_call_target="tpu_custom_call" | custom-call | tf_op jit(solution)/shard_map/pallas_call | solution.py:1277
  754.2 1.2 slice_bitcast_fusion.11
  755.4 1.2 slice.228
  756.6 1.3 slice.229
  759.3 1.3 slice.232
  760.6 3.0 fusion.8
  763.6 1.4 slice_bitcast_fusion.7
  765.9 1.3 copy.137
  (233 shorter events, 30.7 us)
Async XLA Ops:
  7.2 6.1 copy-start.57
  7.2 6.1 copy-start.58
  7.2 6.1 copy-start.59
  7.2 6.1 copy-start.60
  7.2 6.2 copy-start.26
  7.2 6.2 copy-start.27
  7.2 6.2 copy-start.28
  7.3 6.2 copy-start.7
  7.3 6.2 copy-start.29
  7.3 128.9 %all-gather.3.cloned.1.call-start = ((), (), s32[]{:S(2)}) async-start(), calls=%async_computation.2 | async-start | bytes 2621440 | tf_op jit(solution)/shard_map/all_gather | solution.py:1320
  10.5 2.9 copy-start.55
  88.5 1.9 copy-start.53
  91.3 245.0 %all-gather.5.cloned.1.call-start = ((), (), s32[]{:S(2)}) async-start(), calls=%async_computation.3 | async-start | bytes 10813440 | tf_op jit(solution)/shard_map/all_gather | solution.py:1472
  91.9 3.5 copy-start.36
  99.4 3.9 copy-start.40
  99.5 7.9 %copy-start.49 = (bf16[176,2048]{1,0:T(8,128)(2,1)S(1)}, bf16[176,2048]{1,0:T(8,128)(2,1)}, u32[]{:S(2)}) copy-start(bf16[176,2048]{1,0:T(8,128)(2,1)} %param.32) | copy-start | bytes 2162692
  99.5 7.8 %copy-start.50 = (bf16[176,2048]{1,0:T(8,128)(2,1)S(1)}, bf16[176,2048]{1,0:T(8,128)(2,1)}, u32[]{:S(2)}) copy-start(bf16[176,2048]{1,0:T(8,128)(2,1)} %param.31) | copy-start | bytes 2162692
  99.5 7.8 %copy-start.51 = (bf16[176,2048]{1,0:T(8,128)(2,1)S(1)}, bf16[176,2048]{1,0:T(8,128)(2,1)}, u32[]{:S(2)}) copy-start(bf16[176,2048]{1,0:T(8,128)(2,1)} %param.33) | copy-start | bytes 2162692
  121.3 51.5 %copy-start = (bf16[1024,1536]{1,0:T(8,128)(2,1)}, bf16[1024,1536]{1,0:T(8,128)(2,1)S(1)}, u32[]{:S(2)}) copy-start(bf16[1024,1536]{1,0:T(8,128)(2,1)S(1)} %get-tuple-element.244) | copy-start | bytes 9437188
  172.8 418.8 %reduce-scatter.3.cloned.1.call-start = ((), (), s32[]{:S(2)}) async-start(), calls=%async_computation.4 | async-start | bytes 10813440 | tf_op jit(solution)/shard_map/reduce_scatter | solution.py:1519
  176.0 21.5 %collective-permute-start.1 = (bf16[4,4,64,512]{3,2,1,0:T(8,128)(2,1)}, bf16[4,4,64,512]{3,2,1,0:T(8,128)(2,1)}, u32[]{:S(2)}, u32[]{:S(2)}) collective-permute-start(bf16[4,4,64,512]{3,2,1,0:T(8,128)(2,1)} %reshape_squeeze.6), channel_id=1, source_target_pairs={{0,1},{1,0},{2,3},{3,2},{4,5},{5,4},{6,7},{7,6},{8,9},{9,8},{10,11... | collective-permute-start | bytes 3145736 | tf_op jit(solution)/shard_map/ppermute | solution.py:1317
  176.3 43.6 %collective-permute-start = (bf16[4,64,2048]{2,1,0:T(8,128)(2,1)S(1)}, bf16[4,64,2048]{2,1,0:T(8,128)(2,1)}, u32[]{:S(2)}, u32[]{:S(2)}) collective-permute-start(bf16[4,64,2048]{2,1,0:T(8,128)(2,1)S(1)} %get-tuple-element.214), channel_id=1, source_target_pairs={{0,1},{1,0},{2,3},{3,2},{4,5},{5,4},{6,7},{7,6},{8,9},{9,8},{10,11... | collective-permute-start | bytes 3145736 | tf_op jit(solution)/shard_map/ppermute | solution.py:1317
  199.7 44.0 %copy-start.45 = (bf16[4,4,2,64,512]{4,3,2,1,0:T(8,128)(2,1)}, bf16[4,4,2,64,512]{4,3,2,1,0:T(8,128)(2,1)S(1)}, u32[]{:S(2)}) copy-start(bf16[4,4,2,64,512]{4,3,2,1,0:T(8,128)(2,1)S(1)} %copy.97) | copy-start | bytes 6291460
  199.7 23.0 %copy-start.34 = (bf16[1024,2048]{1,0:T(8,128)(2,1)S(1)}, bf16[1024,2048]{1,0:T(8,128)(2,1)}, u32[]{:S(2)}) copy-start(bf16[1024,2048]{1,0:T(8,128)(2,1)} %fusion.1) | copy-start | bytes 12582916
  222.7 3.7 copy-start.2
  222.7 3.7 copy-start.4
  222.7 3.7 copy-start.6
  243.7 4.3 copy-start.12
  243.7 4.3 copy-start.30
  243.7 4.3 copy-start.8
  335.0 1.3 copy-start.9
  363.3 18.1 %copy-start.32 = (bf16[2048,704]{1,0:T(8,128)(2,1)}, bf16[2048,704]{1,0:T(8,128)(2,1)S(1)}, u32[]{:S(2)}) copy-start(bf16[2048,704]{1,0:T(8,128)(2,1)S(1)} %get-tuple-element.92.product) | copy-start | bytes 8650756
  363.3 11.5 %copy-start.61 = (bf16[8,256,2048]{2,1,0:T(8,128)(2,1)S(1)}, bf16[8,256,2048]{2,1,0:T(8,128)(2,1)}, u32[]{:S(2)}) copy-start(bf16[8,256,2048]{2,1,0:T(8,128)(2,1)} %get-tuple-element.86) | copy-start | bytes 25165828
  363.3 11.5 %copy-start.63 = (bf16[2048,704]{1,0:T(8,128)(2,1)S(1)}, bf16[2048,704]{1,0:T(8,128)(2,1)}, u32[]{:S(2)}) copy-start(bf16[2048,704]{1,0:T(8,128)(2,1)} %get-tuple-element.93.grad_gate) | copy-start | bytes 8650756
  363.3 18.1 %slice-start = ((s8[8388608]{0:T(1024)(128)(4,1)}), s8[4194304]{0:T(1024)(128)(4,1)S(1)}, s32[]{:S(2)}) async-start(s8[8388608]{0:T(1024)(128)(4,1)} %bitcast.285), calls=%async_computation.6 | async-start | bytes 8388608
  374.8 6.6 slice-start.1
  391.9 241.5 %reduce-scatter.5.cloned.1.call-start = ((), (), s32[]{:S(2)}) async-start(), calls=%async_computation.5 | async-start | bytes 1310720 | tf_op jit(solution)/shard_map/reduce_scatter | solution.py:1323
  394.1 1.9 copy-start.33
  396.0 26.0 %copy-start.10 = (f32[256,2048]{1,0:T(8,128)S(1)}, f32[256,2048]{1,0:T(8,128)}, u32[]{:S(2)}) copy-start(f32[256,2048]{1,0:T(8,128)} %copy-done.9) | copy-start | bytes 6291460
  422.1 66.2 %copy-start.31 = (bf16[8,128,512]{2,1,0:T(8,128)(2,1)S(1)}, bf16[8,128,512]{2,1,0:T(8,128)(2,1)}, u32[]{:S(2)}) copy-start(bf16[8,128,512]{2,1,0:T(8,128)(2,1)} %copy-done.30) | copy-start | bytes 3145732
  488.2 5.4 copy-start.17
  488.3 7.6 copy-start.62
  493.6 6.4 copy-start.37
  493.7 2.7 copy-start.46
  494.7 29.5 %collective-permute-start.2 = (bf16[4,4,64,512]{3,2,1,0:T(8,128)(2,1)}, bf16[4,4,64,512]{3,2,1,0:T(8,128)(2,1)}, u32[]{:S(2)}, u32[]{:S(2)}) collective-permute-start(bf16[4,4,64,512]{3,2,1,0:T(8,128)(2,1)} %select_bitcast_fusion), channel_id=1, source_target_pairs={{0,1},{1,0},{2,3},{3,2},{4,5},{5,4},{6,7},{7,6},{8,9},{9,8},{10,11... | collective-permute-start | bytes 3145736 | tf_op jit(solution)/shard_map/ppermute | solution.py:1317
  496.4 5.5 copy-start.13
  524.2 4.1 copy-start.44
  524.2 2.7 copy-start.38
  588.9 2.4 copy-start.20
  588.9 2.4 copy-start.22
  591.3 61.2 %collective-permute-start.3 = (bf16[256,2048]{1,0:T(8,128)(2,1)}, bf16[256,2048]{1,0:T(8,128)(2,1)}, u32[]{:S(2)}, u32[]{:S(2)}) collective-permute-start(bf16[256,2048]{1,0:T(8,128)(2,1)} %slice_bitcast_fusion.4), channel_id=1, source_target_pairs={{0,1},{1,0},{2,3},{3,2},{4,5},{5,4},{6,7},{7,6},{8,9},{9,8},{10,11... | collective-permute-start | bytes 3145736 | tf_op jit(solution)/shard_map/ppermute | solution.py:1317
  597.2 27.6 %copy-start.35 = (bf16[1024,2048]{1,0:T(8,128)(2,1)S(1)}, bf16[1024,2048]{1,0:T(8,128)(2,1)}, u32[]{:S(2)}) copy-start(bf16[1024,2048]{1,0:T(8,128)(2,1)} %fusion.1) | copy-start | bytes 12582916
  624.8 2.0 copy-start.42
  624.8 2.7 copy-start.54
  624.8 3.6 copy-start.23
  627.7 3.4 copy-start.43
  631.0 6.0 copy-start.41
  634.5 13.9 %collective-permute-start.4 = (bf16[64,512]{1,0:T(8,128)(2,1)S(1)}, bf16[64,512]{1,0:T(8,128)(2,1)S(1)}, u32[]{:S(2)}, u32[]{:S(2)}) collective-permute-start(bf16[64,512]{1,0:T(8,128)(2,1)S(1)} %get-tuple-element.235), channel_id=1, source_target_pairs={{0,24},{8,16},{16,8},{24,0},{1,25},{9,17},{17,9},{25,1},{2,26},{10... | collective-permute-start | bytes 196616 | tf_op jit(solution)/shard_map/ppermute | solution.py:1328
  636.6 11.8 %collective-permute-start.5 = (bf16[64,512]{1,0:T(8,128)(2,1)S(1)}, bf16[64,512]{1,0:T(8,128)(2,1)S(1)}, u32[]{:S(2)}, u32[]{:S(2)}) collective-permute-start(bf16[64,512]{1,0:T(8,128)(2,1)S(1)} %get-tuple-element.234), channel_id=1, source_target_pairs={{0,16},{8,24},{16,0},{24,8},{1,17},{9,25},{17,1},{25,9},{2,18},{10... | collective-permute-start | bytes 196616 | tf_op jit(solution)/shard_map/ppermute | solution.py:1328
  636.9 11.5 %collective-permute-start.6 = (bf16[64,512]{1,0:T(8,128)(2,1)S(1)}, bf16[64,512]{1,0:T(8,128)(2,1)S(1)}, u32[]{:S(2)}, u32[]{:S(2)}) collective-permute-start(bf16[64,512]{1,0:T(8,128)(2,1)S(1)} %get-tuple-element.233), channel_id=1, source_target_pairs={{0,8},{8,0},{16,24},{24,16},{1,9},{9,1},{17,25},{25,17},{2,10},{10... | collective-permute-start | bytes 196616 | tf_op jit(solution)/shard_map/ppermute | solution.py:1328
  652.5 108.0 %copy-start.11 = (f32[256,2048]{1,0:T(8,128)S(1)}, f32[256,2048]{1,0:T(8,128)}, u32[]{:S(2)}) copy-start(f32[256,2048]{1,0:T(8,128)} %copy-done.9) | copy-start | bytes 6291460
  652.5 108.0 %copy-start.56 = (f32[256]{0:T(256)S(1)}, f32[256]{0:T(256)}, u32[]{:S(2)}) copy-start(f32[256]{0:T(256)} %copy-done.55) | copy-start | bytes 3076
  758.7 4.9 copy-start.48
  763.6 2.3 copy-start.47
  (13 other events, 14.0 us)
Sparse Core Ops, SparseCore 0:
  91.5 44.6 all-gather.2
  172.9 159.1 all-gather.4
  392.0 153.8 reduce-scatter.2
  594.0 26.2 reduce-scatter.4

commit v7 on v6

--- a/solution.py
+++ b/solution.py
@@ -1050,12 +1050,11 @@
 
 
 def final_kernel(
-    outer, dp, mats, gates, pre_hbm, gate_hbm, kqv_hbm, g_hbm, grad_rank, w_rank, tok,
+    outer, dp, mats, gates, grad_pre, grad_gate, w_kqv, w_g, grad_rank, w_rank, tok,
     base, gain, small, *refs,
 ):
     out, tokens_grad, out_small, refs = refs[0], refs[1], refs[2], refs[3:]
     (
-        grad_pre, grad_gate, w_kqv, w_g,
         from_x, from_below, from_above, total, parts, from_core, to_y, from_y, gain_grad,
         to_all, from_all,
         load, x_s, x_r, up_s, up_r, down_s, down_r, core_s, core_r, y_s, y_r, all_s, all_r,
@@ -1100,20 +1099,12 @@
 
     for m in range(3):
         across(m, block_of(0)).start()
-    operands = [
-        pltpu.make_async_copy(src, dst, load.at[4 + n])
-        for n, (src, dst) in enumerate(
-            [(pre_hbm, grad_pre), (gate_hbm, grad_gate), (kqv_hbm, w_kqv), (g_hbm, w_g)]
-        )
-    ]
     loads = [
         pltpu.make_async_copy(mats.at[m, 0] if m < 3 else gates, total.at[m], load.at[m])
         for m in range(4)
     ]
-    for copy in operands + loads:
+    for copy in loads:
         copy.start()
-    for copy in operands:
-        copy.wait()
 
     def grad_in(g):
         some = pl.ds(g * rows, rows)
@@ -1276,21 +1267,20 @@
     payload = (small.shape[1] + 8, 128)
     return pl.pallas_call(
         functools.partial(final_kernel, outer, dp),
-        in_specs=[in_hbm()] * (2 + len(operands)) + [in_vmem()] * (len(rest) + 1),
+        in_specs=[in_hbm()] * 2 + [in_vmem()] * (len(operands) + len(rest) + 1),
         out_specs=[in_vmem()] * 3,
         out_shape=[
             jax.ShapeDtypeStruct((4, high, width), F32),
             jax.ShapeDtypeStruct((rows, width), F32),
             jax.ShapeDtypeStruct(payload, F32),
         ],
-        scratch_shapes=[pltpu.VMEM(x.shape, BF16) for x in operands]
-        + [pltpu.VMEM((3, outer, high, width), BF16)]
+        scratch_shapes=[pltpu.VMEM((3, outer, high, width), BF16)]
         + [blocks] * 3
         + [
             pltpu.VMEM((4, rows, width), BF16), pltpu.VMEM((2, rows, width), BF16), buffer,
             buffer, pltpu.VMEM((1, width), F32),
             pltpu.VMEM((devices,) + payload, F32), pltpu.VMEM((devices,) + payload, F32),
-            dma((8,)),
+            dma((4,)),
         ]
         + [dma((4, outer))] * 6
         + [dma((2,))] * 2

time: 787 us -> 786 us (level)
  transfers between devices with their start and end apart: 11 -> 11, of which waited for: 3 -> 3; matrix products, arithmetic and copies ran while one was open for 12% -> 13% of each run, Pallas kernels for 38% -> 38%
where the time goes in v7:
time: 786 us; the launch traced here: 773 us
  Pallas kernels  533 us (68%)
  matrix products  76.6 us (10%)
  local copies, waits for them, and re-layouts  55.1 us (7%)
  waiting for transfers between devices  54.1 us (7%)
  other arithmetic  33.1 us (4%)
  between operations  15 us (2%)
    pallas_call x1, Pallas kernels, finish(): pl.pallas_call(functools.partial(final_kernel, outer, dp), in_specs=[in_h...  101 us
    pallas_call x2, Pallas kernels, relay(): pl.pallas_call(functools.partial(relay_kernel, outer, backward), in_specs...  94 us
    pallas_call x1, Pallas kernels, middle(): pl.pallas_call(middle_kernel, in_specs=[in_vmem()] * 4, out_specs=[in_vme...  86.9 us
    dot_general x15, matrix products, mm(): lax.dot_general(a.astype(BF16), b.astype(BF16), (((ca,), (cb,)), ((), ())...  76.6 us
    pallas_call x1, Pallas kernels, gather_all(): pl.pallas_call(functools.partial(gather_kernel, outer, dp), in_specs=[in_...  75 us
    pallas_call x1, Pallas kernels, middle_back(): pl.pallas_call(middle_back_kernel, in_specs=[in_vmem()] * 4, out_specs=[i...  66.1 us
    pallas_call x3, Pallas kernels, per_sequence(): pl.pallas_call(kernel, grid=(count,), in_specs=[spec(x.shape, at) for x,...  57.7 us
    pallas_call x2, Pallas kernels, feed_tiles(): pl.pallas_call(kernel, grid=(rows // step,), in_specs=[spec(x.shape[1]) f...  53 us
  transfers between devices with their start and end apart: 11, of which 3 were waited for; matrix products, arithmetic and copies ran while one was open for 13% of the time, Pallas kernels for 38%

profile of v7, /device:TPU:21, one launch (start us, length us, event | category | flops | bytes accessed | tf_op | source)
XLA Modules:
  0.0 772.9 jit_solution(8972333157303409995)
XLA Ops:
  10.5 2.8 convert_multiply_fusion
  13.5 75.0 %shard_map.288 = (bf16[3,2,4,64,2048]{4,3,2,1,0:T(8,128)(2,1)}, bf16[4,64,512]{2,1,0:T(8,128)(2,1)S(1)}, bf16[4,256,2048]{2,1,0:T(8,128)(2,1)}, bf16[4,256,2048]{2,1,0:T(8,128)(2,1)}, bf16[32,16,128]{2,1,0:T(8,128)(2,1)S(1)}) custom-call(bf16[64,2048]{1,0:T(8,128)(2,1)S(1)} %copy-done.26, bf16[64,2048]{1,0:T(8,128)(2,1)S(1)} %copy-done.27, ...), custom_call_target="tpu_custom_call" | custom-call | tf_op jit(solution)/shard_map/pallas_call | solution.py:587
  91.9 3.2 multiply_reduce_fusion
  95.4 3.0 fusion.1
  99.5 3.7 convolution_convert_fusion.8
  103.2 1.2 exponential-minus-one_negate_fusion
  104.4 1.9 copy.93
  107.4 1.6 pad_maximum_fusion.1
  109.0 12.3 %fusion.2 = (bf16[1024,1536]{1,0:T(8,128)(2,1)S(1)}, f32[1024,1536]{1,0:T(8,128)}) fusion(pred[1536]{0:T(1024)(128)(4,1)S(1)} %iota_compare_fusion, bf16[1024,2048]{1,0:T(8,128)(2,1)} %fusion.1, bf16[1536,2048]{1,0:T(8,128)(2,1)} %bitcast.253), kind=kOutput, calls=%fused_computation.7 | convolution fusion | flops 6451888128 | bytes 19924480 | tf_op jit(solution)/shard_map/dot_general | solution.py:21
  121.3 14.8 %all-gather.3.cloned.1.call-done = bf16[512,2048]{1,0:T(8,128)(2,1)} async-done(((bf16[128,2048]{1,0:T(8,128)(2,1)}), bf16[512,2048]{1,0:T(8,128)(2,1)}) %all-gather.3.cloned.1.call-update) | async-done | bytes 2097168 | tf_op jit(solution)/shard_map/all_gather | solution.py:1310
  136.1 1.0 copy-done.1
  137.2 1.0 copy-done.3
  138.2 33.5 %shard_map.289 = (bf16[8,64,1024]{2,1,0:T(8,128)(2,1)S(1)}, f32[2,8,64]{2,1,0:T(8,128)S(1)}) custom-call(bf16[8,128,1536]{2,1,0:T(8,128)(2,1)S(1)} %bitcast.215, f32[8,128,64]{2,1,0:T(8,128)S(1)} %bitcast.224, f32[8,128,64]{2,1,0:T(8,128)S(1)} %bitcast.228), custom_call_target="tpu_custom_call" | custom-call | tf_op jit(solution)/shard_map/pallas_call | solution.py:835
  172.8 1.7 slice_bitcast_fusion.2
  174.6 1.5 reshape_squeeze.6
  176.3 1.2 collective-permute-start
  178.5 18.9 %collective-permute-done.1 = bf16[4,4,64,512]{3,2,1,0:T(8,128)(2,1)} collective-permute-done((bf16[4,4,64,512]{3,2,1,0:T(8,128)(2,1)}, bf16[4,4,64,512]{3,2,1,0:T(8,128)(2,1)}, u32[]{:S(2)}, u32[]{:S(2)}) %collective-permute-start.1) | collective-permute-done | bytes 1048608 | tf_op jit(solution)/shard_map/ppermute | solution.py:1307
  197.5 1.3 slice_bitcast_fusion.6
  199.7 20.2 %collective-permute-done = bf16[4,64,2048]{2,1,0:T(8,128)(2,1)} collective-permute-done((bf16[4,64,2048]{2,1,0:T(8,128)(2,1)S(1)}, bf16[4,64,2048]{2,1,0:T(8,128)(2,1)}, u32[]{:S(2)}, u32[]{:S(2)}) %collective-permute-start) | collective-permute-done | bytes 1048608 | tf_op jit(solution)/shard_map/ppermute | solution.py:1307
  219.9 1.4 pad_maximum_fusion.2
  221.4 1.3 copy-done.39
  222.7 3.7 fusion.35.gate_ref
  226.4 15.9 %shard_map.290 = (bf16[8,128,512]{2,1,0:T(8,128)(2,1)S(1)}, f32[8,128,512]{2,1,0:T(8,128)S(1)}, f32[8,128,64]{2,1,0:T(8,128)S(1)}) custom-call(bf16[8,128,1536]{2,1,0:T(8,128)(2,1)} %bitcast.216, bf16[8,128,1536]{2,1,0:T(8,128)(2,1)} %bitcast.217, bf16[8,128,1536]{2,1,0:T(8,128)(2,1)} %bitcast.218, f32[8,128,512]{2,1,0:T(8,128)} %fusion.35.gate_ref, ...), custom_call_target="tpu_custom_call" | custom-call | tf_op jit(solution)/shard_map/pallas_call | solution.py:346
  242.4 1.3 copy-done.16
  243.7 4.3 convolution_convert_fusion.1
  248.0 86.9 %shard_map.291 = (f32[256,2048]{1,0:T(8,128)S(1)}, bf16[8,256,2048]{2,1,0:T(8,128)(2,1)}, bf16[8,256,2048]{2,1,0:T(8,128)(2,1)}) custom-call(bf16[4,256,2048]{2,1,0:T(8,128)(2,1)} %bitcast.258, bf16[256,2048]{1,0:T(8,128)(2,1)S(1)} %bitcast.234, f32[1,2048]{1,0:T(1,128)S(1)} %reshape.674.gain, bf16[4,256,2048]{2,1,0:T(8,128)(2,1)} %get-tuple-element.84.extra), custom_call_target="tpu_custom_call" | custom-call | tf_op jit(solution)/shard_map/pallas_call | solution.py:929
  335.0 1.3 copy-done.9
  336.3 27.0 %shard_map.292 = (bf16[2048,704]{1,0:T(8,128)(2,1)S(1)}, bf16[2048,704]{1,0:T(8,128)(2,1)}, bf16[2048,704]{1,0:T(8,128)(2,1)}) custom-call(bf16[2048,2048]{1,0:T(8,128)(2,1)} %bitcast.288, bf16[2048,2048]{1,0:T(8,128)(2,1)} %bitcast.284, bf16[3,704,2048]{2,1,0:T(8,128)(2,1)} %all-gather.5.cloned.1.call-done.w_down.w_act.w_lin, ...), custom_call_target="tpu_custom_call" | custom-call | flops 17716740096 | bytes 42205184 | tf_op jit(solution)/shard_map/pallas_call | solution.py:640
  363.3 11.4 %fusion.5 = bf16[1,704,2048]{2,1,0:T(8,128)(2,1)S(1)} fusion(bf16[2048,704]{1,0:T(8,128)(2,1)} %get-tuple-element.94.grad_lin, bf16[2048,2048]{1,0:T(8,128)(2,1)} %bitcast.289), kind=kOutput, calls=%fused_computation.16 | convolution fusion | flops 5907021824 | bytes 14155776 | tf_op jit(solution)/shard_map/dot_general | solution.py:21
  374.8 6.5 fusion.4
  381.4 6.5 fusion.3
  387.9 4.0 pad_maximum_fusion
  394.2 1.9 copy-done.33
  396.0 26.0 %shard_map.293 = (bf16[2048,2048]{1,0:T(8,128)(2,1)}, bf16[2048,2048]{1,0:T(8,128)(2,1)}) custom-call(bf16[2048,704]{1,0:T(8,128)(2,1)S(1)} %copy-done.33, bf16[2048,704]{1,0:T(8,128)(2,1)} %get-tuple-element.93.grad_gate, bf16[2048,704]{1,0:T(8,128)(2,1)} %get-tuple-element.94.grad_lin, ...), custom_call_target="tpu_custom_call" | custom-call | flops 17716740096 | bytes 42205184 | tf_op jit(solution)/shard_map/pallas_call | solution.py:640
  422.1 66.1 %shard_map.294 = (f32[256,2048]{1,0:T(8,128)S(1)}, f32[1,2048]{1,0:T(1,128)S(1)}, bf16[4,256,2048]{2,1,0:T(8,128)(2,1)}) custom-call(bf16[8,256,2048]{2,1,0:T(8,128)(2,1)} %bitcast.248, f32[256,2048]{1,0:T(8,128)S(1)} %copy-done.10, f32[256,2048]{1,0:T(8,128)} %get-tuple-element.215.grad_out, f32[1,2048]{1,0:T(1,128)S(1)} %reshape.674.gain), custom_call_target="tpu_custom_call" | custom-call | tf_op jit(solution)/shard_map/pallas_call | solution.py:1034
  488.3 5.4 convolution_convert_fusion.6
  493.7 1.1 select_bitcast_fusion
  494.7 1.1 collective-permute-start.2
  496.4 3.7 fusion.36.grad_mixed_ref
  501.9 14.4 %shard_map.295 = (bf16[8,128,512]{2,1,0:T(8,128)(2,1)S(1)}, bf16[8,128,512]{2,1,0:T(8,128)(2,1)S(1)}, f32[8,128,64]{2,1,0:T(8,128)S(1)}, f32[8,64,1024]{2,1,0:T(8,128)}, f32[8,1,512]{2,1,0:T(1,128)S(1)}) custom-call(f32[8,128,512]{2,1,0:T(8,128)} %fusion.36.grad_mixed_ref, f32[8,128,512]{2,1,0:T(8,128)} %fusion.35.gate_ref, f32[8,128,512]{2,1,0:T(8,128)} %copy-done.16, ...), custom_call_target="tpu_custom_call" | custom-call | tf_op jit(solution)/shard_map/pallas_call | solution.py:346
  519.3 4.9 convolution_convert_fusion.5
  524.2 2.1 fusion.31
  526.9 1.4 fusion.10
  528.4 60.5 %shard_map.296 = (bf16[8,64,1024]{2,1,0:T(8,128)(2,1)S(1)}, bf16[2,256,2048]{2,1,0:T(8,128)(2,1)S(1)}, bf16[256,2048]{1,0:T(8,128)(2,1)S(1)}) custom-call(f32[8,64,1024]{2,1,0:T(8,128)} %get-tuple-element.104.refs_0_, f32[2,8,64]{2,1,0:T(8,128)S(1)} %get-tuple-element.105.refs_1_, bf16[8,256,2048]{2,1,0:T(8,128)(2,1)} %bitcast.247, ...), custom_call_target="tpu_custom_call" | custom-call | tf_op jit(solution)/shard_map/pallas_call | solution.py:835
  588.9 1.3 copy-done.15
  590.2 1.1 slice_bitcast_fusion.4
  591.6 2.3 copy.102
  594.9 1.2 copy-done.19
  597.2 27.4 %shard_map.297 = (bf16[8,128,1536]{2,1,0:T(8,128)(2,1)}, bf16[8,128,64]{2,1,0:T(8,128)(2,1)S(1)}) custom-call(bf16[8,128,512]{2,1,0:T(8,128)(2,1)S(1)} %copy-done.19, f32[8,128,64]{2,1,0:T(8,128)S(1)} %copy-done.25, f32[8,128,64]{2,1,0:T(8,128)S(1)} %copy-done.13, bf16[8,128,1536]{2,1,0:T(8,128)(2,1)} %bitcast.221, bf16[8,128,1536]{2,1,0:T(8,128)(2,1)} %bitcast.222, ...), custom_call_target="tpu_custom_call" | custom-call | tf_op jit(solution)/shard_map/pallas_call | solution.py:346
  624.8 1.3 fusion.37
  628.4 2.6 add_convert_fusion
  631.0 2.4 bitcast_convert_fusion
  633.4 1.1 dynamic-slice_bitcast_fusion
  634.5 2.1 collective-permute-start.4
  637.1 11.3 %convolution_convert_fusion = bf16[1536,2048]{1,0:T(8,128)(2,1)} fusion(bf16[1024,1536]{1,0:T(8,128)(2,1)S(1)} %bitcast.260, bf16[1024,2048]{1,0:T(8,128)(2,1)} %fusion.1), kind=kOutput, calls=%fused_computation.6 | convolution fusion | flops 6445596672 | bytes 13631488 | tf_op jit(solution)/shard_map/dot_general | solution.py:21
  650.8 1.8 reshape.677
  652.6 100.6 %shard_map.298 = (f32[4,64,2048]{2,1,0:T(8,128)}, f32[256,2048]{1,0:T(8,128)}, f32[24,128]{1,0:T(8,128)}) custom-call(bf16[3,2,4,64,2048]{4,3,2,1,0:T(8,128)(2,1)} %bitcast.255, bf16[4,64,2048]{2,1,0:T(8,128)(2,1)} %bitcast.256, bf16[1024,1536]{1,0:T(8,128)(2,1)} %bitcast.259, bf16[1024,512]{1,0:T(8,128)(2,1)} %bitcast.239, bf16[1536,2048]{1,0:T(8,128)(2,1)} %bitcast.254, ...), custom_call_target="tpu_custom_call" | custom-call | tf_op jit(solution)/shard_map/pallas_call | solution.py:1268
  753.1 1.2 slice_bitcast_fusion.11
  754.3 1.2 slice.228
  755.5 1.3 slice.229
  758.2 1.3 slice.232
  759.5 3.0 fusion.8
  762.5 1.4 slice_bitcast_fusion.7
  764.9 1.3 copy.137
  (233 shorter events, 30.7 us)
Async XLA Ops:
  7.2 6.1 copy-start.57
  7.2 6.1 copy-start.58
  7.2 6.1 copy-start.59
  7.2 6.1 copy-start.60
  7.2 6.2 copy-start.26
  7.2 6.2 copy-start.27
  7.2 6.2 copy-start.28
  7.3 6.2 copy-start.7
  7.3 6.2 copy-start.29
  7.3 128.9 %all-gather.3.cloned.1.call-start = ((), (), s32[]{:S(2)}) async-start(), calls=%async_computation.2 | async-start | bytes 2621440 | tf_op jit(solution)/shard_map/all_gather | solution.py:1310
  10.5 2.9 copy-start.55
  88.5 1.9 copy-start.53
  91.3 245.0 %all-gather.5.cloned.1.call-start = ((), (), s32[]{:S(2)}) async-start(), calls=%async_computation.3 | async-start | bytes 10813440 | tf_op jit(solution)/shard_map/all_gather | solution.py:1462
  91.9 3.5 copy-start.36
  99.4 3.9 copy-start.40
  99.5 7.9 %copy-start.49 = (bf16[176,2048]{1,0:T(8,128)(2,1)S(1)}, bf16[176,2048]{1,0:T(8,128)(2,1)}, u32[]{:S(2)}) copy-start(bf16[176,2048]{1,0:T(8,128)(2,1)} %param.32) | copy-start | bytes 2162692
  99.5 7.8 %copy-start.50 = (bf16[176,2048]{1,0:T(8,128)(2,1)S(1)}, bf16[176,2048]{1,0:T(8,128)(2,1)}, u32[]{:S(2)}) copy-start(bf16[176,2048]{1,0:T(8,128)(2,1)} %param.31) | copy-start | bytes 2162692
  99.5 7.8 %copy-start.51 = (bf16[176,2048]{1,0:T(8,128)(2,1)S(1)}, bf16[176,2048]{1,0:T(8,128)(2,1)}, u32[]{:S(2)}) copy-start(bf16[176,2048]{1,0:T(8,128)(2,1)} %param.33) | copy-start | bytes 2162692
  121.3 51.5 %copy-start = (bf16[1024,1536]{1,0:T(8,128)(2,1)}, bf16[1024,1536]{1,0:T(8,128)(2,1)S(1)}, u32[]{:S(2)}) copy-start(bf16[1024,1536]{1,0:T(8,128)(2,1)S(1)} %get-tuple-element.244) | copy-start | bytes 9437188
  172.8 418.8 %reduce-scatter.3.cloned.1.call-start = ((), (), s32[]{:S(2)}) async-start(), calls=%async_computation.4 | async-start | bytes 10813440 | tf_op jit(solution)/shard_map/reduce_scatter | solution.py:1509
  176.0 21.5 %collective-permute-start.1 = (bf16[4,4,64,512]{3,2,1,0:T(8,128)(2,1)}, bf16[4,4,64,512]{3,2,1,0:T(8,128)(2,1)}, u32[]{:S(2)}, u32[]{:S(2)}) collective-permute-start(bf16[4,4,64,512]{3,2,1,0:T(8,128)(2,1)} %reshape_squeeze.6), channel_id=1, source_target_pairs={{0,1},{1,0},{2,3},{3,2},{4,5},{5,4},{6,7},{7,6},{8,9},{9,8},{10,11... | collective-permute-start | bytes 3145736 | tf_op jit(solution)/shard_map/ppermute | solution.py:1307
  176.3 43.6 %collective-permute-start = (bf16[4,64,2048]{2,1,0:T(8,128)(2,1)S(1)}, bf16[4,64,2048]{2,1,0:T(8,128)(2,1)}, u32[]{:S(2)}, u32[]{:S(2)}) collective-permute-start(bf16[4,64,2048]{2,1,0:T(8,128)(2,1)S(1)} %get-tuple-element.214), channel_id=1, source_target_pairs={{0,1},{1,0},{2,3},{3,2},{4,5},{5,4},{6,7},{7,6},{8,9},{9,8},{10,11... | collective-permute-start | bytes 3145736 | tf_op jit(solution)/shard_map/ppermute | solution.py:1307
  199.7 44.0 %copy-start.45 = (bf16[4,4,2,64,512]{4,3,2,1,0:T(8,128)(2,1)}, bf16[4,4,2,64,512]{4,3,2,1,0:T(8,128)(2,1)S(1)}, u32[]{:S(2)}) copy-start(bf16[4,4,2,64,512]{4,3,2,1,0:T(8,128)(2,1)S(1)} %copy.97) | copy-start | bytes 6291460
  199.7 23.0 %copy-start.34 = (bf16[1024,2048]{1,0:T(8,128)(2,1)S(1)}, bf16[1024,2048]{1,0:T(8,128)(2,1)}, u32[]{:S(2)}) copy-start(bf16[1024,2048]{1,0:T(8,128)(2,1)} %fusion.1) | copy-start | bytes 12582916
  222.7 3.7 copy-start.2
  222.7 3.7 copy-start.4
  222.7 3.7 copy-start.6
  243.7 4.3 copy-start.12
  243.7 4.3 copy-start.30
  243.7 4.3 copy-start.8
  335.0 1.3 copy-start.9
  363.3 18.1 %copy-start.32 = (bf16[2048,704]{1,0:T(8,128)(2,1)}, bf16[2048,704]{1,0:T(8,128)(2,1)S(1)}, u32[]{:S(2)}) copy-start(bf16[2048,704]{1,0:T(8,128)(2,1)S(1)} %get-tuple-element.92.product) | copy-start | bytes 8650756
  363.3 11.5 %copy-start.61 = (bf16[8,256,2048]{2,1,0:T(8,128)(2,1)S(1)}, bf16[8,256,2048]{2,1,0:T(8,128)(2,1)}, u32[]{:S(2)}) copy-start(bf16[8,256,2048]{2,1,0:T(8,128)(2,1)} %get-tuple-element.86) | copy-start | bytes 25165828
  363.3 11.5 %copy-start.63 = (bf16[2048,704]{1,0:T(8,128)(2,1)S(1)}, bf16[2048,704]{1,0:T(8,128)(2,1)}, u32[]{:S(2)}) copy-start(bf16[2048,704]{1,0:T(8,128)(2,1)} %get-tuple-element.93.grad_gate) | copy-start | bytes 8650756
  363.3 18.1 %slice-start = ((s8[8388608]{0:T(1024)(128)(4,1)}), s8[4194304]{0:T(1024)(128)(4,1)S(1)}, s32[]{:S(2)}) async-start(s8[8388608]{0:T(1024)(128)(4,1)} %bitcast.285), calls=%async_computation.6 | async-start | bytes 8388608
  374.8 6.6 slice-start.1
  391.9 241.5 %reduce-scatter.5.cloned.1.call-start = ((), (), s32[]{:S(2)}) async-start(), calls=%async_computation.5 | async-start | bytes 1310720 | tf_op jit(solution)/shard_map/reduce_scatter | solution.py:1313
  394.1 1.9 copy-start.33
  396.0 26.0 %copy-start.10 = (f32[256,2048]{1,0:T(8,128)S(1)}, f32[256,2048]{1,0:T(8,128)}, u32[]{:S(2)}) copy-start(f32[256,2048]{1,0:T(8,128)} %copy-done.9) | copy-start | bytes 6291460
  422.1 66.2 %copy-start.31 = (bf16[8,128,512]{2,1,0:T(8,128)(2,1)S(1)}, bf16[8,128,512]{2,1,0:T(8,128)(2,1)}, u32[]{:S(2)}) copy-start(bf16[8,128,512]{2,1,0:T(8,128)(2,1)} %copy-done.30) | copy-start | bytes 3145732
  488.2 5.4 copy-start.17
  488.3 7.6 copy-start.62
  493.6 6.4 copy-start.37
  493.7 2.7 copy-start.46
  494.7 29.5 %collective-permute-start.2 = (bf16[4,4,64,512]{3,2,1,0:T(8,128)(2,1)}, bf16[4,4,64,512]{3,2,1,0:T(8,128)(2,1)}, u32[]{:S(2)}, u32[]{:S(2)}) collective-permute-start(bf16[4,4,64,512]{3,2,1,0:T(8,128)(2,1)} %select_bitcast_fusion), channel_id=1, source_target_pairs={{0,1},{1,0},{2,3},{3,2},{4,5},{5,4},{6,7},{7,6},{8,9},{9,8},{10,11... | collective-permute-start | bytes 3145736 | tf_op jit(solution)/shard_map/ppermute | solution.py:1307
  496.4 5.5 copy-start.13
  524.2 4.1 copy-start.44
  524.2 2.7 copy-start.38
  588.9 2.4 copy-start.20
  588.9 2.4 copy-start.22
  591.3 61.2 %collective-permute-start.3 = (bf16[256,2048]{1,0:T(8,128)(2,1)}, bf16[256,2048]{1,0:T(8,128)(2,1)}, u32[]{:S(2)}, u32[]{:S(2)}) collective-permute-start(bf16[256,2048]{1,0:T(8,128)(2,1)} %slice_bitcast_fusion.4), channel_id=1, source_target_pairs={{0,1},{1,0},{2,3},{3,2},{4,5},{5,4},{6,7},{7,6},{8,9},{9,8},{10,11... | collective-permute-start | bytes 3145736 | tf_op jit(solution)/shard_map/ppermute | solution.py:1307
  597.2 27.6 %copy-start.35 = (bf16[1024,2048]{1,0:T(8,128)(2,1)S(1)}, bf16[1024,2048]{1,0:T(8,128)(2,1)}, u32[]{:S(2)}) copy-start(bf16[1024,2048]{1,0:T(8,128)(2,1)} %fusion.1) | copy-start | bytes 12582916
  624.8 2.0 copy-start.42
  624.8 2.7 copy-start.54
  624.8 3.6 copy-start.23
  627.7 3.4 copy-start.43
  631.0 6.0 copy-start.41
  634.5 13.9 %collective-permute-start.4 = (bf16[64,512]{1,0:T(8,128)(2,1)S(1)}, bf16[64,512]{1,0:T(8,128)(2,1)S(1)}, u32[]{:S(2)}, u32[]{:S(2)}) collective-permute-start(bf16[64,512]{1,0:T(8,128)(2,1)S(1)} %get-tuple-element.235), channel_id=1, source_target_pairs={{0,24},{8,16},{16,8},{24,0},{1,25},{9,17},{17,9},{25,1},{2,26},{10... | collective-permute-start | bytes 196616 | tf_op jit(solution)/shard_map/ppermute | solution.py:1318
  636.6 11.8 %collective-permute-start.5 = (bf16[64,512]{1,0:T(8,128)(2,1)S(1)}, bf16[64,512]{1,0:T(8,128)(2,1)S(1)}, u32[]{:S(2)}, u32[]{:S(2)}) collective-permute-start(bf16[64,512]{1,0:T(8,128)(2,1)S(1)} %get-tuple-element.234), channel_id=1, source_target_pairs={{0,16},{8,24},{16,0},{24,8},{1,17},{9,25},{17,1},{25,9},{2,18},{10... | collective-permute-start | bytes 196616 | tf_op jit(solution)/shard_map/ppermute | solution.py:1318
  636.9 11.5 %collective-permute-start.6 = (bf16[64,512]{1,0:T(8,128)(2,1)S(1)}, bf16[64,512]{1,0:T(8,128)(2,1)S(1)}, u32[]{:S(2)}, u32[]{:S(2)}) collective-permute-start(bf16[64,512]{1,0:T(8,128)(2,1)S(1)} %get-tuple-element.233), channel_id=1, source_target_pairs={{0,8},{8,0},{16,24},{24,16},{1,9},{9,1},{17,25},{25,17},{2,10},{10... | collective-permute-start | bytes 196616 | tf_op jit(solution)/shard_map/ppermute | solution.py:1318
  652.5 106.9 %copy-start.11 = (f32[256,2048]{1,0:T(8,128)S(1)}, f32[256,2048]{1,0:T(8,128)}, u32[]{:S(2)}) copy-start(f32[256,2048]{1,0:T(8,128)} %copy-done.9) | copy-start | bytes 6291460
  652.5 106.9 %copy-start.56 = (f32[256]{0:T(256)S(1)}, f32[256]{0:T(256)}, u32[]{:S(2)}) copy-start(f32[256]{0:T(256)} %copy-done.55) | copy-start | bytes 3076
  757.6 4.9 copy-start.48
  762.5 2.3 copy-start.47
  (13 other events, 14.0 us)
Sparse Core Ops, SparseCore 0:
  91.5 44.6 all-gather.2
  172.9 159.1 all-gather.4
  392.0 153.8 reduce-scatter.2
  594.0 26.2 reduce-scatter.4
